TPU v7x, 256 devices: a whole 4x4x8 slice. The times are simulated.
256 devices in a mesh: lat: 16 (over y_lo, z), lon: 16 (over y_hi, x, core).
Axes of the slice: x: 4, y: 4 (y_hi: 2, y_lo: 2; y = y_hi * 2 + y_lo), z: 8, core: 2. Of those that a mesh axis runs over, the one named last changes fastest.
Arguments:
- tokens: bfloat16 [128, 128, 2560], P('lon', 'lat'), may hold values from -6 to 6
- w_qkv: bfloat16 [16, 480, 2560], P('lat'), may hold values from -0.125 to 0.125
- key_mask: int32 [128, 128], replicated, may hold values 0 or 1
- band_of_row: int32 [128], replicated, may hold values from 0 to 31, as said below
- radius: int32 [16], replicated, may hold values from 1 to 4, as said below
- qk_scale: float32 [16], replicated, may hold values from 24 to 64
Outputs:
- attended: bfloat16 [16, 128, 20480], P('lat', 'lon')
Inputs may be any that keep to these rules, and one draw needn't show every extreme that they name: `band_of_row`: band numbers never fall along the rows; every aligned block of 8 rows holds exactly two bands, each a run of consecutive rows inside the block, and band numbers count up from 0 without gaps. Some head has radius 4.
All inputs are finite; a program needn't handle non-finite values.
Results may differ from a plain program's by a relative error of at most 0.012.
Values may be sent and summed in bfloat16 or wider, within the bound.
No kernel may reach another device: no remote copies, remote signals or barrier semaphores. Data moves between devices by JAX's collectives and lax.ppermute only.
A program may use at most 192 MiB of HBM per device.

v0:
```python
import math

import jax
import jax.numpy as jnp
from jax import lax
from jax.sharding import PartitionSpec as P

HEAD_DIM = 160
BLOCK_ROWS = 8
WIN = 4


epsilon = 1e-06


def with_halo(block, sides, width):
    for axis, dim in sides:
        count = lax.axis_size(axis)
        forward = [(i, i + 1) for i in range(count - 1)]
        forward.append((count - 1, 0))
        backward = [(target, source) for source, target in forward]
        low = lax.ppermute(
            lax.slice_in_dim(block, block.shape[dim] - width, None, axis=dim), axis, forward
        )
        high = lax.ppermute(lax.slice_in_dim(block, 0, width, axis=dim), axis, backward)
        block = jnp.concatenate([low, block, high], axis=dim)
    return block


def rms_last(values):
    return values * lax.rsqrt(jnp.mean(values * values, axis=-1, keepdims=True) + epsilon)


def zonal_terms(
    partial_value, query_blocks, keyval_blocks, query_cols, band_ids, key_usable, factor
):
    key_count = keyval_blocks.shape[2]
    slab_cols = math.gcd(key_count, 64)
    inner_rows = jnp.arange(BLOCK_ROWS)
    diagonal = (inner_rows[:, None] == inner_rows[None, :])[None, None, None, :, None, :]
    same_band = (band_ids[:, :, None] == band_ids[:, None, :])[None, :, None, :, None, :]
    scaling = factor[:, None, None, None, None, None]

    def slab_step(sums_now, slab_index):
        summed, denominator = sums_now
        slab_first = slab_index * slab_cols
        slab_part = lax.dynamic_slice_in_dim(keyval_blocks, slab_first, slab_cols, 2)
        slab_usable = lax.dynamic_slice_in_dim(key_usable, slab_first, slab_cols, 0)
        key_cols = slab_first + jnp.arange(slab_cols)
        scores = jnp.einsum(
            "hcbid,hkbjd->hbcikj", query_blocks, slab_part[0], preferred_element_type=jnp.float32
        )
        self_pair = (query_cols[:, None] == key_cols[None, :])[
            None, None, :, None, :, None
        ] & diagonal
        usable = (jnp.transpose(slab_usable, (1, 0, 2)) == 1)[None, :, None, None, :, :]
        allowed = same_band & (usable | self_pair)
        weights = jnp.where(allowed, jnp.exp(scores * scaling), 0.0)
        summed = summed + jnp.einsum(
            "hbcikj,hkbjd->hbcid",
            weights.astype(jnp.bfloat16),
            slab_part[1],
            preferred_element_type=jnp.float32,
        )
        denominator = denominator + jnp.sum(weights, axis=(4, 5))
        return ((summed, denominator), None)

    result, unused = lax.scan(slab_step, partial_value, jnp.arange(key_count // slab_cols))
    return result


def window_part(queries, rim, key_mask, col_first, reach, factor):
    head_count, col_count, flat_width = queries.shape
    n_rows = flat_width // HEAD_DIM
    blocks = n_rows // BLOCK_ROWS
    wide_cols = col_count + 2 * WIN
    query_blocks = queries.reshape(head_count, col_count, blocks, BLOCK_ROWS, HEAD_DIM)
    padded = jnp.pad(
        rim.reshape(2, head_count, wide_cols, n_rows, HEAD_DIM),
        ((0, 0), (0, 0), (0, 0), (WIN, WIN), (0, 0)),
    )
    padded = padded.reshape(2, head_count, wide_cols, blocks + 1, BLOCK_ROWS, HEAD_DIM)
    keyval = jnp.concatenate([padded[:, :, :, :-1], padded[:, :, :, 1:]], axis=4)
    circle = jnp.concatenate([key_mask[-WIN:], key_mask, key_mask[:WIN]], axis=0)
    mask_cols = lax.dynamic_slice_in_dim(circle, col_first, wide_cols, 0)
    mask_rows = jnp.pad(mask_cols, ((0, 0), (WIN, WIN))).reshape(wide_cols, blocks + 1, BLOCK_ROWS)
    mask_wide = jnp.concatenate([mask_rows[:, :-1], mask_rows[:, 1:]], axis=2)
    col_gap = jnp.abs(jnp.arange(wide_cols)[None, :] - WIN - jnp.arange(col_count)[:, None])
    row_gap = jnp.abs(jnp.arange(2 * BLOCK_ROWS)[None, :] - WIN - jnp.arange(BLOCK_ROWS)[:, None])
    reach_limit = reach[:, None, None, None, None, None]
    within = (col_gap[None, None, :, None, :, None] <= reach_limit) & (
        row_gap[None, None, None, :, None, :] <= reach_limit
    )
    self_pair = (col_gap == 0)[None, None, :, None, :, None] & (row_gap == 0)[
        None, None, None, :, None, :
    ]
    usable = (jnp.transpose(mask_wide, (1, 0, 2)) == 1)[None, :, None, None, :, :]
    allowed = within & (usable | self_pair)
    scores = jnp.einsum(
        "hcbid,hkbjd->hbcikj", query_blocks, keyval[0], preferred_element_type=jnp.float32
    )
    weights = jnp.where(allowed, jnp.exp(scores * factor[:, None, None, None, None, None]), 0.0)
    summed = jnp.einsum(
        "hbcikj,hkbjd->hbcid",
        weights.astype(jnp.bfloat16),
        keyval[1],
        preferred_element_type=jnp.float32,
    )
    denominator = jnp.sum(weights, axis=(4, 5))
    result = summed / denominator[..., None]
    return jnp.transpose(result, (0, 2, 1, 3, 4)).reshape(head_count, col_count, flat_width)


def body(tokens, w_qkv, key_mask, band_of_row, radius, qk_scale):
    head_count = w_qkv.shape[0]
    col_count = tokens.shape[0]
    n_rows = band_of_row.shape[0]
    blocks = n_rows // BLOCK_ROWS
    lat_place = lax.axis_index("lat")
    lon_place = lax.axis_index("lon")
    col_first = lon_place * col_count
    reach = lax.dynamic_slice_in_dim(radius, lat_place * head_count, head_count, 0)
    factor = lax.dynamic_slice_in_dim(qk_scale, lat_place * head_count, head_count, 0) / HEAD_DIM
    shard_piece = lax.all_gather(tokens, "lat", axis=1, tiled=True)
    normed = rms_last(shard_piece.astype(jnp.float32)).astype(jnp.bfloat16)
    projected = jnp.einsum("crd,hed->hcre", normed, w_qkv, preferred_element_type=jnp.float32)
    queries = rms_last(projected[..., :HEAD_DIM]).astype(jnp.bfloat16)
    key_rows = rms_last(projected[..., HEAD_DIM : 2 * HEAD_DIM]).astype(jnp.bfloat16)
    value_rows = projected[..., 2 * HEAD_DIM :].astype(jnp.bfloat16)
    stacked = jnp.stack([queries, key_rows, value_rows])
    qkv_rows = stacked.reshape(3, head_count, col_count, shard_piece.shape[1] * HEAD_DIM)
    keyval = qkv_rows[1:]
    rim = with_halo(keyval, (("lon", 2),), WIN)
    window = window_part(qkv_rows[0], rim, key_mask, col_first, reach, factor)
    query_blocks = qkv_rows[0].reshape(head_count, col_count, blocks, BLOCK_ROWS, HEAD_DIM)
    band_ids = band_of_row.reshape(blocks, BLOCK_ROWS)
    query_cols = col_first + jnp.arange(col_count)
    start_sums = (
        jnp.zeros((head_count, blocks, col_count, BLOCK_ROWS, HEAD_DIM), jnp.float32),
        jnp.zeros((head_count, blocks, col_count, BLOCK_ROWS), jnp.float32),
    )
    shard_piece = lax.all_gather(keyval, "lon", axis=2, tiled=True)
    key_count = shard_piece.shape[2]
    keyval_blocks = shard_piece.reshape(2, head_count, key_count, blocks, BLOCK_ROWS, HEAD_DIM)
    key_usable = key_mask.reshape(key_count, blocks, BLOCK_ROWS)
    summed, denominator = zonal_terms(
        start_sums, query_blocks, keyval_blocks, query_cols, band_ids, key_usable, factor
    )
    zonal = (summed / denominator[..., None]).astype(jnp.bfloat16)
    zonal = jnp.transpose(zonal, (0, 2, 1, 3, 4)).reshape(head_count, col_count, n_rows * HEAD_DIM)
    return (window + zonal.astype(jnp.float32)).astype(jnp.bfloat16)


def solution(mesh):
    in_specs = (P("lon", "lat", None), P("lat", None, None), P(), P(), P(), P())
    out_specs = P("lat", "lon", None)
    return jax.shard_map(body, mesh=mesh, in_specs=in_specs, out_specs=out_specs, check_vma=False)
```

profile of v0, /device:TPU:1, one launch (start us, length us, event | category | flops | bytes accessed | tf_op | source)
XLA Modules:
  0.0 362.9 jit_solution(1569820953845852)
XLA Ops:
  7.3 77.0 %all-gather.3.cloned.1.call-done = bf16[8,128,2560]{2,1,0:T(8,128)(2,1)} async-done(((bf16[8,8,2560]{2,1,0:T(8,128)(2,1)}), bf16[8,128,2560]{2,1,0:T(8,128)(2,1)}) %all-gather.3.cloned.1.call-update) | async-done | bytes 5242896 | tf_op jit(solution)/shard_map/all_gather | solution.py:124
  84.3 3.7 %fusion.26 = f32[8,128]{1,0:T(8,128)S(1)} fusion(bf16[8,128,2560]{2,1,0:T(8,128)(2,1)} %all-gather.3.cloned.1.call-done), kind=kLoop, calls=%fused_computation.28 | loop fusion | flops 7863296 | bytes 5246976 | tf_op jit(solution)/shard_map/reduce_sum | solution.py:31
  88.4 2.9 fusion.41
  100.5 9.0 %collective-permute-start = (bf16[2,1,4,20480]{3,2,1,0:T(4,128)(2,1)S(1)}, bf16[2,1,4,20480]{3,2,1,0:T(4,128)(2,1)S(1)}, u32[]{:S(2)}, u32[]{:S(2)}) collective-permute-start(bf16[2,1,4,20480]{3,2,1,0:T(4,128)(2,1)S(1)} %get-tuple-element.176), channel_id=1, source_target_pairs={{0,1},{1,2},{2,3},{3,4},{4,5},{5,6},{6,7},{7,8},{8,9},{9,10},{10,1... | collective-permute-start | bytes 983048 | tf_op jit(solution)/shard_map/ppermute | solution.py:22
  111.1 1.9 slice_bitcast_fusion
  119.1 2.9 copy.101
  122.0 2.6 pad_bitcast_fusion
  125.0 2.0 fusion.39
  127.0 6.3 %fusion.28 = (f32[16,8,8]{2,1,0:T(8,128)}, f32[16,8,8,16,16]{4,2,3,1,0:T(8,128)}) fusion(f32[]{:T(128)} %bitcast.18, pred[8,8,16,16]{3,1,2,0:T(8,128)(4,1)S(1)} %copy-done.7, pred[16,16,16]{2,1,0:T(8,128)(4,1)S(1)} %copy.69, pred[8,8,16,16]{3,1,2,0:T(8,128)(4,1)S(1)} %copy-done.9, bf16[1,1,16,16,16,160]{5,4,3,2,0,1:T(8,128)(2,1)S(1)} %get-tuple-element.170, ...), kind=kOutput, calls=%fused_computation.31 | convolution fusion | flops 85195776 | bytes 2727940 | tf_op jit(solution)/shard_map/hcbid,hkbjd->hbcikj/dot_general | solution.py:99
  133.3 54.7 %all-gather.5.cloned.1.call-done = bf16[2,1,128,20480]{3,2,1,0:T(8,128)(2,1)} async-done(((bf16[2,1,8,20480]{3,2,1,0:T(8,128)(2,1)}), bf16[2,1,128,20480]{3,2,1,0:T(8,128)(2,1)}) %all-gather.5.cloned.1.call-update) | async-done | bytes 10485776 | tf_op jit(solution)/shard_map/all_gather | solution.py:142
  188.0 14.2 %copy.80 = bf16[2,1,128,20480]{2,3,0,1:T(8,128)(2,1)} copy(bf16[2,1,128,20480]{3,2,1,0:T(8,128)(2,1)} %all-gather.5.cloned.1.call-done) | data formatting | bytes 20971520 | tf_op jit(solution)/shard_map/all_gather | solution.py:142
  202.2 24.1 %copy.82 = bf16[2,1,128,16,8,160]{5,4,2,3,1,0:T(8,128)(2,1)} copy(bf16[2,1,128,16,8,160]{2,5,4,3,0,1:T(8,128)(2,1)} %bitcast.138) | data formatting | bytes 20971520
  226.3 120.8 %while.13 = (s32[]{:T(128)}, f32[1,16,8,8,160]{4,3,2,1,0:T(8,128)}, f32[1,16,8,8]{3,2,1,0:T(8,128)}, s32[2]{0:T(128)S(1)}, s32[128,16,8]{0,2,1:T(8,128)S(1)}, /*...) while((s32[]{:T(128)}, f32[1,16,8,8,160]{4,3,2,1,0:T(8,128)}, ...), condition=%wide.region_6.7_spmd.clone, body=%wide.region_4.6_spmd.clone.sunk | while | flops 339061376 | bytes 24318392 | solution.py:68
  227.7 15.3 %fusion.78 = f32[16,64,8,8,8]{4,2,3,1,0:T(8,128)} fusion(bf16[2,1,128,16,8,160]{5,4,2,3,1,0:T(8,128)(2,1)} %get-tuple-element.290, s32[]{:T(128)S(6)} %select_n.46, bf16[1,8,16,8,160]{4,3,1,2,0:T(8,128)(2,1)S(1)} %get-tuple-element.291), kind=kOutput, calls=%fused_computation.5.clone.1 | convolution fusion | flops 167772160 | bytes 6619140 | tf_op jit(solution)/shard_map/while/body/eval_jaxpr/hcbid,hkbjd->hbcikj/dot_general | solution.py:50
  243.1 24.3 %copy.138 = f32[16,64,8,8,8]{1,2,4,3,0:T(8,128)} copy(f32[16,64,8,8,8]{4,2,3,1,0:T(8,128)} %fusion.78) | data formatting | bytes 4194304 | tf_op jit(solution)/shard_map/while/body/eval_jaxpr/hcbid,hkbjd->hbcikj/dot_general | solution.py:50
  267.8 8.9 %fusion.81 = (f32[16,8,8]{2,1,0:T(8,128)S(1)}, bf16[16,8,8,64,8]{3,4,2,1,0:T(8,128)(2,1)S(1)}) fusion(f32[16,64,8,8,8]{1,2,4,3,0:T(8,128)} %copy.138, f32[]{:T(128)} %bitcast.137, pred[8,8,64,8]{2,3,1,0:T(8,128)(4,1)S(1)} %broadcast_and_fusion.4, pred[16,64,8]{1,2,0:T(8,128)(4,1)S(1)} %fusion.80, pred[16,8,8]{2,1,0:T(8,128)(4,1)S(1)} %compare_bitcast_fusion.2), kind=kLoop, calls=%fused_computation.9.clone.1 | loop fusion | flops 3144704 | bytes 3191812 | tf_op jit(solution)/shard_map/while/body/eval_jaxpr/reduce_sum | solution.py:65
  276.7 4.5 %dynamic-slice_bitcast_fusion.6 = bf16[64,16,8,160,1]{3,2,0,1,4:T(8,128)(2,1)} fusion(bf16[2,1,128,16,8,160]{5,4,2,3,1,0:T(8,128)(2,1)} %get-tuple-element.290, s32[]{:T(128)S(6)} %add.153, s32[]{:T(128)S(6)} %select_n.46), kind=kLoop, calls=%fused_computation.3.clone.1 | loop fusion | bytes 5242888 | tf_op jit(solution)/shard_map/reshape.18
  281.2 4.4 %fusion.82 = f32[1,16,8,8,160]{4,3,2,1,0:T(8,128)} fusion(bf16[64,16,8,160,1]{3,2,0,1,4:T(8,128)(2,1)} %dynamic-slice_bitcast_fusion.6, bf16[16,8,8,64,8]{3,4,2,1,0:T(8,128)(2,1)S(1)} %get-tuple-element.253, f32[1,16,8,8,160]{4,3,2,1,0:T(8,128)} %get-tuple-element.271, pred[]{:T(512)S(6)} %compare.5), kind=kOutput, calls=%fused_computation.13.clone.1 | convolution fusion | flops 168099840 | bytes 4980737 | tf_op jit(solution)/shard_map/while/body/eval_jaxpr/hbcikj,hkbjd->hbcid/dot_general | solution.py:59
  287.6 15.3 %fusion.78 = f32[16,64,8,8,8]{4,2,3,1,0:T(8,128)} fusion(bf16[2,1,128,16,8,160]{5,4,2,3,1,0:T(8,128)(2,1)} %get-tuple-element.290, s32[]{:T(128)S(6)} %select_n.46, bf16[1,8,16,8,160]{4,3,1,2,0:T(8,128)(2,1)S(1)} %get-tuple-element.291), kind=kOutput, calls=%fused_computation.5.clone.1 | convolution fusion | flops 167772160 | bytes 6619140 | tf_op jit(solution)/shard_map/while/body/eval_jaxpr/hcbid,hkbjd->hbcikj/dot_general | solution.py:50
  302.9 24.3 %copy.138 = f32[16,64,8,8,8]{1,2,4,3,0:T(8,128)} copy(f32[16,64,8,8,8]{4,2,3,1,0:T(8,128)} %fusion.78) | data formatting | bytes 4194304 | tf_op jit(solution)/shard_map/while/body/eval_jaxpr/hcbid,hkbjd->hbcikj/dot_general | solution.py:50
  327.7 8.9 %fusion.81 = (f32[16,8,8]{2,1,0:T(8,128)S(1)}, bf16[16,8,8,64,8]{3,4,2,1,0:T(8,128)(2,1)S(1)}) fusion(f32[16,64,8,8,8]{1,2,4,3,0:T(8,128)} %copy.138, f32[]{:T(128)} %bitcast.137, pred[8,8,64,8]{2,3,1,0:T(8,128)(4,1)S(1)} %broadcast_and_fusion.4, pred[16,64,8]{1,2,0:T(8,128)(4,1)S(1)} %fusion.80, pred[16,8,8]{2,1,0:T(8,128)(4,1)S(1)} %compare_bitcast_fusion.2), kind=kLoop, calls=%fused_computation.9.clone.1 | loop fusion | flops 3144704 | bytes 3191812 | tf_op jit(solution)/shard_map/while/body/eval_jaxpr/reduce_sum | solution.py:65
  336.5 4.5 %dynamic-slice_bitcast_fusion.6 = bf16[64,16,8,160,1]{3,2,0,1,4:T(8,128)(2,1)} fusion(bf16[2,1,128,16,8,160]{5,4,2,3,1,0:T(8,128)(2,1)} %get-tuple-element.290, s32[]{:T(128)S(6)} %add.153, s32[]{:T(128)S(6)} %select_n.46), kind=kLoop, calls=%fused_computation.3.clone.1 | loop fusion | bytes 5242888 | tf_op jit(solution)/shard_map/reshape.18
  341.0 4.7 %fusion.82 = f32[1,16,8,8,160]{4,3,2,1,0:T(8,128)} fusion(bf16[64,16,8,160,1]{3,2,0,1,4:T(8,128)(2,1)} %dynamic-slice_bitcast_fusion.6, bf16[16,8,8,64,8]{3,4,2,1,0:T(8,128)(2,1)S(1)} %get-tuple-element.253, f32[1,16,8,8,160]{4,3,2,1,0:T(8,128)} %get-tuple-element.271, pred[]{:T(512)S(6)} %compare.5), kind=kOutput, calls=%fused_computation.13.clone.1 | convolution fusion | flops 168099840 | bytes 4980737 | tf_op jit(solution)/shard_map/while/body/eval_jaxpr/hbcikj,hkbjd->hbcid/dot_general | solution.py:59
  347.2 7.3 %fusion.52 = bf16[1,8,16,8,160]{4,3,1,2,0:T(8,128)(2,1)S(1)} fusion(bf16[1,1,16,16,16,160]{5,4,3,2,0,1:T(8,128)(2,1)} %get-tuple-element.171, f32[16,8,8,16,16]{4,2,3,1,0:T(8,128)} %get-tuple-element.185, f32[]{:T(128)} %bitcast.18, pred[8,8,16,16]{3,1,2,0:T(8,128)(4,1)S(1)} %copy-done.8, pred[16,16,16]{2,1,0:T(8,128)(4,1)S(1)} %copy-done.12, ...), kind=kOutput, calls=%fused_computation.54 | convolution fusion | flops 86179840 | bytes 3387396 | tf_op jit(solution)/shard_map/hbcikj,hkbjd->hbcid/dot_general | solution.py:103
  (98 shorter events, 23.3 us)
Async XLA Ops:
  6.5 81.5 %copy-start = (bf16[1,480,2560]{2,1,0:T(8,128)(2,1)S(1)}, bf16[1,480,2560]{2,1,0:T(8,128)(2,1)}, u32[]{:S(2)}) copy-start(bf16[1,480,2560]{2,1,0:T(8,128)(2,1)} %param.9) | copy-start | bytes 7372804
  6.5 77.8 %all-gather.3.cloned.1.call-start = ((), (), s32[]{:S(2)}) async-start(), calls=%async_computation | async-start | bytes 5570560 | tf_op jit(solution)/shard_map/all_gather | solution.py:124
  7.3 180.7 %all-gather.5.cloned.1.call-start = ((), (), s32[]{:S(2)}) async-start(), calls=%async_computation.1 | async-start | bytes 11141120 | tf_op jit(solution)/shard_map/all_gather | solution.py:142
  84.3 4.0 %copy-start.3 = (bf16[8,128,2560]{2,1,0:T(8,128)(2,1)S(1)}, bf16[8,128,2560]{2,1,0:T(8,128)(2,1)}, u32[]{:S(2)}) copy-start(bf16[8,128,2560]{2,1,0:T(8,128)(2,1)} %all-gather.3.cloned.1.call-done) | copy-start | bytes 15728644
  91.3 1.3 copy-start.2
  93.6 2.7 copy-start.6
  93.6 3.0 copy-start.14
  94.6 15.0 %copy-start.15 = (f32[16]{0:T(128)S(1)}, f32[16]{0:T(128)}, u32[]{:S(2)}) copy-start(f32[16]{0:T(128)} %param.13) | copy-start | bytes 196
  94.7 15.5 %copy-start.13 = (s32[128]{0:T(128)S(1)}, s32[128]{0:T(128)}, u32[]{:S(2)}) copy-start(s32[128]{0:T(128)} %param.11) | copy-start | bytes 1540
  94.7 16.2 %copy-start.5 = (bf16[1,8,128,160]{2,3,1,0:T(8,128)(2,1)S(1)}, bf16[1,8,128,160]{2,3,1,0:T(8,128)(2,1)}, u32[]{:S(2)}) copy-start(bf16[1,8,128,160]{2,3,1,0:T(8,128)(2,1)} %get-tuple-element.174) | copy-start | bytes 983044
  95.5 0.8 copy-start.4
  100.5 13.0 %collective-permute-start = (bf16[2,1,4,20480]{3,2,1,0:T(4,128)(2,1)S(1)}, bf16[2,1,4,20480]{3,2,1,0:T(4,128)(2,1)S(1)}, u32[]{:S(2)}, u32[]{:S(2)}) collective-permute-start(bf16[2,1,4,20480]{3,2,1,0:T(4,128)(2,1)S(1)} %get-tuple-element.176), channel_id=1, source_target_pairs={{0,1},{1,2},{2,3},{3,4},{4,5},{5,6},{6,7},{7,8},{8,9},{9,10},{10,1... | collective-permute-start | bytes 983048 | tf_op jit(solution)/shard_map/ppermute | solution.py:22
  109.4 6.8 %collective-permute-start.1 = (bf16[2,1,4,20480]{3,2,1,0:T(4,128)(2,1)S(1)}, bf16[2,1,4,20480]{3,2,1,0:T(4,128)(2,1)S(1)}, u32[]{:S(2)}, u32[]{:S(2)}) collective-permute-start(bf16[2,1,4,20480]{3,2,1,0:T(4,128)(2,1)S(1)} %get-tuple-element.177), channel_id=1, source_target_pairs={{1,0},{2,1},{3,2},{4,3},{5,4},{6,5},{7,6},{8,7},{9,8},{10,9},{11,1... | collective-permute-start | bytes 983048 | tf_op jit(solution)/shard_map/ppermute | solution.py:25
  109.6 17.3 %copy-start.11 = (pred[16,16,16]{2,1,0:T(8,128)(4,1)}, pred[16,16,16]{2,1,0:T(8,128)(4,1)S(1)}, u32[]{:S(2)}) copy-start(pred[16,16,16]{2,1,0:T(8,128)(4,1)S(1)} %copy.69) | copy-start | bytes 12292
  125.0 2.0 copy-start.7
  125.0 2.0 copy-start.9
  226.3 120.9 %copy-start.8 = (pred[8,8,16,16]{3,1,2,0:T(8,128)(4,1)S(1)}, pred[8,8,16,16]{3,1,2,0:T(8,128)(4,1)}, u32[]{:S(2)}) copy-start(pred[8,8,16,16]{3,1,2,0:T(8,128)(4,1)} %get-tuple-element.188) | copy-start | bytes 49156
  226.3 120.9 %copy-start.10 = (pred[8,8,16,16]{3,1,2,0:T(8,128)(4,1)S(1)}, pred[8,8,16,16]{3,1,2,0:T(8,128)(4,1)}, u32[]{:S(2)}) copy-start(pred[8,8,16,16]{3,1,2,0:T(8,128)(4,1)} %get-tuple-element.189) | copy-start | bytes 49156
  226.3 120.9 %copy-start.12 = (pred[16,16,16]{2,1,0:T(8,128)(4,1)S(1)}, pred[16,16,16]{2,1,0:T(8,128)(4,1)}, u32[]{:S(2)}) copy-start(pred[16,16,16]{2,1,0:T(8,128)(4,1)} %copy-done.11) | copy-start | bytes 12292
  226.3 120.9 %copy-start.16 = (f32[16,8,8]{2,1,0:T(8,128)S(1)}, f32[16,8,8]{2,1,0:T(8,128)}, u32[]{:S(2)}) copy-start(f32[16,8,8]{2,1,0:T(8,128)} %get-tuple-element.184) | copy-start | bytes 12292
  347.2 8.9 %copy-start.1 = (bf16[1,480,2560]{2,1,0:T(8,128)(2,1)S(1)}, bf16[1,480,2560]{2,1,0:T(8,128)(2,1)}, u32[]{:S(2)}) copy-start(bf16[1,480,2560]{2,1,0:T(8,128)(2,1)} %param.9) | copy-start | bytes 7372804
Sparse Core Ops, SparseCore 0:
  9.2 75.1 all-gather.2
  96.4 91.5 all-gather.4
where the time goes:
time: 365 us; the launch traced here: 363 us
  waiting for transfers between devices  134 us (37%)
  local copies, waits for them, and re-layouts  117 us (32%)
  matrix products  56.3 us (15%)
  other arithmetic  30.2 us (8%)
  between operations  14.4 us (4%)
  starting transfers between devices  9.04 us (2%)
    all_gather x1, waiting for transfers between devices, body(): shard_piece = lax.all_gather(tokens, 'lat', axis=1, tiled=True)  77 us
    all_gather x1, waiting for transfers between devices, body(): shard_piece = lax.all_gather(keyval, 'lon', axis=2, tiled=True)  54.7 us
    dot_general x2, local copies, waits for them, and re-layouts, slab_step(): jnp.einsum('hcbid,hkbjd->hbcikj', query_blocks, slab_part[0], preferred_e...  48.7 us
    dot_general x2, matrix products, slab_step(): jnp.einsum('hcbid,hkbjd->hbcikj', query_blocks, slab_part[0], preferred_e...  30.7 us
    unnamed x40, local copies, waits for them, and re-layouts  29.6 us
    reduce_sum x2, other arithmetic, slab_step(): denominator = denominator + jnp.sum(weights, axis=(4, 5))  17.7 us
    all_gather x1, local copies, waits for them, and re-layouts, body(): shard_piece = lax.all_gather(keyval, 'lon', axis=2, tiled=True)  14.2 us
    dot_general x2, matrix products, slab_step(): jnp.einsum('hbcikj,hkbjd->hbcid', weights.astype(jnp.bfloat16), slab_part...  9.07 us
  transfers between devices with their start and end apart: 4, of which 4 were waited for; matrix products, arithmetic and copies ran while one was open for 7% of the time, Pallas kernels for 0%

commit v1 on v0

v1 whole, which is shorter than its diff:
```python
import functools

import jax
import jax.numpy as jnp
from jax import lax
from jax.experimental import pallas as pl
from jax.experimental.pallas import tpu as pltpu
from jax.sharding import Mesh, PartitionSpec as P

HEAD_DIM = 160
QKV = 3 * HEAD_DIM
ROWS = 8
WIN = 4
COLS = 128
HALF = COLS // 2
KEY_ROWS = ROWS + 2 * WIN
EPS = 1e-06
BIG = 1e30
LOG2E = 1.4426950408889634
LAT, LON = 16, 16
AXES = ("y_lo", "z", "y_hi", "x", "core")
SIZES = (2, 8, 2, 4, 2)
NT = (((1,), (1,)), ((), ()))
MIB = 1024 * 1024


def place_of(block):
    y_lo, rest = block // 8, block % 8
    side, k = rest // 4, rest % 4
    return y_lo, side ^ y_lo, k if side == 0 else 3 - k


def block_of(y_lo, y_hi, x):
    side = y_hi ^ y_lo
    return y_lo * 8 + side * 4 + jnp.where(side == 0, x, 3 - x)


def flat(*pairs):
    index = 0
    for coordinate, size in pairs:
        index = index * size + coordinate
    return index


def spread_perm():
    pairs = []
    for y_lo in range(2):
        for z in range(8):
            for y_hi in range(2):
                for x in range(4):
                    _, to_y_hi, to_x = place_of(y_lo * 8 + z)
                    pairs.append(
                        (
                            flat((y_lo, 2), (z, 8), (y_hi, 2), (x, 4)),
                            flat((y_lo, 2), (y_hi * 4 + x, 8), (to_y_hi, 2), (to_x, 4)),
                        )
                    )
    return pairs


def neighbour_perm(step, cross):
    pairs = []
    for block in range(16):
        if not 0 <= block + step < 16:
            continue
        for core in range(2):
            here, there = place_of(block), place_of(block + step)
            source = flat((here[0], 2), (here[1], 2), (here[2], 4), (core, 2))
            target = flat((there[0], 2), (there[1], 2), (there[2], 4), (core ^ cross, 2))
            pairs.append((source, target))
    return pairs


def return_perm(k):
    pairs = []
    for y_lo in range(2):
        for s in range(8):
            for core in range(2):
                source = flat((y_lo, 2), (s, 8), (core, 2))
                pairs.append((source, flat((core, 2), (s ^ k, 8), (y_lo, 2))))
    return pairs


SWAP = [(0, 1), (1, 0)]


def project_kernel(flag_ref, *refs):
    shards, (own_ref, other_ref) = refs[:8], refs[8:10]
    keep, send, keep_top, keep_bottom, send_top, send_bottom, x_ref = refs[10:]
    for i in range(8):
        x_ref[64 * i : 64 * (i + 1), :] = shards[i][...]
    lane = lax.broadcasted_iota(jnp.int32, (1, QKV), 1)
    is_q = lane < HEAD_DIM
    is_k = (lane >= HEAD_DIM) & (lane < 2 * HEAD_DIM)
    for w_ref, own in ((own_ref, 1), (other_ref, 0)):
        p = lax.dot_general(x_ref[...], w_ref[...], NT, preferred_element_type=jnp.float32)
        squares = p * p
        q_mean = jnp.sum(jnp.where(is_q, squares, 0.0), axis=-1, keepdims=True) / HEAD_DIM
        k_mean = jnp.sum(jnp.where(is_k, squares, 0.0), axis=-1, keepdims=True) / HEAD_DIM
        scale = jnp.where(is_q, lax.rsqrt(q_mean + EPS), jnp.where(is_k, lax.rsqrt(k_mean + EPS), 1.0))
        p = (p * scale).reshape(8, ROWS, 8, QKV)
        for r in range(ROWS):
            row = p[:, r].reshape(HALF, QKV).astype(jnp.bfloat16)

            def store(whole, top, bottom):
                whole[r] = row
                if r < WIN:
                    top[r] = row[:, 128:]
                else:
                    bottom[r - WIN] = row[:, 128:]

            @pl.when(flag_ref[0] == own)
            def _():
                store(keep, keep_top, keep_bottom)

            @pl.when(flag_ref[0] != own)
            def _():
                store(send, send_top, send_bottom)


def project(flag, shards, own, other):
    whole = jax.ShapeDtypeStruct((ROWS, HALF, QKV), jnp.bfloat16)
    edge = jax.ShapeDtypeStruct((WIN, HALF, QKV - 128), jnp.bfloat16)
    vmem = pl.BlockSpec(memory_space=pltpu.VMEM)
    return pl.pallas_call(
        project_kernel,
        out_shape=[whole, whole, edge, edge, edge, edge],
        in_specs=[pl.BlockSpec(memory_space=pltpu.SMEM)] + [vmem] * 10,
        out_specs=[vmem] * 6,
        scratch_shapes=[pltpu.VMEM((512, own.shape[1]), jnp.bfloat16)],
        compiler_params=pltpu.CompilerParams(vmem_limit_bytes=32 * MIB),
        cost_estimate=pl.CostEstimate(
            flops=2 * 512 * 960 * 2560, bytes_accessed=8 * MIB, transcendentals=0
        ),
        name="project",
    )(flag, *shards, own, other)


def attend_kernel(ints, factor_ref, keep, other, keep_t, other_t, keep_b, other_b, bias, band, *refs):
    chunks, (ks, vs, masks, out) = refs[:8], refs[8:]
    z, core, radius, main = ints[0], ints[1], ints[2], ints[3]
    factor = factor_ref[0]
    ones = jnp.where(lax.broadcasted_iota(jnp.int32, (HALF, 96), 1) == 0, 1.0, 0.0).astype(jnp.bfloat16)

    def place(row, half, key, value):
        at = pl.ds(row * COLS + half * HALF, HALF)
        ks[at, :] = key
        vs[at, :HEAD_DIM] = value
        vs[at, HEAD_DIM:] = ones

    for half, (body, top, bottom) in enumerate(((keep, keep_t, keep_b), (other, other_t, other_b))):
        for r in range(ROWS):
            whole = body[r]
            place(WIN + r, half, whole[:, HEAD_DIM : 2 * HEAD_DIM], whole[:, 2 * HEAD_DIM :])
        for r in range(WIN):
            for edge, row in ((top, r), (bottom, r + WIN + ROWS)):
                whole = edge[r]
                place(row, half, whole[:, 32 : 32 + HEAD_DIM], whole[:, 32 + HEAD_DIM :])

    def column(shape, dim):
        at = lax.broadcasted_iota(jnp.int32, shape, dim)
        return ((z + (at >> 3)) & 7) * 16 + (core ^ (at >> 6)) * 8 + (at & 7)

    gap = (column((COLS, COLS), 0) - column((COLS, COLS), 1) + radius) & (COLS - 1)
    near = jnp.where(gap <= 2 * radius, 1.0, 0.0)
    for d in range(WIN + 1):
        masks[d] = jnp.where(radius >= d, near, 0.0)
    eye = lax.broadcasted_iota(jnp.int32, (COLS, COLS), 0) == lax.broadcasted_iota(jnp.int32, (COLS, COLS), 1)

    for r in range(ROWS):
        query = jnp.concatenate([keep[r][:, :HEAD_DIM], other[r][:, :HEAD_DIM]], axis=0)
        zonal_parts, window_parts = [], []
        for row in range(KEY_ROWS):
            inside = WIN <= row < WIN + ROWS
            near_row = abs(row - WIN - r) <= WIN
            if not (inside or near_row):
                continue
            scores = lax.dot_general(
                query, ks[row * COLS : (row + 1) * COLS, :], NT, preferred_element_type=jnp.float32
            )
            shift = bias[row : row + 1, :]
            if row - WIN == r:
                shift = jnp.where(eye, 0.0, shift)
            weights = jnp.exp2(scores * factor + shift)
            if inside:
                same = band[r * ROWS + row - WIN]
                zonal_parts.append((weights * same).astype(jnp.bfloat16))
            if near_row:
                window_parts.append((weights * masks[abs(row - WIN - r)]).astype(jnp.bfloat16))
        zonal = jnp.dot(
            jnp.concatenate(zonal_parts, axis=1),
            vs[WIN * COLS : (WIN + ROWS) * COLS, :],
            preferred_element_type=jnp.float32,
        )
        window = jnp.dot(
            jnp.concatenate(window_parts, axis=1),
            vs[r * COLS : (r + 2 * WIN + 1) * COLS, :],
            preferred_element_type=jnp.float32,
        )
        zonal = zonal[:, :HEAD_DIM] / zonal[:, HEAD_DIM : HEAD_DIM + 1]
        window = window[:, :HEAD_DIM] / window[:, HEAD_DIM : HEAD_DIM + 1]
        total = window + zonal.astype(jnp.bfloat16).astype(jnp.float32)
        out[:, :, :, r * HEAD_DIM : (r + 1) * HEAD_DIM] = total.reshape(2, 8, 8, HEAD_DIM)
    for k in range(8):
        group = ints[4 + k]
        chunks[k][0] = out[main, group].astype(jnp.bfloat16)
        chunks[k][1] = out[1 - main, group].astype(jnp.bfloat16)


def attend(ints, factor, parts, bias, band):
    smem = pl.BlockSpec(memory_space=pltpu.SMEM)
    vmem = pl.BlockSpec(memory_space=pltpu.VMEM)
    chunk = jax.ShapeDtypeStruct((2, 8, ROWS * HEAD_DIM), jnp.bfloat16)
    return pl.pallas_call(
        attend_kernel,
        out_shape=[chunk] * 8,
        in_specs=[smem, smem] + [vmem] * 7 + [smem],
        out_specs=[vmem] * 8,
        scratch_shapes=[
            pltpu.VMEM((KEY_ROWS * COLS, HEAD_DIM), jnp.bfloat16),
            pltpu.VMEM((KEY_ROWS * COLS, 256), jnp.bfloat16),
            pltpu.VMEM((WIN + 1, COLS, COLS), jnp.float32),
            pltpu.VMEM((2, 8, 8, ROWS * HEAD_DIM), jnp.float32),
        ],
        compiler_params=pltpu.CompilerParams(vmem_limit_bytes=32 * MIB),
        cost_estimate=pl.CostEstimate(
            flops=3 * 10**9, bytes_accessed=4 * MIB, transcendentals=2 * 10**6
        ),
        name="attend",
    )(ints, factor, *parts, bias, band)


def assemble_kernel(at, *refs):
    mains, got, out = refs[:8], refs[8], refs[9]
    width = ROWS * HEAD_DIM
    for k in range(8):
        out[0, :, pl.ds(pl.multiple_of(at[k] * width, 128), width)] = mains[k][0]
        out[0, :, pl.ds(pl.multiple_of(at[8 + k] * width, 128), width)] = got[k]


def assemble(at, mains, got):
    vmem = pl.BlockSpec(memory_space=pltpu.VMEM)
    return pl.pallas_call(
        assemble_kernel,
        out_shape=jax.ShapeDtypeStruct((1, 8, LAT * ROWS * HEAD_DIM), jnp.bfloat16),
        in_specs=[pl.BlockSpec(memory_space=pltpu.SMEM)] + [vmem] * 9,
        out_specs=vmem,
        name="assemble",
    )(at, *mains, got)


def body(tokens, w_qkv, key_mask, band_of_row, radius, qk_scale):
    y_lo, z, y_hi, x, core = (lax.axis_index(a) for a in AXES)
    sector = y_hi * 4 + x
    block = block_of(y_lo, y_hi, x)
    head = core * 8 + z
    model = tokens.shape[-1]

    wide = tokens.astype(jnp.float32)
    normed = wide * lax.rsqrt(jnp.mean(wide * wide, axis=-1, keepdims=True) + EPS)
    normed = jnp.transpose(normed.astype(jnp.bfloat16), (1, 0, 2)).reshape(64, model)
    first = lax.ppermute(normed, ("y_lo", "z", "y_hi", "x"), spread_perm())

    own = w_qkv[0]
    rows = QKV // 2
    half = lax.dynamic_slice_in_dim(own, core * rows, rows, 0)
    mine = lax.ppermute(half, "y_lo", SWAP)
    theirs = lax.ppermute(mine, "core", SWAP)
    other = jnp.concatenate(
        [jnp.where(core == 0, mine, theirs), jnp.where(core == 0, theirs, mine)], axis=0
    )

    up = [(i, (i + 1) % 8) for i in range(8)]
    down = [(i, (i - 1) % 8) for i in range(8)]
    shards = [first] + [None] * 7
    a = b = first
    for k in range(1, 4):
        a = lax.ppermute(a, "z", up)
        b = lax.ppermute(b, "z", down)
        shards[8 - k] = a
        shards[k] = b
    a = lax.ppermute(a[:32], "z", up)
    b = lax.ppermute(b[32:], "z", down)
    shards[4] = jnp.concatenate([a, b], axis=0)

    flag = jnp.where(core == y_lo, 1, 0).astype(jnp.int32).reshape(1)
    keep, send, keep_top, keep_bottom, send_top, send_bottom = project(flag, shards, own, other)

    ring = ("y_lo", "y_hi", "x", "core")
    received = lax.ppermute(send, "core", SWAP)
    keep_t = lax.ppermute(keep_bottom, ring, neighbour_perm(1, 0))
    keep_b = lax.ppermute(keep_top, ring, neighbour_perm(-1, 0))
    other_t = lax.ppermute(send_bottom, ring, neighbour_perm(1, 1))
    other_b = lax.ppermute(send_top, ring, neighbour_perm(-1, 1))

    padded = jnp.pad(key_mask, ((0, 0), (WIN, WIN)))
    usable = lax.dynamic_slice_in_dim(padded, block * ROWS, KEY_ROWS, 1)
    usable = usable.reshape(8, 2, 8, KEY_ROWS)
    twice = jnp.concatenate([usable, usable], axis=0)
    usable = lax.dynamic_slice_in_dim(twice, z, 8, 0)
    usable = jnp.where(core == 0, usable, usable[:, ::-1])
    bias = jnp.where(jnp.transpose(usable, (3, 1, 0, 2)).reshape(KEY_ROWS, COLS) == 1, 0.0, -BIG)
    ids = lax.dynamic_slice_in_dim(band_of_row, block * ROWS, ROWS, 0)
    band = (ids[:, None] == ids[None, :]).astype(jnp.float32).reshape(ROWS * ROWS)

    groups = [((sector ^ k) - z) & 7 for k in range(8)]
    reach = lax.dynamic_index_in_dim(radius, head, keepdims=False)
    ints = jnp.stack([z, core, reach, core ^ y_lo] + groups).astype(jnp.int32)
    factor = lax.dynamic_slice_in_dim(qk_scale, head, 1, 0) / HEAD_DIM * LOG2E
    parts = (keep, received, keep_t, other_t, keep_b, other_b)
    chunks = attend(ints, factor, parts, bias, band)

    landed = [lax.ppermute(chunks[k], ring, return_perm(k)) for k in range(8)]
    give = jnp.stack([part[1] for part in landed])
    got = lax.ppermute(give, "core", SWAP)
    at = []
    for from_y_lo in (core, 1 - core):
        for k in range(8):
            source = sector ^ k
            at.append(block_of(from_y_lo, source >> 2, source & 3))
    return assemble(jnp.stack(at).astype(jnp.int32), landed, got)


def solution(mesh):
    wide = Mesh(mesh.devices.reshape(SIZES), AXES)
    lat, lon = ("y_lo", "z"), ("y_hi", "x", "core")
    in_specs = (P(lon, lat, None), P(lat, None, None), P(), P(), P(), P())
    out_specs = P(lat, lon, None)
    return jax.shard_map(body, mesh=wide, in_specs=in_specs, out_specs=out_specs, check_vma=False)
```

time: 365 us -> 147 us (0.40)
  local copies, waits for them, and re-layouts: 117 us -> 8.99 us
  waiting for transfers between devices: 134 us -> 33.1 us
  starting transfers between devices: 9.04 us -> 89.7 us
  matrix products: 56.3 us -> 0 us
  other arithmetic: 30.2 us -> 2.4 us
  between operations: 14.4 us -> 1.16 us
  Pallas kernels: 0 us -> 9.76 us
    all_gather x2 -> x0, waiting for transfers between devices: 132 us -> none  [the longest x1 77 us: body(): shard_piece = lax.all_gather(tokens, 'lat', axis=1, tiled=True)]
    ppermute x2 -> x25, starting transfers between devices: 9 us -> 89.7 us  [the longest x3 39.1 us: body(): a = lax.ppermute(a, 'z', up)]
    dot_general x7 -> x0, matrix products: 56.3 us -> none  [the longest x2 30.7 us: slab_step(): jnp.einsum('hcbid,hkbjd->hbcikj', query_blocks, slab_part[0], preferred_e...]
    dot_general x2 -> x0, local copies, waits for them, and re-layouts: 48.7 us -> none  [slab_step(): jnp.einsum('hcbid,hkbjd->hbcikj', query_blocks, slab_part[0], preferred_e...]
    ppermute x2 -> x25, waiting for transfers between devices: 1.68 us -> 33.1 us  [the longest x3 10.4 us: body(): a = lax.ppermute(a, 'z', up)]
    unnamed x40 -> x43, local copies, waits for them, and re-layouts: 29.6 us -> 4.74 us
    reduce_sum x4 -> x1, other arithmetic: 21.5 us -> 0.15 us  [body(): jnp.mean(wide * wide, axis=-1, keepdims=True) + EPS]
    all_gather x1 -> x0, local copies, waits for them, and re-layouts: 14.2 us -> none  [body(): shard_piece = lax.all_gather(keyval, 'lon', axis=2, tiled=True)]
  transfers between devices with their start and end apart: 4 -> 25, of which waited for: 4 -> 12; matrix products, arithmetic and copies ran while one was open for 7% -> 2% of each run, Pallas kernels for 0% -> 0%
where the time goes in v1:
time: 147 us; the launch traced here: 145 us
  starting transfers between devices  89.7 us (61%)
  waiting for transfers between devices  33.1 us (23%)
  Pallas kernels  9.76 us (7%)
  local copies, waits for them, and re-layouts  8.99 us (6%)
  other arithmetic  2.4 us (2%)
    ppermute x3, starting transfers between devices, body(): a = lax.ppermute(a, 'z', up)  39.1 us
    ppermute x8, starting transfers between devices, body(): landed = [lax.ppermute(chunks[k], ring, return_perm(k)) for k in range(8)]  18.2 us
    ppermute x3, waiting for transfers between devices, body(): a = lax.ppermute(a, 'z', up)  10.4 us
    ppermute x1, starting transfers between devices, body(): received = lax.ppermute(send, 'core', SWAP)  7.02 us
    ppermute x1, starting transfers between devices, body(): keep_t = lax.ppermute(keep_bottom, ring, neighbour_perm(1, 0))  6.79 us
    ppermute x8, waiting for transfers between devices, body(): landed = [lax.ppermute(chunks[k], ring, return_perm(k)) for k in range(8)]  6.63 us
    ppermute x1, starting transfers between devices, body(): theirs = lax.ppermute(mine, 'core', SWAP)  4.87 us
    unnamed x43, local copies, waits for them, and re-layouts  4.74 us
  transfers between devices with their start and end apart: 25, of which 12 were waited for; matrix products, arithmetic and copies ran while one was open for 2% of the time, Pallas kernels for 0%

profile of v1, /device:TPU:1, one launch (start us, length us, event | category | flops | bytes accessed | tf_op | source)
XLA Modules:
  0.0 145.1 jit_solution(15813944151898138192)
XLA Ops:
  1.4 2.2 %collective-permute-start.9 = (bf16[240,2560]{1,0:T(8,128)(2,1)S(1)}, bf16[240,2560]{1,0:T(8,128)(2,1)}, u32[]{:S(2)}, u32[]{:S(2)}) collective-permute-start(bf16[240,2560]{1,0:T(8,128)(2,1)S(1)} %dynamic-slice_bitcast_fusion), channel_id=1, source_target_pairs={{0,128},{128,0},{1,129},{129,1},{2,130},{130,2},{3,131},{131,3},{4... | collective-permute-start | bytes 3686408 | tf_op jit(solution)/shard_map/ppermute | solution.py:267
  4.8 34.4 %collective-permute-start.4 = (bf16[64,2560]{1,0:T(8,128)(2,1)S(1)}, bf16[64,2560]{1,0:T(8,128)(2,1)S(1)}, u32[]{:S(2)}, u32[]{:S(2)}) collective-permute-start(bf16[64,2560]{1,0:T(8,128)(2,1)S(1)} %collective-permute-done.refs_0_), channel_id=1, source_target_pairs={{0,16},{16,32},{32,48},{48,64},{64,80},{80,96},{96,112},{112,0},{1... | collective-permute-start | bytes 983048 | tf_op jit(solution)/shard_map/ppermute | solution.py:278
  39.1 1.8 %collective-permute-start.1 = (bf16[64,2560]{1,0:T(8,128)(2,1)S(1)}, bf16[64,2560]{1,0:T(8,128)(2,1)S(1)}, u32[]{:S(2)}, u32[]{:S(2)}) collective-permute-start(bf16[64,2560]{1,0:T(8,128)(2,1)S(1)} %collective-permute-done.refs_0_), channel_id=1, source_target_pairs={{0,112},{16,0},{32,16},{48,32},{64,48},{80,64},{96,80},{112,96},{1... | collective-permute-start | bytes 983048 | tf_op jit(solution)/shard_map/ppermute | solution.py:279
  40.9 4.9 %collective-permute-start.10 = (bf16[240,2560]{1,0:T(8,128)(2,1)}, bf16[240,2560]{1,0:T(8,128)(2,1)}, u32[]{:S(2)}, u32[]{:S(2)}) collective-permute-start(bf16[240,2560]{1,0:T(8,128)(2,1)} %collective-permute-done.9), channel_id=1, source_target_pairs={{0,1},{1,0},{2,3},{3,2},{4,5},{5,4},{6,7},{7,6},{8,9},{9,8},{10,11... | collective-permute-start | bytes 3686408 | tf_op jit(solution)/shard_map/ppermute | solution.py:268
  45.8 2.7 %collective-permute-start.5 = (bf16[64,2560]{1,0:T(8,128)(2,1)S(1)}, bf16[64,2560]{1,0:T(8,128)(2,1)S(1)}, u32[]{:S(2)}, u32[]{:S(2)}) collective-permute-start(bf16[64,2560]{1,0:T(8,128)(2,1)S(1)} %collective-permute-done.4.refs_7_), channel_id=1, source_target_pairs={{0,16},{16,32},{32,48},{48,64},{64,80},{80,96},{96,112},{112,0},{1... | collective-permute-start | bytes 983048 | tf_op jit(solution)/shard_map/ppermute | solution.py:278
  49.2 4.5 %collective-permute-done.5.refs_6_ = bf16[64,2560]{1,0:T(8,128)(2,1)S(1)} collective-permute-done((bf16[64,2560]{1,0:T(8,128)(2,1)S(1)}, bf16[64,2560]{1,0:T(8,128)(2,1)S(1)}, u32[]{:S(2)}, u32[]{:S(2)}) %collective-permute-start.5) | collective-permute-done | bytes 327712 | tf_op jit(solution)/shard_map/ppermute | solution.py:278
  53.6 2.1 %collective-permute-start.6 = (bf16[64,2560]{1,0:T(8,128)(2,1)S(1)}, bf16[64,2560]{1,0:T(8,128)(2,1)S(1)}, u32[]{:S(2)}, u32[]{:S(2)}) collective-permute-start(bf16[64,2560]{1,0:T(8,128)(2,1)S(1)} %collective-permute-done.5.refs_6_), channel_id=1, source_target_pairs={{0,16},{16,32},{32,48},{48,64},{64,80},{80,96},{96,112},{112,0},{1... | collective-permute-start | bytes 983048 | tf_op jit(solution)/shard_map/ppermute | solution.py:278
  56.6 6.0 %collective-permute-done.6.refs_5_ = bf16[64,2560]{1,0:T(8,128)(2,1)S(1)} collective-permute-done((bf16[64,2560]{1,0:T(8,128)(2,1)S(1)}, bf16[64,2560]{1,0:T(8,128)(2,1)S(1)}, u32[]{:S(2)}, u32[]{:S(2)}) %collective-permute-start.6) | collective-permute-done | bytes 327712 | tf_op jit(solution)/shard_map/ppermute | solution.py:278
  65.7 4.3 %collective-permute-done.7 = bf16[32,2560]{1,0:T(8,128)(2,1)S(1)} collective-permute-done((bf16[32,2560]{1,0:T(8,128)(2,1)S(1)}, bf16[32,2560]{1,0:T(8,128)(2,1)S(1)}, u32[]{:S(2)}, u32[]{:S(2)}) %collective-permute-start.7) | collective-permute-done | bytes 163872 | tf_op jit(solution)/shard_map/ppermute | solution.py:282
  71.7 1.8 %broadcast_select_fusion.1 = (bf16[240,2560]{1,0:T(8,128)(2,1)S(1)}, bf16[240,2560]{1,0:T(8,128)(2,1)S(1)}) fusion(bf16[240,2560]{1,0:T(8,128)(2,1)} %collective-permute-done.9, bf16[240,2560]{1,0:T(8,128)(2,1)} %collective-permute-done.10, pred[]{:T(512)S(6)} %eq.99), kind=kLoop, calls=%fused_computation.3 | loop fusion | flops 1228800 | bytes 4915201 | tf_op jit(solution)/shard_map/jit(_where)/select_n | solution.py:270
  75.2 3.6 %project.1 = (bf16[8,64,480]{2,1,0:T(8,128)(2,1)S(1)}, bf16[8,64,480]{2,1,0:T(8,128)(2,1)S(1)}, bf16[4,64,352]{2,1,0:T(8,128)(2,1)S(1)}, bf16[4,64,352]{2,1,0:T(...) custom-call(s32[1]{0:T(128)} %bitcast.27.flag_ref, ...), custom_call_target="tpu_custom_call" | custom-call | flops 2516582400 | bytes 8388608 | tf_op jit(solution)/shard_map/project/pallas_call | solution.py:125
  80.3 7.0 %collective-permute-start.11 = (bf16[8,64,480]{2,1,0:T(8,128)(2,1)S(1)}, bf16[8,64,480]{2,1,0:T(8,128)(2,1)S(1)}, u32[]{:S(2)}, u32[]{:S(2)}) collective-permute-start(bf16[8,64,480]{2,1,0:T(8,128)(2,1)S(1)} %get-tuple-element.20), channel_id=1, source_target_pairs={{0,1},{1,0},{2,3},{3,2},{4,5},{5,4},{6,7},{7,6},{8,9},{9,8},{10,11... | collective-permute-start | bytes 1474568 | tf_op jit(solution)/shard_map/ppermute | solution.py:290
  87.6 6.8 %collective-permute-start.12 = (bf16[4,64,352]{2,1,0:T(8,128)(2,1)}, bf16[4,64,352]{2,1,0:T(8,128)(2,1)S(1)}, u32[]{:S(2)}, u32[]{:S(2)}) collective-permute-start(bf16[4,64,352]{2,1,0:T(8,128)(2,1)} %copy-done.1), channel_id=1, source_target_pairs={{0,2},{1,3},{2,4},{3,5},{4,6},{5,7},{6,14},{7,15},{14,12},{15,13},... | collective-permute-start | bytes 540680 | tf_op jit(solution)/shard_map/ppermute | solution.py:291
  94.4 3.7 %collective-permute-start.13 = (bf16[4,64,352]{2,1,0:T(8,128)(2,1)S(1)}, bf16[4,64,352]{2,1,0:T(8,128)(2,1)S(1)}, u32[]{:S(2)}, u32[]{:S(2)}) collective-permute-start(bf16[4,64,352]{2,1,0:T(8,128)(2,1)S(1)} %get-tuple-element.22), channel_id=1, source_target_pairs={{0,3},{1,2},{2,5},{3,4},{4,7},{5,6},{6,15},{7,14},{14,13},{15,12},... | collective-permute-start | bytes 540680 | tf_op jit(solution)/shard_map/ppermute | solution.py:293
  103.5 2.9 %collective-permute-done.14.keep_b = bf16[4,64,352]{2,1,0:T(8,128)(2,1)S(1)} collective-permute-done((bf16[4,64,352]{2,1,0:T(8,128)(2,1)S(1)}, bf16[4,64,352]{2,1,0:T(8,128)(2,1)S(1)}, u32[]{:S(2)}, u32[]{:S(2)}) %collective-permute-start.14) | collective-permute-done | bytes 180256 | tf_op jit(solution)/shard_map/ppermute | solution.py:292
  106.3 4.6 %collective-permute-done.15.other_b = bf16[4,64,352]{2,1,0:T(8,128)(2,1)S(1)} collective-permute-done((bf16[4,64,352]{2,1,0:T(8,128)(2,1)S(1)}, bf16[4,64,352]{2,1,0:T(8,128)(2,1)S(1)}, u32[]{:S(2)}, u32[]{:S(2)}) %collective-permute-start.15) | collective-permute-done | bytes 180256 | tf_op jit(solution)/shard_map/ppermute | solution.py:294
  111.9 4.3 %attend.1 = (bf16[2,8,1280]{2,1,0:T(8,128)(2,1)S(1)}, bf16[2,8,1280]{2,1,0:T(8,128)(2,1)S(1)}, bf16[2,8,1280]{2,1,0:T(8,128)(2,1)S(1)}, bf16[2,8,1280]{2,1,0:T(8...) custom-call(s32[12]{0:T(128)S(1)} %stack.119.ints, ...), custom_call_target="tpu_custom_call" | custom-call | flops 3000000000 | bytes 4194304 | tf_op jit(solution)/shard_map/attend/pallas_call | solution.py:214
  116.2 2.8 %collective-permute-start.16 = (bf16[2,8,1280]{2,1,0:T(8,128)(2,1)S(1)}, bf16[2,8,1280]{2,1,0:T(8,128)(2,1)S(1)}, u32[]{:S(2)}, u32[]{:S(2)}) collective-permute-start(bf16[2,8,1280]{2,1,0:T(8,128)(2,1)S(1)} %get-tuple-element.25), channel_id=1, source_target_pairs={{0,0},{1,128},{2,2},{3,130},{4,4},{5,132},{6,6},{7,134},{8,8},{9,1... | collective-permute-start | bytes 122888 | tf_op jit(solution)/shard_map/ppermute | solution.py:313
  119.0 1.8 %collective-permute-start.17 = (bf16[2,8,1280]{2,1,0:T(8,128)(2,1)S(1)}, bf16[2,8,1280]{2,1,0:T(8,128)(2,1)S(1)}, u32[]{:S(2)}, u32[]{:S(2)}) collective-permute-start(bf16[2,8,1280]{2,1,0:T(8,128)(2,1)S(1)} %get-tuple-element.26), channel_id=1, source_target_pairs={{0,2},{1,130},{2,0},{3,128},{4,6},{5,134},{6,4},{7,132},{8,10},{9,... | collective-permute-start | bytes 122888 | tf_op jit(solution)/shard_map/ppermute | solution.py:313
  120.8 4.4 %collective-permute-start.18 = (bf16[2,8,1280]{2,1,0:T(8,128)(2,1)S(1)}, bf16[2,8,1280]{2,1,0:T(8,128)(2,1)S(1)}, u32[]{:S(2)}, u32[]{:S(2)}) collective-permute-start(bf16[2,8,1280]{2,1,0:T(8,128)(2,1)S(1)} %get-tuple-element.27), channel_id=1, source_target_pairs={{0,4},{1,132},{2,6},{3,134},{4,0},{5,128},{6,2},{7,130},{8,12},{9,... | collective-permute-start | bytes 122888 | tf_op jit(solution)/shard_map/ppermute | solution.py:313
  127.6 6.7 %collective-permute-start.22 = (bf16[2,8,1280]{2,1,0:T(8,128)(2,1)S(1)}, bf16[2,8,1280]{2,1,0:T(8,128)(2,1)S(1)}, u32[]{:S(2)}, u32[]{:S(2)}) collective-permute-start(bf16[2,8,1280]{2,1,0:T(8,128)(2,1)S(1)} %get-tuple-element.31), channel_id=1, source_target_pairs={{0,12},{1,140},{2,14},{3,142},{4,8},{5,136},{6,10},{7,138},{8,4},{... | collective-permute-start | bytes 122888 | tf_op jit(solution)/shard_map/ppermute | solution.py:313
  134.5 1.8 %collective-permute-done.22.refs_6_ = bf16[2,8,1280]{2,1,0:T(8,128)(2,1)S(1)} collective-permute-done((bf16[2,8,1280]{2,1,0:T(8,128)(2,1)S(1)}, bf16[2,8,1280]{2,1,0:T(8,128)(2,1)S(1)}, u32[]{:S(2)}, u32[]{:S(2)}) %collective-permute-start.22) | collective-permute-done | bytes 40992 | tf_op jit(solution)/shard_map/ppermute | solution.py:313
  136.3 4.8 %collective-permute-done.23.refs_7_ = bf16[2,8,1280]{2,1,0:T(8,128)(2,1)S(1)} collective-permute-done((bf16[2,8,1280]{2,1,0:T(8,128)(2,1)S(1)}, bf16[2,8,1280]{2,1,0:T(8,128)(2,1)S(1)}, u32[]{:S(2)}, u32[]{:S(2)}) %collective-permute-start.23) | collective-permute-done | bytes 40992 | tf_op jit(solution)/shard_map/ppermute | solution.py:313
  143.3 1.9 %assemble.1 = bf16[1,8,20480]{2,1,0:T(8,128)(2,1)} custom-call(s32[16]{0:T(128)} %stack.107.at, bf16[2,8,1280]{2,1,0:T(8,128)(2,1)} %copy-done.6, bf16[2,8,1280]{2,1,0:T(8,128)(2,1)} %copy-done.7, bf16[2,8,1280]{2,1,0:T(8,128)(2,1)} %copy-done.8, bf16[2,8,1280]{2,1,0:T(8,128)(2,1)} %copy-done.9, bf16[2,8,1280]{2,1,0:T(8,128)(2,1)} %copy-done.10, ...), custom_call_target="tpu_custom_call" | custom-call | tf_op jit(solution)/shard_map/assemble/pallas_call | solution.py:243
  (95 shorter events, 22.3 us)
Async XLA Ops:
  1.4 39.5 %collective-permute-start.9 = (bf16[240,2560]{1,0:T(8,128)(2,1)S(1)}, bf16[240,2560]{1,0:T(8,128)(2,1)}, u32[]{:S(2)}, u32[]{:S(2)}) collective-permute-start(bf16[240,2560]{1,0:T(8,128)(2,1)S(1)} %dynamic-slice_bitcast_fusion), channel_id=1, source_target_pairs={{0,128},{128,0},{1,129},{129,1},{2,130},{130,2},{3,131},{131,3},{4... | collective-permute-start | bytes 3686408 | tf_op jit(solution)/shard_map/ppermute | solution.py:267
  4.8 41.0 %collective-permute-start.4 = (bf16[64,2560]{1,0:T(8,128)(2,1)S(1)}, bf16[64,2560]{1,0:T(8,128)(2,1)S(1)}, u32[]{:S(2)}, u32[]{:S(2)}) collective-permute-start(bf16[64,2560]{1,0:T(8,128)(2,1)S(1)} %collective-permute-done.refs_0_), channel_id=1, source_target_pairs={{0,16},{16,32},{32,48},{48,64},{64,80},{80,96},{96,112},{112,0},{1... | collective-permute-start | bytes 983048 | tf_op jit(solution)/shard_map/ppermute | solution.py:278
  39.1 10.1 %collective-permute-start.1 = (bf16[64,2560]{1,0:T(8,128)(2,1)S(1)}, bf16[64,2560]{1,0:T(8,128)(2,1)S(1)}, u32[]{:S(2)}, u32[]{:S(2)}) collective-permute-start(bf16[64,2560]{1,0:T(8,128)(2,1)S(1)} %collective-permute-done.refs_0_), channel_id=1, source_target_pairs={{0,112},{16,0},{32,16},{48,32},{64,48},{80,64},{96,80},{112,96},{1... | collective-permute-start | bytes 983048 | tf_op jit(solution)/shard_map/ppermute | solution.py:279
  40.9 30.8 %collective-permute-start.10 = (bf16[240,2560]{1,0:T(8,128)(2,1)}, bf16[240,2560]{1,0:T(8,128)(2,1)}, u32[]{:S(2)}, u32[]{:S(2)}) collective-permute-start(bf16[240,2560]{1,0:T(8,128)(2,1)} %collective-permute-done.9), channel_id=1, source_target_pairs={{0,1},{1,0},{2,3},{3,2},{4,5},{5,4},{6,7},{7,6},{8,9},{9,8},{10,11... | collective-permute-start | bytes 3686408 | tf_op jit(solution)/shard_map/ppermute | solution.py:268
  45.8 7.9 %collective-permute-start.5 = (bf16[64,2560]{1,0:T(8,128)(2,1)S(1)}, bf16[64,2560]{1,0:T(8,128)(2,1)S(1)}, u32[]{:S(2)}, u32[]{:S(2)}) collective-permute-start(bf16[64,2560]{1,0:T(8,128)(2,1)S(1)} %collective-permute-done.4.refs_7_), channel_id=1, source_target_pairs={{0,16},{16,32},{32,48},{48,64},{64,80},{80,96},{96,112},{112,0},{1... | collective-permute-start | bytes 983048 | tf_op jit(solution)/shard_map/ppermute | solution.py:278
  49.2 7.3 %collective-permute-start.2 = (bf16[64,2560]{1,0:T(8,128)(2,1)S(1)}, bf16[64,2560]{1,0:T(8,128)(2,1)S(1)}, u32[]{:S(2)}, u32[]{:S(2)}) collective-permute-start(bf16[64,2560]{1,0:T(8,128)(2,1)S(1)} %collective-permute-done.1.refs_1_), channel_id=1, source_target_pairs={{0,112},{16,0},{32,16},{48,32},{64,48},{80,64},{96,80},{112,96},{1... | collective-permute-start | bytes 983048 | tf_op jit(solution)/shard_map/ppermute | solution.py:279
  53.6 8.9 %collective-permute-start.6 = (bf16[64,2560]{1,0:T(8,128)(2,1)S(1)}, bf16[64,2560]{1,0:T(8,128)(2,1)S(1)}, u32[]{:S(2)}, u32[]{:S(2)}) collective-permute-start(bf16[64,2560]{1,0:T(8,128)(2,1)S(1)} %collective-permute-done.5.refs_6_), channel_id=1, source_target_pairs={{0,16},{16,32},{32,48},{48,64},{64,80},{80,96},{96,112},{112,0},{1... | collective-permute-start | bytes 983048 | tf_op jit(solution)/shard_map/ppermute | solution.py:278
  56.5 8.4 %collective-permute-start.3 = (bf16[64,2560]{1,0:T(8,128)(2,1)S(1)}, bf16[64,2560]{1,0:T(8,128)(2,1)S(1)}, u32[]{:S(2)}, u32[]{:S(2)}) collective-permute-start(bf16[64,2560]{1,0:T(8,128)(2,1)S(1)} %collective-permute-done.2.refs_2_), channel_id=1, source_target_pairs={{0,112},{16,0},{32,16},{48,32},{64,48},{80,64},{96,80},{112,96},{1... | collective-permute-start | bytes 983048 | tf_op jit(solution)/shard_map/ppermute | solution.py:279
  62.6 7.4 %collective-permute-start.7 = (bf16[32,2560]{1,0:T(8,128)(2,1)S(1)}, bf16[32,2560]{1,0:T(8,128)(2,1)S(1)}, u32[]{:S(2)}, u32[]{:S(2)}) collective-permute-start(bf16[32,2560]{1,0:T(8,128)(2,1)S(1)} %slice.40), channel_id=1, source_target_pairs={{0,16},{16,32},{32,48},{48,64},{64,80},{80,96},{96,112},{112,0},{1... | collective-permute-start | bytes 491528 | tf_op jit(solution)/shard_map/ppermute | solution.py:282
  64.8 6.8 %collective-permute-start.8 = (bf16[32,2560]{1,0:T(8,128)(2,1)S(1)}, bf16[32,2560]{1,0:T(8,128)(2,1)S(1)}, u32[]{:S(2)}, u32[]{:S(2)}) collective-permute-start(bf16[32,2560]{1,0:T(8,128)(2,1)S(1)} %slice.41), channel_id=1, source_target_pairs={{0,112},{16,0},{32,16},{48,32},{64,48},{80,64},{96,80},{112,96},{1... | collective-permute-start | bytes 491528 | tf_op jit(solution)/shard_map/ppermute | solution.py:283
  80.3 30.6 %collective-permute-start.11 = (bf16[8,64,480]{2,1,0:T(8,128)(2,1)S(1)}, bf16[8,64,480]{2,1,0:T(8,128)(2,1)S(1)}, u32[]{:S(2)}, u32[]{:S(2)}) collective-permute-start(bf16[8,64,480]{2,1,0:T(8,128)(2,1)S(1)} %get-tuple-element.20), channel_id=1, source_target_pairs={{0,1},{1,0},{2,3},{3,2},{4,5},{5,4},{6,7},{7,6},{8,9},{9,8},{10,11... | collective-permute-start | bytes 1474568 | tf_op jit(solution)/shard_map/ppermute | solution.py:290
  87.6 15.8 %collective-permute-start.12 = (bf16[4,64,352]{2,1,0:T(8,128)(2,1)}, bf16[4,64,352]{2,1,0:T(8,128)(2,1)S(1)}, u32[]{:S(2)}, u32[]{:S(2)}) collective-permute-start(bf16[4,64,352]{2,1,0:T(8,128)(2,1)} %copy-done.1), channel_id=1, source_target_pairs={{0,2},{1,3},{2,4},{3,5},{4,6},{5,7},{6,14},{7,15},{14,12},{15,13},... | collective-permute-start | bytes 540680 | tf_op jit(solution)/shard_map/ppermute | solution.py:291
  94.4 9.0 %collective-permute-start.13 = (bf16[4,64,352]{2,1,0:T(8,128)(2,1)S(1)}, bf16[4,64,352]{2,1,0:T(8,128)(2,1)S(1)}, u32[]{:S(2)}, u32[]{:S(2)}) collective-permute-start(bf16[4,64,352]{2,1,0:T(8,128)(2,1)S(1)} %get-tuple-element.22), channel_id=1, source_target_pairs={{0,3},{1,2},{2,5},{3,4},{4,7},{5,6},{6,15},{7,14},{14,13},{15,12},... | collective-permute-start | bytes 540680 | tf_op jit(solution)/shard_map/ppermute | solution.py:293
  98.2 8.2 %collective-permute-start.14 = (bf16[4,64,352]{2,1,0:T(8,128)(2,1)S(1)}, bf16[4,64,352]{2,1,0:T(8,128)(2,1)S(1)}, u32[]{:S(2)}, u32[]{:S(2)}) collective-permute-start(bf16[4,64,352]{2,1,0:T(8,128)(2,1)S(1)} %get-tuple-element.23), channel_id=1, source_target_pairs={{2,0},{3,1},{4,2},{5,3},{6,4},{7,5},{14,6},{15,7},{12,14},{13,15},... | collective-permute-start | bytes 540680 | tf_op jit(solution)/shard_map/ppermute | solution.py:292
  99.5 11.4 %collective-permute-start.15 = (bf16[4,64,352]{2,1,0:T(8,128)(2,1)S(1)}, bf16[4,64,352]{2,1,0:T(8,128)(2,1)S(1)}, u32[]{:S(2)}, u32[]{:S(2)}) collective-permute-start(bf16[4,64,352]{2,1,0:T(8,128)(2,1)S(1)} %get-tuple-element.24), channel_id=1, source_target_pairs={{2,1},{3,0},{4,3},{5,2},{6,5},{7,4},{14,7},{15,6},{12,15},{13,14},... | collective-permute-start | bytes 540680 | tf_op jit(solution)/shard_map/ppermute | solution.py:294
  116.2 10.3 %collective-permute-start.16 = (bf16[2,8,1280]{2,1,0:T(8,128)(2,1)S(1)}, bf16[2,8,1280]{2,1,0:T(8,128)(2,1)S(1)}, u32[]{:S(2)}, u32[]{:S(2)}) collective-permute-start(bf16[2,8,1280]{2,1,0:T(8,128)(2,1)S(1)} %get-tuple-element.25), channel_id=1, source_target_pairs={{0,0},{1,128},{2,2},{3,130},{4,4},{5,132},{6,6},{7,134},{8,8},{9,1... | collective-permute-start | bytes 122888 | tf_op jit(solution)/shard_map/ppermute | solution.py:313
  119.0 8.6 %collective-permute-start.17 = (bf16[2,8,1280]{2,1,0:T(8,128)(2,1)S(1)}, bf16[2,8,1280]{2,1,0:T(8,128)(2,1)S(1)}, u32[]{:S(2)}, u32[]{:S(2)}) collective-permute-start(bf16[2,8,1280]{2,1,0:T(8,128)(2,1)S(1)} %get-tuple-element.26), channel_id=1, source_target_pairs={{0,2},{1,130},{2,0},{3,128},{4,6},{5,134},{6,4},{7,132},{8,10},{9,... | collective-permute-start | bytes 122888 | tf_op jit(solution)/shard_map/ppermute | solution.py:313
  120.8 13.5 %collective-permute-start.18 = (bf16[2,8,1280]{2,1,0:T(8,128)(2,1)S(1)}, bf16[2,8,1280]{2,1,0:T(8,128)(2,1)S(1)}, u32[]{:S(2)}, u32[]{:S(2)}) collective-permute-start(bf16[2,8,1280]{2,1,0:T(8,128)(2,1)S(1)} %get-tuple-element.27), channel_id=1, source_target_pairs={{0,4},{1,132},{2,6},{3,134},{4,0},{5,128},{6,2},{7,130},{8,12},{9,... | collective-permute-start | bytes 122888 | tf_op jit(solution)/shard_map/ppermute | solution.py:313
  125.2 9.2 %collective-permute-start.19 = (bf16[2,8,1280]{2,1,0:T(8,128)(2,1)S(1)}, bf16[2,8,1280]{2,1,0:T(8,128)(2,1)S(1)}, u32[]{:S(2)}, u32[]{:S(2)}) collective-permute-start(bf16[2,8,1280]{2,1,0:T(8,128)(2,1)S(1)} %get-tuple-element.28), channel_id=1, source_target_pairs={{0,6},{1,134},{2,4},{3,132},{4,2},{5,130},{6,0},{7,128},{8,14},{9,... | collective-permute-start | bytes 122888 | tf_op jit(solution)/shard_map/ppermute | solution.py:313
  125.2 9.2 %collective-permute-start.20 = (bf16[2,8,1280]{2,1,0:T(8,128)(2,1)S(1)}, bf16[2,8,1280]{2,1,0:T(8,128)(2,1)S(1)}, u32[]{:S(2)}, u32[]{:S(2)}) collective-permute-start(bf16[2,8,1280]{2,1,0:T(8,128)(2,1)S(1)} %get-tuple-element.29), channel_id=1, source_target_pairs={{0,8},{1,136},{2,10},{3,138},{4,12},{5,140},{6,14},{7,142},{8,0},{... | collective-permute-start | bytes 122888 | tf_op jit(solution)/shard_map/ppermute | solution.py:313
  126.5 8.0 %collective-permute-start.21 = (bf16[2,8,1280]{2,1,0:T(8,128)(2,1)S(1)}, bf16[2,8,1280]{2,1,0:T(8,128)(2,1)S(1)}, u32[]{:S(2)}, u32[]{:S(2)}) collective-permute-start(bf16[2,8,1280]{2,1,0:T(8,128)(2,1)S(1)} %get-tuple-element.30), channel_id=1, source_target_pairs={{0,10},{1,138},{2,8},{3,136},{4,14},{5,142},{6,12},{7,140},{8,2},{... | collective-permute-start | bytes 122888 | tf_op jit(solution)/shard_map/ppermute | solution.py:313
  127.6 8.7 %collective-permute-start.22 = (bf16[2,8,1280]{2,1,0:T(8,128)(2,1)S(1)}, bf16[2,8,1280]{2,1,0:T(8,128)(2,1)S(1)}, u32[]{:S(2)}, u32[]{:S(2)}) collective-permute-start(bf16[2,8,1280]{2,1,0:T(8,128)(2,1)S(1)} %get-tuple-element.31), channel_id=1, source_target_pairs={{0,12},{1,140},{2,14},{3,142},{4,8},{5,136},{6,10},{7,138},{8,4},{... | collective-permute-start | bytes 122888 | tf_op jit(solution)/shard_map/ppermute | solution.py:313
  134.3 6.8 %collective-permute-start.23 = (bf16[2,8,1280]{2,1,0:T(8,128)(2,1)S(1)}, bf16[2,8,1280]{2,1,0:T(8,128)(2,1)S(1)}, u32[]{:S(2)}, u32[]{:S(2)}) collective-permute-start(bf16[2,8,1280]{2,1,0:T(8,128)(2,1)S(1)} %get-tuple-element.32), channel_id=1, source_target_pairs={{0,14},{1,142},{2,12},{3,140},{4,10},{5,138},{6,8},{7,136},{8,6},{... | collective-permute-start | bytes 122888 | tf_op jit(solution)/shard_map/ppermute | solution.py:313
  141.2 1.4 collective-permute-start.24
  (19 other events, 209.3 us)

commit v2 on v1

v2 whole, which is shorter than its diff:
```python
import jax
import jax.numpy as jnp
from jax import lax
from jax.experimental import pallas as pl
from jax.experimental.pallas import tpu as pltpu
from jax.sharding import Mesh, PartitionSpec as P

HEAD_DIM = 160
QKV = 3 * HEAD_DIM
ROWS = 8
WIN = 4
COLS = 128
HALF = COLS // 2
KEY_ROWS = ROWS + 2 * WIN
EPS = 1e-06
BIG = 1e30
LOG2E = 1.4426950408889634
LAT, LON = 16, 16
AXES = ("y_lo", "z", "y_hi", "x", "core")
SIZES = (2, 8, 2, 4, 2)
NT = (((1,), (1,)), ((), ()))
MIB = 1024 * 1024
SMEM = pl.BlockSpec(memory_space=pltpu.SMEM)
VMEM = pl.BlockSpec(memory_space=pltpu.VMEM)


def place_of(block):
    y_lo, rest = block // 8, block % 8
    side, k = rest // 4, rest % 4
    return y_lo, side ^ y_lo, k if side == 0 else 3 - k


def block_of(y_lo, y_hi, x):
    side = y_hi ^ y_lo
    return y_lo * 8 + side * 4 + jnp.where(side == 0, x, 3 - x)


def flat(*pairs):
    index = 0
    for coordinate, size in pairs:
        index = index * size + coordinate
    return index


def spread_perm():
    pairs = []
    for y_lo in range(2):
        for z in range(8):
            _, to_y_hi, to_x = place_of(y_lo * 8 + z)
            for s in range(8):
                for core in range(2):
                    to_z = (s + 2 * z + core) % 8
                    source = flat((y_lo, 2), (z, 8), (s, 8), (core, 2))
                    target = flat((y_lo, 2), (to_z, 8), (to_y_hi, 2), (to_x, 4), (core, 2))
                    pairs.append((source, target))
    return pairs


def neighbour_perm(step):
    pairs = []
    for block in range(16):
        if 0 <= block + step < 16:
            here, there = place_of(block), place_of(block + step)
            pairs.append(
                (
                    flat((here[0], 2), (here[1], 2), (here[2], 4)),
                    flat((there[0], 2), (there[1], 2), (there[2], 4)),
                )
            )
    return pairs


def return_perm(k):
    pairs = []
    for y_lo in range(2):
        for s in range(8):
            for core in range(2):
                source = flat((y_lo, 2), (s, 8), (core, 2))
                pairs.append((source, flat((core, 2), (s ^ k, 8), (y_lo, 2))))
    return pairs


SWAP = [(0, 1), (1, 0)]


def project_kernel(flag_ref, *refs):
    pieces, (own_ref, other_ref) = refs[:16], refs[16:18]
    keep, send, x_ref = refs[18:]
    for i in range(16):
        x_ref[32 * i : 32 * (i + 1), :] = pieces[i][...]
    lane = lax.broadcasted_iota(jnp.int32, (1, QKV), 1)
    is_q = lane < HEAD_DIM
    is_k = (lane >= HEAD_DIM) & (lane < 2 * HEAD_DIM)
    for w_ref, own in ((own_ref, 1), (other_ref, 0)):
        p = lax.dot_general(x_ref[...], w_ref[...], NT, preferred_element_type=jnp.float32)
        squares = p * p
        q_mean = jnp.sum(jnp.where(is_q, squares, 0.0), axis=-1, keepdims=True) / HEAD_DIM
        k_mean = jnp.sum(jnp.where(is_k, squares, 0.0), axis=-1, keepdims=True) / HEAD_DIM
        scale = jnp.where(is_q, lax.rsqrt(q_mean + EPS), jnp.where(is_k, lax.rsqrt(k_mean + EPS), 1.0))
        p = (p * scale).reshape(8, ROWS, 8, QKV)
        for r in range(ROWS):
            row = p[:, r].reshape(HALF, QKV).astype(jnp.bfloat16)

            @pl.when(flag_ref[0] == own)
            def _():
                keep[r] = row

            @pl.when(flag_ref[0] != own)
            def _():
                send[r] = row


def project(flag, pieces, own, other):
    whole = jax.ShapeDtypeStruct((ROWS, HALF, QKV), jnp.bfloat16)
    return pl.pallas_call(
        project_kernel,
        out_shape=[whole, whole],
        in_specs=[SMEM] + [VMEM] * 18,
        out_specs=[VMEM] * 2,
        scratch_shapes=[pltpu.VMEM((512, own.shape[1]), jnp.bfloat16)],
        compiler_params=pltpu.CompilerParams(vmem_limit_bytes=32 * MIB),
        cost_estimate=pl.CostEstimate(
            flops=2 * 512 * 960 * 2560, bytes_accessed=8 * MIB, transcendentals=0
        ),
        name="project",
    )(flag, *pieces, own, other)


def edges_kernel(keep, other, top, bottom):
    for r in range(WIN):
        for edge, row, turn in ((top, r, 16), (bottom, r + WIN, HALF - 16)):
            whole = jnp.concatenate([keep[row][:, HEAD_DIM:], other[row][:, HEAD_DIM:]], axis=1)
            edge[r, : HALF - turn] = whole[turn:]
            edge[r, HALF - turn :] = whole[:turn]


def edges(keep, other):
    edge = jax.ShapeDtypeStruct((WIN, HALF, 4 * HEAD_DIM), jnp.bfloat16)
    return pl.pallas_call(
        edges_kernel,
        out_shape=[edge, edge],
        in_specs=[VMEM] * 2,
        out_specs=[VMEM] * 2,
        cost_estimate=pl.CostEstimate(flops=0, bytes_accessed=MIB, transcendentals=0),
        name="edges",
    )(keep, other)


def put(ks, vs, row, half, key, value):
    at = pl.ds(row * COLS + half * HALF, HALF)
    ks[at, :] = key
    vs[at, :HEAD_DIM] = value
    first = lax.broadcasted_iota(jnp.int32, (HALF, 256 - HEAD_DIM), 1) == 0
    vs[at, HEAD_DIM:] = jnp.where(first, 1.0, 0.0).astype(jnp.bfloat16)


def fill_masks(ints, masks):
    base, core, radius = ints[0], ints[1], ints[2]

    def column(dim):
        at = lax.broadcasted_iota(jnp.int32, (COLS, COLS), dim)
        side = core ^ (at >> 6)
        return ((base + (at >> 3) - side) & 7) * 16 + side * 8 + (at & 7)

    gap = (column(0) - column(1) + radius) & (COLS - 1)
    near = jnp.where(gap <= 2 * radius, 1.0, 0.0)
    for d in range(WIN + 1):
        masks[d] = jnp.where(radius >= d, near, 0.0)


def query_of(keep, other, r):
    return jnp.concatenate([keep[r][:, :HEAD_DIM], other[r][:, :HEAD_DIM]], axis=0)


def scores_of(query, ks, row):
    keys = ks[row * COLS : (row + 1) * COLS, :]
    return lax.dot_general(query, keys, NT, preferred_element_type=jnp.float32)


def inner_kernel(ints, factor_ref, keep, other, bias, band, zonal_ref, window_ref, ks, vs, masks):
    factor = factor_ref[0]
    for half, part in enumerate((keep, other)):
        for r in range(ROWS):
            whole = part[r]
            put(ks, vs, r, half, whole[:, HEAD_DIM : 2 * HEAD_DIM], whole[:, 2 * HEAD_DIM :])
    fill_masks(ints, masks)
    eye = lax.broadcasted_iota(jnp.int32, (COLS, COLS), 0) == lax.broadcasted_iota(jnp.int32, (COLS, COLS), 1)
    for r in range(ROWS):
        query = query_of(keep, other, r)
        low, high = max(0, r - WIN), min(ROWS, r + WIN + 1)
        zonal_parts, window_parts = [], []
        for row in range(ROWS):
            shift = bias[WIN + row : WIN + row + 1, :]
            if row == r:
                shift = jnp.where(eye, 0.0, shift)
            weights = jnp.exp2(scores_of(query, ks, row) * factor + shift)
            zonal_parts.append((weights * band[r * ROWS + row]).astype(jnp.bfloat16))
            if low <= row < high:
                window_parts.append((weights * masks[abs(row - r)]).astype(jnp.bfloat16))
        zonal = jnp.dot(jnp.concatenate(zonal_parts, axis=1), vs[...], preferred_element_type=jnp.float32)
        window_ref[r] = jnp.dot(
            jnp.concatenate(window_parts, axis=1),
            vs[low * COLS : high * COLS, :],
            preferred_element_type=jnp.float32,
        )
        zonal_ref[r] = (zonal[:, :HEAD_DIM] / zonal[:, HEAD_DIM : HEAD_DIM + 1]).astype(jnp.bfloat16)


def inner(ints, factor, keep, other, bias, band):
    return pl.pallas_call(
        inner_kernel,
        out_shape=[
            jax.ShapeDtypeStruct((ROWS, COLS, HEAD_DIM), jnp.bfloat16),
            jax.ShapeDtypeStruct((ROWS, COLS, 256), jnp.float32),
        ],
        in_specs=[SMEM, SMEM] + [VMEM] * 3 + [SMEM],
        out_specs=[VMEM] * 2,
        scratch_shapes=[
            pltpu.VMEM((ROWS * COLS, HEAD_DIM), jnp.bfloat16),
            pltpu.VMEM((ROWS * COLS, 256), jnp.bfloat16),
            pltpu.VMEM((WIN + 1, COLS, COLS), jnp.float32),
        ],
        compiler_params=pltpu.CompilerParams(vmem_limit_bytes=32 * MIB),
        cost_estimate=pl.CostEstimate(
            flops=3 * 10**9, bytes_accessed=4 * MIB, transcendentals=10**6
        ),
        name="inner",
    )(ints, factor, keep, other, bias, band)


def outer_kernel(ints, factor_ref, keep, other, top, bottom, bias, zonal_ref, window_ref, *refs):
    chunks, (ks, vs, masks, out) = refs[:8], refs[8:]
    factor = factor_ref[0]
    for edge, first in ((top, 0), (bottom, WIN)):
        for r in range(WIN):
            whole = edge[r]
            for half in range(2):
                at = half * 2 * HEAD_DIM
                key, value = whole[:, at : at + HEAD_DIM], whole[:, at + HEAD_DIM : at + 2 * HEAD_DIM]
                put(ks, vs, first + r, half, key, value)
    fill_masks(ints, masks)
    for r in range(ROWS):
        query = query_of(keep, other, r)
        rows = range(r, WIN) if r < WIN else range(WIN, r + 1)
        parts = []
        for row in rows:
            gap = r + WIN - row if r < WIN else ROWS + row - WIN - r
            line = row if r < WIN else row + ROWS
            weights = jnp.exp2(scores_of(query, ks, row) * factor + bias[line : line + 1, :])
            parts.append((weights * masks[gap]).astype(jnp.bfloat16))
        values = vs[rows[0] * COLS : (rows[-1] + 1) * COLS, :]
        window = window_ref[r] + jnp.dot(
            jnp.concatenate(parts, axis=1), values, preferred_element_type=jnp.float32
        )
        window = window[:, :HEAD_DIM] / window[:, HEAD_DIM : HEAD_DIM + 1]
        total = window + zonal_ref[r].astype(jnp.float32)
        out[:, :, :, r * HEAD_DIM : (r + 1) * HEAD_DIM] = total.reshape(2, 8, 8, HEAD_DIM)
    for k in range(8):
        chunks[k][0] = out[ints[3], ints[4 + k]].astype(jnp.bfloat16)
        chunks[k][1] = out[1 - ints[3], ints[12 + k]].astype(jnp.bfloat16)


def outer(ints, factor, keep, other, top, bottom, bias, zonal, window):
    chunk = jax.ShapeDtypeStruct((2, 8, ROWS * HEAD_DIM), jnp.bfloat16)
    return pl.pallas_call(
        outer_kernel,
        out_shape=[chunk] * 8,
        in_specs=[SMEM, SMEM] + [VMEM] * 7,
        out_specs=[VMEM] * 8,
        scratch_shapes=[
            pltpu.VMEM((2 * WIN * COLS, HEAD_DIM), jnp.bfloat16),
            pltpu.VMEM((2 * WIN * COLS, 256), jnp.bfloat16),
            pltpu.VMEM((WIN + 1, COLS, COLS), jnp.float32),
            pltpu.VMEM((2, 8, 8, ROWS * HEAD_DIM), jnp.float32),
        ],
        compiler_params=pltpu.CompilerParams(vmem_limit_bytes=32 * MIB),
        cost_estimate=pl.CostEstimate(
            flops=10**9, bytes_accessed=4 * MIB, transcendentals=10**6
        ),
        name="outer",
    )(ints, factor, keep, other, top, bottom, bias, zonal, window)


def assemble_kernel(at, *refs):
    mains, got, out = refs[:8], refs[8], refs[9]
    width = ROWS * HEAD_DIM
    for k in range(8):
        out[0, :, pl.ds(pl.multiple_of(at[k] * width, 128), width)] = mains[k][0]
        out[0, :, pl.ds(pl.multiple_of(at[8 + k] * width, 128), width)] = got[k]


def assemble(at, mains, got):
    return pl.pallas_call(
        assemble_kernel,
        out_shape=jax.ShapeDtypeStruct((1, 8, LAT * ROWS * HEAD_DIM), jnp.bfloat16),
        in_specs=[SMEM] + [VMEM] * 9,
        out_specs=VMEM,
        name="assemble",
    )(at, *mains, got)


def body(tokens, w_qkv, key_mask, band_of_row, radius, qk_scale):
    y_lo, z, y_hi, x, core = (lax.axis_index(a) for a in AXES)
    sector = y_hi * 4 + x
    block = block_of(y_lo, y_hi, x)
    head = core * 8 + z
    model = tokens.shape[-1]

    wide = tokens.astype(jnp.float32)
    normed = wide * lax.rsqrt(jnp.mean(wide * wide, axis=-1, keepdims=True) + EPS)
    normed = jnp.transpose(normed.astype(jnp.bfloat16), (1, 0, 2)).reshape(64, model)
    first = [lax.ppermute(normed[at : at + 32], AXES, spread_perm()) for at in (0, 32)]

    own = w_qkv[0]
    rows = QKV // 2
    half = lax.dynamic_slice_in_dim(own, core * rows, rows, 0)
    *first, half = lax.optimization_barrier((*first, half))
    mine = lax.ppermute(half, "y_lo", SWAP)

    up = [(i, (i + 1) % 8) for i in range(8)]
    down = [(i, (i - 1) % 8) for i in range(8)]
    shards = [first] + [[None, None] for _ in range(7)]
    a, b = list(first), list(first)
    for k in range(1, 5):
        for h in range(2):
            if k < 4 or h == 0:
                a[h] = shards[8 - k][h] = lax.ppermute(a[h], "z", up)
            if k < 4 or h == 1:
                b[h] = shards[k][h] = lax.ppermute(b[h], "z", down)
        if k == 3:
            mine, *both = lax.optimization_barrier((mine, *a, *b))
            a, b = both[:2], both[2:]
            theirs = lax.ppermute(mine, "core", SWAP)
    other_w = jnp.concatenate(
        [jnp.where(core == 0, mine, theirs), jnp.where(core == 0, theirs, mine)], axis=0
    )
    pieces = [shards[i][h] for i in range(8) for h in range(2)]

    flag = jnp.where(core == y_lo, 1, 0).astype(jnp.int32).reshape(1)
    keep, send = project(flag, pieces, own, other_w)
    other = lax.ppermute(send, "core", SWAP)
    top_rows, bottom_rows = edges(keep, other)
    ring = ("y_lo", "y_hi", "x")
    top = lax.ppermute(bottom_rows, ring, neighbour_perm(1))
    bottom = lax.ppermute(top_rows, ring, neighbour_perm(-1))

    base = (z - 2 * block) & 7
    padded = jnp.pad(key_mask, ((0, 0), (WIN, WIN)))
    usable = lax.dynamic_slice_in_dim(padded, block * ROWS, KEY_ROWS, 1)
    usable = usable.reshape(8, 2, 8, KEY_ROWS)
    twice = jnp.concatenate([usable, usable], axis=0)
    halves = []
    for side in (core, 1 - core):
        start = ((base - side) & 7, side, 0, 0)
        halves.append(lax.dynamic_slice(twice, start, (8, 1, 8, KEY_ROWS)).reshape(HALF, KEY_ROWS))
    usable = jnp.transpose(jnp.concatenate(halves, axis=0))
    bias = jnp.where(usable == 1, 0.0, -BIG)
    ids = lax.dynamic_slice_in_dim(band_of_row, block * ROWS, ROWS, 0)
    band = (ids[:, None] == ids[None, :]).astype(jnp.float32).reshape(ROWS * ROWS)

    groups = [((sector ^ k) - base + side) & 7 for side in (y_lo, 1 - y_lo) for k in range(8)]
    reach = lax.dynamic_index_in_dim(radius, head, keepdims=False)
    ints = jnp.stack([base, core, reach, core ^ y_lo] + groups).astype(jnp.int32)
    factor = lax.dynamic_slice_in_dim(qk_scale, head, 1, 0) / HEAD_DIM * LOG2E
    zonal, window = inner(ints, factor, keep, other, bias, band)
    chunks = outer(ints, factor, keep, other, top, bottom, bias, zonal, window)

    corners = ("y_lo", "y_hi", "x", "core")
    landed = [lax.ppermute(chunks[k], corners, return_perm(k)) for k in range(8)]
    give = jnp.stack([part[1] for part in landed])
    got = lax.ppermute(give, "core", SWAP)
    at = []
    for from_y_lo in (core, 1 - core):
        for k in range(8):
            source = sector ^ k
            at.append(block_of(from_y_lo, source >> 2, source & 3))
    return assemble(jnp.stack(at).astype(jnp.int32), landed, got)


def solution(mesh):
    wide = Mesh(mesh.devices.reshape(SIZES), AXES)
    lat, lon = ("y_lo", "z"), ("y_hi", "x", "core")
    in_specs = (P(lon, lat, None), P(lat, None, None), P(), P(), P(), P())
    out_specs = P(lat, lon, None)
    return jax.shard_map(body, mesh=wide, in_specs=in_specs, out_specs=out_specs, check_vma=False)
```

time: 147 us -> 124 us (0.84); the launches traced: 145 us -> 124 us
  starting transfers between devices: 89.7 us -> 71.2 us
  waiting for transfers between devices: 33.1 us -> 25.8 us
  Pallas kernels: 9.76 us -> 13.2 us
  other arithmetic: 2.4 us -> 4.41 us
    ppermute x22 -> x27, starting transfers between devices: 82.6 us -> 62.7 us  [the longest x7 19.8 us: body(): a[h] = shards[8 - k][h] = lax.ppermute(a[h], 'z', up)]
    ppermute x22 -> x27, waiting for transfers between devices: 32.6 us -> 25.1 us  [the longest x8 6.63 us: body(): lax.ppermute(chunks[k], corners, return_perm(k))]
    pallas_call x2 -> x4, Pallas kernels: 7.91 us -> 11.3 us  [the longest x1 3.61 us: project(): pl.pallas_call(project_kernel, out_shape=[whole, whole], in_specs=[SMEM]...]
  transfers between devices with their start and end apart: 25 -> 30, of which waited for: 12 -> 16; matrix products, arithmetic and copies ran while one was open for 2% -> 5% of each run, Pallas kernels for 0% -> 3%
where the time goes in v2:
time: 124 us
  starting transfers between devices  71.2 us (57%)
  waiting for transfers between devices  25.8 us (21%)
  Pallas kernels  13.2 us (11%)
  local copies, waits for them, and re-layouts  7.95 us (6%)
  other arithmetic  4.41 us (4%)
    ppermute x7, starting transfers between devices, body(): a[h] = shards[8 - k][h] = lax.ppermute(a[h], 'z', up)  19.8 us
    ppermute x8, starting transfers between devices, body(): lax.ppermute(chunks[k], corners, return_perm(k))  18.4 us
    ppermute x2, starting transfers between devices, body(): lax.ppermute(normed[at:at + 32], AXES, spread_perm())  10.2 us
    ppermute x7, starting transfers between devices, body(): b[h] = shards[k][h] = lax.ppermute(b[h], 'z', down)  8.76 us
    ppermute x8, waiting for transfers between devices, body(): lax.ppermute(chunks[k], corners, return_perm(k))  6.63 us
    ppermute x7, waiting for transfers between devices, body(): b[h] = shards[k][h] = lax.ppermute(b[h], 'z', down)  6.62 us
    ppermute x1, starting transfers between devices, body(): theirs = lax.ppermute(mine, 'core', SWAP)  5.01 us
    ppermute x1, waiting for transfers between devices, body(): bottom = lax.ppermute(top_rows, ring, neighbour_perm(-1))  4.85 us
  transfers between devices with their start and end apart: 30, of which 16 were waited for; matrix products, arithmetic and copies ran while one was open for 5% of the time, Pallas kernels for 3%

profile of v2, /device:TPU:1, one launch (start us, length us, event | category | flops | bytes accessed | tf_op | source)
XLA Modules:
  0.0 123.8 jit_solution(18087813041858097143)
XLA Ops:
  2.4 4.4 %collective-permute-start = (bf16[32,2560]{1,0:T(8,128)(2,1)S(1)}, bf16[32,2560]{1,0:T(8,128)(2,1)S(1)}, u32[]{:S(2)}, u32[]{:S(2)}) collective-permute-start(bf16[32,2560]{1,0:T(8,128)(2,1)S(1)} %bitcast.56), channel_id=1, source_target_pairs={{0,0},{1,17},{2,16},{3,33},{4,32},{5,49},{6,48},{7,65},{8,64},{9,8... | collective-permute-start | bytes 491528 | tf_op jit(solution)/shard_map/ppermute | solution.py:312
  6.8 5.8 %collective-permute-start.1 = (bf16[32,2560]{1,0:T(8,128)(2,1)S(1)}, bf16[32,2560]{1,0:T(8,128)(2,1)S(1)}, u32[]{:S(2)}, u32[]{:S(2)}) collective-permute-start(bf16[32,2560]{1,0:T(8,128)(2,1)S(1)} %bitcast.57), channel_id=1, source_target_pairs={{0,0},{1,17},{2,16},{3,33},{4,32},{5,49},{6,48},{7,65},{8,64},{9,8... | collective-permute-start | bytes 491528 | tf_op jit(solution)/shard_map/ppermute | solution.py:312
  14.0 2.5 %collective-permute-done.1.refs_1_ = bf16[32,2560]{1,0:T(8,128)(2,1)S(1)} collective-permute-done((bf16[32,2560]{1,0:T(8,128)(2,1)S(1)}, bf16[32,2560]{1,0:T(8,128)(2,1)S(1)}, u32[]{:S(2)}, u32[]{:S(2)}) %collective-permute-start.1) | collective-permute-done | bytes 163872 | tf_op jit(solution)/shard_map/ppermute | solution.py:312
  16.5 3.6 %collective-permute-start.8 = (bf16[240,2560]{1,0:T(8,128)(2,1)S(1)}, bf16[240,2560]{1,0:T(8,128)(2,1)}, u32[]{:S(2)}, u32[]{:S(2)}) collective-permute-start(bf16[240,2560]{1,0:T(8,128)(2,1)S(1)} %dynamic-slice_bitcast_fusion), channel_id=1, source_target_pairs={{0,128},{128,0},{1,129},{129,1},{2,130},{130,2},{3,131},{131,3},{4... | collective-permute-start | bytes 3686408 | tf_op jit(solution)/shard_map/ppermute | solution.py:318
  20.0 5.4 %collective-permute-start.9 = (bf16[32,2560]{1,0:T(8,128)(2,1)S(1)}, bf16[32,2560]{1,0:T(8,128)(2,1)S(1)}, u32[]{:S(2)}, u32[]{:S(2)}) collective-permute-start(bf16[32,2560]{1,0:T(8,128)(2,1)S(1)} %collective-permute-done.refs_0_), channel_id=1, source_target_pairs={{0,16},{16,32},{32,48},{48,64},{64,80},{80,96},{96,112},{112,0},{1... | collective-permute-start | bytes 491528 | tf_op jit(solution)/shard_map/ppermute | solution.py:327
  25.4 4.7 %collective-permute-start.12 = (bf16[32,2560]{1,0:T(8,128)(2,1)S(1)}, bf16[32,2560]{1,0:T(8,128)(2,1)S(1)}, u32[]{:S(2)}, u32[]{:S(2)}) collective-permute-start(bf16[32,2560]{1,0:T(8,128)(2,1)S(1)} %collective-permute-done.1.refs_1_), channel_id=1, source_target_pairs={{0,16},{16,32},{32,48},{48,64},{64,80},{80,96},{96,112},{112,0},{1... | collective-permute-start | bytes 491528 | tf_op jit(solution)/shard_map/ppermute | solution.py:327
  30.6 3.1 %collective-permute-start.10 = (bf16[32,2560]{1,0:T(8,128)(2,1)S(1)}, bf16[32,2560]{1,0:T(8,128)(2,1)S(1)}, u32[]{:S(2)}, u32[]{:S(2)}) collective-permute-start(bf16[32,2560]{1,0:T(8,128)(2,1)S(1)} %collective-permute-done.9.refs_14_), channel_id=1, source_target_pairs={{0,16},{16,32},{32,48},{48,64},{64,80},{80,96},{96,112},{112,0},{1... | collective-permute-start | bytes 491528 | tf_op jit(solution)/shard_map/ppermute | solution.py:327
  33.6 3.4 %collective-permute-start.13 = (bf16[32,2560]{1,0:T(8,128)(2,1)S(1)}, bf16[32,2560]{1,0:T(8,128)(2,1)S(1)}, u32[]{:S(2)}, u32[]{:S(2)}) collective-permute-start(bf16[32,2560]{1,0:T(8,128)(2,1)S(1)} %collective-permute-done.12.refs_15_), channel_id=1, source_target_pairs={{0,16},{16,32},{32,48},{48,64},{64,80},{80,96},{96,112},{112,0},{1... | collective-permute-start | bytes 491528 | tf_op jit(solution)/shard_map/ppermute | solution.py:327
  38.4 3.1 %collective-permute-start.5 = (bf16[32,2560]{1,0:T(8,128)(2,1)S(1)}, bf16[32,2560]{1,0:T(8,128)(2,1)S(1)}, u32[]{:S(2)}, u32[]{:S(2)}) collective-permute-start(bf16[32,2560]{1,0:T(8,128)(2,1)S(1)} %collective-permute-done.3.refs_3_), channel_id=1, source_target_pairs={{0,112},{16,0},{32,16},{48,32},{64,48},{80,64},{96,80},{112,96},{1... | collective-permute-start | bytes 491528 | tf_op jit(solution)/shard_map/ppermute | solution.py:329
  45.6 2.9 %collective-permute-start.7 = (bf16[32,2560]{1,0:T(8,128)(2,1)S(1)}, bf16[32,2560]{1,0:T(8,128)(2,1)S(1)}, u32[]{:S(2)}, u32[]{:S(2)}) collective-permute-start(bf16[32,2560]{1,0:T(8,128)(2,1)S(1)} %collective-permute-done.5.refs_5_), channel_id=1, source_target_pairs={{0,112},{16,0},{32,16},{48,32},{64,48},{80,64},{96,80},{112,96},{1... | collective-permute-start | bytes 491528 | tf_op jit(solution)/shard_map/ppermute | solution.py:329
  50.4 2.1 %collective-permute-done.7.refs_7_ = bf16[32,2560]{1,0:T(8,128)(2,1)S(1)} collective-permute-done((bf16[32,2560]{1,0:T(8,128)(2,1)S(1)}, bf16[32,2560]{1,0:T(8,128)(2,1)S(1)}, u32[]{:S(2)}, u32[]{:S(2)}) %collective-permute-start.7) | collective-permute-done | bytes 163872 | tf_op jit(solution)/shard_map/ppermute | solution.py:329
  52.5 5.0 %collective-permute-start.17 = (bf16[240,2560]{1,0:T(8,128)(2,1)}, bf16[240,2560]{1,0:T(8,128)(2,1)}, u32[]{:S(2)}, u32[]{:S(2)}) collective-permute-start(bf16[240,2560]{1,0:T(8,128)(2,1)} %collective-permute-done.8), channel_id=1, source_target_pairs={{0,1},{1,0},{2,3},{3,2},{4,5},{5,4},{6,7},{7,6},{8,9},{9,8},{10,11... | collective-permute-start | bytes 3686408 | tf_op jit(solution)/shard_map/ppermute | solution.py:333
  62.4 2.1 %collective-permute-done.15.refs_8_ = bf16[32,2560]{1,0:T(8,128)(2,1)S(1)} collective-permute-done((bf16[32,2560]{1,0:T(8,128)(2,1)S(1)}, bf16[32,2560]{1,0:T(8,128)(2,1)S(1)}, u32[]{:S(2)}, u32[]{:S(2)}) %collective-permute-start.15) | collective-permute-done | bytes 163872 | tf_op jit(solution)/shard_map/ppermute | solution.py:327
  65.9 3.6 %project.1 = (bf16[8,64,480]{2,1,0:T(8,128)(2,1)S(1)}, bf16[8,64,480]{2,1,0:T(8,128)(2,1)S(1)}) custom-call(s32[1]{0:T(128)} %bitcast.35.flag_ref, bf16[32,2560]{1,0:T(8,128)(2,1)S(1)} %collective-permute-done.refs_0_, bf16[32,2560]{1,0:T(8,128)(2,1)S(1)} %collective-permute-done.1.refs_1_, bf16[32,2560]{1,0:T(8,128)(2,1)S(1)} %collective-permute-done.2.refs_2_, ...), custom_call_target="tpu_custom_call" | custom-call | flops 2516582400 | bytes 8388608 | tf_op jit(solution)/shard_map/project/pallas_call | solution.py:115
  73.4 2.3 %edges.1 = (bf16[4,64,640]{2,1,0:T(8,128)(2,1)}, bf16[4,64,640]{2,1,0:T(8,128)(2,1)}) custom-call(bf16[8,64,480]{2,1,0:T(8,128)(2,1)} %copy-done.1, bf16[8,64,480]{2,1,0:T(8,128)(2,1)} %copy-done.3), custom_call_target="tpu_custom_call" | custom-call | bytes 1048576 | tf_op jit(solution)/shard_map/edges/pallas_call | solution.py:139
  75.7 3.5 %collective-permute-start.19 = (bf16[4,64,640]{2,1,0:T(8,128)(2,1)}, bf16[4,64,640]{2,1,0:T(8,128)(2,1)S(1)}, u32[]{:S(2)}, u32[]{:S(2)}) collective-permute-start(bf16[4,64,640]{2,1,0:T(8,128)(2,1)} %get-tuple-element.33), channel_id=1, source_target_pairs={{0,2},{2,4},{4,6},{6,14},{14,12},{12,10},{10,8},{8,136},{136,138},... | collective-permute-start | bytes 983048 | tf_op jit(solution)/shard_map/ppermute | solution.py:344
  84.3 3.4 %inner.1 = (bf16[8,128,160]{2,1,0:T(8,128)(2,1)S(1)}, f32[8,128,256]{2,1,0:T(8,128)S(1)}) custom-call(s32[20]{0:T(128)S(1)} %stack.151.ints, f32[1]{0:T(128)S(6)} %mul.124.factor_ref, bf16[8,64,480]{2,1,0:T(8,128)(2,1)S(1)} %copy-done.2, bf16[8,64,480]{2,1,0:T(8,128)(2,1)S(1)} %copy-done.4, f32[16,128]{1,0:T(8,128)S(1)} %select_bitcast_fusion.bias, ...), custom_call_target="tpu_custom_call" | custom-call | flops 3000000000 | bytes 4194304 | tf_op jit(solution)/shard_map/inner/pallas_call | solution.py:210
  87.7 4.9 %collective-permute-done.20.bottom = bf16[4,64,640]{2,1,0:T(8,128)(2,1)S(1)} collective-permute-done((bf16[4,64,640]{2,1,0:T(8,128)(2,1)}, bf16[4,64,640]{2,1,0:T(8,128)(2,1)S(1)}, u32[]{:S(2)}, u32[]{:S(2)}) %collective-permute-start.20) | collective-permute-done | bytes 327712 | tf_op jit(solution)/shard_map/ppermute | solution.py:345
  92.5 2.1 %outer.1 = (bf16[2,8,1280]{2,1,0:T(8,128)(2,1)S(1)}, bf16[2,8,1280]{2,1,0:T(8,128)(2,1)S(1)}, bf16[2,8,1280]{2,1,0:T(8,128)(2,1)S(1)}, bf16[2,8,1280]{2,1,0:T(8,...) custom-call(s32[20]{0:T(128)S(1)} %stack.151.ints, ...), custom_call_target="tpu_custom_call" | custom-call | flops 1000000000 | bytes 4194304 | tf_op jit(solution)/shard_map/outer/pallas_call | solution.py:265
  96.5 2.7 %collective-permute-start.22 = (bf16[2,8,1280]{2,1,0:T(8,128)(2,1)S(1)}, bf16[2,8,1280]{2,1,0:T(8,128)(2,1)S(1)}, u32[]{:S(2)}, u32[]{:S(2)}) collective-permute-start(bf16[2,8,1280]{2,1,0:T(8,128)(2,1)S(1)} %get-tuple-element.38), channel_id=1, source_target_pairs={{0,2},{1,130},{2,0},{3,128},{4,6},{5,134},{6,4},{7,132},{8,10},{9,... | collective-permute-start | bytes 122888 | tf_op jit(solution)/shard_map/ppermute | solution.py:369
  99.2 2.9 %collective-permute-start.23 = (bf16[2,8,1280]{2,1,0:T(8,128)(2,1)S(1)}, bf16[2,8,1280]{2,1,0:T(8,128)(2,1)S(1)}, u32[]{:S(2)}, u32[]{:S(2)}) collective-permute-start(bf16[2,8,1280]{2,1,0:T(8,128)(2,1)S(1)} %get-tuple-element.39), channel_id=1, source_target_pairs={{0,4},{1,132},{2,6},{3,134},{4,0},{5,128},{6,2},{7,130},{8,12},{9,... | collective-permute-start | bytes 122888 | tf_op jit(solution)/shard_map/ppermute | solution.py:369
  105.7 7.2 %collective-permute-start.27 = (bf16[2,8,1280]{2,1,0:T(8,128)(2,1)S(1)}, bf16[2,8,1280]{2,1,0:T(8,128)(2,1)S(1)}, u32[]{:S(2)}, u32[]{:S(2)}) collective-permute-start(bf16[2,8,1280]{2,1,0:T(8,128)(2,1)S(1)} %get-tuple-element.43), channel_id=1, source_target_pairs={{0,12},{1,140},{2,14},{3,142},{4,8},{5,136},{6,10},{7,138},{8,4},{... | collective-permute-start | bytes 122888 | tf_op jit(solution)/shard_map/ppermute | solution.py:369
  113.1 2.1 %collective-permute-done.27.refs_6_ = bf16[2,8,1280]{2,1,0:T(8,128)(2,1)S(1)} collective-permute-done((bf16[2,8,1280]{2,1,0:T(8,128)(2,1)S(1)}, bf16[2,8,1280]{2,1,0:T(8,128)(2,1)S(1)}, u32[]{:S(2)}, u32[]{:S(2)}) %collective-permute-start.27) | collective-permute-done | bytes 40992 | tf_op jit(solution)/shard_map/ppermute | solution.py:369
  115.2 4.5 %collective-permute-done.28.refs_7_ = bf16[2,8,1280]{2,1,0:T(8,128)(2,1)S(1)} collective-permute-done((bf16[2,8,1280]{2,1,0:T(8,128)(2,1)S(1)}, bf16[2,8,1280]{2,1,0:T(8,128)(2,1)S(1)}, u32[]{:S(2)}, u32[]{:S(2)}) %collective-permute-start.28) | collective-permute-done | bytes 40992 | tf_op jit(solution)/shard_map/ppermute | solution.py:369
  (106 shorter events, 35.6 us)
Async XLA Ops:
  2.4 11.6 %collective-permute-start = (bf16[32,2560]{1,0:T(8,128)(2,1)S(1)}, bf16[32,2560]{1,0:T(8,128)(2,1)S(1)}, u32[]{:S(2)}, u32[]{:S(2)}) collective-permute-start(bf16[32,2560]{1,0:T(8,128)(2,1)S(1)} %bitcast.56), channel_id=1, source_target_pairs={{0,0},{1,17},{2,16},{3,33},{4,32},{5,49},{6,48},{7,65},{8,64},{9,8... | collective-permute-start | bytes 491528 | tf_op jit(solution)/shard_map/ppermute | solution.py:312
  6.8 9.7 %collective-permute-start.1 = (bf16[32,2560]{1,0:T(8,128)(2,1)S(1)}, bf16[32,2560]{1,0:T(8,128)(2,1)S(1)}, u32[]{:S(2)}, u32[]{:S(2)}) collective-permute-start(bf16[32,2560]{1,0:T(8,128)(2,1)S(1)} %bitcast.57), channel_id=1, source_target_pairs={{0,0},{1,17},{2,16},{3,33},{4,32},{5,49},{6,48},{7,65},{8,64},{9,8... | collective-permute-start | bytes 491528 | tf_op jit(solution)/shard_map/ppermute | solution.py:312
  16.5 36.0 %collective-permute-start.8 = (bf16[240,2560]{1,0:T(8,128)(2,1)S(1)}, bf16[240,2560]{1,0:T(8,128)(2,1)}, u32[]{:S(2)}, u32[]{:S(2)}) collective-permute-start(bf16[240,2560]{1,0:T(8,128)(2,1)S(1)} %dynamic-slice_bitcast_fusion), channel_id=1, source_target_pairs={{0,128},{128,0},{1,129},{129,1},{2,130},{130,2},{3,131},{131,3},{4... | collective-permute-start | bytes 3686408 | tf_op jit(solution)/shard_map/ppermute | solution.py:318
  20.0 10.5 %collective-permute-start.9 = (bf16[32,2560]{1,0:T(8,128)(2,1)S(1)}, bf16[32,2560]{1,0:T(8,128)(2,1)S(1)}, u32[]{:S(2)}, u32[]{:S(2)}) collective-permute-start(bf16[32,2560]{1,0:T(8,128)(2,1)S(1)} %collective-permute-done.refs_0_), channel_id=1, source_target_pairs={{0,16},{16,32},{32,48},{48,64},{64,80},{80,96},{96,112},{112,0},{1... | collective-permute-start | bytes 491528 | tf_op jit(solution)/shard_map/ppermute | solution.py:327
  25.4 8.2 %collective-permute-start.12 = (bf16[32,2560]{1,0:T(8,128)(2,1)S(1)}, bf16[32,2560]{1,0:T(8,128)(2,1)S(1)}, u32[]{:S(2)}, u32[]{:S(2)}) collective-permute-start(bf16[32,2560]{1,0:T(8,128)(2,1)S(1)} %collective-permute-done.1.refs_1_), channel_id=1, source_target_pairs={{0,16},{16,32},{32,48},{48,64},{64,80},{80,96},{96,112},{112,0},{1... | collective-permute-start | bytes 491528 | tf_op jit(solution)/shard_map/ppermute | solution.py:327
  30.1 6.9 %collective-permute-start.2 = (bf16[32,2560]{1,0:T(8,128)(2,1)S(1)}, bf16[32,2560]{1,0:T(8,128)(2,1)S(1)}, u32[]{:S(2)}, u32[]{:S(2)}) collective-permute-start(bf16[32,2560]{1,0:T(8,128)(2,1)S(1)} %collective-permute-done.refs_0_), channel_id=1, source_target_pairs={{0,112},{16,0},{32,16},{48,32},{64,48},{80,64},{96,80},{112,96},{1... | collective-permute-start | bytes 491528 | tf_op jit(solution)/shard_map/ppermute | solution.py:329
  30.1 8.3 %collective-permute-start.3 = (bf16[32,2560]{1,0:T(8,128)(2,1)S(1)}, bf16[32,2560]{1,0:T(8,128)(2,1)S(1)}, u32[]{:S(2)}, u32[]{:S(2)}) collective-permute-start(bf16[32,2560]{1,0:T(8,128)(2,1)S(1)} %collective-permute-done.1.refs_1_), channel_id=1, source_target_pairs={{0,112},{16,0},{32,16},{48,32},{64,48},{80,64},{96,80},{112,96},{1... | collective-permute-start | bytes 491528 | tf_op jit(solution)/shard_map/ppermute | solution.py:329
  30.6 10.9 %collective-permute-start.10 = (bf16[32,2560]{1,0:T(8,128)(2,1)S(1)}, bf16[32,2560]{1,0:T(8,128)(2,1)S(1)}, u32[]{:S(2)}, u32[]{:S(2)}) collective-permute-start(bf16[32,2560]{1,0:T(8,128)(2,1)S(1)} %collective-permute-done.9.refs_14_), channel_id=1, source_target_pairs={{0,16},{16,32},{32,48},{48,64},{64,80},{80,96},{96,112},{112,0},{1... | collective-permute-start | bytes 491528 | tf_op jit(solution)/shard_map/ppermute | solution.py:327
  33.6 7.9 %collective-permute-start.13 = (bf16[32,2560]{1,0:T(8,128)(2,1)S(1)}, bf16[32,2560]{1,0:T(8,128)(2,1)S(1)}, u32[]{:S(2)}, u32[]{:S(2)}) collective-permute-start(bf16[32,2560]{1,0:T(8,128)(2,1)S(1)} %collective-permute-done.12.refs_15_), channel_id=1, source_target_pairs={{0,16},{16,32},{32,48},{48,64},{64,80},{80,96},{96,112},{112,0},{1... | collective-permute-start | bytes 491528 | tf_op jit(solution)/shard_map/ppermute | solution.py:327
  38.4 7.2 %collective-permute-start.5 = (bf16[32,2560]{1,0:T(8,128)(2,1)S(1)}, bf16[32,2560]{1,0:T(8,128)(2,1)S(1)}, u32[]{:S(2)}, u32[]{:S(2)}) collective-permute-start(bf16[32,2560]{1,0:T(8,128)(2,1)S(1)} %collective-permute-done.3.refs_3_), channel_id=1, source_target_pairs={{0,112},{16,0},{32,16},{48,32},{64,48},{80,64},{96,80},{112,96},{1... | collective-permute-start | bytes 491528 | tf_op jit(solution)/shard_map/ppermute | solution.py:329
  41.5 7.0 %collective-permute-start.11 = (bf16[32,2560]{1,0:T(8,128)(2,1)S(1)}, bf16[32,2560]{1,0:T(8,128)(2,1)S(1)}, u32[]{:S(2)}, u32[]{:S(2)}) collective-permute-start(bf16[32,2560]{1,0:T(8,128)(2,1)S(1)} %collective-permute-done.10.refs_12_), channel_id=1, source_target_pairs={{0,16},{16,32},{32,48},{48,64},{64,80},{80,96},{96,112},{112,0},{1... | collective-permute-start | bytes 491528 | tf_op jit(solution)/shard_map/ppermute | solution.py:327
  41.6 8.1 %collective-permute-start.14 = (bf16[32,2560]{1,0:T(8,128)(2,1)S(1)}, bf16[32,2560]{1,0:T(8,128)(2,1)S(1)}, u32[]{:S(2)}, u32[]{:S(2)}) collective-permute-start(bf16[32,2560]{1,0:T(8,128)(2,1)S(1)} %collective-permute-done.13.refs_13_), channel_id=1, source_target_pairs={{0,16},{16,32},{32,48},{48,64},{64,80},{80,96},{96,112},{112,0},{1... | collective-permute-start | bytes 491528 | tf_op jit(solution)/shard_map/ppermute | solution.py:327
  45.6 6.9 %collective-permute-start.7 = (bf16[32,2560]{1,0:T(8,128)(2,1)S(1)}, bf16[32,2560]{1,0:T(8,128)(2,1)S(1)}, u32[]{:S(2)}, u32[]{:S(2)}) collective-permute-start(bf16[32,2560]{1,0:T(8,128)(2,1)S(1)} %collective-permute-done.5.refs_5_), channel_id=1, source_target_pairs={{0,112},{16,0},{32,16},{48,32},{64,48},{80,64},{96,80},{112,96},{1... | collective-permute-start | bytes 491528 | tf_op jit(solution)/shard_map/ppermute | solution.py:329
  52.5 7.9 %collective-permute-start.17 = (bf16[240,2560]{1,0:T(8,128)(2,1)}, bf16[240,2560]{1,0:T(8,128)(2,1)}, u32[]{:S(2)}, u32[]{:S(2)}) collective-permute-start(bf16[240,2560]{1,0:T(8,128)(2,1)} %collective-permute-done.8), channel_id=1, source_target_pairs={{0,1},{1,0},{2,3},{3,2},{4,5},{5,4},{6,7},{7,6},{8,9},{9,8},{10,11... | collective-permute-start | bytes 3686408 | tf_op jit(solution)/shard_map/ppermute | solution.py:333
  57.5 7.0 %collective-permute-start.15 = (bf16[32,2560]{1,0:T(8,128)(2,1)S(1)}, bf16[32,2560]{1,0:T(8,128)(2,1)S(1)}, u32[]{:S(2)}, u32[]{:S(2)}) collective-permute-start(bf16[32,2560]{1,0:T(8,128)(2,1)S(1)} %collective-permute-done.11.refs_10_), channel_id=1, source_target_pairs={{0,16},{16,32},{32,48},{48,64},{64,80},{80,96},{96,112},{112,0},{1... | collective-permute-start | bytes 491528 | tf_op jit(solution)/shard_map/ppermute | solution.py:327
  75.7 12.0 %collective-permute-start.19 = (bf16[4,64,640]{2,1,0:T(8,128)(2,1)}, bf16[4,64,640]{2,1,0:T(8,128)(2,1)S(1)}, u32[]{:S(2)}, u32[]{:S(2)}) collective-permute-start(bf16[4,64,640]{2,1,0:T(8,128)(2,1)} %get-tuple-element.33), channel_id=1, source_target_pairs={{0,2},{2,4},{4,6},{6,14},{14,12},{12,10},{10,8},{8,136},{136,138},... | collective-permute-start | bytes 983048 | tf_op jit(solution)/shard_map/ppermute | solution.py:344
  79.2 13.4 %collective-permute-start.20 = (bf16[4,64,640]{2,1,0:T(8,128)(2,1)}, bf16[4,64,640]{2,1,0:T(8,128)(2,1)S(1)}, u32[]{:S(2)}, u32[]{:S(2)}) collective-permute-start(bf16[4,64,640]{2,1,0:T(8,128)(2,1)} %get-tuple-element.34), channel_id=1, source_target_pairs={{2,0},{4,2},{6,4},{14,6},{12,14},{10,12},{8,10},{136,8},{138,136},... | collective-permute-start | bytes 983048 | tf_op jit(solution)/shard_map/ppermute | solution.py:345
  94.6 10.5 %collective-permute-start.21 = (bf16[2,8,1280]{2,1,0:T(8,128)(2,1)S(1)}, bf16[2,8,1280]{2,1,0:T(8,128)(2,1)S(1)}, u32[]{:S(2)}, u32[]{:S(2)}) collective-permute-start(bf16[2,8,1280]{2,1,0:T(8,128)(2,1)S(1)} %get-tuple-element.37), channel_id=1, source_target_pairs={{0,0},{1,128},{2,2},{3,130},{4,4},{5,132},{6,6},{7,134},{8,8},{9,1... | collective-permute-start | bytes 122888 | tf_op jit(solution)/shard_map/ppermute | solution.py:369
  96.5 9.2 %collective-permute-start.22 = (bf16[2,8,1280]{2,1,0:T(8,128)(2,1)S(1)}, bf16[2,8,1280]{2,1,0:T(8,128)(2,1)S(1)}, u32[]{:S(2)}, u32[]{:S(2)}) collective-permute-start(bf16[2,8,1280]{2,1,0:T(8,128)(2,1)S(1)} %get-tuple-element.38), channel_id=1, source_target_pairs={{0,2},{1,130},{2,0},{3,128},{4,6},{5,134},{6,4},{7,132},{8,10},{9,... | collective-permute-start | bytes 122888 | tf_op jit(solution)/shard_map/ppermute | solution.py:369
  99.2 13.7 %collective-permute-start.23 = (bf16[2,8,1280]{2,1,0:T(8,128)(2,1)S(1)}, bf16[2,8,1280]{2,1,0:T(8,128)(2,1)S(1)}, u32[]{:S(2)}, u32[]{:S(2)}) collective-permute-start(bf16[2,8,1280]{2,1,0:T(8,128)(2,1)S(1)} %get-tuple-element.39), channel_id=1, source_target_pairs={{0,4},{1,132},{2,6},{3,134},{4,0},{5,128},{6,2},{7,130},{8,12},{9,... | collective-permute-start | bytes 122888 | tf_op jit(solution)/shard_map/ppermute | solution.py:369
  102.1 11.0 %collective-permute-start.24 = (bf16[2,8,1280]{2,1,0:T(8,128)(2,1)S(1)}, bf16[2,8,1280]{2,1,0:T(8,128)(2,1)S(1)}, u32[]{:S(2)}, u32[]{:S(2)}) collective-permute-start(bf16[2,8,1280]{2,1,0:T(8,128)(2,1)S(1)} %get-tuple-element.40), channel_id=1, source_target_pairs={{0,6},{1,134},{2,4},{3,132},{4,2},{5,130},{6,0},{7,128},{8,14},{9,... | collective-permute-start | bytes 122888 | tf_op jit(solution)/shard_map/ppermute | solution.py:369
  103.1 10.0 %collective-permute-start.25 = (bf16[2,8,1280]{2,1,0:T(8,128)(2,1)S(1)}, bf16[2,8,1280]{2,1,0:T(8,128)(2,1)S(1)}, u32[]{:S(2)}, u32[]{:S(2)}) collective-permute-start(bf16[2,8,1280]{2,1,0:T(8,128)(2,1)S(1)} %get-tuple-element.41), channel_id=1, source_target_pairs={{0,8},{1,136},{2,10},{3,138},{4,12},{5,140},{6,14},{7,142},{8,0},{... | collective-permute-start | bytes 122888 | tf_op jit(solution)/shard_map/ppermute | solution.py:369
  105.1 8.0 %collective-permute-start.26 = (bf16[2,8,1280]{2,1,0:T(8,128)(2,1)S(1)}, bf16[2,8,1280]{2,1,0:T(8,128)(2,1)S(1)}, u32[]{:S(2)}, u32[]{:S(2)}) collective-permute-start(bf16[2,8,1280]{2,1,0:T(8,128)(2,1)S(1)} %get-tuple-element.42), channel_id=1, source_target_pairs={{0,10},{1,138},{2,8},{3,136},{4,14},{5,142},{6,12},{7,140},{8,2},{... | collective-permute-start | bytes 122888 | tf_op jit(solution)/shard_map/ppermute | solution.py:369
  105.7 9.5 %collective-permute-start.27 = (bf16[2,8,1280]{2,1,0:T(8,128)(2,1)S(1)}, bf16[2,8,1280]{2,1,0:T(8,128)(2,1)S(1)}, u32[]{:S(2)}, u32[]{:S(2)}) collective-permute-start(bf16[2,8,1280]{2,1,0:T(8,128)(2,1)S(1)} %get-tuple-element.43), channel_id=1, source_target_pairs={{0,12},{1,140},{2,14},{3,142},{4,8},{5,136},{6,10},{7,138},{8,4},{... | collective-permute-start | bytes 122888 | tf_op jit(solution)/shard_map/ppermute | solution.py:369
  (24 other events, 154.1 us)

commit v3 on v2

--- a/solution.py
+++ b/solution.py
@@ -83,75 +83,94 @@
 SWAP = [(0, 1), (1, 0)]
 
 
-def project_kernel(flag_ref, *refs):
-    pieces, (own_ref, other_ref) = refs[:16], refs[16:18]
-    keep, send, x_ref = refs[18:]
+def gather(pieces, x_ref):
     for i in range(16):
         x_ref[32 * i : 32 * (i + 1), :] = pieces[i][...]
+
+
+def normalized(p):
     lane = lax.broadcasted_iota(jnp.int32, (1, QKV), 1)
     is_q = lane < HEAD_DIM
     is_k = (lane >= HEAD_DIM) & (lane < 2 * HEAD_DIM)
-    for w_ref, own in ((own_ref, 1), (other_ref, 0)):
-        p = lax.dot_general(x_ref[...], w_ref[...], NT, preferred_element_type=jnp.float32)
-        squares = p * p
-        q_mean = jnp.sum(jnp.where(is_q, squares, 0.0), axis=-1, keepdims=True) / HEAD_DIM
-        k_mean = jnp.sum(jnp.where(is_k, squares, 0.0), axis=-1, keepdims=True) / HEAD_DIM
-        scale = jnp.where(is_q, lax.rsqrt(q_mean + EPS), jnp.where(is_k, lax.rsqrt(k_mean + EPS), 1.0))
-        p = (p * scale).reshape(8, ROWS, 8, QKV)
-        for r in range(ROWS):
-            row = p[:, r].reshape(HALF, QKV).astype(jnp.bfloat16)
-
-            @pl.when(flag_ref[0] == own)
-            def _():
-                keep[r] = row
-
-            @pl.when(flag_ref[0] != own)
-            def _():
-                send[r] = row
-
-
-def project(flag, pieces, own, other):
+    squares = p * p
+    q_mean = jnp.sum(jnp.where(is_q, squares, 0.0), axis=-1, keepdims=True) / HEAD_DIM
+    k_mean = jnp.sum(jnp.where(is_k, squares, 0.0), axis=-1, keepdims=True) / HEAD_DIM
+    scale = jnp.where(is_q, lax.rsqrt(q_mean + EPS), jnp.where(is_k, lax.rsqrt(k_mean + EPS), 1.0))
+    p = (p * scale).reshape(8, ROWS, 8, QKV)
+    return [p[:, r].reshape(HALF, QKV).astype(jnp.bfloat16) for r in range(ROWS)]
+
+
+def project_own_kernel(*refs):
+    pieces, w_ref, rows, x_ref = refs[:16], refs[16], refs[17], refs[18]
+    gather(pieces, x_ref)
+    p = lax.dot_general(x_ref[...], w_ref[...], NT, preferred_element_type=jnp.float32)
+    for r, row in enumerate(normalized(p)):
+        rows[r] = row
+
+
+def project_own(pieces, own):
+    return pl.pallas_call(
+        project_own_kernel,
+        out_shape=jax.ShapeDtypeStruct((ROWS, HALF, QKV), jnp.bfloat16),
+        in_specs=[VMEM] * 17,
+        out_specs=VMEM,
+        scratch_shapes=[pltpu.VMEM((512, own.shape[1]), jnp.bfloat16)],
+        compiler_params=pltpu.CompilerParams(vmem_limit_bytes=16 * MIB),
+        cost_estimate=pl.CostEstimate(
+            flops=2 * 512 * 480 * 2560, bytes_accessed=5 * MIB, transcendentals=0
+        ),
+        name="project_own",
+    )(*pieces, own)
+
+
+def project_other_kernel(flags, *refs):
+    pieces, (mine, theirs, own_rows), (keep, send, top, bottom, x_ref) = refs[:16], refs[16:19], refs[19:]
+    gather(pieces, x_ref)
+    width = mine.shape[1]
+    near = pl.ds(pl.multiple_of(flags[1] * width, width), width)
+    far = pl.ds(pl.multiple_of((1 - flags[1]) * width, width), width)
+    p = lax.dot_general(x_ref[:, near], mine[...], NT, preferred_element_type=jnp.float32)
+    p += lax.dot_general(x_ref[:, far], theirs[...], NT, preferred_element_type=jnp.float32)
+    for r, row in enumerate(normalized(p)):
+
+        def store(first, second):
+            keep[r] = first
+            send[r] = second
+            edge = top if r < WIN else bottom
+            edge[r % WIN] = jnp.concatenate([first[:, HEAD_DIM:], second[:, HEAD_DIM:]], axis=1)
+
+        @pl.when(flags[0] == 1)
+        def _():
+            store(own_rows[r], row)
+
+        @pl.when(flags[0] != 1)
+        def _():
+            store(row, own_rows[r])
+
+
+def project_other(flags, pieces, mine, theirs, own_rows):
     whole = jax.ShapeDtypeStruct((ROWS, HALF, QKV), jnp.bfloat16)
-    return pl.pallas_call(
-        project_kernel,
-        out_shape=[whole, whole],
-        in_specs=[SMEM] + [VMEM] * 18,
-        out_specs=[VMEM] * 2,
-        scratch_shapes=[pltpu.VMEM((512, own.shape[1]), jnp.bfloat16)],
-        compiler_params=pltpu.CompilerParams(vmem_limit_bytes=32 * MIB),
-        cost_estimate=pl.CostEstimate(
-            flops=2 * 512 * 960 * 2560, bytes_accessed=8 * MIB, transcendentals=0
-        ),
-        name="project",
-    )(flag, *pieces, own, other)
-
-
-def edges_kernel(keep, other, top, bottom):
-    for r in range(WIN):
-        for edge, row, turn in ((top, r, 16), (bottom, r + WIN, HALF - 16)):
-            whole = jnp.concatenate([keep[row][:, HEAD_DIM:], other[row][:, HEAD_DIM:]], axis=1)
-            edge[r, : HALF - turn] = whole[turn:]
-            edge[r, HALF - turn :] = whole[:turn]
-
-
-def edges(keep, other):
     edge = jax.ShapeDtypeStruct((WIN, HALF, 4 * HEAD_DIM), jnp.bfloat16)
     return pl.pallas_call(
-        edges_kernel,
-        out_shape=[edge, edge],
-        in_specs=[VMEM] * 2,
-        out_specs=[VMEM] * 2,
-        cost_estimate=pl.CostEstimate(flops=0, bytes_accessed=MIB, transcendentals=0),
-        name="edges",
-    )(keep, other)
-
-
-def put(ks, vs, row, half, key, value):
-    at = pl.ds(row * COLS + half * HALF, HALF)
+        project_other_kernel,
+        out_shape=[whole, whole, edge, edge],
+        in_specs=[SMEM] + [VMEM] * 19,
+        out_specs=[VMEM] * 4,
+        scratch_shapes=[pltpu.VMEM((512, 2 * mine.shape[1]), jnp.bfloat16)],
+        compiler_params=pltpu.CompilerParams(vmem_limit_bytes=16 * MIB),
+        cost_estimate=pl.CostEstimate(
+            flops=2 * 512 * 480 * 2560, bytes_accessed=5 * MIB, transcendentals=0
+        ),
+        name="project_other",
+    )(flags, *pieces, mine, theirs, own_rows)
+
+
+def put(ks, vs, first, key, value):
+    at = pl.ds(first, key.shape[0])
     ks[at, :] = key
     vs[at, :HEAD_DIM] = value
-    first = lax.broadcasted_iota(jnp.int32, (HALF, 256 - HEAD_DIM), 1) == 0
-    vs[at, HEAD_DIM:] = jnp.where(first, 1.0, 0.0).astype(jnp.bfloat16)
+    is_one = lax.broadcasted_iota(jnp.int32, (key.shape[0], 256 - HEAD_DIM), 1) == 0
+    vs[at, HEAD_DIM:] = jnp.where(is_one, 1.0, 0.0).astype(jnp.bfloat16)
 
 
 def fill_masks(ints, masks):
@@ -182,7 +201,7 @@
     for half, part in enumerate((keep, other)):
         for r in range(ROWS):
             whole = part[r]
-            put(ks, vs, r, half, whole[:, HEAD_DIM : 2 * HEAD_DIM], whole[:, 2 * HEAD_DIM :])
+            put(ks, vs, r * COLS + half * HALF, whole[:, HEAD_DIM : 2 * HEAD_DIM], whole[:, 2 * HEAD_DIM :])
     fill_masks(ints, masks)
     eye = lax.broadcasted_iota(jnp.int32, (COLS, COLS), 0) == lax.broadcasted_iota(jnp.int32, (COLS, COLS), 1)
     for r in range(ROWS):
@@ -220,7 +239,7 @@
             pltpu.VMEM((ROWS * COLS, 256), jnp.bfloat16),
             pltpu.VMEM((WIN + 1, COLS, COLS), jnp.float32),
         ],
-        compiler_params=pltpu.CompilerParams(vmem_limit_bytes=32 * MIB),
+        compiler_params=pltpu.CompilerParams(vmem_limit_bytes=16 * MIB),
         cost_estimate=pl.CostEstimate(
             flops=3 * 10**9, bytes_accessed=4 * MIB, transcendentals=10**6
         ),
@@ -228,16 +247,16 @@
     )(ints, factor, keep, other, bias, band)
 
 
-def outer_kernel(ints, factor_ref, keep, other, top, bottom, bias, zonal_ref, window_ref, *refs):
+def outer_kernel(ints, factor_ref, keep, other, top, top_far, bottom, bottom_far, bias, zonal_ref, window_ref, *refs):
     chunks, (ks, vs, masks, out) = refs[:8], refs[8:]
     factor = factor_ref[0]
-    for edge, first in ((top, 0), (bottom, WIN)):
+    for edge, half, first, turn in ((top, 0, 0, 16), (top_far, 1, 0, 16), (bottom, 0, WIN, 48), (bottom_far, 1, WIN, 48)):
+        at = half * 2 * HEAD_DIM
         for r in range(WIN):
-            whole = edge[r]
-            for half in range(2):
-                at = half * 2 * HEAD_DIM
-                key, value = whole[:, at : at + HEAD_DIM], whole[:, at + HEAD_DIM : at + 2 * HEAD_DIM]
-                put(ks, vs, first + r, half, key, value)
+            whole = edge[r][:, at : at + 2 * HEAD_DIM]
+            to = (first + r) * COLS + half * HALF
+            for part, start in ((whole[: HALF - turn], to + turn), (whole[HALF - turn :], to)):
+                put(ks, vs, start, part[:, :HEAD_DIM], part[:, HEAD_DIM:])
     fill_masks(ints, masks)
     for r in range(ROWS):
         query = query_of(keep, other, r)
@@ -260,12 +279,12 @@
         chunks[k][1] = out[1 - ints[3], ints[12 + k]].astype(jnp.bfloat16)
 
 
-def outer(ints, factor, keep, other, top, bottom, bias, zonal, window):
+def outer(ints, factor, *operands):
     chunk = jax.ShapeDtypeStruct((2, 8, ROWS * HEAD_DIM), jnp.bfloat16)
     return pl.pallas_call(
         outer_kernel,
         out_shape=[chunk] * 8,
-        in_specs=[SMEM, SMEM] + [VMEM] * 7,
+        in_specs=[SMEM, SMEM] + [VMEM] * 9,
         out_specs=[VMEM] * 8,
         scratch_shapes=[
             pltpu.VMEM((2 * WIN * COLS, HEAD_DIM), jnp.bfloat16),
@@ -273,12 +292,12 @@
             pltpu.VMEM((WIN + 1, COLS, COLS), jnp.float32),
             pltpu.VMEM((2, 8, 8, ROWS * HEAD_DIM), jnp.float32),
         ],
-        compiler_params=pltpu.CompilerParams(vmem_limit_bytes=32 * MIB),
+        compiler_params=pltpu.CompilerParams(vmem_limit_bytes=16 * MIB),
         cost_estimate=pl.CostEstimate(
             flops=10**9, bytes_accessed=4 * MIB, transcendentals=10**6
         ),
         name="outer",
-    )(ints, factor, keep, other, top, bottom, bias, zonal, window)
+    )(ints, factor, *operands)
 
 
 def assemble_kernel(at, *refs):
@@ -295,6 +314,8 @@
         out_shape=jax.ShapeDtypeStruct((1, 8, LAT * ROWS * HEAD_DIM), jnp.bfloat16),
         in_specs=[SMEM] + [VMEM] * 9,
         out_specs=VMEM,
+        compiler_params=pltpu.CompilerParams(vmem_limit_bytes=4 * MIB),
+        cost_estimate=pl.CostEstimate(flops=0, bytes_accessed=MIB, transcendentals=0),
         name="assemble",
     )(at, *mains, got)
 
@@ -309,40 +330,7 @@
     wide = tokens.astype(jnp.float32)
     normed = wide * lax.rsqrt(jnp.mean(wide * wide, axis=-1, keepdims=True) + EPS)
     normed = jnp.transpose(normed.astype(jnp.bfloat16), (1, 0, 2)).reshape(64, model)
-    first = [lax.ppermute(normed[at : at + 32], AXES, spread_perm()) for at in (0, 32)]
-
-    own = w_qkv[0]
-    rows = QKV // 2
-    half = lax.dynamic_slice_in_dim(own, core * rows, rows, 0)
-    *first, half = lax.optimization_barrier((*first, half))
-    mine = lax.ppermute(half, "y_lo", SWAP)
-
-    up = [(i, (i + 1) % 8) for i in range(8)]
-    down = [(i, (i - 1) % 8) for i in range(8)]
-    shards = [first] + [[None, None] for _ in range(7)]
-    a, b = list(first), list(first)
-    for k in range(1, 5):
-        for h in range(2):
-            if k < 4 or h == 0:
-                a[h] = shards[8 - k][h] = lax.ppermute(a[h], "z", up)
-            if k < 4 or h == 1:
-                b[h] = shards[k][h] = lax.ppermute(b[h], "z", down)
-        if k == 3:
-            mine, *both = lax.optimization_barrier((mine, *a, *b))
-            a, b = both[:2], both[2:]
-            theirs = lax.ppermute(mine, "core", SWAP)
-    other_w = jnp.concatenate(
-        [jnp.where(core == 0, mine, theirs), jnp.where(core == 0, theirs, mine)], axis=0
-    )
-    pieces = [shards[i][h] for i in range(8) for h in range(2)]
-
-    flag = jnp.where(core == y_lo, 1, 0).astype(jnp.int32).reshape(1)
-    keep, send = project(flag, pieces, own, other_w)
-    other = lax.ppermute(send, "core", SWAP)
-    top_rows, bottom_rows = edges(keep, other)
-    ring = ("y_lo", "y_hi", "x")
-    top = lax.ppermute(bottom_rows, ring, neighbour_perm(1))
-    bottom = lax.ppermute(top_rows, ring, neighbour_perm(-1))
+    first = lax.ppermute(normed, AXES, spread_perm())
 
     base = (z - 2 * block) & 7
     padded = jnp.pad(key_mask, ((0, 0), (WIN, WIN)))
@@ -357,24 +345,59 @@
     bias = jnp.where(usable == 1, 0.0, -BIG)
     ids = lax.dynamic_slice_in_dim(band_of_row, block * ROWS, ROWS, 0)
     band = (ids[:, None] == ids[None, :]).astype(jnp.float32).reshape(ROWS * ROWS)
-
     groups = [((sector ^ k) - base + side) & 7 for side in (y_lo, 1 - y_lo) for k in range(8)]
     reach = lax.dynamic_index_in_dim(radius, head, keepdims=False)
     ints = jnp.stack([base, core, reach, core ^ y_lo] + groups).astype(jnp.int32)
     factor = lax.dynamic_slice_in_dim(qk_scale, head, 1, 0) / HEAD_DIM * LOG2E
-    zonal, window = inner(ints, factor, keep, other, bias, band)
-    chunks = outer(ints, factor, keep, other, top, bottom, bias, zonal, window)
-
-    corners = ("y_lo", "y_hi", "x", "core")
-    landed = [lax.ppermute(chunks[k], corners, return_perm(k)) for k in range(8)]
-    give = jnp.stack([part[1] for part in landed])
-    got = lax.ppermute(give, "core", SWAP)
     at = []
     for from_y_lo in (core, 1 - core):
         for k in range(8):
             source = sector ^ k
             at.append(block_of(from_y_lo, source >> 2, source & 3))
-    return assemble(jnp.stack(at).astype(jnp.int32), landed, got)
+    at = jnp.stack(at).astype(jnp.int32)
+    flags = jnp.stack([core == y_lo, core]).astype(jnp.int32)
+
+    own = w_qkv[0]
+    half = lax.dynamic_slice_in_dim(own, core * (model // 2), model // 2, 1)
+    first, half, bias, band, ints, factor, at, flags = lax.optimization_barrier(
+        (first, half, bias, band, ints, factor, at, flags)
+    )
+    mine = lax.ppermute(half, "y_lo", SWAP)
+
+    up = [(i, (i + 1) % 8) for i in range(8)]
+    down = [(i, (i - 1) % 8) for i in range(8)]
+    shards = [[first[:32], first[32:]]] + [[None, None] for _ in range(7)]
+    a, b = list(shards[0]), list(shards[0])
+    for k in range(1, 5):
+        for h in range(2):
+            if k < 4 or h == 0:
+                a[h] = shards[8 - k][h] = lax.ppermute(a[h], "z", up)
+            if k < 4 or h == 1:
+                b[h] = shards[k][h] = lax.ppermute(b[h], "z", down)
+    last = ((4, 0), (4, 1), (5, 1), (3, 0))
+    mine, *ends = lax.optimization_barrier((mine, *(shards[i][h] for i, h in last)))
+    for (i, h), end in zip(last, ends):
+        shards[i][h] = end
+    theirs = lax.ppermute(mine, "core", SWAP)
+    pieces = [shards[i][h] for i in range(8) for h in range(2)]
+
+    own_rows = project_own(pieces, own)
+    keep, send, top_rows, bottom_rows = project_other(flags, pieces, mine, theirs, own_rows)
+    ring = ("y_lo", "y_hi", "x")
+    top = lax.ppermute(bottom_rows, ring, neighbour_perm(1))
+    bottom = lax.ppermute(top_rows, ring, neighbour_perm(-1))
+    other = lax.ppermute(send, "core", SWAP)
+    zonal, window = inner(ints, factor, keep, other, bias, band)
+    top, bottom, window = lax.optimization_barrier((top, bottom, window))
+    top_far = lax.ppermute(top, "core", SWAP)
+    bottom_far = lax.ppermute(bottom, "core", SWAP)
+    chunks = outer(ints, factor, keep, other, top, top_far, bottom, bottom_far, bias, zonal, window)
+
+    corners = ("y_lo", "y_hi", "x", "core")
+    landed = [lax.ppermute(chunks[k], corners, return_perm(k)) for k in range(8)]
+    give = jnp.stack([part[1] for part in landed])
+    got = lax.ppermute(give, "core", SWAP)
+    return assemble(at, landed, got)
 
 
 def solution(mesh):

time: 124 us -> 118 us (0.952)
  local copies, waits for them, and re-layouts: 7.95 us -> 2.78 us
  waiting for transfers between devices: 25.8 us -> 28.6 us
  other arithmetic: 4.41 us -> 2.68 us
  Pallas kernels: 13.2 us -> 11.5 us
    ppermute x7, starting transfers between devices: 19.8 us -> 1.72 us  [body(): a[h] = shards[8 - k][h] = lax.ppermute(a[h], 'z', up)]
    ppermute x7, starting transfers between devices: 8.76 us -> 26.7 us  [body(): b[h] = shards[k][h] = lax.ppermute(b[h], 'z', down)]
    ppermute x8, starting transfers between devices: 18.4 us -> 23.5 us  [body(): lax.ppermute(chunks[k], corners, return_perm(k))]
    ppermute x2 -> x3, starting transfers between devices: 10.2 us -> 5.57 us  [the longest x1 4.38 us: body(): first = lax.ppermute(normed, AXES, spread_perm())]
    ppermute x7, waiting for transfers between devices: 6.62 us -> 2 us  [body(): b[h] = shards[k][h] = lax.ppermute(b[h], 'z', down)]
    ppermute x7, waiting for transfers between devices: 3.41 us -> 6.91 us  [body(): a[h] = shards[8 - k][h] = lax.ppermute(a[h], 'z', up)]
    unnamed x43 -> x17, local copies, waits for them, and re-layouts: 3.38 us -> 0.04 us
    ppermute x2 -> x3, waiting for transfers between devices: 2.45 us -> 5.77 us  [the longest x1 4.05 us: body(): first = lax.ppermute(normed, AXES, spread_perm())]
  transfers between devices with their start and end apart: 30 -> 31, of which waited for: 16 -> 14; matrix products, arithmetic and copies ran while one was open for 5% -> 3% of each run, Pallas kernels for 3% -> 4%
where the time goes in v3:
time: 118 us; the launch traced here: 117 us
  starting transfers between devices  70.7 us (60%)
  waiting for transfers between devices  28.6 us (24%)
  Pallas kernels  11.5 us (10%)
  local copies, waits for them, and re-layouts  2.78 us (2%)
  other arithmetic  2.68 us (2%)
    ppermute x7, starting transfers between devices, body(): b[h] = shards[k][h] = lax.ppermute(b[h], 'z', down)  26.7 us
    ppermute x8, starting transfers between devices, body(): lax.ppermute(chunks[k], corners, return_perm(k))  23.5 us
    ppermute x7, waiting for transfers between devices, body(): a[h] = shards[8 - k][h] = lax.ppermute(a[h], 'z', up)  6.91 us
    ppermute x8, waiting for transfers between devices, body(): lax.ppermute(chunks[k], corners, return_perm(k))  5.48 us
    ppermute x1, starting transfers between devices, body(): first = lax.ppermute(normed, AXES, spread_perm())  4.38 us
    ppermute x1, starting transfers between devices, body(): mine = lax.ppermute(half, 'y_lo', SWAP)  4.08 us
    ppermute x1, waiting for transfers between devices, body(): first = lax.ppermute(normed, AXES, spread_perm())  4.05 us
    ppermute x1, starting transfers between devices, body(): theirs = lax.ppermute(mine, 'core', SWAP)  4.04 us
  transfers between devices with their start and end apart: 31, of which 14 were waited for; matrix products, arithmetic and copies ran while one was open for 3% of the time, Pallas kernels for 4%

profile of v3, /device:TPU:1, one launch (start us, length us, event | category | flops | bytes accessed | tf_op | source)
XLA Modules:
  0.0 117.4 jit_solution(7663635742314017291)
XLA Ops:
  2.5 4.4 %collective-permute-start = (bf16[64,2560]{1,0:T(8,128)(2,1)S(1)}, bf16[64,2560]{1,0:T(8,128)(2,1)S(1)}, u32[]{:S(2)}, u32[]{:S(2)}) collective-permute-start(bf16[64,2560]{1,0:T(8,128)(2,1)S(1)} %bitcast.52), channel_id=1, source_target_pairs={{0,0},{1,17},{2,16},{3,33},{4,32},{5,49},{6,48},{7,65},{8,64},{9,8... | collective-permute-start | bytes 983048 | tf_op jit(solution)/shard_map/ppermute | solution.py:333
  10.8 4.0 %collective-permute-done = bf16[64,2560]{1,0:T(8,128)(2,1)S(1)} collective-permute-done((bf16[64,2560]{1,0:T(8,128)(2,1)S(1)}, bf16[64,2560]{1,0:T(8,128)(2,1)S(1)}, u32[]{:S(2)}, u32[]{:S(2)}) %collective-permute-start) | collective-permute-done | bytes 327712 | tf_op jit(solution)/shard_map/ppermute | solution.py:333
  14.8 4.1 %collective-permute-start.5 = (bf16[480,1280]{1,0:T(8,128)(2,1)S(1)}, bf16[480,1280]{1,0:T(8,128)(2,1)S(1)}, u32[]{:S(2)}, u32[]{:S(2)}) collective-permute-start(bf16[480,1280]{1,0:T(8,128)(2,1)S(1)} %dynamic-slice_bitcast_fusion), channel_id=1, source_target_pairs={{0,128},{128,0},{1,129},{129,1},{2,130},{130,2},{3,131},{131,3},{4... | collective-permute-start | bytes 3686408 | tf_op jit(solution)/shard_map/ppermute | solution.py:365
  18.9 7.5 %collective-permute-start.2 = (bf16[32,2560]{1,0:T(8,128)(2,1)S(1)}, bf16[32,2560]{1,0:T(8,128)(2,1)S(1)}, u32[]{:S(2)}, u32[]{:S(2)}) collective-permute-start(bf16[32,2560]{1,0:T(8,128)(2,1)S(1)} %get-tuple-element.65.refs_1_), channel_id=1, source_target_pairs={{0,112},{16,0},{32,16},{48,32},{64,48},{80,64},{96,80},{112,96},{1... | collective-permute-start | bytes 491528 | tf_op jit(solution)/shard_map/ppermute | solution.py:376
  29.4 3.4 %collective-permute-start.4 = (bf16[32,2560]{1,0:T(8,128)(2,1)S(1)}, bf16[32,2560]{1,0:T(8,128)(2,1)S(1)}, u32[]{:S(2)}, u32[]{:S(2)}) collective-permute-start(bf16[32,2560]{1,0:T(8,128)(2,1)S(1)} %collective-permute-done.2.refs_3_), channel_id=1, source_target_pairs={{0,112},{16,0},{32,16},{48,32},{64,48},{80,64},{96,80},{112,96},{1... | collective-permute-start | bytes 491528 | tf_op jit(solution)/shard_map/ppermute | solution.py:376
  32.8 3.2 %collective-permute-done.12.refs_15_ = bf16[32,2560]{1,0:T(8,128)(2,1)S(1)} collective-permute-done((bf16[32,2560]{1,0:T(8,128)(2,1)S(1)}, bf16[32,2560]{1,0:T(8,128)(2,1)S(1)}, u32[]{:S(2)}, u32[]{:S(2)}) %collective-permute-start.12) | collective-permute-done | bytes 163872 | tf_op jit(solution)/shard_map/ppermute | solution.py:374
  36.0 2.7 %collective-permute-start.3 = (bf16[32,2560]{1,0:T(8,128)(2,1)S(1)}, bf16[32,2560]{1,0:T(8,128)(2,1)S(1)}, u32[]{:S(2)}, u32[]{:S(2)}) collective-permute-start(bf16[32,2560]{1,0:T(8,128)(2,1)S(1)} %collective-permute-done.1.refs_2_), channel_id=1, source_target_pairs={{0,112},{16,0},{32,16},{48,32},{64,48},{80,64},{96,80},{112,96},{1... | collective-permute-start | bytes 491528 | tf_op jit(solution)/shard_map/ppermute | solution.py:376
  38.7 4.8 %collective-permute-start.10 = (bf16[32,2560]{1,0:T(8,128)(2,1)S(1)}, bf16[32,2560]{1,0:T(8,128)(2,1)S(1)}, u32[]{:S(2)}, u32[]{:S(2)}) collective-permute-start(bf16[32,2560]{1,0:T(8,128)(2,1)S(1)} %collective-permute-done.4.refs_5_), channel_id=1, source_target_pairs={{0,112},{16,0},{32,16},{48,32},{64,48},{80,64},{96,80},{112,96},{1... | collective-permute-start | bytes 491528 | tf_op jit(solution)/shard_map/ppermute | solution.py:376
  43.6 4.5 %collective-permute-start.15 = (bf16[32,2560]{1,0:T(8,128)(2,1)S(1)}, bf16[32,2560]{1,0:T(8,128)(2,1)S(1)}, u32[]{:S(2)}, u32[]{:S(2)}) collective-permute-start(bf16[32,2560]{1,0:T(8,128)(2,1)S(1)} %collective-permute-done.3.refs_4_), channel_id=1, source_target_pairs={{0,112},{16,0},{32,16},{48,32},{64,48},{80,64},{96,80},{112,96},{1... | collective-permute-start | bytes 491528 | tf_op jit(solution)/shard_map/ppermute | solution.py:376
  48.1 2.8 %collective-permute-start.11 = (bf16[32,2560]{1,0:T(8,128)(2,1)S(1)}, bf16[32,2560]{1,0:T(8,128)(2,1)S(1)}, u32[]{:S(2)}, u32[]{:S(2)}) collective-permute-start(bf16[32,2560]{1,0:T(8,128)(2,1)S(1)} %collective-permute-done.10.refs_7_), channel_id=1, source_target_pairs={{0,112},{16,0},{32,16},{48,32},{64,48},{80,64},{96,80},{112,96},{1... | collective-permute-start | bytes 491528 | tf_op jit(solution)/shard_map/ppermute | solution.py:376
  54.0 2.2 %collective-permute-done.9.refs_8_ = bf16[32,2560]{1,0:T(8,128)(2,1)S(1)} collective-permute-done((bf16[32,2560]{1,0:T(8,128)(2,1)S(1)}, bf16[32,2560]{1,0:T(8,128)(2,1)S(1)}, u32[]{:S(2)}, u32[]{:S(2)}) %collective-permute-start.9) | collective-permute-done | bytes 163872 | tf_op jit(solution)/shard_map/ppermute | solution.py:374
  56.3 4.0 %collective-permute-start.16 = (bf16[480,1280]{1,0:T(8,128)(2,1)S(1)}, bf16[480,1280]{1,0:T(8,128)(2,1)S(1)}, u32[]{:S(2)}, u32[]{:S(2)}) collective-permute-start(bf16[480,1280]{1,0:T(8,128)(2,1)S(1)} %collective-permute-done.5.refs_16_), channel_id=1, source_target_pairs={{0,1},{1,0},{2,3},{3,2},{4,5},{5,4},{6,7},{7,6},{8,9},{9,8},{10,11... | collective-permute-start | bytes 3686408 | tf_op jit(solution)/shard_map/ppermute | solution.py:381
  62.8 3.1 %project_other.1 = (bf16[8,64,480]{2,1,0:T(8,128)(2,1)S(1)}, bf16[8,64,480]{2,1,0:T(8,128)(2,1)S(1)}, bf16[4,64,640]{2,1,0:T(8,128)(2,1)S(1)}, bf16[4,64,640]{2,1,0:T(8,128)(2,1)S(1)}) custom-call(s32[2]{0:T(128)S(1)} %pad_add_fusion.flags, bf16[32,2560]{1,0:T(8,128)(2,1)S(1)} %get-tuple-element.66.refs_0_, bf16[32,2560]{1,0:T(8,128)(2,1)S(1)} %get-tuple-element.65.refs_1_, ...), custom_call_target="tpu_custom_call" | custom-call | flops 1258291200 | bytes 5242880 | tf_op jit(solution)/shard_map/project_other/pallas_call | solution.py:154
  66.5 3.3 %collective-permute-start.18 = (bf16[4,64,640]{2,1,0:T(8,128)(2,1)S(1)}, bf16[4,64,640]{2,1,0:T(8,128)(2,1)S(1)}, u32[]{:S(2)}, u32[]{:S(2)}) collective-permute-start(bf16[4,64,640]{2,1,0:T(8,128)(2,1)S(1)} %get-tuple-element.48), channel_id=1, source_target_pairs={{0,2},{2,4},{4,6},{6,14},{14,12},{12,10},{10,8},{8,136},{136,138},... | collective-permute-start | bytes 983048 | tf_op jit(solution)/shard_map/ppermute | solution.py:387
  71.1 3.4 %inner.1 = (bf16[8,128,160]{2,1,0:T(8,128)(2,1)S(1)}, f32[8,128,256]{2,1,0:T(8,128)S(1)}) custom-call(s32[20]{0:T(128)S(1)} %stack.144.ints, f32[1]{0:T(128)S(6)} %mul.112.factor_ref, bf16[8,64,480]{2,1,0:T(8,128)(2,1)S(1)} %get-tuple-element.46.keep, bf16[8,64,480]{2,1,0:T(8,128)(2,1)S(1)} %collective-permute-done.17.other, ...), custom_call_target="tpu_custom_call" | custom-call | flops 3000000000 | bytes 4194304 | tf_op jit(solution)/shard_map/inner/pallas_call | solution.py:229
  74.5 2.3 %collective-permute-done.18.top = bf16[4,64,640]{2,1,0:T(8,128)(2,1)S(1)} collective-permute-done((bf16[4,64,640]{2,1,0:T(8,128)(2,1)S(1)}, bf16[4,64,640]{2,1,0:T(8,128)(2,1)S(1)}, u32[]{:S(2)}, u32[]{:S(2)}) %collective-permute-start.18) | collective-permute-done | bytes 327712 | tf_op jit(solution)/shard_map/ppermute | solution.py:387
  76.8 3.8 %collective-permute-done.19.bottom = bf16[4,64,640]{2,1,0:T(8,128)(2,1)S(1)} collective-permute-done((bf16[4,64,640]{2,1,0:T(8,128)(2,1)S(1)}, bf16[4,64,640]{2,1,0:T(8,128)(2,1)S(1)}, u32[]{:S(2)}, u32[]{:S(2)}) %collective-permute-start.19) | collective-permute-done | bytes 327712 | tf_op jit(solution)/shard_map/ppermute | solution.py:388
  83.6 2.1 %outer.1 = (bf16[2,8,1280]{2,1,0:T(8,128)(2,1)S(1)}, bf16[2,8,1280]{2,1,0:T(8,128)(2,1)S(1)}, bf16[2,8,1280]{2,1,0:T(8,128)(2,1)S(1)}, bf16[2,8,1280]{2,1,0:T(8,...) custom-call(s32[20]{0:T(128)S(1)} %stack.144.ints, ...), custom_call_target="tpu_custom_call" | custom-call | flops 1000000000 | bytes 4194304 | tf_op jit(solution)/shard_map/outer/pallas_call | solution.py:284
  85.6 1.9 %collective-permute-start.22 = (bf16[2,8,1280]{2,1,0:T(8,128)(2,1)S(1)}, bf16[2,8,1280]{2,1,0:T(8,128)(2,1)S(1)}, u32[]{:S(2)}, u32[]{:S(2)}) collective-permute-start(bf16[2,8,1280]{2,1,0:T(8,128)(2,1)S(1)} %get-tuple-element.57), channel_id=1, source_target_pairs={{0,0},{1,128},{2,2},{3,130},{4,4},{5,132},{6,6},{7,134},{8,8},{9,1... | collective-permute-start | bytes 122888 | tf_op jit(solution)/shard_map/ppermute | solution.py:397
  87.5 4.8 %collective-permute-start.23 = (bf16[2,8,1280]{2,1,0:T(8,128)(2,1)S(1)}, bf16[2,8,1280]{2,1,0:T(8,128)(2,1)S(1)}, u32[]{:S(2)}, u32[]{:S(2)}) collective-permute-start(bf16[2,8,1280]{2,1,0:T(8,128)(2,1)S(1)} %get-tuple-element.58), channel_id=1, source_target_pairs={{0,2},{1,130},{2,0},{3,128},{4,6},{5,134},{6,4},{7,132},{8,10},{9,... | collective-permute-start | bytes 122888 | tf_op jit(solution)/shard_map/ppermute | solution.py:397
  92.3 7.9 %collective-permute-start.24 = (bf16[2,8,1280]{2,1,0:T(8,128)(2,1)S(1)}, bf16[2,8,1280]{2,1,0:T(8,128)(2,1)S(1)}, u32[]{:S(2)}, u32[]{:S(2)}) collective-permute-start(bf16[2,8,1280]{2,1,0:T(8,128)(2,1)S(1)} %get-tuple-element.59), channel_id=1, source_target_pairs={{0,4},{1,132},{2,6},{3,134},{4,0},{5,128},{6,2},{7,130},{8,12},{9,... | collective-permute-start | bytes 122888 | tf_op jit(solution)/shard_map/ppermute | solution.py:397
  100.2 2.4 %collective-permute-start.27 = (bf16[2,8,1280]{2,1,0:T(8,128)(2,1)S(1)}, bf16[2,8,1280]{2,1,0:T(8,128)(2,1)S(1)}, u32[]{:S(2)}, u32[]{:S(2)}) collective-permute-start(bf16[2,8,1280]{2,1,0:T(8,128)(2,1)S(1)} %get-tuple-element.62), channel_id=1, source_target_pairs={{0,10},{1,138},{2,8},{3,136},{4,14},{5,142},{6,12},{7,140},{8,2},{... | collective-permute-start | bytes 122888 | tf_op jit(solution)/shard_map/ppermute | solution.py:397
  102.6 5.3 %collective-permute-start.28 = (bf16[2,8,1280]{2,1,0:T(8,128)(2,1)S(1)}, bf16[2,8,1280]{2,1,0:T(8,128)(2,1)S(1)}, u32[]{:S(2)}, u32[]{:S(2)}) collective-permute-start(bf16[2,8,1280]{2,1,0:T(8,128)(2,1)S(1)} %get-tuple-element.63), channel_id=1, source_target_pairs={{0,12},{1,140},{2,14},{3,142},{4,8},{5,136},{6,10},{7,138},{8,4},{... | collective-permute-start | bytes 122888 | tf_op jit(solution)/shard_map/ppermute | solution.py:397
  110.0 4.6 %collective-permute-done.29.refs_7_ = bf16[2,8,1280]{2,1,0:T(8,128)(2,1)S(1)} collective-permute-done((bf16[2,8,1280]{2,1,0:T(8,128)(2,1)S(1)}, bf16[2,8,1280]{2,1,0:T(8,128)(2,1)S(1)}, u32[]{:S(2)}, u32[]{:S(2)}) %collective-permute-start.29) | collective-permute-done | bytes 40992 | tf_op jit(solution)/shard_map/ppermute | solution.py:397
  (80 shorter events, 23.8 us)
Async XLA Ops:
  2.5 12.3 %collective-permute-start = (bf16[64,2560]{1,0:T(8,128)(2,1)S(1)}, bf16[64,2560]{1,0:T(8,128)(2,1)S(1)}, u32[]{:S(2)}, u32[]{:S(2)}) collective-permute-start(bf16[64,2560]{1,0:T(8,128)(2,1)S(1)} %bitcast.52), channel_id=1, source_target_pairs={{0,0},{1,17},{2,16},{3,33},{4,32},{5,49},{6,48},{7,65},{8,64},{9,8... | collective-permute-start | bytes 983048 | tf_op jit(solution)/shard_map/ppermute | solution.py:333
  14.8 41.4 %collective-permute-start.5 = (bf16[480,1280]{1,0:T(8,128)(2,1)S(1)}, bf16[480,1280]{1,0:T(8,128)(2,1)S(1)}, u32[]{:S(2)}, u32[]{:S(2)}) collective-permute-start(bf16[480,1280]{1,0:T(8,128)(2,1)S(1)} %dynamic-slice_bitcast_fusion), channel_id=1, source_target_pairs={{0,128},{128,0},{1,129},{129,1},{2,130},{130,2},{3,131},{131,3},{4... | collective-permute-start | bytes 3686408 | tf_op jit(solution)/shard_map/ppermute | solution.py:365
  18.9 10.5 %collective-permute-start.2 = (bf16[32,2560]{1,0:T(8,128)(2,1)S(1)}, bf16[32,2560]{1,0:T(8,128)(2,1)S(1)}, u32[]{:S(2)}, u32[]{:S(2)}) collective-permute-start(bf16[32,2560]{1,0:T(8,128)(2,1)S(1)} %get-tuple-element.65.refs_1_), channel_id=1, source_target_pairs={{0,112},{16,0},{32,16},{48,32},{64,48},{80,64},{96,80},{112,96},{1... | collective-permute-start | bytes 491528 | tf_op jit(solution)/shard_map/ppermute | solution.py:376
  26.4 9.6 %collective-permute-start.12 = (bf16[32,2560]{1,0:T(8,128)(2,1)S(1)}, bf16[32,2560]{1,0:T(8,128)(2,1)S(1)}, u32[]{:S(2)}, u32[]{:S(2)}) collective-permute-start(bf16[32,2560]{1,0:T(8,128)(2,1)S(1)} %get-tuple-element.65.refs_1_), channel_id=1, source_target_pairs={{0,16},{16,32},{32,48},{48,64},{64,80},{80,96},{96,112},{112,0},{1... | collective-permute-start | bytes 491528 | tf_op jit(solution)/shard_map/ppermute | solution.py:374
  28.0 8.0 %collective-permute-start.1 = (bf16[32,2560]{1,0:T(8,128)(2,1)S(1)}, bf16[32,2560]{1,0:T(8,128)(2,1)S(1)}, u32[]{:S(2)}, u32[]{:S(2)}) collective-permute-start(bf16[32,2560]{1,0:T(8,128)(2,1)S(1)} %get-tuple-element.66.refs_0_), channel_id=1, source_target_pairs={{0,112},{16,0},{32,16},{48,32},{64,48},{80,64},{96,80},{112,96},{1... | collective-permute-start | bytes 491528 | tf_op jit(solution)/shard_map/ppermute | solution.py:376
  29.4 9.3 %collective-permute-start.4 = (bf16[32,2560]{1,0:T(8,128)(2,1)S(1)}, bf16[32,2560]{1,0:T(8,128)(2,1)S(1)}, u32[]{:S(2)}, u32[]{:S(2)}) collective-permute-start(bf16[32,2560]{1,0:T(8,128)(2,1)S(1)} %collective-permute-done.2.refs_3_), channel_id=1, source_target_pairs={{0,112},{16,0},{32,16},{48,32},{64,48},{80,64},{96,80},{112,96},{1... | collective-permute-start | bytes 491528 | tf_op jit(solution)/shard_map/ppermute | solution.py:376
  32.8 10.7 %collective-permute-start.7 = (bf16[32,2560]{1,0:T(8,128)(2,1)S(1)}, bf16[32,2560]{1,0:T(8,128)(2,1)S(1)}, u32[]{:S(2)}, u32[]{:S(2)}) collective-permute-start(bf16[32,2560]{1,0:T(8,128)(2,1)S(1)} %collective-permute-done.6.refs_14_), channel_id=1, source_target_pairs={{0,16},{16,32},{32,48},{48,64},{64,80},{80,96},{96,112},{112,0},{1... | collective-permute-start | bytes 491528 | tf_op jit(solution)/shard_map/ppermute | solution.py:374
  36.0 7.5 %collective-permute-start.13 = (bf16[32,2560]{1,0:T(8,128)(2,1)S(1)}, bf16[32,2560]{1,0:T(8,128)(2,1)S(1)}, u32[]{:S(2)}, u32[]{:S(2)}) collective-permute-start(bf16[32,2560]{1,0:T(8,128)(2,1)S(1)} %collective-permute-done.12.refs_15_), channel_id=1, source_target_pairs={{0,16},{16,32},{32,48},{48,64},{64,80},{80,96},{96,112},{112,0},{1... | collective-permute-start | bytes 491528 | tf_op jit(solution)/shard_map/ppermute | solution.py:374
  36.0 7.6 %collective-permute-start.3 = (bf16[32,2560]{1,0:T(8,128)(2,1)S(1)}, bf16[32,2560]{1,0:T(8,128)(2,1)S(1)}, u32[]{:S(2)}, u32[]{:S(2)}) collective-permute-start(bf16[32,2560]{1,0:T(8,128)(2,1)S(1)} %collective-permute-done.1.refs_2_), channel_id=1, source_target_pairs={{0,112},{16,0},{32,16},{48,32},{64,48},{80,64},{96,80},{112,96},{1... | collective-permute-start | bytes 491528 | tf_op jit(solution)/shard_map/ppermute | solution.py:376
  38.7 9.4 %collective-permute-start.10 = (bf16[32,2560]{1,0:T(8,128)(2,1)S(1)}, bf16[32,2560]{1,0:T(8,128)(2,1)S(1)}, u32[]{:S(2)}, u32[]{:S(2)}) collective-permute-start(bf16[32,2560]{1,0:T(8,128)(2,1)S(1)} %collective-permute-done.4.refs_5_), channel_id=1, source_target_pairs={{0,112},{16,0},{32,16},{48,32},{64,48},{80,64},{96,80},{112,96},{1... | collective-permute-start | bytes 491528 | tf_op jit(solution)/shard_map/ppermute | solution.py:376
  43.5 7.4 %collective-permute-start.8 = (bf16[32,2560]{1,0:T(8,128)(2,1)S(1)}, bf16[32,2560]{1,0:T(8,128)(2,1)S(1)}, u32[]{:S(2)}, u32[]{:S(2)}) collective-permute-start(bf16[32,2560]{1,0:T(8,128)(2,1)S(1)} %collective-permute-done.7.refs_12_), channel_id=1, source_target_pairs={{0,16},{16,32},{32,48},{48,64},{64,80},{80,96},{96,112},{112,0},{1... | collective-permute-start | bytes 491528 | tf_op jit(solution)/shard_map/ppermute | solution.py:374
  43.5 8.9 %collective-permute-start.14 = (bf16[32,2560]{1,0:T(8,128)(2,1)S(1)}, bf16[32,2560]{1,0:T(8,128)(2,1)S(1)}, u32[]{:S(2)}, u32[]{:S(2)}) collective-permute-start(bf16[32,2560]{1,0:T(8,128)(2,1)S(1)} %collective-permute-done.13.refs_13_), channel_id=1, source_target_pairs={{0,16},{16,32},{32,48},{48,64},{64,80},{80,96},{96,112},{112,0},{1... | collective-permute-start | bytes 491528 | tf_op jit(solution)/shard_map/ppermute | solution.py:374
  43.6 8.8 %collective-permute-start.15 = (bf16[32,2560]{1,0:T(8,128)(2,1)S(1)}, bf16[32,2560]{1,0:T(8,128)(2,1)S(1)}, u32[]{:S(2)}, u32[]{:S(2)}) collective-permute-start(bf16[32,2560]{1,0:T(8,128)(2,1)S(1)} %collective-permute-done.3.refs_4_), channel_id=1, source_target_pairs={{0,112},{16,0},{32,16},{48,32},{64,48},{80,64},{96,80},{112,96},{1... | collective-permute-start | bytes 491528 | tf_op jit(solution)/shard_map/ppermute | solution.py:376
  56.3 6.6 %collective-permute-start.16 = (bf16[480,1280]{1,0:T(8,128)(2,1)S(1)}, bf16[480,1280]{1,0:T(8,128)(2,1)S(1)}, u32[]{:S(2)}, u32[]{:S(2)}) collective-permute-start(bf16[480,1280]{1,0:T(8,128)(2,1)S(1)} %collective-permute-done.5.refs_16_), channel_id=1, source_target_pairs={{0,1},{1,0},{2,3},{3,2},{4,5},{5,4},{6,7},{7,6},{8,9},{9,8},{10,11... | collective-permute-start | bytes 3686408 | tf_op jit(solution)/shard_map/ppermute | solution.py:381
  66.5 10.4 %collective-permute-start.18 = (bf16[4,64,640]{2,1,0:T(8,128)(2,1)S(1)}, bf16[4,64,640]{2,1,0:T(8,128)(2,1)S(1)}, u32[]{:S(2)}, u32[]{:S(2)}) collective-permute-start(bf16[4,64,640]{2,1,0:T(8,128)(2,1)S(1)} %get-tuple-element.48), channel_id=1, source_target_pairs={{0,2},{2,4},{4,6},{6,14},{14,12},{12,10},{10,8},{8,136},{136,138},... | collective-permute-start | bytes 983048 | tf_op jit(solution)/shard_map/ppermute | solution.py:387
  69.8 10.8 %collective-permute-start.19 = (bf16[4,64,640]{2,1,0:T(8,128)(2,1)S(1)}, bf16[4,64,640]{2,1,0:T(8,128)(2,1)S(1)}, u32[]{:S(2)}, u32[]{:S(2)}) collective-permute-start(bf16[4,64,640]{2,1,0:T(8,128)(2,1)S(1)} %get-tuple-element.49), channel_id=1, source_target_pairs={{2,0},{4,2},{6,4},{14,6},{12,14},{10,12},{8,10},{136,8},{138,136},... | collective-permute-start | bytes 983048 | tf_op jit(solution)/shard_map/ppermute | solution.py:388
  85.6 14.6 %collective-permute-start.22 = (bf16[2,8,1280]{2,1,0:T(8,128)(2,1)S(1)}, bf16[2,8,1280]{2,1,0:T(8,128)(2,1)S(1)}, u32[]{:S(2)}, u32[]{:S(2)}) collective-permute-start(bf16[2,8,1280]{2,1,0:T(8,128)(2,1)S(1)} %get-tuple-element.57), channel_id=1, source_target_pairs={{0,0},{1,128},{2,2},{3,130},{4,4},{5,132},{6,6},{7,134},{8,8},{9,1... | collective-permute-start | bytes 122888 | tf_op jit(solution)/shard_map/ppermute | solution.py:397
  87.5 15.1 %collective-permute-start.23 = (bf16[2,8,1280]{2,1,0:T(8,128)(2,1)S(1)}, bf16[2,8,1280]{2,1,0:T(8,128)(2,1)S(1)}, u32[]{:S(2)}, u32[]{:S(2)}) collective-permute-start(bf16[2,8,1280]{2,1,0:T(8,128)(2,1)S(1)} %get-tuple-element.58), channel_id=1, source_target_pairs={{0,2},{1,130},{2,0},{3,128},{4,6},{5,134},{6,4},{7,132},{8,10},{9,... | collective-permute-start | bytes 122888 | tf_op jit(solution)/shard_map/ppermute | solution.py:397
  92.3 15.6 %collective-permute-start.24 = (bf16[2,8,1280]{2,1,0:T(8,128)(2,1)S(1)}, bf16[2,8,1280]{2,1,0:T(8,128)(2,1)S(1)}, u32[]{:S(2)}, u32[]{:S(2)}) collective-permute-start(bf16[2,8,1280]{2,1,0:T(8,128)(2,1)S(1)} %get-tuple-element.59), channel_id=1, source_target_pairs={{0,4},{1,132},{2,6},{3,134},{4,0},{5,128},{6,2},{7,130},{8,12},{9,... | collective-permute-start | bytes 122888 | tf_op jit(solution)/shard_map/ppermute | solution.py:397
  100.2 8.9 %collective-permute-start.25 = (bf16[2,8,1280]{2,1,0:T(8,128)(2,1)S(1)}, bf16[2,8,1280]{2,1,0:T(8,128)(2,1)S(1)}, u32[]{:S(2)}, u32[]{:S(2)}) collective-permute-start(bf16[2,8,1280]{2,1,0:T(8,128)(2,1)S(1)} %get-tuple-element.60), channel_id=1, source_target_pairs={{0,6},{1,134},{2,4},{3,132},{4,2},{5,130},{6,0},{7,128},{8,14},{9,... | collective-permute-start | bytes 122888 | tf_op jit(solution)/shard_map/ppermute | solution.py:397
  100.2 9.0 %collective-permute-start.26 = (bf16[2,8,1280]{2,1,0:T(8,128)(2,1)S(1)}, bf16[2,8,1280]{2,1,0:T(8,128)(2,1)S(1)}, u32[]{:S(2)}, u32[]{:S(2)}) collective-permute-start(bf16[2,8,1280]{2,1,0:T(8,128)(2,1)S(1)} %get-tuple-element.61), channel_id=1, source_target_pairs={{0,8},{1,136},{2,10},{3,138},{4,12},{5,140},{6,14},{7,142},{8,0},{... | collective-permute-start | bytes 122888 | tf_op jit(solution)/shard_map/ppermute | solution.py:397
  100.2 9.0 %collective-permute-start.27 = (bf16[2,8,1280]{2,1,0:T(8,128)(2,1)S(1)}, bf16[2,8,1280]{2,1,0:T(8,128)(2,1)S(1)}, u32[]{:S(2)}, u32[]{:S(2)}) collective-permute-start(bf16[2,8,1280]{2,1,0:T(8,128)(2,1)S(1)} %get-tuple-element.62), channel_id=1, source_target_pairs={{0,10},{1,138},{2,8},{3,136},{4,14},{5,142},{6,12},{7,140},{8,2},{... | collective-permute-start | bytes 122888 | tf_op jit(solution)/shard_map/ppermute | solution.py:397
  102.6 7.4 %collective-permute-start.28 = (bf16[2,8,1280]{2,1,0:T(8,128)(2,1)S(1)}, bf16[2,8,1280]{2,1,0:T(8,128)(2,1)S(1)}, u32[]{:S(2)}, u32[]{:S(2)}) collective-permute-start(bf16[2,8,1280]{2,1,0:T(8,128)(2,1)S(1)} %get-tuple-element.63), channel_id=1, source_target_pairs={{0,12},{1,140},{2,14},{3,142},{4,8},{5,136},{6,10},{7,138},{8,4},{... | collective-permute-start | bytes 122888 | tf_op jit(solution)/shard_map/ppermute | solution.py:397
  107.9 6.7 %collective-permute-start.29 = (bf16[2,8,1280]{2,1,0:T(8,128)(2,1)S(1)}, bf16[2,8,1280]{2,1,0:T(8,128)(2,1)S(1)}, u32[]{:S(2)}, u32[]{:S(2)}) collective-permute-start(bf16[2,8,1280]{2,1,0:T(8,128)(2,1)S(1)} %get-tuple-element.64), channel_id=1, source_target_pairs={{0,14},{1,142},{2,12},{3,140},{4,10},{5,138},{6,8},{7,136},{8,6},{... | collective-permute-start | bytes 122888 | tf_op jit(solution)/shard_map/ppermute | solution.py:397
  (12 other events, 69.4 us)

commit v4 on v3

v4 whole, which is shorter than its diff:
```python
import jax
import jax.numpy as jnp
from jax import lax
from jax.experimental import pallas as pl
from jax.experimental.pallas import tpu as pltpu
from jax.sharding import Mesh, PartitionSpec as P

HEAD_DIM = 160
QKV = 3 * HEAD_DIM
ROWS = 8
WIN = 4
COLS = 128
HALF = COLS // 2
KEY_ROWS = ROWS + 2 * WIN
EPS = 1e-06
BIG = 1e30
LOG2E = 1.4426950408889634
LAT, LON = 16, 16
AXES = ("y_lo", "z", "y_hi", "x", "core")
SIZES = (2, 8, 2, 4, 2)
NT = (((1,), (1,)), ((), ()))
MIB = 1024 * 1024
SMEM = pl.BlockSpec(memory_space=pltpu.SMEM)
VMEM = pl.BlockSpec(memory_space=pltpu.VMEM)


def place_of(block):
    y_lo, rest = block // 8, block % 8
    side, k = rest // 4, rest % 4
    return y_lo, side ^ y_lo, k if side == 0 else 3 - k


def block_of(y_lo, y_hi, x):
    side = y_hi ^ y_lo
    return y_lo * 8 + side * 4 + jnp.where(side == 0, x, 3 - x)


def flat(*pairs):
    index = 0
    for coordinate, size in pairs:
        index = index * size + coordinate
    return index


def spread_perm():
    pairs = []
    for y_lo in range(2):
        for z in range(8):
            _, to_y_hi, to_x = place_of(y_lo * 8 + z)
            for s in range(8):
                for core in range(2):
                    to_z = (s + 2 * z + 4 * core) % 8
                    source = flat((y_lo, 2), (z, 8), (s, 8), (core, 2))
                    target = flat((y_lo, 2), (to_z, 8), (to_y_hi, 2), (to_x, 4), (core, 2))
                    pairs.append((source, target))
    return pairs


def neighbour_perm(step):
    pairs = []
    for block in range(16):
        if 0 <= block + step < 16:
            here, there = place_of(block), place_of(block + step)
            pairs.append(
                (
                    flat((here[0], 2), (here[1], 2), (here[2], 4)),
                    flat((there[0], 2), (there[1], 2), (there[2], 4)),
                )
            )
    return pairs


def return_perm(k):
    pairs = []
    for y_lo in range(2):
        for s in range(8):
            for core in range(2):
                source = flat((y_lo, 2), (s, 8), (core, 2))
                pairs.append((source, flat((core, 2), (s ^ k, 8), (y_lo, 2))))
    return pairs


SWAP = [(0, 1), (1, 0)]


def normalized(p):
    lane = lax.broadcasted_iota(jnp.int32, (1, QKV), 1)
    is_q = lane < HEAD_DIM
    is_k = (lane >= HEAD_DIM) & (lane < 2 * HEAD_DIM)
    squares = p * p
    q_mean = jnp.sum(jnp.where(is_q, squares, 0.0), axis=-1, keepdims=True) / HEAD_DIM
    k_mean = jnp.sum(jnp.where(is_k, squares, 0.0), axis=-1, keepdims=True) / HEAD_DIM
    scale = jnp.where(is_q, lax.rsqrt(q_mean + EPS), jnp.where(is_k, lax.rsqrt(k_mean + EPS), 1.0))
    groups = p.shape[0] // (8 * ROWS)
    p = (p * scale).reshape(groups, ROWS, 8, QKV)
    return [p[:, r].reshape(8 * groups, QKV).astype(jnp.bfloat16) for r in range(ROWS)]


def project_kernel(flags, *refs):
    pieces, (own, mine, theirs), (keep, send, top, bottom, x_ref) = refs[:-8], refs[-8:-5], refs[-5:]
    for i, piece in enumerate(pieces):
        x_ref[32 * i : 32 * (i + 1), :] = piece[...]
    width = mine.shape[1]
    near = pl.ds(pl.multiple_of(flags[1] * width, width), width)
    far = pl.ds(pl.multiple_of((1 - flags[1]) * width, width), width)
    p = lax.dot_general(x_ref[...], own[...], NT, preferred_element_type=jnp.float32)
    own_rows = normalized(p)
    p = lax.dot_general(x_ref[:, near], mine[...], NT, preferred_element_type=jnp.float32)
    p += lax.dot_general(x_ref[:, far], theirs[...], NT, preferred_element_type=jnp.float32)
    other_rows = normalized(p)

    def store(first, second):
        for r in range(ROWS):
            keep[r] = first[r]
            send[r] = second[r]
            edge = top if r < WIN else bottom
            edge[r % WIN] = jnp.concatenate([first[r][:, HEAD_DIM:], second[r][:, HEAD_DIM:]], axis=1)

    @pl.when(flags[0] == 1)
    def _():
        store(own_rows, other_rows)

    @pl.when(flags[0] != 1)
    def _():
        store(other_rows, own_rows)


def project(flags, pieces, own, mine, theirs, cost):
    tokens = 32 * len(pieces)
    whole = jax.ShapeDtypeStruct((ROWS, tokens // 8, QKV), jnp.bfloat16)
    edge = jax.ShapeDtypeStruct((WIN, tokens // 8, 4 * HEAD_DIM), jnp.bfloat16)
    return pl.pallas_call(
        project_kernel,
        out_shape=[whole, whole, edge, edge],
        in_specs=[SMEM] + [VMEM] * (len(pieces) + 3),
        out_specs=[VMEM] * 4,
        scratch_shapes=[pltpu.VMEM((tokens, own.shape[1]), jnp.bfloat16)],
        compiler_params=pltpu.CompilerParams(vmem_limit_bytes=20 * MIB),
        cost_estimate=pl.CostEstimate(
            flops=cost, bytes_accessed=MIB, transcendentals=0
        ),
        name=f"project_{tokens}",
    )(flags, *pieces, own, mine, theirs)


def put(ks, vs, first, key, value):
    at = pl.ds(first, key.shape[0])
    ks[at, :] = key
    vs[at, :HEAD_DIM] = value
    is_one = lax.broadcasted_iota(jnp.int32, (key.shape[0], 256 - HEAD_DIM), 1) == 0
    vs[at, HEAD_DIM:] = jnp.where(is_one, 1.0, 0.0).astype(jnp.bfloat16)


def group_of(i):
    return i ^ ((i >> 1) & 2)


def columns(base, core, shape, dim):
    at = lax.broadcasted_iota(jnp.int32, shape, dim)
    side = core ^ (at >> 6)
    return ((base + group_of((at >> 3) & 7) - 4 * side) & 7) * 16 + side * 8 + (at & 7)


def fill_masks(masks, first, query_base, key_base, core, radius):
    square = (COLS, COLS)
    gap = (columns(query_base, core, square, 0) - columns(key_base, core, square, 1) + radius) & (COLS - 1)
    near = jnp.where(gap <= 2 * radius, 1.0, 0.0)
    for d in range(WIN + 1):
        masks[first + d] = jnp.where(radius >= d, near, 0.0)


def shifts(usable, key_base, core):
    square = (COLS, COLS)
    there = lax.broadcasted_iota(jnp.int32, square, 0) == columns(key_base, core, square, 1)
    moved = jnp.dot(usable[...], jnp.where(there, 1.0, 0.0), preferred_element_type=jnp.float32)
    return jnp.where(moved > 0.5, 0.0, -BIG)


def query_of(parts, r):
    return jnp.concatenate([part[r][:, :HEAD_DIM] for part in parts], axis=0)


def scores_of(query, ks, row):
    keys = ks[row * COLS : (row + 1) * COLS, :]
    return lax.dot_general(query, keys, NT, preferred_element_type=jnp.float32)


def inner_kernel(ints, factor_ref, band, usable, *refs):
    parts, (zonal_ref, window_ref, ks, vs, masks) = refs[:4], refs[4:]
    factor = factor_ref[0]
    start = 0
    for part in parts:
        for r in range(ROWS):
            whole = part[r]
            put(ks, vs, r * COLS + start, whole[:, HEAD_DIM : 2 * HEAD_DIM], whole[:, 2 * HEAD_DIM :])
        start += part.shape[1]
    fill_masks(masks, 0, ints[0], ints[0], ints[1], ints[2])
    bias = shifts(usable, ints[0], ints[1])
    eye = lax.broadcasted_iota(jnp.int32, (COLS, COLS), 0) == lax.broadcasted_iota(jnp.int32, (COLS, COLS), 1)
    for r in range(ROWS):
        query = query_of(parts, r)
        low, high = max(0, r - WIN), min(ROWS, r + WIN + 1)
        zonal_parts, window_parts = [], []
        for row in range(ROWS):
            shift = bias[WIN + row : WIN + row + 1, :]
            if row == r:
                shift = jnp.where(eye, 0.0, shift)
            weights = jnp.exp2(scores_of(query, ks, row) * factor + shift)
            zonal_parts.append((weights * band[r * ROWS + row]).astype(jnp.bfloat16))
            if low <= row < high:
                window_parts.append((weights * masks[abs(row - r)]).astype(jnp.bfloat16))
        zonal = jnp.dot(jnp.concatenate(zonal_parts, axis=1), vs[...], preferred_element_type=jnp.float32)
        window_ref[r] = jnp.dot(
            jnp.concatenate(window_parts, axis=1),
            vs[low * COLS : high * COLS, :],
            preferred_element_type=jnp.float32,
        )
        zonal_ref[r] = (zonal[:, :HEAD_DIM] / zonal[:, HEAD_DIM : HEAD_DIM + 1]).astype(jnp.bfloat16)


def inner(ints, factor, band, usable, parts):
    return pl.pallas_call(
        inner_kernel,
        out_shape=[
            jax.ShapeDtypeStruct((ROWS, COLS, HEAD_DIM), jnp.bfloat16),
            jax.ShapeDtypeStruct((ROWS, COLS, 256), jnp.float32),
        ],
        in_specs=[SMEM] * 3 + [VMEM] * 5,
        out_specs=[VMEM] * 2,
        scratch_shapes=[
            pltpu.VMEM((ROWS * COLS, HEAD_DIM), jnp.bfloat16),
            pltpu.VMEM((ROWS * COLS, 256), jnp.bfloat16),
            pltpu.VMEM((WIN + 1, COLS, COLS), jnp.float32),
        ],
        compiler_params=pltpu.CompilerParams(vmem_limit_bytes=16 * MIB),
        cost_estimate=pl.CostEstimate(flops=10**7, bytes_accessed=10**5, transcendentals=0),
        name="inner",
    )(ints, factor, band, usable, *parts)


def outer_kernel(ints, factor_ref, usable, zonal_ref, window_ref, *refs):
    parts, edges, chunks, (ks, vs, masks, out) = refs[:4], refs[4:12], refs[12:20], refs[20:]
    factor = factor_ref[0]
    base, core, radius = ints[0], ints[1], ints[2]
    for side in range(2):
        start = 0
        for e, edge in enumerate(edges[4 * side : 4 * side + 4]):
            at = 2 * HEAD_DIM * (e // 2)
            for r in range(WIN):
                whole = edge[r][:, at : at + 2 * HEAD_DIM]
                put(ks, vs, (side * WIN + r) * COLS + start, whole[:, :HEAD_DIM], whole[:, HEAD_DIM:])
            start += edge.shape[1]
    fill_masks(masks, 0, base, base + 2, core, radius)
    fill_masks(masks, WIN + 1, base, base - 2, core, radius)
    above, below = shifts(usable, base + 2, core), shifts(usable, base - 2, core)
    for r in range(ROWS):
        query = query_of(parts, r)
        rows = range(r, WIN) if r < WIN else range(WIN, r + 1)
        window_parts = []
        for row in rows:
            gap = r + WIN - row if r < WIN else ROWS + row - WIN - r
            shift = above[row : row + 1, :] if r < WIN else below[row + ROWS : row + ROWS + 1, :]
            weights = jnp.exp2(scores_of(query, ks, row) * factor + shift)
            mask = masks[gap] if r < WIN else masks[WIN + 1 + gap]
            window_parts.append((weights * mask).astype(jnp.bfloat16))
        values = vs[rows[0] * COLS : (rows[-1] + 1) * COLS, :]
        window = window_ref[r] + jnp.dot(
            jnp.concatenate(window_parts, axis=1), values, preferred_element_type=jnp.float32
        )
        window = window[:, :HEAD_DIM] / window[:, HEAD_DIM : HEAD_DIM + 1]
        total = window + zonal_ref[r].astype(jnp.float32)
        out[:, :, :, r * HEAD_DIM : (r + 1) * HEAD_DIM] = total.reshape(2, 8, 8, HEAD_DIM)
    for k in range(8):
        chunks[k][0] = out[ints[3], ints[4 + k]].astype(jnp.bfloat16)
        chunks[k][1] = out[1 - ints[3], ints[12 + k]].astype(jnp.bfloat16)


def outer(ints, factor, usable, zonal, window, parts, edges):
    chunk = jax.ShapeDtypeStruct((2, 8, ROWS * HEAD_DIM), jnp.bfloat16)
    return pl.pallas_call(
        outer_kernel,
        out_shape=[chunk] * 8,
        in_specs=[SMEM, SMEM] + [VMEM] * 15,
        out_specs=[VMEM] * 8,
        scratch_shapes=[
            pltpu.VMEM((2 * WIN * COLS, HEAD_DIM), jnp.bfloat16),
            pltpu.VMEM((2 * WIN * COLS, 256), jnp.bfloat16),
            pltpu.VMEM((2 * WIN + 2, COLS, COLS), jnp.float32),
            pltpu.VMEM((2, 8, 8, ROWS * HEAD_DIM), jnp.float32),
        ],
        compiler_params=pltpu.CompilerParams(vmem_limit_bytes=16 * MIB),
        cost_estimate=pl.CostEstimate(
            flops=10**9, bytes_accessed=4 * MIB, transcendentals=10**6
        ),
        name="outer",
    )(ints, factor, usable, zonal, window, *parts, *edges)


def assemble_kernel(at, *refs):
    mains, got, out = refs[:8], refs[8], refs[9]
    width = ROWS * HEAD_DIM
    for k in range(8):
        out[0, :, pl.ds(pl.multiple_of(at[k] * width, 128), width)] = mains[k][0]
        out[0, :, pl.ds(pl.multiple_of(at[8 + k] * width, 128), width)] = got[k]


def assemble(at, mains, got):
    return pl.pallas_call(
        assemble_kernel,
        out_shape=jax.ShapeDtypeStruct((1, 8, LAT * ROWS * HEAD_DIM), jnp.bfloat16),
        in_specs=[SMEM] + [VMEM] * 9,
        out_specs=VMEM,
        compiler_params=pltpu.CompilerParams(vmem_limit_bytes=4 * MIB),
        cost_estimate=pl.CostEstimate(flops=0, bytes_accessed=MIB, transcendentals=0),
        name="assemble",
    )(at, *mains, got)


def body(tokens, w_qkv, key_mask, band_of_row, radius, qk_scale):
    y_lo, z, y_hi, x, core = (lax.axis_index(a) for a in AXES)
    sector = y_hi * 4 + x
    block = block_of(y_lo, y_hi, x)
    head = core * 8 + z
    model = tokens.shape[-1]

    wide = tokens.astype(jnp.float32)
    normed = wide * lax.rsqrt(jnp.mean(wide * wide, axis=-1, keepdims=True) + EPS)
    normed = jnp.transpose(normed.astype(jnp.bfloat16), (1, 0, 2)).reshape(64, model)
    first = lax.ppermute(normed, AXES, spread_perm())

    own = w_qkv[0]
    half = lax.dynamic_slice_in_dim(own, core * (model // 2), model // 2, 1)
    mine = lax.ppermute(half, "y_lo", SWAP)

    base = (z - 2 * block) & 7
    padded = jnp.pad(key_mask, ((0, 0), (WIN, WIN)))
    usable = lax.dynamic_slice_in_dim(padded, block * ROWS, KEY_ROWS, 1)
    usable = jnp.transpose(usable).astype(jnp.float32)
    ids = lax.dynamic_slice_in_dim(band_of_row, block * ROWS, ROWS, 0)
    band = (ids[:, None] == ids[None, :]).astype(jnp.float32).reshape(ROWS * ROWS)
    groups = [
        group_of(((sector ^ k) - base + 4 * side) & 7) for side in (y_lo, 1 - y_lo) for k in range(8)
    ]
    reach = lax.dynamic_index_in_dim(radius, head, keepdims=False)
    ints = jnp.stack([base, core, reach, core ^ y_lo] + groups).astype(jnp.int32)
    factor = lax.dynamic_slice_in_dim(qk_scale, head, 1, 0) / HEAD_DIM * LOG2E
    at = []
    for from_y_lo in (core, 1 - core):
        for k in range(8):
            source = sector ^ k
            at.append(block_of(from_y_lo, source >> 2, source & 3))
    at = jnp.stack(at).astype(jnp.int32)
    flags = jnp.stack([core == y_lo, core]).astype(jnp.int32)

    first, usable, band, ints, factor, at, flags = lax.optimization_barrier(
        (first, usable, band, ints, factor, at, flags)
    )

    up = [(i, (i + 1) % 8) for i in range(8)]
    down = [(i, (i - 1) % 8) for i in range(8)]
    shards = [[first[:32], first[32:]]] + [[None, None] for _ in range(7)]
    a, b = list(shards[0]), list(shards[0])
    for k in range(1, 5):
        for h in range(2):
            if k < 4 or h == 0:
                a[h] = shards[8 - k][h] = lax.ppermute(a[h], "z", up)
            if k < 4 or h == 1:
                b[h] = shards[k][h] = lax.ppermute(b[h], "z", down)
    tied = [(i, h) for i in (3, 5) for h in range(2)]
    mine, *values = lax.optimization_barrier((mine, *(shards[i][h] for i, h in tied)))
    for (i, h), value in zip(tied, values):
        shards[i][h] = value
    theirs = lax.ppermute(mine, "core", SWAP)

    ring = ("y_lo", "y_hi", "x")
    keeps, others, tops, bottoms = [], [], [], []
    for group, cost in (((0, 1, 2, 3, 6, 7), 2 * 10**10), ((4, 5), 10**8)):
        pieces = [shards[i][h] for i in group for h in range(2)]
        keep, send, top_rows, bottom_rows = project(flags, pieces, own, mine, theirs, cost)
        keeps.append(keep)
        tops.append(lax.ppermute(bottom_rows, ring, neighbour_perm(1)))
        bottoms.append(lax.ppermute(top_rows, ring, neighbour_perm(-1)))
        others.append(lax.ppermute(send, "core", SWAP))
    parts = keeps + others
    zonal, window = inner(ints, factor, band, usable, parts)
    edges = []
    for halo in (tops, bottoms):
        *halo, window = lax.optimization_barrier((*halo, window))
        edges += [*halo, *(lax.ppermute(part, "core", SWAP) for part in halo)]
    chunks = outer(ints, factor, usable, zonal, window, parts, edges)

    corners = ("y_lo", "y_hi", "x", "core")
    landed = [lax.ppermute(chunks[k], corners, return_perm(k)) for k in range(8)]
    give = jnp.stack([part[1] for part in landed])
    got = lax.ppermute(give, "core", SWAP)
    return assemble(at, landed, got)


def solution(mesh):
    wide = Mesh(mesh.devices.reshape(SIZES), AXES)
    lat, lon = ("y_lo", "z"), ("y_hi", "x", "core")
    in_specs = (P(lon, lat, None), P(lat, None, None), P(), P(), P(), P())
    out_specs = P(lat, lon, None)
    return jax.shard_map(body, mesh=wide, in_specs=in_specs, out_specs=out_specs, check_vma=False)
```

time: 118 us -> 118 us (level)
  waiting for transfers between devices: 28.6 us -> 20.5 us
  starting transfers between devices: 70.7 us -> 74.7 us
  local copies, waits for them, and re-layouts: 2.78 us -> 5.02 us
  Pallas kernels: 11.5 us -> 13.7 us
    ppermute x7, starting transfers between devices: 26.7 us -> 19 us  [body(): b[h] = shards[k][h] = lax.ppermute(b[h], 'z', down)]
    ppermute x5 -> x10, waiting for transfers between devices: 7.83 us -> 1.75 us  [the longest x4 1.28 us: body(): edges += [*halo, *(lax.ppermute(part, 'core', SWAP) for part in halo)]]
    ppermute x1, starting transfers between devices: 4.04 us -> 9.48 us  [body(): theirs = lax.ppermute(mine, 'core', SWAP)]
    ppermute x1, starting transfers between devices: 4.38 us -> 9.65 us  [body(): first = lax.ppermute(normed, AXES, spread_perm())]
    ppermute x5 -> x10, starting transfers between devices: 6.3 us -> 11 us  [the longest x2 5.55 us: body(): tops.append(lax.ppermute(bottom_rows, ring, neighbour_perm(1)))]
    ppermute x1, waiting for transfers between devices: 4.05 us -> 0.01 us  [body(): first = lax.ppermute(normed, AXES, spread_perm())]
    dynamic_slice x1, local copies, waits for them, and re-layouts: 0.09 us -> 2.57 us  [body(): half = lax.dynamic_slice_in_dim(own, core * (model // 2), model // 2, 1)]
    ppermute x8, starting transfers between devices: 23.5 us -> 21.1 us  [body(): lax.ppermute(chunks[k], corners, return_perm(k))]
  transfers between devices with their start and end apart: 31 -> 36, of which waited for: 14 -> 15; matrix products, arithmetic and copies ran while one was open for 3% -> 4% of each run, Pallas kernels for 4% -> 9%
where the time goes in v4:
time: 118 us; the launch traced here: 117 us
  starting transfers between devices  74.7 us (63%)
  waiting for transfers between devices  20.5 us (17%)
  Pallas kernels  13.7 us (12%)
  local copies, waits for them, and re-layouts  5.02 us (4%)
  other arithmetic  2.39 us (2%)
    ppermute x8, starting transfers between devices, body(): lax.ppermute(chunks[k], corners, return_perm(k))  21.1 us
    ppermute x7, starting transfers between devices, body(): b[h] = shards[k][h] = lax.ppermute(b[h], 'z', down)  19 us
    ppermute x1, starting transfers between devices, body(): first = lax.ppermute(normed, AXES, spread_perm())  9.65 us
    ppermute x1, starting transfers between devices, body(): theirs = lax.ppermute(mine, 'core', SWAP)  9.48 us
    ppermute x7, waiting for transfers between devices, body(): a[h] = shards[8 - k][h] = lax.ppermute(a[h], 'z', up)  7.47 us
    pallas_call x2, Pallas kernels, project(): pl.pallas_call(project_kernel, out_shape=[whole, whole, edge, edge], in_s...  6.95 us
    ppermute x8, waiting for transfers between devices, body(): lax.ppermute(chunks[k], corners, return_perm(k))  6.67 us
    ppermute x2, starting transfers between devices, body(): tops.append(lax.ppermute(bottom_rows, ring, neighbour_perm(1)))  5.55 us
  transfers between devices with their start and end apart: 36, of which 15 were waited for; matrix products, arithmetic and copies ran while one was open for 4% of the time, Pallas kernels for 9%

profile of v4, /device:TPU:1, one launch (start us, length us, event | category | flops | bytes accessed | tf_op | source)
XLA Modules:
  0.0 117.4 jit_solution(11356789466725115053)
XLA Ops:
  2.4 9.6 %collective-permute-start = (bf16[64,2560]{1,0:T(8,128)(2,1)S(1)}, bf16[64,2560]{1,0:T(8,128)(2,1)S(1)}, u32[]{:S(2)}, u32[]{:S(2)}) collective-permute-start(bf16[64,2560]{1,0:T(8,128)(2,1)S(1)} %bitcast.48), channel_id=1, source_target_pairs={{0,0},{1,65},{2,16},{3,81},{4,32},{5,97},{6,48},{7,113},{8,64},{9,... | collective-permute-start | bytes 983048 | tf_op jit(solution)/shard_map/ppermute | solution.py:329
  12.1 2.6 %dynamic-slice_bitcast_fusion = bf16[480,1280]{1,0:T(8,128)(2,1)} fusion(bf16[1,480,2560]{2,1,0:T(8,128)(2,1)} %param.7, s32[]{:T(128)S(6)} %select_n.86), kind=kLoop, calls=%fused_computation | loop fusion | bytes 2457604 | tf_op jit(solution)/shard_map/dynamic_slice | solution.py:332
  14.6 3.0 %collective-permute-start.5 = (bf16[480,1280]{1,0:T(8,128)(2,1)}, bf16[480,1280]{1,0:T(8,128)(2,1)}, u32[]{:S(2)}, u32[]{:S(2)}) collective-permute-start(bf16[480,1280]{1,0:T(8,128)(2,1)} %dynamic-slice_bitcast_fusion), channel_id=1, source_target_pairs={{0,128},{128,0},{1,129},{129,1},{2,130},{130,2},{3,131},{131,3},{4... | collective-permute-start | bytes 3686408 | tf_op jit(solution)/shard_map/ppermute | solution.py:333
  21.0 4.5 %collective-permute-start.1 = (bf16[32,2560]{1,0:T(8,128)(2,1)S(1)}, bf16[32,2560]{1,0:T(8,128)(2,1)S(1)}, u32[]{:S(2)}, u32[]{:S(2)}) collective-permute-start(bf16[32,2560]{1,0:T(8,128)(2,1)S(1)} %get-tuple-element.78.refs_0_), channel_id=1, source_target_pairs={{0,112},{16,0},{32,16},{48,32},{64,48},{80,64},{96,80},{112,96},{1... | collective-permute-start | bytes 491528 | tf_op jit(solution)/shard_map/ppermute | solution.py:368
  27.8 3.1 %collective-permute-start.3 = (bf16[32,2560]{1,0:T(8,128)(2,1)S(1)}, bf16[32,2560]{1,0:T(8,128)(2,1)S(1)}, u32[]{:S(2)}, u32[]{:S(2)}) collective-permute-start(bf16[32,2560]{1,0:T(8,128)(2,1)S(1)} %collective-permute-done.1.refs_2_), channel_id=1, source_target_pairs={{0,112},{16,0},{32,16},{48,32},{64,48},{80,64},{96,80},{112,96},{1... | collective-permute-start | bytes 491528 | tf_op jit(solution)/shard_map/ppermute | solution.py:368
  30.9 1.8 %collective-permute-start.4 = (bf16[32,2560]{1,0:T(8,128)(2,1)S(1)}, bf16[32,2560]{1,0:T(8,128)(2,1)S(1)}, u32[]{:S(2)}, u32[]{:S(2)}) collective-permute-start(bf16[32,2560]{1,0:T(8,128)(2,1)S(1)} %collective-permute-done.2.refs_3_), channel_id=1, source_target_pairs={{0,112},{16,0},{32,16},{48,32},{64,48},{80,64},{96,80},{112,96},{1... | collective-permute-start | bytes 491528 | tf_op jit(solution)/shard_map/ppermute | solution.py:368
  34.0 3.4 %collective-permute-start.6 = (bf16[32,2560]{1,0:T(8,128)(2,1)S(1)}, bf16[32,2560]{1,0:T(8,128)(2,1)S(1)}, u32[]{:S(2)}, u32[]{:S(2)}) collective-permute-start(bf16[32,2560]{1,0:T(8,128)(2,1)S(1)} %collective-permute-done.3.refs_4_), channel_id=1, source_target_pairs={{0,112},{16,0},{32,16},{48,32},{64,48},{80,64},{96,80},{112,96},{1... | collective-permute-start | bytes 491528 | tf_op jit(solution)/shard_map/ppermute | solution.py:368
  37.5 3.4 %collective-permute-start.7 = (bf16[32,2560]{1,0:T(8,128)(2,1)S(1)}, bf16[32,2560]{1,0:T(8,128)(2,1)S(1)}, u32[]{:S(2)}, u32[]{:S(2)}) collective-permute-start(bf16[32,2560]{1,0:T(8,128)(2,1)S(1)} %collective-permute-done.4.refs_5_), channel_id=1, source_target_pairs={{0,112},{16,0},{32,16},{48,32},{64,48},{80,64},{96,80},{112,96},{1... | collective-permute-start | bytes 491528 | tf_op jit(solution)/shard_map/ppermute | solution.py:368
  42.4 2.1 %collective-permute-done.7.refs_7_ = bf16[32,2560]{1,0:T(8,128)(2,1)S(1)} collective-permute-done((bf16[32,2560]{1,0:T(8,128)(2,1)S(1)}, bf16[32,2560]{1,0:T(8,128)(2,1)S(1)}, u32[]{:S(2)}, u32[]{:S(2)}) %collective-permute-start.7) | collective-permute-done | bytes 163872 | tf_op jit(solution)/shard_map/ppermute | solution.py:368
  44.5 1.8 %collective-permute-done.10.refs_2_ = bf16[32,2560]{1,0:T(8,128)(2,1)S(1)} collective-permute-done((bf16[32,2560]{1,0:T(8,128)(2,1)S(1)}, bf16[32,2560]{1,0:T(8,128)(2,1)S(1)}, u32[]{:S(2)}, u32[]{:S(2)}) %collective-permute-start.10) | collective-permute-done | bytes 163872 | tf_op jit(solution)/shard_map/ppermute | solution.py:366
  46.3 3.0 %collective-permute-done.13.refs_3_ = bf16[32,2560]{1,0:T(8,128)(2,1)S(1)} collective-permute-done((bf16[32,2560]{1,0:T(8,128)(2,1)S(1)}, bf16[32,2560]{1,0:T(8,128)(2,1)S(1)}, u32[]{:S(2)}, u32[]{:S(2)}) %collective-permute-start.13) | collective-permute-done | bytes 163872 | tf_op jit(solution)/shard_map/ppermute | solution.py:366
  49.3 9.5 %collective-permute-start.14 = (bf16[480,1280]{1,0:T(8,128)(2,1)}, bf16[480,1280]{1,0:T(8,128)(2,1)S(1)}, u32[]{:S(2)}, u32[]{:S(2)}) collective-permute-start(bf16[480,1280]{1,0:T(8,128)(2,1)} %collective-permute-done.5.refs_13_.refs_5_), channel_id=1, source_target_pairs={{0,1},{1,0},{2,3},{3,2},{4,5},{5,4},{6,7},{7,6},{8,9},{9,8},{10,11... | collective-permute-start | bytes 3686408 | tf_op jit(solution)/shard_map/ppermute | solution.py:373
  58.8 2.7 %collective-permute-start.16 = (bf16[32,2560]{1,0:T(8,128)(2,1)S(1)}, bf16[32,2560]{1,0:T(8,128)(2,1)S(1)}, u32[]{:S(2)}, u32[]{:S(2)}) collective-permute-start(bf16[32,2560]{1,0:T(8,128)(2,1)S(1)} %collective-permute-done.7.refs_7_), channel_id=1, source_target_pairs={{0,112},{16,0},{32,16},{48,32},{64,48},{80,64},{96,80},{112,96},{1... | collective-permute-start | bytes 491528 | tf_op jit(solution)/shard_map/ppermute | solution.py:368
  61.6 3.9 %project_384.1 = (bf16[8,48,480]{2,1,0:T(8,128)(2,1)S(1)}, bf16[8,48,480]{2,1,0:T(8,128)(2,1)S(1)}, bf16[4,48,640]{2,1,0:T(8,128)(2,1)S(1)}, bf16[4,48,640]{2,1,0:T(8,128)(2,1)S(1)}) custom-call(s32[2]{0:T(128)S(1)} %pad_add_fusion.flags, bf16[32,2560]{1,0:T(8,128)(2,1)S(1)} %get-tuple-element.78.refs_0_, bf16[32,2560]{1,0:T(8,128)(2,1)S(1)} %get-tuple-element.77.refs_1_, ...), custom_call_target="tpu_custom_call" | custom-call | flops 20000000000 | bytes 1048576 | tf_op jit(solution)/shard_map/project_384/pallas_call | solution.py:132
  68.7 3.1 %project_128.1 = (bf16[8,16,480]{2,1,0:T(8,128)(2,1)S(1)}, bf16[8,16,480]{2,1,0:T(8,128)(2,1)S(1)}, bf16[4,16,640]{2,1,0:T(8,128)(2,1)S(1)}, bf16[4,16,640]{2,1,0:T(8,128)(2,1)S(1)}) custom-call(s32[2]{0:T(128)S(1)} %pad_add_fusion.flags, bf16[32,2560]{1,0:T(8,128)(2,1)S(1)} %collective-permute-done.15.refs_0_, ...), custom_call_target="tpu_custom_call" | custom-call | flops 100000000 | bytes 1048576 | tf_op jit(solution)/shard_map/project_128/pallas_call | solution.py:132
  71.9 4.3 %collective-permute-start.22 = (bf16[4,16,640]{2,1,0:T(8,128)(2,1)S(1)}, bf16[4,16,640]{2,1,0:T(8,128)(2,1)S(1)}, u32[]{:S(2)}, u32[]{:S(2)}) collective-permute-start(bf16[4,16,640]{2,1,0:T(8,128)(2,1)S(1)} %get-tuple-element.61), channel_id=1, source_target_pairs={{0,2},{2,4},{4,6},{6,14},{14,12},{12,10},{10,8},{8,136},{136,138},... | collective-permute-start | bytes 245768 | tf_op jit(solution)/shard_map/ppermute | solution.py:381
  77.4 3.4 %inner.1 = (bf16[8,128,160]{2,1,0:T(8,128)(2,1)S(1)}, f32[8,128,256]{2,1,0:T(8,128)S(1)}) custom-call(s32[20]{0:T(128)S(1)} %stack.144.ints, f32[1]{0:T(128)S(6)} %mul.133.factor_ref, f32[64]{0:T(128)S(1)} %reshape.21.band, f32[16,128]{1,0:T(8,128)S(1)} %fusion.4.usable, bf16[8,48,480]{2,1,0:T(8,128)(2,1)S(1)} %get-tuple-element.51.refs_0_, ...), custom_call_target="tpu_custom_call" | custom-call | flops 10000000 | bytes 100000 | tf_op jit(solution)/shard_map/inner/pallas_call | solution.py:222
  84.8 2.1 %outer.1 = (bf16[2,8,1280]{2,1,0:T(8,128)(2,1)S(1)}, bf16[2,8,1280]{2,1,0:T(8,128)(2,1)S(1)}, bf16[2,8,1280]{2,1,0:T(8,128)(2,1)S(1)}, bf16[2,8,1280]{2,1,0:T(8,...) custom-call(s32[20]{0:T(128)S(1)} %stack.144.ints, ...), custom_call_target="tpu_custom_call" | custom-call | flops 1000000000 | bytes 4194304 | tf_op jit(solution)/shard_map/outer/pallas_call | solution.py:280
  86.8 2.1 %collective-permute-start.27 = (bf16[2,8,1280]{2,1,0:T(8,128)(2,1)S(1)}, bf16[2,8,1280]{2,1,0:T(8,128)(2,1)S(1)}, u32[]{:S(2)}, u32[]{:S(2)}) collective-permute-start(bf16[2,8,1280]{2,1,0:T(8,128)(2,1)S(1)} %get-tuple-element.69), channel_id=1, source_target_pairs={{0,0},{1,128},{2,2},{3,130},{4,4},{5,132},{6,6},{7,134},{8,8},{9,1... | collective-permute-start | bytes 122888 | tf_op jit(solution)/shard_map/ppermute | solution.py:393
  89.0 3.8 %collective-permute-start.28 = (bf16[2,8,1280]{2,1,0:T(8,128)(2,1)S(1)}, bf16[2,8,1280]{2,1,0:T(8,128)(2,1)S(1)}, u32[]{:S(2)}, u32[]{:S(2)}) collective-permute-start(bf16[2,8,1280]{2,1,0:T(8,128)(2,1)S(1)} %get-tuple-element.70), channel_id=1, source_target_pairs={{0,2},{1,130},{2,0},{3,128},{4,6},{5,134},{6,4},{7,132},{8,10},{9,... | collective-permute-start | bytes 122888 | tf_op jit(solution)/shard_map/ppermute | solution.py:393
  92.7 6.3 %collective-permute-start.29 = (bf16[2,8,1280]{2,1,0:T(8,128)(2,1)S(1)}, bf16[2,8,1280]{2,1,0:T(8,128)(2,1)S(1)}, u32[]{:S(2)}, u32[]{:S(2)}) collective-permute-start(bf16[2,8,1280]{2,1,0:T(8,128)(2,1)S(1)} %get-tuple-element.71), channel_id=1, source_target_pairs={{0,4},{1,132},{2,6},{3,134},{4,0},{5,128},{6,2},{7,130},{8,12},{9,... | collective-permute-start | bytes 122888 | tf_op jit(solution)/shard_map/ppermute | solution.py:393
  101.4 6.6 %collective-permute-start.33 = (bf16[2,8,1280]{2,1,0:T(8,128)(2,1)S(1)}, bf16[2,8,1280]{2,1,0:T(8,128)(2,1)S(1)}, u32[]{:S(2)}, u32[]{:S(2)}) collective-permute-start(bf16[2,8,1280]{2,1,0:T(8,128)(2,1)S(1)} %get-tuple-element.75), channel_id=1, source_target_pairs={{0,12},{1,140},{2,14},{3,142},{4,8},{5,136},{6,10},{7,138},{8,4},{... | collective-permute-start | bytes 122888 | tf_op jit(solution)/shard_map/ppermute | solution.py:393
  108.1 2.0 %collective-permute-done.33.refs_6_ = bf16[2,8,1280]{2,1,0:T(8,128)(2,1)S(1)} collective-permute-done((bf16[2,8,1280]{2,1,0:T(8,128)(2,1)S(1)}, bf16[2,8,1280]{2,1,0:T(8,128)(2,1)S(1)}, u32[]{:S(2)}, u32[]{:S(2)}) %collective-permute-start.33) | collective-permute-done | bytes 40992 | tf_op jit(solution)/shard_map/ppermute | solution.py:393
  110.1 4.6 %collective-permute-done.34.refs_7_ = bf16[2,8,1280]{2,1,0:T(8,128)(2,1)S(1)} collective-permute-done((bf16[2,8,1280]{2,1,0:T(8,128)(2,1)S(1)}, bf16[2,8,1280]{2,1,0:T(8,128)(2,1)S(1)}, u32[]{:S(2)}, u32[]{:S(2)}) %collective-permute-start.34) | collective-permute-done | bytes 40992 | tf_op jit(solution)/shard_map/ppermute | solution.py:393
  (87 shorter events, 23.8 us)
Async XLA Ops:
  2.4 18.6 %collective-permute-start = (bf16[64,2560]{1,0:T(8,128)(2,1)S(1)}, bf16[64,2560]{1,0:T(8,128)(2,1)S(1)}, u32[]{:S(2)}, u32[]{:S(2)}) collective-permute-start(bf16[64,2560]{1,0:T(8,128)(2,1)S(1)} %bitcast.48), channel_id=1, source_target_pairs={{0,0},{1,65},{2,16},{3,81},{4,32},{5,97},{6,48},{7,113},{8,64},{9,... | collective-permute-start | bytes 983048 | tf_op jit(solution)/shard_map/ppermute | solution.py:329
  14.6 34.7 %collective-permute-start.5 = (bf16[480,1280]{1,0:T(8,128)(2,1)}, bf16[480,1280]{1,0:T(8,128)(2,1)}, u32[]{:S(2)}, u32[]{:S(2)}) collective-permute-start(bf16[480,1280]{1,0:T(8,128)(2,1)} %dynamic-slice_bitcast_fusion), channel_id=1, source_target_pairs={{0,128},{128,0},{1,129},{129,1},{2,130},{130,2},{3,131},{131,3},{4... | collective-permute-start | bytes 3686408 | tf_op jit(solution)/shard_map/ppermute | solution.py:333
  21.0 6.8 %collective-permute-start.1 = (bf16[32,2560]{1,0:T(8,128)(2,1)S(1)}, bf16[32,2560]{1,0:T(8,128)(2,1)S(1)}, u32[]{:S(2)}, u32[]{:S(2)}) collective-permute-start(bf16[32,2560]{1,0:T(8,128)(2,1)S(1)} %get-tuple-element.78.refs_0_), channel_id=1, source_target_pairs={{0,112},{16,0},{32,16},{48,32},{64,48},{80,64},{96,80},{112,96},{1... | collective-permute-start | bytes 491528 | tf_op jit(solution)/shard_map/ppermute | solution.py:368
  25.6 7.0 %collective-permute-start.8 = (bf16[32,2560]{1,0:T(8,128)(2,1)S(1)}, bf16[32,2560]{1,0:T(8,128)(2,1)S(1)}, u32[]{:S(2)}, u32[]{:S(2)}) collective-permute-start(bf16[32,2560]{1,0:T(8,128)(2,1)S(1)} %get-tuple-element.78.refs_0_), channel_id=1, source_target_pairs={{0,16},{16,32},{32,48},{48,64},{64,80},{80,96},{96,112},{112,0},{1... | collective-permute-start | bytes 491528 | tf_op jit(solution)/shard_map/ppermute | solution.py:366
  27.0 6.8 %collective-permute-start.11 = (bf16[32,2560]{1,0:T(8,128)(2,1)S(1)}, bf16[32,2560]{1,0:T(8,128)(2,1)S(1)}, u32[]{:S(2)}, u32[]{:S(2)}) collective-permute-start(bf16[32,2560]{1,0:T(8,128)(2,1)S(1)} %get-tuple-element.77.refs_1_), channel_id=1, source_target_pairs={{0,16},{16,32},{32,48},{48,64},{64,80},{80,96},{96,112},{112,0},{1... | collective-permute-start | bytes 491528 | tf_op jit(solution)/shard_map/ppermute | solution.py:366
  32.7 8.3 %collective-permute-start.9 = (bf16[32,2560]{1,0:T(8,128)(2,1)S(1)}, bf16[32,2560]{1,0:T(8,128)(2,1)S(1)}, u32[]{:S(2)}, u32[]{:S(2)}) collective-permute-start(bf16[32,2560]{1,0:T(8,128)(2,1)S(1)} %collective-permute-done.8.refs_10_), channel_id=1, source_target_pairs={{0,16},{16,32},{32,48},{48,64},{64,80},{80,96},{96,112},{112,0},{1... | collective-permute-start | bytes 491528 | tf_op jit(solution)/shard_map/ppermute | solution.py:366
  33.8 8.6 %collective-permute-start.12 = (bf16[32,2560]{1,0:T(8,128)(2,1)S(1)}, bf16[32,2560]{1,0:T(8,128)(2,1)S(1)}, u32[]{:S(2)}, u32[]{:S(2)}) collective-permute-start(bf16[32,2560]{1,0:T(8,128)(2,1)S(1)} %collective-permute-done.11.refs_11_), channel_id=1, source_target_pairs={{0,16},{16,32},{32,48},{48,64},{64,80},{80,96},{96,112},{112,0},{1... | collective-permute-start | bytes 491528 | tf_op jit(solution)/shard_map/ppermute | solution.py:366
  34.0 8.4 %collective-permute-start.6 = (bf16[32,2560]{1,0:T(8,128)(2,1)S(1)}, bf16[32,2560]{1,0:T(8,128)(2,1)S(1)}, u32[]{:S(2)}, u32[]{:S(2)}) collective-permute-start(bf16[32,2560]{1,0:T(8,128)(2,1)S(1)} %collective-permute-done.3.refs_4_), channel_id=1, source_target_pairs={{0,112},{16,0},{32,16},{48,32},{64,48},{80,64},{96,80},{112,96},{1... | collective-permute-start | bytes 491528 | tf_op jit(solution)/shard_map/ppermute | solution.py:368
  37.5 7.0 %collective-permute-start.7 = (bf16[32,2560]{1,0:T(8,128)(2,1)S(1)}, bf16[32,2560]{1,0:T(8,128)(2,1)S(1)}, u32[]{:S(2)}, u32[]{:S(2)}) collective-permute-start(bf16[32,2560]{1,0:T(8,128)(2,1)S(1)} %collective-permute-done.4.refs_5_), channel_id=1, source_target_pairs={{0,112},{16,0},{32,16},{48,32},{64,48},{80,64},{96,80},{112,96},{1... | collective-permute-start | bytes 491528 | tf_op jit(solution)/shard_map/ppermute | solution.py:368
  42.4 6.9 %collective-permute-start.13 = (bf16[32,2560]{1,0:T(8,128)(2,1)S(1)}, bf16[32,2560]{1,0:T(8,128)(2,1)S(1)}, u32[]{:S(2)}, u32[]{:S(2)}) collective-permute-start(bf16[32,2560]{1,0:T(8,128)(2,1)S(1)} %collective-permute-done.12.refs_9_), channel_id=1, source_target_pairs={{0,16},{16,32},{32,48},{48,64},{64,80},{80,96},{96,112},{112,0},{1... | collective-permute-start | bytes 491528 | tf_op jit(solution)/shard_map/ppermute | solution.py:366
  49.3 12.2 %collective-permute-start.14 = (bf16[480,1280]{1,0:T(8,128)(2,1)}, bf16[480,1280]{1,0:T(8,128)(2,1)S(1)}, u32[]{:S(2)}, u32[]{:S(2)}) collective-permute-start(bf16[480,1280]{1,0:T(8,128)(2,1)} %collective-permute-done.5.refs_13_.refs_5_), channel_id=1, source_target_pairs={{0,1},{1,0},{2,3},{3,2},{4,5},{5,4},{6,7},{7,6},{8,9},{9,8},{10,11... | collective-permute-start | bytes 3686408 | tf_op jit(solution)/shard_map/ppermute | solution.py:373
  58.8 9.8 %collective-permute-start.15 = (bf16[32,2560]{1,0:T(8,128)(2,1)S(1)}, bf16[32,2560]{1,0:T(8,128)(2,1)S(1)}, u32[]{:S(2)}, u32[]{:S(2)}) collective-permute-start(bf16[32,2560]{1,0:T(8,128)(2,1)S(1)} %collective-permute-done.10.refs_2_), channel_id=1, source_target_pairs={{0,16},{16,32},{32,48},{48,64},{64,80},{80,96},{96,112},{112,0},{1... | collective-permute-start | bytes 491528 | tf_op jit(solution)/shard_map/ppermute | solution.py:366
  58.8 9.8 %collective-permute-start.16 = (bf16[32,2560]{1,0:T(8,128)(2,1)S(1)}, bf16[32,2560]{1,0:T(8,128)(2,1)S(1)}, u32[]{:S(2)}, u32[]{:S(2)}) collective-permute-start(bf16[32,2560]{1,0:T(8,128)(2,1)S(1)} %collective-permute-done.7.refs_7_), channel_id=1, source_target_pairs={{0,112},{16,0},{32,16},{48,32},{64,48},{80,64},{96,80},{112,96},{1... | collective-permute-start | bytes 491528 | tf_op jit(solution)/shard_map/ppermute | solution.py:368
  65.4 12.0 %collective-permute-start.17 = (bf16[8,48,480]{2,1,0:T(8,128)(2,1)S(1)}, bf16[8,48,480]{2,1,0:T(8,128)(2,1)S(1)}, u32[]{:S(2)}, u32[]{:S(2)}) collective-permute-start(bf16[8,48,480]{2,1,0:T(8,128)(2,1)S(1)} %get-tuple-element.55), channel_id=1, source_target_pairs={{0,1},{1,0},{2,3},{3,2},{4,5},{5,4},{6,7},{7,6},{8,9},{9,8},{10,11... | collective-permute-start | bytes 1105928 | tf_op jit(solution)/shard_map/ppermute | solution.py:383
  66.0 14.8 %collective-permute-start.21 = (bf16[4,48,640]{2,1,0:T(8,128)(2,1)S(1)}, bf16[4,48,640]{2,1,0:T(8,128)(2,1)S(1)}, u32[]{:S(2)}, u32[]{:S(2)}) collective-permute-start(bf16[4,48,640]{2,1,0:T(8,128)(2,1)S(1)} %get-tuple-element.60), channel_id=1, source_target_pairs={{0,2},{2,4},{4,6},{6,14},{14,12},{12,10},{10,8},{8,136},{136,138},... | collective-permute-start | bytes 737288 | tf_op jit(solution)/shard_map/ppermute | solution.py:381
  67.3 14.0 %collective-permute-start.19 = (bf16[4,48,640]{2,1,0:T(8,128)(2,1)S(1)}, bf16[4,48,640]{2,1,0:T(8,128)(2,1)S(1)}, u32[]{:S(2)}, u32[]{:S(2)}) collective-permute-start(bf16[4,48,640]{2,1,0:T(8,128)(2,1)S(1)} %get-tuple-element.58), channel_id=1, source_target_pairs={{2,0},{4,2},{6,4},{14,6},{12,14},{10,12},{8,10},{136,8},{138,136},... | collective-permute-start | bytes 737288 | tf_op jit(solution)/shard_map/ppermute | solution.py:382
  71.9 9.0 %collective-permute-start.22 = (bf16[4,16,640]{2,1,0:T(8,128)(2,1)S(1)}, bf16[4,16,640]{2,1,0:T(8,128)(2,1)S(1)}, u32[]{:S(2)}, u32[]{:S(2)}) collective-permute-start(bf16[4,16,640]{2,1,0:T(8,128)(2,1)S(1)} %get-tuple-element.61), channel_id=1, source_target_pairs={{0,2},{2,4},{4,6},{6,14},{14,12},{12,10},{10,8},{8,136},{136,138},... | collective-permute-start | bytes 245768 | tf_op jit(solution)/shard_map/ppermute | solution.py:381
  86.8 13.5 %collective-permute-start.27 = (bf16[2,8,1280]{2,1,0:T(8,128)(2,1)S(1)}, bf16[2,8,1280]{2,1,0:T(8,128)(2,1)S(1)}, u32[]{:S(2)}, u32[]{:S(2)}) collective-permute-start(bf16[2,8,1280]{2,1,0:T(8,128)(2,1)S(1)} %get-tuple-element.69), channel_id=1, source_target_pairs={{0,0},{1,128},{2,2},{3,130},{4,4},{5,132},{6,6},{7,134},{8,8},{9,1... | collective-permute-start | bytes 122888 | tf_op jit(solution)/shard_map/ppermute | solution.py:393
  89.0 12.5 %collective-permute-start.28 = (bf16[2,8,1280]{2,1,0:T(8,128)(2,1)S(1)}, bf16[2,8,1280]{2,1,0:T(8,128)(2,1)S(1)}, u32[]{:S(2)}, u32[]{:S(2)}) collective-permute-start(bf16[2,8,1280]{2,1,0:T(8,128)(2,1)S(1)} %get-tuple-element.70), channel_id=1, source_target_pairs={{0,2},{1,130},{2,0},{3,128},{4,6},{5,134},{6,4},{7,132},{8,10},{9,... | collective-permute-start | bytes 122888 | tf_op jit(solution)/shard_map/ppermute | solution.py:393
  92.7 15.3 %collective-permute-start.29 = (bf16[2,8,1280]{2,1,0:T(8,128)(2,1)S(1)}, bf16[2,8,1280]{2,1,0:T(8,128)(2,1)S(1)}, u32[]{:S(2)}, u32[]{:S(2)}) collective-permute-start(bf16[2,8,1280]{2,1,0:T(8,128)(2,1)S(1)} %get-tuple-element.71), channel_id=1, source_target_pairs={{0,4},{1,132},{2,6},{3,134},{4,0},{5,128},{6,2},{7,130},{8,12},{9,... | collective-permute-start | bytes 122888 | tf_op jit(solution)/shard_map/ppermute | solution.py:393
  99.0 9.1 %collective-permute-start.30 = (bf16[2,8,1280]{2,1,0:T(8,128)(2,1)S(1)}, bf16[2,8,1280]{2,1,0:T(8,128)(2,1)S(1)}, u32[]{:S(2)}, u32[]{:S(2)}) collective-permute-start(bf16[2,8,1280]{2,1,0:T(8,128)(2,1)S(1)} %get-tuple-element.72), channel_id=1, source_target_pairs={{0,6},{1,134},{2,4},{3,132},{4,2},{5,130},{6,0},{7,128},{8,14},{9,... | collective-permute-start | bytes 122888 | tf_op jit(solution)/shard_map/ppermute | solution.py:393
  99.0 9.1 %collective-permute-start.31 = (bf16[2,8,1280]{2,1,0:T(8,128)(2,1)S(1)}, bf16[2,8,1280]{2,1,0:T(8,128)(2,1)S(1)}, u32[]{:S(2)}, u32[]{:S(2)}) collective-permute-start(bf16[2,8,1280]{2,1,0:T(8,128)(2,1)S(1)} %get-tuple-element.73), channel_id=1, source_target_pairs={{0,8},{1,136},{2,10},{3,138},{4,12},{5,140},{6,14},{7,142},{8,0},{... | collective-permute-start | bytes 122888 | tf_op jit(solution)/shard_map/ppermute | solution.py:393
  100.3 7.8 %collective-permute-start.32 = (bf16[2,8,1280]{2,1,0:T(8,128)(2,1)S(1)}, bf16[2,8,1280]{2,1,0:T(8,128)(2,1)S(1)}, u32[]{:S(2)}, u32[]{:S(2)}) collective-permute-start(bf16[2,8,1280]{2,1,0:T(8,128)(2,1)S(1)} %get-tuple-element.74), channel_id=1, source_target_pairs={{0,10},{1,138},{2,8},{3,136},{4,14},{5,142},{6,12},{7,140},{8,2},{... | collective-permute-start | bytes 122888 | tf_op jit(solution)/shard_map/ppermute | solution.py:393
  101.4 8.7 %collective-permute-start.33 = (bf16[2,8,1280]{2,1,0:T(8,128)(2,1)S(1)}, bf16[2,8,1280]{2,1,0:T(8,128)(2,1)S(1)}, u32[]{:S(2)}, u32[]{:S(2)}) collective-permute-start(bf16[2,8,1280]{2,1,0:T(8,128)(2,1)S(1)} %get-tuple-element.75), channel_id=1, source_target_pairs={{0,12},{1,140},{2,14},{3,142},{4,8},{5,136},{6,10},{7,138},{8,4},{... | collective-permute-start | bytes 122888 | tf_op jit(solution)/shard_map/ppermute | solution.py:393
  (17 other events, 133.1 us)

commit v5 on v4

--- a/solution.py
+++ b/solution.py
@@ -56,17 +56,24 @@
     return pairs
 
 
-def neighbour_perm(step):
+def ring_perm():
+    pairs = []
+    for z in range(8):
+        for core in range(2):
+            there = (z + 1 - 2 * core) % 8
+            pairs.append((flat((z, 8), (core, 2)), flat((there, 8), (core, 2))))
+    return pairs
+
+
+def neighbour_perm():
     pairs = []
     for block in range(16):
-        if 0 <= block + step < 16:
-            here, there = place_of(block), place_of(block + step)
-            pairs.append(
-                (
-                    flat((here[0], 2), (here[1], 2), (here[2], 4)),
-                    flat((there[0], 2), (there[1], 2), (there[2], 4)),
-                )
-            )
+        for core in range(2):
+            if 0 <= block + 1 - 2 * core < 16:
+                here, there = place_of(block), place_of(block + 1 - 2 * core)
+                source = flat((here[0], 2), (here[1], 2), (here[2], 4), (core, 2))
+                target = flat((there[0], 2), (there[1], 2), (there[2], 4), (core, 2))
+                pairs.append((source, target))
     return pairs
 
 
@@ -97,9 +104,9 @@
 
 
 def project_kernel(flags, *refs):
-    pieces, (own, mine, theirs), (keep, send, top, bottom, x_ref) = refs[:-8], refs[-8:-5], refs[-5:]
-    for i, piece in enumerate(pieces):
-        x_ref[32 * i : 32 * (i + 1), :] = piece[...]
+    pieces, (own, mine, theirs), (keep, send, edge, give, x_ref) = refs[:8], refs[8:11], refs[11:]
+    for g, piece in enumerate(pieces):
+        x_ref[64 * g : 64 * (g + 1), :] = piece[...]
     width = mine.shape[1]
     near = pl.ds(pl.multiple_of(flags[1] * width, width), width)
     far = pl.ds(pl.multiple_of((1 - flags[1]) * width, width), width)
@@ -113,8 +120,6 @@
         for r in range(ROWS):
             keep[r] = first[r]
             send[r] = second[r]
-            edge = top if r < WIN else bottom
-            edge[r % WIN] = jnp.concatenate([first[r][:, HEAD_DIM:], second[r][:, HEAD_DIM:]], axis=1)
 
     @pl.when(flags[0] == 1)
     def _():
@@ -124,22 +129,34 @@
     def _():
         store(other_rows, own_rows)
 
-
-def project(flags, pieces, own, mine, theirs, cost):
-    tokens = 32 * len(pieces)
-    whole = jax.ShapeDtypeStruct((ROWS, tokens // 8, QKV), jnp.bfloat16)
-    edge = jax.ShapeDtypeStruct((WIN, tokens // 8, 4 * HEAD_DIM), jnp.bfloat16)
+    def store_edges(top, bottom):
+        for r in range(ROWS):
+            row = jnp.concatenate([keep[r][:, HEAD_DIM:], send[r][:, HEAD_DIM:]], axis=1)
+            (top if r < WIN else bottom)[r % WIN] = row
+
+    @pl.when(flags[1] == 0)
+    def _():
+        store_edges(give, edge)
+
+    @pl.when(flags[1] != 0)
+    def _():
+        store_edges(edge, give)
+
+
+def project(flags, pieces, own, mine, theirs):
+    whole = jax.ShapeDtypeStruct((ROWS, HALF, QKV), jnp.bfloat16)
+    part = jax.ShapeDtypeStruct((WIN, HALF, 4 * HEAD_DIM), jnp.bfloat16)
     return pl.pallas_call(
         project_kernel,
-        out_shape=[whole, whole, edge, edge],
-        in_specs=[SMEM] + [VMEM] * (len(pieces) + 3),
+        out_shape=[whole, whole, part, part],
+        in_specs=[SMEM] + [VMEM] * 11,
         out_specs=[VMEM] * 4,
-        scratch_shapes=[pltpu.VMEM((tokens, own.shape[1]), jnp.bfloat16)],
+        scratch_shapes=[pltpu.VMEM((512, own.shape[1]), jnp.bfloat16)],
         compiler_params=pltpu.CompilerParams(vmem_limit_bytes=20 * MIB),
         cost_estimate=pl.CostEstimate(
-            flops=cost, bytes_accessed=MIB, transcendentals=0
+            flops=2 * 512 * 960 * 2560, bytes_accessed=8 * MIB, transcendentals=0
         ),
-        name=f"project_{tokens}",
+        name="project",
     )(flags, *pieces, own, mine, theirs)
 
 
@@ -151,14 +168,22 @@
     vs[at, HEAD_DIM:] = jnp.where(is_one, 1.0, 0.0).astype(jnp.bfloat16)
 
 
-def group_of(i):
-    return i ^ ((i >> 1) & 2)
-
-
 def columns(base, core, shape, dim):
     at = lax.broadcasted_iota(jnp.int32, shape, dim)
     side = core ^ (at >> 6)
-    return ((base + group_of((at >> 3) & 7) - 4 * side) & 7) * 16 + side * 8 + (at & 7)
+    g = (at >> 3) & 7
+    j = (g + 1) >> 1
+    ch = side ^ jnp.where(g == 0, 0, 1 - (g & 1))
+    sector = (base + jnp.where(side == 1, j, -j) - 4 * ch) & 7
+    return sector * 16 + ch * 8 + (at & 7)
+
+
+def group_at(sector, ch, base, core):
+    i = (sector - base + 4 * ch) & 7
+    side = jnp.where((i & 3) == 0, ch, jnp.where(i < 4, 1, 0))
+    j = jnp.minimum(i, 8 - i)
+    g = jnp.where(i == 0, 0, 2 * j - jnp.where(ch == side, 1, 0))
+    return 8 * (side ^ core) + g
 
 
 def fill_masks(masks, first, query_base, key_base, core, radius):
@@ -186,7 +211,7 @@
 
 
 def inner_kernel(ints, factor_ref, band, usable, *refs):
-    parts, (zonal_ref, window_ref, ks, vs, masks) = refs[:4], refs[4:]
+    parts, (zonal_ref, window_ref, ks, vs, masks) = refs[:2], refs[2:]
     factor = factor_ref[0]
     start = 0
     for part in parts:
@@ -225,7 +250,7 @@
             jax.ShapeDtypeStruct((ROWS, COLS, HEAD_DIM), jnp.bfloat16),
             jax.ShapeDtypeStruct((ROWS, COLS, 256), jnp.float32),
         ],
-        in_specs=[SMEM] * 3 + [VMEM] * 5,
+        in_specs=[SMEM] * 3 + [VMEM] * 3,
         out_specs=[VMEM] * 2,
         scratch_shapes=[
             pltpu.VMEM((ROWS * COLS, HEAD_DIM), jnp.bfloat16),
@@ -239,17 +264,15 @@
 
 
 def outer_kernel(ints, factor_ref, usable, zonal_ref, window_ref, *refs):
-    parts, edges, chunks, (ks, vs, masks, out) = refs[:4], refs[4:12], refs[12:20], refs[20:]
+    parts, (own, oth, far_own, far_oth), chunks, (ks, vs, masks, out) = refs[:2], refs[2:6], refs[6:14], refs[14:]
     factor = factor_ref[0]
     base, core, radius = ints[0], ints[1], ints[2]
-    for side in range(2):
-        start = 0
-        for e, edge in enumerate(edges[4 * side : 4 * side + 4]):
-            at = 2 * HEAD_DIM * (e // 2)
-            for r in range(WIN):
-                whole = edge[r][:, at : at + 2 * HEAD_DIM]
-                put(ks, vs, (side * WIN + r) * COLS + start, whole[:, :HEAD_DIM], whole[:, HEAD_DIM:])
-            start += edge.shape[1]
+    for edge, side, half, second in ((own, core, 0, 0), (oth, core, 1, 1), (far_own, 1 - core, 1, 1), (far_oth, 1 - core, 0, 0)):
+        at = 2 * HEAD_DIM * second
+        for r in range(WIN):
+            whole = edge[r][:, at : at + 2 * HEAD_DIM]
+            first = pl.multiple_of(side * (WIN * COLS) + r * COLS + half * HALF, HALF)
+            put(ks, vs, first, whole[:, :HEAD_DIM], whole[:, HEAD_DIM:])
     fill_masks(masks, 0, base, base + 2, core, radius)
     fill_masks(masks, WIN + 1, base, base - 2, core, radius)
     above, below = shifts(usable, base + 2, core), shifts(usable, base - 2, core)
@@ -269,10 +292,10 @@
         )
         window = window[:, :HEAD_DIM] / window[:, HEAD_DIM : HEAD_DIM + 1]
         total = window + zonal_ref[r].astype(jnp.float32)
-        out[:, :, :, r * HEAD_DIM : (r + 1) * HEAD_DIM] = total.reshape(2, 8, 8, HEAD_DIM)
+        out[:, :, r * HEAD_DIM : (r + 1) * HEAD_DIM] = total.reshape(16, 8, HEAD_DIM)
     for k in range(8):
-        chunks[k][0] = out[ints[3], ints[4 + k]].astype(jnp.bfloat16)
-        chunks[k][1] = out[1 - ints[3], ints[12 + k]].astype(jnp.bfloat16)
+        chunks[k][0] = out[ints[3 + k]].astype(jnp.bfloat16)
+        chunks[k][1] = out[ints[11 + k]].astype(jnp.bfloat16)
 
 
 def outer(ints, factor, usable, zonal, window, parts, edges):
@@ -280,13 +303,13 @@
     return pl.pallas_call(
         outer_kernel,
         out_shape=[chunk] * 8,
-        in_specs=[SMEM, SMEM] + [VMEM] * 15,
+        in_specs=[SMEM, SMEM] + [VMEM] * 9,
         out_specs=[VMEM] * 8,
         scratch_shapes=[
             pltpu.VMEM((2 * WIN * COLS, HEAD_DIM), jnp.bfloat16),
             pltpu.VMEM((2 * WIN * COLS, 256), jnp.bfloat16),
             pltpu.VMEM((2 * WIN + 2, COLS, COLS), jnp.float32),
-            pltpu.VMEM((2, 8, 8, ROWS * HEAD_DIM), jnp.float32),
+            pltpu.VMEM((16, 8, ROWS * HEAD_DIM), jnp.float32),
         ],
         compiler_params=pltpu.CompilerParams(vmem_limit_bytes=16 * MIB),
         cost_estimate=pl.CostEstimate(
@@ -339,10 +362,10 @@
     ids = lax.dynamic_slice_in_dim(band_of_row, block * ROWS, ROWS, 0)
     band = (ids[:, None] == ids[None, :]).astype(jnp.float32).reshape(ROWS * ROWS)
     groups = [
-        group_of(((sector ^ k) - base + 4 * side) & 7) for side in (y_lo, 1 - y_lo) for k in range(8)
+        group_at(sector ^ k, side, base, core) for side in (y_lo, 1 - y_lo) for k in range(8)
     ]
     reach = lax.dynamic_index_in_dim(radius, head, keepdims=False)
-    ints = jnp.stack([base, core, reach, core ^ y_lo] + groups).astype(jnp.int32)
+    ints = jnp.stack([base, core, reach] + groups).astype(jnp.int32)
     factor = lax.dynamic_slice_in_dim(qk_scale, head, 1, 0) / HEAD_DIM * LOG2E
     at = []
     for from_y_lo in (core, 1 - core):
@@ -356,40 +379,27 @@
         (first, usable, band, ints, factor, at, flags)
     )
 
-    up = [(i, (i + 1) % 8) for i in range(8)]
-    down = [(i, (i - 1) % 8) for i in range(8)]
-    shards = [[first[:32], first[32:]]] + [[None, None] for _ in range(7)]
-    a, b = list(shards[0]), list(shards[0])
+    a, b = first, lax.ppermute(first, "core", SWAP)
+    pieces = [first]
     for k in range(1, 5):
-        for h in range(2):
-            if k < 4 or h == 0:
-                a[h] = shards[8 - k][h] = lax.ppermute(a[h], "z", up)
-            if k < 4 or h == 1:
-                b[h] = shards[k][h] = lax.ppermute(b[h], "z", down)
-    tied = [(i, h) for i in (3, 5) for h in range(2)]
-    mine, *values = lax.optimization_barrier((mine, *(shards[i][h] for i, h in tied)))
-    for (i, h), value in zip(tied, values):
-        shards[i][h] = value
+        a = lax.ppermute(a, ("z", "core"), ring_perm())
+        pieces.append(a)
+        if k < 4:
+            b = lax.ppermute(b, ("z", "core"), ring_perm())
+            pieces.append(b)
+    mine, *pieces[5:7] = lax.optimization_barrier((mine, *pieces[5:7]))
     theirs = lax.ppermute(mine, "core", SWAP)
 
-    ring = ("y_lo", "y_hi", "x")
-    keeps, others, tops, bottoms = [], [], [], []
-    for group, cost in (((0, 1, 2, 3, 6, 7), 2 * 10**10), ((4, 5), 10**8)):
-        pieces = [shards[i][h] for i in group for h in range(2)]
-        keep, send, top_rows, bottom_rows = project(flags, pieces, own, mine, theirs, cost)
-        keeps.append(keep)
-        tops.append(lax.ppermute(bottom_rows, ring, neighbour_perm(1)))
-        bottoms.append(lax.ppermute(top_rows, ring, neighbour_perm(-1)))
-        others.append(lax.ppermute(send, "core", SWAP))
-    parts = keeps + others
+    corners = ("y_lo", "y_hi", "x", "core")
+    keep, send, edge, give = project(flags, pieces, own, mine, theirs)
+    halo_own = lax.ppermute(edge, corners, neighbour_perm())
+    halo_oth = lax.ppermute(lax.ppermute(give, "core", SWAP), corners, neighbour_perm())
+    parts = keep, lax.ppermute(send, "core", SWAP)
     zonal, window = inner(ints, factor, band, usable, parts)
-    edges = []
-    for halo in (tops, bottoms):
-        *halo, window = lax.optimization_barrier((*halo, window))
-        edges += [*halo, *(lax.ppermute(part, "core", SWAP) for part in halo)]
-    chunks = outer(ints, factor, usable, zonal, window, parts, edges)
-
-    corners = ("y_lo", "y_hi", "x", "core")
+    halo_own, halo_oth, window = lax.optimization_barrier((halo_own, halo_oth, window))
+    halos = [halo_own, halo_oth] + [lax.ppermute(halo, "core", SWAP) for halo in (halo_own, halo_oth)]
+    chunks = outer(ints, factor, usable, zonal, window, parts, halos)
+
     landed = [lax.ppermute(chunks[k], corners, return_perm(k)) for k in range(8)]
     give = jnp.stack([part[1] for part in landed])
     got = lax.ppermute(give, "core", SWAP)

time: 118 us -> 113 us (0.958)
  starting transfers between devices: 74.7 us -> 66 us
  waiting for transfers between devices: 20.5 us -> 29.1 us
  Pallas kernels: 13.7 us -> 10.8 us
  local copies, waits for them, and re-layouts: 5.02 us -> 2.6 us
    ppermute x1, starting transfers between devices: 3.03 us -> 10.5 us  [body(): mine = lax.ppermute(half, 'y_lo', SWAP)]
    ppermute x1, starting transfers between devices: 9.48 us -> 2.21 us  [body(): theirs = lax.ppermute(mine, 'core', SWAP)]
    ppermute x24 -> x14, starting transfers between devices: 31.4 us -> 25.7 us  [the longest x4 13.6 us: body(): a = lax.ppermute(a, ('z', 'core'), ring_perm())]
    ppermute x1, waiting for transfers between devices: 0.01 us -> 5.55 us  [body(): mine = lax.ppermute(half, 'y_lo', SWAP)]
    ppermute x8, starting transfers between devices: 21.1 us -> 17.7 us  [body(): lax.ppermute(chunks[k], corners, return_perm(k))]
    pallas_call x2 -> x1, Pallas kernels: 6.95 us -> 3.93 us  [project(): pl.pallas_call(project_kernel, out_shape=[whole, whole, part, part], in_s...]
    ppermute x24 -> x14, waiting for transfers between devices: 12.3 us -> 15.1 us  [the longest x4 7.56 us: body(): a = lax.ppermute(a, ('z', 'core'), ring_perm())]
    dynamic_slice x1, local copies, waits for them, and re-layouts: 2.57 us -> 0.08 us  [body(): half = lax.dynamic_slice_in_dim(own, core * (model // 2), model // 2, 1)]
  transfers between devices with their start and end apart: 36 -> 26, of which waited for: 15 -> 14; matrix products, arithmetic and copies ran while one was open for 4% -> 2% of each run, Pallas kernels for 9% -> 3%
where the time goes in v5:
time: 113 us
  starting transfers between devices  66 us (58%)
  waiting for transfers between devices  29.1 us (26%)
  Pallas kernels  10.8 us (10%)
  local copies, waits for them, and re-layouts  2.6 us (2%)
  other arithmetic  2.6 us (2%)
  between operations  1.73 us (2%)
    ppermute x8, starting transfers between devices, body(): lax.ppermute(chunks[k], corners, return_perm(k))  17.7 us
    ppermute x4, starting transfers between devices, body(): a = lax.ppermute(a, ('z', 'core'), ring_perm())  13.6 us
    ppermute x1, starting transfers between devices, body(): mine = lax.ppermute(half, 'y_lo', SWAP)  10.5 us
    ppermute x1, starting transfers between devices, body(): first = lax.ppermute(normed, AXES, spread_perm())  9.65 us
    ppermute x4, waiting for transfers between devices, body(): a = lax.ppermute(a, ('z', 'core'), ring_perm())  7.56 us
    ppermute x3, starting transfers between devices, body(): b = lax.ppermute(b, ('z', 'core'), ring_perm())  7.22 us
    ppermute x8, waiting for transfers between devices, body(): lax.ppermute(chunks[k], corners, return_perm(k))  6.23 us
    ppermute x1, waiting for transfers between devices, body(): mine = lax.ppermute(half, 'y_lo', SWAP)  5.55 us
  transfers between devices with their start and end apart: 26, of which 14 were waited for; matrix products, arithmetic and copies ran while one was open for 2% of the time, Pallas kernels for 3%

profile of v5, /device:TPU:1, one launch (start us, length us, event | category | flops | bytes accessed | tf_op | source)
XLA Modules:
  0.0 112.9 jit_solution(2224446013664003939)
XLA Ops:
  2.6 9.6 %collective-permute-start = (bf16[64,2560]{1,0:T(8,128)(2,1)S(1)}, bf16[64,2560]{1,0:T(8,128)(2,1)S(1)}, u32[]{:S(2)}, u32[]{:S(2)}) collective-permute-start(bf16[64,2560]{1,0:T(8,128)(2,1)S(1)} %bitcast.46), channel_id=1, source_target_pairs={{0,0},{1,65},{2,16},{3,81},{4,32},{5,97},{6,48},{7,113},{8,64},{9,... | collective-permute-start | bytes 983048 | tf_op jit(solution)/shard_map/ppermute | solution.py:352
  17.5 10.5 %collective-permute-start.6 = (bf16[480,1280]{1,0:T(8,128)(2,1)S(1)}, bf16[480,1280]{1,0:T(8,128)(2,1)S(1)}, u32[]{:S(2)}, u32[]{:S(2)}) collective-permute-start(bf16[480,1280]{1,0:T(8,128)(2,1)S(1)} %dynamic-slice_bitcast_fusion), channel_id=1, source_target_pairs={{0,128},{128,0},{1,129},{129,1},{2,130},{130,2},{3,131},{131,3},{4... | collective-permute-start | bytes 3686408 | tf_op jit(solution)/shard_map/ppermute | solution.py:356
  28.0 3.6 %collective-permute-start.1 = (bf16[64,2560]{1,0:T(8,128)(2,1)S(1)}, bf16[64,2560]{1,0:T(8,128)(2,1)S(1)}, u32[]{:S(2)}, u32[]{:S(2)}) collective-permute-start(bf16[64,2560]{1,0:T(8,128)(2,1)S(1)} %collective-permute-done.refs_0_), channel_id=1, source_target_pairs={{0,16},{1,113},{16,32},{17,1},{32,48},{33,17},{48,64},{49,33},{64,... | collective-permute-start | bytes 983048 | tf_op jit(solution)/shard_map/ppermute | solution.py:385
  32.6 3.0 %collective-permute-done.1.refs_1_ = bf16[64,2560]{1,0:T(8,128)(2,1)S(1)} collective-permute-done((bf16[64,2560]{1,0:T(8,128)(2,1)S(1)}, bf16[64,2560]{1,0:T(8,128)(2,1)S(1)}, u32[]{:S(2)}, u32[]{:S(2)}) %collective-permute-start.1) | collective-permute-done | bytes 327712 | tf_op jit(solution)/shard_map/ppermute | solution.py:385
  35.6 3.1 %collective-permute-start.4 = (bf16[64,2560]{1,0:T(8,128)(2,1)S(1)}, bf16[64,2560]{1,0:T(8,128)(2,1)S(1)}, u32[]{:S(2)}, u32[]{:S(2)}) collective-permute-start(bf16[64,2560]{1,0:T(8,128)(2,1)S(1)} %collective-permute-done.1.refs_1_), channel_id=1, source_target_pairs={{0,16},{1,113},{16,32},{17,1},{32,48},{33,17},{48,64},{49,33},{64,... | collective-permute-start | bytes 983048 | tf_op jit(solution)/shard_map/ppermute | solution.py:385
  39.2 3.1 %collective-permute-start.5 = (bf16[64,2560]{1,0:T(8,128)(2,1)S(1)}, bf16[64,2560]{1,0:T(8,128)(2,1)S(1)}, u32[]{:S(2)}, u32[]{:S(2)}) collective-permute-start(bf16[64,2560]{1,0:T(8,128)(2,1)S(1)} %collective-permute-done.3.refs_2_), channel_id=1, source_target_pairs={{0,16},{1,113},{16,32},{17,1},{32,48},{33,17},{48,64},{49,33},{64,... | collective-permute-start | bytes 983048 | tf_op jit(solution)/shard_map/ppermute | solution.py:388
  42.8 3.1 %collective-permute-start.7 = (bf16[64,2560]{1,0:T(8,128)(2,1)S(1)}, bf16[64,2560]{1,0:T(8,128)(2,1)S(1)}, u32[]{:S(2)}, u32[]{:S(2)}) collective-permute-start(bf16[64,2560]{1,0:T(8,128)(2,1)S(1)} %collective-permute-done.4.refs_3_), channel_id=1, source_target_pairs={{0,16},{1,113},{16,32},{17,1},{32,48},{33,17},{48,64},{49,33},{64,... | collective-permute-start | bytes 983048 | tf_op jit(solution)/shard_map/ppermute | solution.py:385
  46.3 3.1 %collective-permute-start.8 = (bf16[64,2560]{1,0:T(8,128)(2,1)S(1)}, bf16[64,2560]{1,0:T(8,128)(2,1)S(1)}, u32[]{:S(2)}, u32[]{:S(2)}) collective-permute-start(bf16[64,2560]{1,0:T(8,128)(2,1)S(1)} %collective-permute-done.5.refs_4_), channel_id=1, source_target_pairs={{0,16},{1,113},{16,32},{17,1},{32,48},{33,17},{48,64},{49,33},{64,... | collective-permute-start | bytes 983048 | tf_op jit(solution)/shard_map/ppermute | solution.py:388
  49.4 5.6 %collective-permute-done.6.refs_9_ = bf16[480,1280]{1,0:T(8,128)(2,1)S(1)} collective-permute-done((bf16[480,1280]{1,0:T(8,128)(2,1)S(1)}, bf16[480,1280]{1,0:T(8,128)(2,1)S(1)}, u32[]{:S(2)}, u32[]{:S(2)}) %collective-permute-start.6) | collective-permute-done | bytes 1228832 | tf_op jit(solution)/shard_map/ppermute | solution.py:356
  55.0 2.2 %collective-permute-start.10 = (bf16[480,1280]{1,0:T(8,128)(2,1)S(1)}, bf16[480,1280]{1,0:T(8,128)(2,1)S(1)}, u32[]{:S(2)}, u32[]{:S(2)}) collective-permute-start(bf16[480,1280]{1,0:T(8,128)(2,1)S(1)} %collective-permute-done.6.refs_9_), channel_id=1, source_target_pairs={{0,1},{1,0},{2,3},{3,2},{4,5},{5,4},{6,7},{7,6},{8,9},{9,8},{10,11... | collective-permute-start | bytes 3686408 | tf_op jit(solution)/shard_map/ppermute | solution.py:391
  57.2 3.8 %collective-permute-start.9 = (bf16[64,2560]{1,0:T(8,128)(2,1)S(1)}, bf16[64,2560]{1,0:T(8,128)(2,1)S(1)}, u32[]{:S(2)}, u32[]{:S(2)}) collective-permute-start(bf16[64,2560]{1,0:T(8,128)(2,1)S(1)} %collective-permute-done.7.refs_5_), channel_id=1, source_target_pairs={{0,16},{1,113},{16,32},{17,1},{32,48},{33,17},{48,64},{49,33},{64,... | collective-permute-start | bytes 983048 | tf_op jit(solution)/shard_map/ppermute | solution.py:385
  61.0 4.0 %collective-permute-done.9.refs_7_ = bf16[64,2560]{1,0:T(8,128)(2,1)S(1)} collective-permute-done((bf16[64,2560]{1,0:T(8,128)(2,1)S(1)}, bf16[64,2560]{1,0:T(8,128)(2,1)S(1)}, u32[]{:S(2)}, u32[]{:S(2)}) %collective-permute-start.9) | collective-permute-done | bytes 327712 | tf_op jit(solution)/shard_map/ppermute | solution.py:385
  65.0 3.9 %project.1 = (bf16[8,64,480]{2,1,0:T(8,128)(2,1)S(1)}, bf16[8,64,480]{2,1,0:T(8,128)(2,1)S(1)}, bf16[4,64,640]{2,1,0:T(8,128)(2,1)S(1)}, bf16[4,64,640]{2,1,0:T(8,128)(2,1)S(1)}) custom-call(s32[2]{0:T(128)S(1)} %pad_add_fusion.flags, bf16[64,2560]{1,0:T(8,128)(2,1)S(1)} %collective-permute-done.refs_0_, ...), custom_call_target="tpu_custom_call" | custom-call | flops 2516582400 | bytes 8388608 | tf_op jit(solution)/shard_map/project/pallas_call | solution.py:149
  68.9 1.5 %collective-permute-start.13 = (bf16[4,64,640]{2,1,0:T(8,128)(2,1)S(1)}, bf16[4,64,640]{2,1,0:T(8,128)(2,1)S(1)}, u32[]{:S(2)}, u32[]{:S(2)}) collective-permute-start(bf16[4,64,640]{2,1,0:T(8,128)(2,1)S(1)} %get-tuple-element.46), channel_id=1, source_target_pairs={{0,1},{1,0},{2,3},{3,2},{4,5},{5,4},{6,7},{7,6},{8,9},{9,8},{10,11... | collective-permute-start | bytes 983048 | tf_op jit(solution)/shard_map/ppermute | solution.py:396
  73.3 3.4 %inner.1 = (bf16[8,128,160]{2,1,0:T(8,128)(2,1)S(1)}, f32[8,128,256]{2,1,0:T(8,128)S(1)}) custom-call(s32[19]{0:T(128)S(1)} %stack.140.ints, f32[1]{0:T(128)S(6)} %mul.261.factor_ref, f32[64]{0:T(128)S(1)} %reshape.21.band, f32[16,128]{1,0:T(8,128)S(1)} %fusion.4.usable, bf16[8,64,480]{2,1,0:T(8,128)(2,1)S(1)} %get-tuple-element.42.refs_0_, ...), custom_call_target="tpu_custom_call" | custom-call | flops 10000000 | bytes 100000 | tf_op jit(solution)/shard_map/inner/pallas_call | solution.py:247
  76.7 1.6 %collective-permute-done.12.refs_2_ = bf16[4,64,640]{2,1,0:T(8,128)(2,1)S(1)} collective-permute-done((bf16[4,64,640]{2,1,0:T(8,128)(2,1)S(1)}, bf16[4,64,640]{2,1,0:T(8,128)(2,1)S(1)}, u32[]{:S(2)}, u32[]{:S(2)}) %collective-permute-start.12) | collective-permute-done | bytes 327712 | tf_op jit(solution)/shard_map/ppermute | solution.py:395
  78.4 3.5 %collective-permute-done.14.refs_3_ = bf16[4,64,640]{2,1,0:T(8,128)(2,1)S(1)} collective-permute-done((bf16[4,64,640]{2,1,0:T(8,128)(2,1)S(1)}, bf16[4,64,640]{2,1,0:T(8,128)(2,1)S(1)}, u32[]{:S(2)}, u32[]{:S(2)}) %collective-permute-start.14) | collective-permute-done | bytes 327712 | tf_op jit(solution)/shard_map/ppermute | solution.py:396
  84.0 2.2 %outer.1 = (bf16[2,8,1280]{2,1,0:T(8,128)(2,1)S(1)}, bf16[2,8,1280]{2,1,0:T(8,128)(2,1)S(1)}, bf16[2,8,1280]{2,1,0:T(8,128)(2,1)S(1)}, bf16[2,8,1280]{2,1,0:T(8,...) custom-call(s32[19]{0:T(128)S(1)} %stack.140.ints, ...), custom_call_target="tpu_custom_call" | custom-call | flops 1000000000 | bytes 4194304 | tf_op jit(solution)/shard_map/outer/pallas_call | solution.py:303
  86.2 3.9 %collective-permute-start.17 = (bf16[2,8,1280]{2,1,0:T(8,128)(2,1)S(1)}, bf16[2,8,1280]{2,1,0:T(8,128)(2,1)S(1)}, u32[]{:S(2)}, u32[]{:S(2)}) collective-permute-start(bf16[2,8,1280]{2,1,0:T(8,128)(2,1)S(1)} %get-tuple-element.51), channel_id=1, source_target_pairs={{0,0},{1,128},{2,2},{3,130},{4,4},{5,132},{6,6},{7,134},{8,8},{9,1... | collective-permute-start | bytes 122888 | tf_op jit(solution)/shard_map/ppermute | solution.py:403
  90.3 4.5 %collective-permute-start.19 = (bf16[2,8,1280]{2,1,0:T(8,128)(2,1)S(1)}, bf16[2,8,1280]{2,1,0:T(8,128)(2,1)S(1)}, u32[]{:S(2)}, u32[]{:S(2)}) collective-permute-start(bf16[2,8,1280]{2,1,0:T(8,128)(2,1)S(1)} %get-tuple-element.53), channel_id=1, source_target_pairs={{0,4},{1,132},{2,6},{3,134},{4,0},{5,128},{6,2},{7,130},{8,12},{9,... | collective-permute-start | bytes 122888 | tf_op jit(solution)/shard_map/ppermute | solution.py:403
  95.0 2.5 %collective-permute-start.21 = (bf16[2,8,1280]{2,1,0:T(8,128)(2,1)S(1)}, bf16[2,8,1280]{2,1,0:T(8,128)(2,1)S(1)}, u32[]{:S(2)}, u32[]{:S(2)}) collective-permute-start(bf16[2,8,1280]{2,1,0:T(8,128)(2,1)S(1)} %get-tuple-element.55), channel_id=1, source_target_pairs={{0,8},{1,136},{2,10},{3,138},{4,12},{5,140},{6,14},{7,142},{8,0},{... | collective-permute-start | bytes 122888 | tf_op jit(solution)/shard_map/ppermute | solution.py:403
  97.5 6.0 %collective-permute-start.23 = (bf16[2,8,1280]{2,1,0:T(8,128)(2,1)S(1)}, bf16[2,8,1280]{2,1,0:T(8,128)(2,1)S(1)}, u32[]{:S(2)}, u32[]{:S(2)}) collective-permute-start(bf16[2,8,1280]{2,1,0:T(8,128)(2,1)S(1)} %get-tuple-element.57), channel_id=1, source_target_pairs={{0,12},{1,140},{2,14},{3,142},{4,8},{5,136},{6,10},{7,138},{8,4},{... | collective-permute-start | bytes 122888 | tf_op jit(solution)/shard_map/ppermute | solution.py:403
  104.0 1.6 %collective-permute-done.23.refs_6_ = bf16[2,8,1280]{2,1,0:T(8,128)(2,1)S(1)} collective-permute-done((bf16[2,8,1280]{2,1,0:T(8,128)(2,1)S(1)}, bf16[2,8,1280]{2,1,0:T(8,128)(2,1)S(1)}, u32[]{:S(2)}, u32[]{:S(2)}) %collective-permute-start.23) | collective-permute-done | bytes 40992 | tf_op jit(solution)/shard_map/ppermute | solution.py:403
  105.6 4.6 %collective-permute-done.24.refs_7_ = bf16[2,8,1280]{2,1,0:T(8,128)(2,1)S(1)} collective-permute-done((bf16[2,8,1280]{2,1,0:T(8,128)(2,1)S(1)}, bf16[2,8,1280]{2,1,0:T(8,128)(2,1)S(1)}, u32[]{:S(2)}, u32[]{:S(2)}) %collective-permute-start.24) | collective-permute-done | bytes 40992 | tf_op jit(solution)/shard_map/ppermute | solution.py:403
  (65 shorter events, 17.1 us)
Async XLA Ops:
  2.6 14.9 %collective-permute-start = (bf16[64,2560]{1,0:T(8,128)(2,1)S(1)}, bf16[64,2560]{1,0:T(8,128)(2,1)S(1)}, u32[]{:S(2)}, u32[]{:S(2)}) collective-permute-start(bf16[64,2560]{1,0:T(8,128)(2,1)S(1)} %bitcast.46), channel_id=1, source_target_pairs={{0,0},{1,65},{2,16},{3,81},{4,32},{5,97},{6,48},{7,113},{8,64},{9,... | collective-permute-start | bytes 983048 | tf_op jit(solution)/shard_map/ppermute | solution.py:352
  17.4 14.2 %collective-permute-start.2 = (bf16[64,2560]{1,0:T(8,128)(2,1)S(1)}, bf16[64,2560]{1,0:T(8,128)(2,1)S(1)}, u32[]{:S(2)}, u32[]{:S(2)}) collective-permute-start(bf16[64,2560]{1,0:T(8,128)(2,1)S(1)} %collective-permute-done.refs_0_), channel_id=1, source_target_pairs={{0,1},{1,0},{2,3},{3,2},{4,5},{5,4},{6,7},{7,6},{8,9},{9,8},{10,11... | collective-permute-start | bytes 983048 | tf_op jit(solution)/shard_map/ppermute | solution.py:382
  17.5 37.4 %collective-permute-start.6 = (bf16[480,1280]{1,0:T(8,128)(2,1)S(1)}, bf16[480,1280]{1,0:T(8,128)(2,1)S(1)}, u32[]{:S(2)}, u32[]{:S(2)}) collective-permute-start(bf16[480,1280]{1,0:T(8,128)(2,1)S(1)} %dynamic-slice_bitcast_fusion), channel_id=1, source_target_pairs={{0,128},{128,0},{1,129},{129,1},{2,130},{130,2},{3,131},{131,3},{4... | collective-permute-start | bytes 3686408 | tf_op jit(solution)/shard_map/ppermute | solution.py:356
  28.0 7.6 %collective-permute-start.1 = (bf16[64,2560]{1,0:T(8,128)(2,1)S(1)}, bf16[64,2560]{1,0:T(8,128)(2,1)S(1)}, u32[]{:S(2)}, u32[]{:S(2)}) collective-permute-start(bf16[64,2560]{1,0:T(8,128)(2,1)S(1)} %collective-permute-done.refs_0_), channel_id=1, source_target_pairs={{0,16},{1,113},{16,32},{17,1},{32,48},{33,17},{48,64},{49,33},{64,... | collective-permute-start | bytes 983048 | tf_op jit(solution)/shard_map/ppermute | solution.py:385
  31.6 7.5 %collective-permute-start.3 = (bf16[64,2560]{1,0:T(8,128)(2,1)S(1)}, bf16[64,2560]{1,0:T(8,128)(2,1)S(1)}, u32[]{:S(2)}, u32[]{:S(2)}) collective-permute-start(bf16[64,2560]{1,0:T(8,128)(2,1)S(1)} %collective-permute-done.2), channel_id=1, source_target_pairs={{0,16},{1,113},{16,32},{17,1},{32,48},{33,17},{48,64},{49,33},{64,... | collective-permute-start | bytes 983048 | tf_op jit(solution)/shard_map/ppermute | solution.py:388
  35.6 7.1 %collective-permute-start.4 = (bf16[64,2560]{1,0:T(8,128)(2,1)S(1)}, bf16[64,2560]{1,0:T(8,128)(2,1)S(1)}, u32[]{:S(2)}, u32[]{:S(2)}) collective-permute-start(bf16[64,2560]{1,0:T(8,128)(2,1)S(1)} %collective-permute-done.1.refs_1_), channel_id=1, source_target_pairs={{0,16},{1,113},{16,32},{17,1},{32,48},{33,17},{48,64},{49,33},{64,... | collective-permute-start | bytes 983048 | tf_op jit(solution)/shard_map/ppermute | solution.py:385
  39.2 7.1 %collective-permute-start.5 = (bf16[64,2560]{1,0:T(8,128)(2,1)S(1)}, bf16[64,2560]{1,0:T(8,128)(2,1)S(1)}, u32[]{:S(2)}, u32[]{:S(2)}) collective-permute-start(bf16[64,2560]{1,0:T(8,128)(2,1)S(1)} %collective-permute-done.3.refs_2_), channel_id=1, source_target_pairs={{0,16},{1,113},{16,32},{17,1},{32,48},{33,17},{48,64},{49,33},{64,... | collective-permute-start | bytes 983048 | tf_op jit(solution)/shard_map/ppermute | solution.py:388
  42.8 12.2 %collective-permute-start.7 = (bf16[64,2560]{1,0:T(8,128)(2,1)S(1)}, bf16[64,2560]{1,0:T(8,128)(2,1)S(1)}, u32[]{:S(2)}, u32[]{:S(2)}) collective-permute-start(bf16[64,2560]{1,0:T(8,128)(2,1)S(1)} %collective-permute-done.4.refs_3_), channel_id=1, source_target_pairs={{0,16},{1,113},{16,32},{17,1},{32,48},{33,17},{48,64},{49,33},{64,... | collective-permute-start | bytes 983048 | tf_op jit(solution)/shard_map/ppermute | solution.py:385
  46.3 8.7 %collective-permute-start.8 = (bf16[64,2560]{1,0:T(8,128)(2,1)S(1)}, bf16[64,2560]{1,0:T(8,128)(2,1)S(1)}, u32[]{:S(2)}, u32[]{:S(2)}) collective-permute-start(bf16[64,2560]{1,0:T(8,128)(2,1)S(1)} %collective-permute-done.5.refs_4_), channel_id=1, source_target_pairs={{0,16},{1,113},{16,32},{17,1},{32,48},{33,17},{48,64},{49,33},{64,... | collective-permute-start | bytes 983048 | tf_op jit(solution)/shard_map/ppermute | solution.py:388
  55.0 10.0 %collective-permute-start.10 = (bf16[480,1280]{1,0:T(8,128)(2,1)S(1)}, bf16[480,1280]{1,0:T(8,128)(2,1)S(1)}, u32[]{:S(2)}, u32[]{:S(2)}) collective-permute-start(bf16[480,1280]{1,0:T(8,128)(2,1)S(1)} %collective-permute-done.6.refs_9_), channel_id=1, source_target_pairs={{0,1},{1,0},{2,3},{3,2},{4,5},{5,4},{6,7},{7,6},{8,9},{9,8},{10,11... | collective-permute-start | bytes 3686408 | tf_op jit(solution)/shard_map/ppermute | solution.py:391
  57.2 7.8 %collective-permute-start.9 = (bf16[64,2560]{1,0:T(8,128)(2,1)S(1)}, bf16[64,2560]{1,0:T(8,128)(2,1)S(1)}, u32[]{:S(2)}, u32[]{:S(2)}) collective-permute-start(bf16[64,2560]{1,0:T(8,128)(2,1)S(1)} %collective-permute-done.7.refs_5_), channel_id=1, source_target_pairs={{0,16},{1,113},{16,32},{17,1},{32,48},{33,17},{48,64},{49,33},{64,... | collective-permute-start | bytes 983048 | tf_op jit(solution)/shard_map/ppermute | solution.py:385
  68.9 3.1 %collective-permute-start.13 = (bf16[4,64,640]{2,1,0:T(8,128)(2,1)S(1)}, bf16[4,64,640]{2,1,0:T(8,128)(2,1)S(1)}, u32[]{:S(2)}, u32[]{:S(2)}) collective-permute-start(bf16[4,64,640]{2,1,0:T(8,128)(2,1)S(1)} %get-tuple-element.46), channel_id=1, source_target_pairs={{0,1},{1,0},{2,3},{3,2},{4,5},{5,4},{6,7},{7,6},{8,9},{9,8},{10,11... | collective-permute-start | bytes 983048 | tf_op jit(solution)/shard_map/ppermute | solution.py:396
  70.4 2.9 %collective-permute-start.11 = (bf16[8,64,480]{2,1,0:T(8,128)(2,1)S(1)}, bf16[8,64,480]{2,1,0:T(8,128)(2,1)S(1)}, u32[]{:S(2)}, u32[]{:S(2)}) collective-permute-start(bf16[8,64,480]{2,1,0:T(8,128)(2,1)S(1)} %get-tuple-element.43), channel_id=1, source_target_pairs={{0,1},{1,0},{2,3},{3,2},{4,5},{5,4},{6,7},{7,6},{8,9},{9,8},{10,11... | collective-permute-start | bytes 1474568 | tf_op jit(solution)/shard_map/ppermute | solution.py:397
  70.5 7.8 %collective-permute-start.12 = (bf16[4,64,640]{2,1,0:T(8,128)(2,1)S(1)}, bf16[4,64,640]{2,1,0:T(8,128)(2,1)S(1)}, u32[]{:S(2)}, u32[]{:S(2)}) collective-permute-start(bf16[4,64,640]{2,1,0:T(8,128)(2,1)S(1)} %get-tuple-element.45), channel_id=1, source_target_pairs={{0,2},{2,4},{3,1},{4,6},{5,3},{6,14},{7,5},{14,12},{15,7},{12,10},... | collective-permute-start | bytes 983048 | tf_op jit(solution)/shard_map/ppermute | solution.py:395
  72.0 9.8 %collective-permute-start.14 = (bf16[4,64,640]{2,1,0:T(8,128)(2,1)S(1)}, bf16[4,64,640]{2,1,0:T(8,128)(2,1)S(1)}, u32[]{:S(2)}, u32[]{:S(2)}) collective-permute-start(bf16[4,64,640]{2,1,0:T(8,128)(2,1)S(1)} %collective-permute-done.13), channel_id=1, source_target_pairs={{0,2},{2,4},{3,1},{4,6},{5,3},{6,14},{7,5},{14,12},{15,7},{12,10},... | collective-permute-start | bytes 983048 | tf_op jit(solution)/shard_map/ppermute | solution.py:396
  81.9 2.1 %collective-permute-start.16 = (bf16[4,64,640]{2,1,0:T(8,128)(2,1)S(1)}, bf16[4,64,640]{2,1,0:T(8,128)(2,1)S(1)}, u32[]{:S(2)}, u32[]{:S(2)}) collective-permute-start(bf16[4,64,640]{2,1,0:T(8,128)(2,1)S(1)} %collective-permute-done.14.refs_3_), channel_id=1, source_target_pairs={{0,1},{1,0},{2,3},{3,2},{4,5},{5,4},{6,7},{7,6},{8,9},{9,8},{10,11... | collective-permute-start | bytes 983048 | tf_op jit(solution)/shard_map/ppermute | solution.py:400
  86.2 11.3 %collective-permute-start.17 = (bf16[2,8,1280]{2,1,0:T(8,128)(2,1)S(1)}, bf16[2,8,1280]{2,1,0:T(8,128)(2,1)S(1)}, u32[]{:S(2)}, u32[]{:S(2)}) collective-permute-start(bf16[2,8,1280]{2,1,0:T(8,128)(2,1)S(1)} %get-tuple-element.51), channel_id=1, source_target_pairs={{0,0},{1,128},{2,2},{3,130},{4,4},{5,132},{6,6},{7,134},{8,8},{9,1... | collective-permute-start | bytes 122888 | tf_op jit(solution)/shard_map/ppermute | solution.py:403
  90.2 7.3 %collective-permute-start.18 = (bf16[2,8,1280]{2,1,0:T(8,128)(2,1)S(1)}, bf16[2,8,1280]{2,1,0:T(8,128)(2,1)S(1)}, u32[]{:S(2)}, u32[]{:S(2)}) collective-permute-start(bf16[2,8,1280]{2,1,0:T(8,128)(2,1)S(1)} %get-tuple-element.52), channel_id=1, source_target_pairs={{0,2},{1,130},{2,0},{3,128},{4,6},{5,134},{6,4},{7,132},{8,10},{9,... | collective-permute-start | bytes 122888 | tf_op jit(solution)/shard_map/ppermute | solution.py:403
  90.3 13.2 %collective-permute-start.19 = (bf16[2,8,1280]{2,1,0:T(8,128)(2,1)S(1)}, bf16[2,8,1280]{2,1,0:T(8,128)(2,1)S(1)}, u32[]{:S(2)}, u32[]{:S(2)}) collective-permute-start(bf16[2,8,1280]{2,1,0:T(8,128)(2,1)S(1)} %get-tuple-element.53), channel_id=1, source_target_pairs={{0,4},{1,132},{2,6},{3,134},{4,0},{5,128},{6,2},{7,130},{8,12},{9,... | collective-permute-start | bytes 122888 | tf_op jit(solution)/shard_map/ppermute | solution.py:403
  94.8 9.1 %collective-permute-start.20 = (bf16[2,8,1280]{2,1,0:T(8,128)(2,1)S(1)}, bf16[2,8,1280]{2,1,0:T(8,128)(2,1)S(1)}, u32[]{:S(2)}, u32[]{:S(2)}) collective-permute-start(bf16[2,8,1280]{2,1,0:T(8,128)(2,1)S(1)} %get-tuple-element.54), channel_id=1, source_target_pairs={{0,6},{1,134},{2,4},{3,132},{4,2},{5,130},{6,0},{7,128},{8,14},{9,... | collective-permute-start | bytes 122888 | tf_op jit(solution)/shard_map/ppermute | solution.py:403
  95.0 9.0 %collective-permute-start.21 = (bf16[2,8,1280]{2,1,0:T(8,128)(2,1)S(1)}, bf16[2,8,1280]{2,1,0:T(8,128)(2,1)S(1)}, u32[]{:S(2)}, u32[]{:S(2)}) collective-permute-start(bf16[2,8,1280]{2,1,0:T(8,128)(2,1)S(1)} %get-tuple-element.55), channel_id=1, source_target_pairs={{0,8},{1,136},{2,10},{3,138},{4,12},{5,140},{6,14},{7,142},{8,0},{... | collective-permute-start | bytes 122888 | tf_op jit(solution)/shard_map/ppermute | solution.py:403
  97.5 6.5 %collective-permute-start.22 = (bf16[2,8,1280]{2,1,0:T(8,128)(2,1)S(1)}, bf16[2,8,1280]{2,1,0:T(8,128)(2,1)S(1)}, u32[]{:S(2)}, u32[]{:S(2)}) collective-permute-start(bf16[2,8,1280]{2,1,0:T(8,128)(2,1)S(1)} %get-tuple-element.56), channel_id=1, source_target_pairs={{0,10},{1,138},{2,8},{3,136},{4,14},{5,142},{6,12},{7,140},{8,2},{... | collective-permute-start | bytes 122888 | tf_op jit(solution)/shard_map/ppermute | solution.py:403
  97.5 8.1 %collective-permute-start.23 = (bf16[2,8,1280]{2,1,0:T(8,128)(2,1)S(1)}, bf16[2,8,1280]{2,1,0:T(8,128)(2,1)S(1)}, u32[]{:S(2)}, u32[]{:S(2)}) collective-permute-start(bf16[2,8,1280]{2,1,0:T(8,128)(2,1)S(1)} %get-tuple-element.57), channel_id=1, source_target_pairs={{0,12},{1,140},{2,14},{3,142},{4,8},{5,136},{6,10},{7,138},{8,4},{... | collective-permute-start | bytes 122888 | tf_op jit(solution)/shard_map/ppermute | solution.py:403
  103.5 6.7 %collective-permute-start.24 = (bf16[2,8,1280]{2,1,0:T(8,128)(2,1)S(1)}, bf16[2,8,1280]{2,1,0:T(8,128)(2,1)S(1)}, u32[]{:S(2)}, u32[]{:S(2)}) collective-permute-start(bf16[2,8,1280]{2,1,0:T(8,128)(2,1)S(1)} %get-tuple-element.58), channel_id=1, source_target_pairs={{0,14},{1,142},{2,12},{3,140},{4,10},{5,138},{6,8},{7,136},{8,6},{... | collective-permute-start | bytes 122888 | tf_op jit(solution)/shard_map/ppermute | solution.py:403
  (7 other events, 72.7 us)

commit v6 on v5

--- a/solution.py
+++ b/solution.py
@@ -80,10 +80,10 @@
 def return_perm(k):
     pairs = []
     for y_lo in range(2):
-        for s in range(8):
+        for y_hi in range(2):
             for core in range(2):
-                source = flat((y_lo, 2), (s, 8), (core, 2))
-                pairs.append((source, flat((core, 2), (s ^ k, 8), (y_lo, 2))))
+                source = flat((y_lo, 2), (y_hi, 2), (core, 2))
+                pairs.append((source, flat((core, 2), (y_hi ^ k, 2), (y_lo, 2))))
     return pairs
 
 
@@ -264,7 +264,7 @@
 
 
 def outer_kernel(ints, factor_ref, usable, zonal_ref, window_ref, *refs):
-    parts, (own, oth, far_own, far_oth), chunks, (ks, vs, masks, out) = refs[:2], refs[2:6], refs[6:14], refs[14:]
+    parts, (own, oth, far_own, far_oth), chunks, (ks, vs, masks, out) = refs[:2], refs[2:6], refs[6:8], refs[8:]
     factor = factor_ref[0]
     base, core, radius = ints[0], ints[1], ints[2]
     for edge, side, half, second in ((own, core, 0, 0), (oth, core, 1, 1), (far_own, 1 - core, 1, 1), (far_oth, 1 - core, 0, 0)):
@@ -294,17 +294,17 @@
         total = window + zonal_ref[r].astype(jnp.float32)
         out[:, :, r * HEAD_DIM : (r + 1) * HEAD_DIM] = total.reshape(16, 8, HEAD_DIM)
     for k in range(8):
-        chunks[k][0] = out[ints[3 + k]].astype(jnp.bfloat16)
-        chunks[k][1] = out[ints[11 + k]].astype(jnp.bfloat16)
+        chunks[k // 4][k % 4, 0] = out[ints[3 + k]].astype(jnp.bfloat16)
+        chunks[k // 4][k % 4, 1] = out[ints[11 + k]].astype(jnp.bfloat16)
 
 
 def outer(ints, factor, usable, zonal, window, parts, edges):
-    chunk = jax.ShapeDtypeStruct((2, 8, ROWS * HEAD_DIM), jnp.bfloat16)
+    chunk = jax.ShapeDtypeStruct((4, 2, 8, ROWS * HEAD_DIM), jnp.bfloat16)
     return pl.pallas_call(
         outer_kernel,
-        out_shape=[chunk] * 8,
+        out_shape=[chunk] * 2,
         in_specs=[SMEM, SMEM] + [VMEM] * 9,
-        out_specs=[VMEM] * 8,
+        out_specs=[VMEM] * 2,
         scratch_shapes=[
             pltpu.VMEM((2 * WIN * COLS, HEAD_DIM), jnp.bfloat16),
             pltpu.VMEM((2 * WIN * COLS, 256), jnp.bfloat16),
@@ -319,24 +319,45 @@
     )(ints, factor, usable, zonal, window, *parts, *edges)
 
 
+def regroup_kernel(near, far, *parts):
+    for k, part in enumerate(parts):
+        part[0] = near[k + 1]
+        part[1] = far[k + 1]
+
+
+def regroup(near, far):
+    part = jax.ShapeDtypeStruct((2, *near.shape[1:]), near.dtype)
+    return pl.pallas_call(
+        regroup_kernel,
+        out_shape=[part] * 3,
+        in_specs=[VMEM] * 2,
+        out_specs=[VMEM] * 3,
+        compiler_params=pltpu.CompilerParams(vmem_limit_bytes=4 * MIB),
+        cost_estimate=pl.CostEstimate(flops=0, bytes_accessed=MIB, transcendentals=0),
+        name="regroup",
+    )(near, far)
+
+
 def assemble_kernel(at, *refs):
-    mains, got, out = refs[:8], refs[8], refs[9]
-    width = ROWS * HEAD_DIM
-    for k in range(8):
-        out[0, :, pl.ds(pl.multiple_of(at[k] * width, 128), width)] = mains[k][0]
-        out[0, :, pl.ds(pl.multiple_of(at[8 + k] * width, 128), width)] = got[k]
-
-
-def assemble(at, mains, got):
+    width, out = ROWS * HEAD_DIM, refs[10]
+    for part in range(2):
+        landed = refs[5 * part : 5 * part + 5]
+        for k in range(8):
+            kind, x = k // 4, k % 4
+            value = landed[kind][0, part] if x == 0 else landed[x + 1][kind, part]
+            out[0, :, pl.ds(pl.multiple_of(at[8 * part + k] * width, 128), width)] = value
+
+
+def assemble(at, landed):
     return pl.pallas_call(
         assemble_kernel,
         out_shape=jax.ShapeDtypeStruct((1, 8, LAT * ROWS * HEAD_DIM), jnp.bfloat16),
-        in_specs=[SMEM] + [VMEM] * 9,
+        in_specs=[SMEM] + [VMEM] * 10,
         out_specs=VMEM,
         compiler_params=pltpu.CompilerParams(vmem_limit_bytes=4 * MIB),
         cost_estimate=pl.CostEstimate(flops=0, bytes_accessed=MIB, transcendentals=0),
         name="assemble",
-    )(at, *mains, got)
+    )(at, *landed)
 
 
 def body(tokens, w_qkv, key_mask, band_of_row, radius, qk_scale):
@@ -387,7 +408,7 @@
         if k < 4:
             b = lax.ppermute(b, ("z", "core"), ring_perm())
             pieces.append(b)
-    mine, *pieces[5:7] = lax.optimization_barrier((mine, *pieces[5:7]))
+    mine, *pieces[3:5] = lax.optimization_barrier((mine, *pieces[3:5]))
     theirs = lax.ppermute(mine, "core", SWAP)
 
     corners = ("y_lo", "y_hi", "x", "core")
@@ -400,10 +421,11 @@
     halos = [halo_own, halo_oth] + [lax.ppermute(halo, "core", SWAP) for halo in (halo_own, halo_oth)]
     chunks = outer(ints, factor, usable, zonal, window, parts, halos)
 
-    landed = [lax.ppermute(chunks[k], corners, return_perm(k)) for k in range(8)]
-    give = jnp.stack([part[1] for part in landed])
-    got = lax.ppermute(give, "core", SWAP)
-    return assemble(at, landed, got)
+    near, far = (lax.ppermute(chunks[k], ("y_lo", "y_hi", "core"), return_perm(k)) for k in range(2))
+    passed = regroup(near, far)
+    along = [[(i, i ^ k) for i in range(4)] for k in range(1, 4)]
+    landed = [near, far] + [lax.ppermute(part, "x", perm) for part, perm in zip(passed, along)]
+    return assemble(at, landed + [lax.ppermute(part, "core", SWAP) for part in landed])
 
 
 def solution(mesh):

time: 113 us -> 109 us (0.965)
  starting transfers between devices: 66 us -> 52.5 us
  waiting for transfers between devices: 29.1 us -> 35.4 us
  local copies, waits for them, and re-layouts: 2.6 us -> 4.85 us
    ppermute x1, starting transfers between devices: 10.5 us -> 3.03 us  [body(): mine = lax.ppermute(half, 'y_lo', SWAP)]
    ppermute x9 -> x10, starting transfers between devices: 17.9 us -> 10.9 us  [the longest x3 5.98 us: body(): lax.ppermute(part, 'x', perm)]
    ppermute x1, waiting for transfers between devices: 5.55 us -> 0.7 us  [body(): mine = lax.ppermute(half, 'y_lo', SWAP)]
    ppermute x4, waiting for transfers between devices: 7.56 us -> 12.2 us  [body(): a = lax.ppermute(a, ('z', 'core'), ring_perm())]
    ppermute x3, waiting for transfers between devices: 0.79 us -> 5.15 us  [body(): b = lax.ppermute(b, ('z', 'core'), ring_perm())]
    ppermute x9 -> x10, waiting for transfers between devices: 7.4 us -> 10.6 us  [the longest x2 5.39 us: body(): lax.ppermute(chunks[k], ('y_lo', 'y_hi', 'core'), return_perm(k))]
    ppermute x3, starting transfers between devices: 7.22 us -> 4.54 us  [body(): b = lax.ppermute(b, ('z', 'core'), ring_perm())]
    dynamic_slice x1, local copies, waits for them, and re-layouts: 0.08 us -> 2.56 us  [body(): half = lax.dynamic_slice_in_dim(own, core * (model // 2), model // 2, 1)]
  transfers between devices with their start and end apart: 26 -> 27, of which waited for: 14 -> 17; matrix products, arithmetic and copies ran while one was open for 2% -> 5% of each run, Pallas kernels for 3% -> 3%
where the time goes in v6:
time: 109 us; the launch traced here: 108 us
  starting transfers between devices  52.5 us (48%)
  waiting for transfers between devices  35.4 us (32%)
  Pallas kernels  11.6 us (11%)
  local copies, waits for them, and re-layouts  4.85 us (4%)
  other arithmetic  2.39 us (2%)
  between operations  1.63 us (1%)
    ppermute x4, starting transfers between devices, body(): a = lax.ppermute(a, ('z', 'core'), ring_perm())  15.1 us
    ppermute x4, waiting for transfers between devices, body(): a = lax.ppermute(a, ('z', 'core'), ring_perm())  12.2 us
    ppermute x1, starting transfers between devices, body(): first = lax.ppermute(normed, AXES, spread_perm())  9.65 us
    ppermute x3, starting transfers between devices, body(): lax.ppermute(part, 'x', perm)  5.98 us
    ppermute x2, waiting for transfers between devices, body(): lax.ppermute(chunks[k], ('y_lo', 'y_hi', 'core'), return_perm(k))  5.39 us
    ppermute x3, waiting for transfers between devices, body(): b = lax.ppermute(b, ('z', 'core'), ring_perm())  5.15 us
    pallas_call x1, Pallas kernels, project(): pl.pallas_call(project_kernel, out_shape=[whole, whole, part, part], in_s...  4.69 us
    ppermute x3, starting transfers between devices, body(): b = lax.ppermute(b, ('z', 'core'), ring_perm())  4.54 us
  transfers between devices with their start and end apart: 27, of which 17 were waited for; matrix products, arithmetic and copies ran while one was open for 5% of the time, Pallas kernels for 3%

profile of v6, /device:TPU:1, one launch (start us, length us, event | category | flops | bytes accessed | tf_op | source)
XLA Modules:
  0.0 108.4 jit_solution(7686558171509301129)
XLA Ops:
  2.4 9.6 %collective-permute-start = (bf16[64,2560]{1,0:T(8,128)(2,1)S(1)}, bf16[64,2560]{1,0:T(8,128)(2,1)S(1)}, u32[]{:S(2)}, u32[]{:S(2)}) collective-permute-start(bf16[64,2560]{1,0:T(8,128)(2,1)S(1)} %bitcast.46), channel_id=1, source_target_pairs={{0,0},{1,65},{2,16},{3,81},{4,32},{5,97},{6,48},{7,113},{8,64},{9,... | collective-permute-start | bytes 983048 | tf_op jit(solution)/shard_map/ppermute | solution.py:373
  12.1 2.6 %dynamic-slice_bitcast_fusion = bf16[480,1280]{1,0:T(8,128)(2,1)} fusion(bf16[1,480,2560]{2,1,0:T(8,128)(2,1)} %param.7, s32[]{:T(128)S(6)} %select_n.345), kind=kLoop, calls=%fused_computation | loop fusion | bytes 2457604 | tf_op jit(solution)/shard_map/dynamic_slice | solution.py:376
  14.6 3.0 %collective-permute-start.4 = (bf16[480,1280]{1,0:T(8,128)(2,1)}, bf16[480,1280]{1,0:T(8,128)(2,1)}, u32[]{:S(2)}, u32[]{:S(2)}) collective-permute-start(bf16[480,1280]{1,0:T(8,128)(2,1)} %dynamic-slice_bitcast_fusion), channel_id=1, source_target_pairs={{0,128},{128,0},{1,129},{129,1},{2,130},{130,2},{3,131},{131,3},{4... | collective-permute-start | bytes 3686408 | tf_op jit(solution)/shard_map/ppermute | solution.py:377
  21.5 9.7 %collective-permute-start.1 = (bf16[64,2560]{1,0:T(8,128)(2,1)S(1)}, bf16[64,2560]{1,0:T(8,128)(2,1)S(1)}, u32[]{:S(2)}, u32[]{:S(2)}) collective-permute-start(bf16[64,2560]{1,0:T(8,128)(2,1)S(1)} %collective-permute-done.refs_0_), channel_id=1, source_target_pairs={{0,16},{1,113},{16,32},{17,1},{32,48},{33,17},{48,64},{49,33},{64,... | collective-permute-start | bytes 983048 | tf_op jit(solution)/shard_map/ppermute | solution.py:406
  32.5 2.8 %collective-permute-done.1.refs_1_ = bf16[64,2560]{1,0:T(8,128)(2,1)S(1)} collective-permute-done((bf16[64,2560]{1,0:T(8,128)(2,1)S(1)}, bf16[64,2560]{1,0:T(8,128)(2,1)S(1)}, u32[]{:S(2)}, u32[]{:S(2)}) %collective-permute-start.1) | collective-permute-done | bytes 327712 | tf_op jit(solution)/shard_map/ppermute | solution.py:406
  35.3 3.1 %collective-permute-start.5 = (bf16[64,2560]{1,0:T(8,128)(2,1)S(1)}, bf16[64,2560]{1,0:T(8,128)(2,1)S(1)}, u32[]{:S(2)}, u32[]{:S(2)}) collective-permute-start(bf16[64,2560]{1,0:T(8,128)(2,1)S(1)} %collective-permute-done.1.refs_1_), channel_id=1, source_target_pairs={{0,16},{1,113},{16,32},{17,1},{32,48},{33,17},{48,64},{49,33},{64,... | collective-permute-start | bytes 983048 | tf_op jit(solution)/shard_map/ppermute | solution.py:406
  38.8 3.1 %collective-permute-start.6 = (bf16[64,2560]{1,0:T(8,128)(2,1)S(1)}, bf16[64,2560]{1,0:T(8,128)(2,1)S(1)}, u32[]{:S(2)}, u32[]{:S(2)}) collective-permute-start(bf16[64,2560]{1,0:T(8,128)(2,1)S(1)} %collective-permute-done.3.refs_2_), channel_id=1, source_target_pairs={{0,16},{1,113},{16,32},{17,1},{32,48},{33,17},{48,64},{49,33},{64,... | collective-permute-start | bytes 983048 | tf_op jit(solution)/shard_map/ppermute | solution.py:409
  43.1 2.8 %collective-permute-done.6.refs_4_ = bf16[64,2560]{1,0:T(8,128)(2,1)S(1)} collective-permute-done((bf16[64,2560]{1,0:T(8,128)(2,1)S(1)}, bf16[64,2560]{1,0:T(8,128)(2,1)S(1)}, u32[]{:S(2)}, u32[]{:S(2)}) %collective-permute-start.6) | collective-permute-done | bytes 327712 | tf_op jit(solution)/shard_map/ppermute | solution.py:409
  45.9 2.5 %collective-permute-start.10 = (bf16[480,1280]{1,0:T(8,128)(2,1)}, bf16[480,1280]{1,0:T(8,128)(2,1)S(1)}, u32[]{:S(2)}, u32[]{:S(2)}) collective-permute-start(bf16[480,1280]{1,0:T(8,128)(2,1)} %collective-permute-done.4.refs_9_), channel_id=1, source_target_pairs={{0,1},{1,0},{2,3},{3,2},{4,5},{5,4},{6,7},{7,6},{8,9},{9,8},{10,11... | collective-permute-start | bytes 3686408 | tf_op jit(solution)/shard_map/ppermute | solution.py:412
  49.2 5.4 %collective-permute-done.7.refs_5_ = bf16[64,2560]{1,0:T(8,128)(2,1)S(1)} collective-permute-done((bf16[64,2560]{1,0:T(8,128)(2,1)S(1)}, bf16[64,2560]{1,0:T(8,128)(2,1)S(1)}, u32[]{:S(2)}, u32[]{:S(2)}) %collective-permute-start.7) | collective-permute-done | bytes 327712 | tf_op jit(solution)/shard_map/ppermute | solution.py:406
  56.2 1.9 %collective-permute-done.8.refs_6_ = bf16[64,2560]{1,0:T(8,128)(2,1)S(1)} collective-permute-done((bf16[64,2560]{1,0:T(8,128)(2,1)S(1)}, bf16[64,2560]{1,0:T(8,128)(2,1)S(1)}, u32[]{:S(2)}, u32[]{:S(2)}) %collective-permute-start.8) | collective-permute-done | bytes 327712 | tf_op jit(solution)/shard_map/ppermute | solution.py:409
  58.1 3.5 %collective-permute-done.9.refs_7_ = bf16[64,2560]{1,0:T(8,128)(2,1)S(1)} collective-permute-done((bf16[64,2560]{1,0:T(8,128)(2,1)S(1)}, bf16[64,2560]{1,0:T(8,128)(2,1)S(1)}, u32[]{:S(2)}, u32[]{:S(2)}) %collective-permute-start.9) | collective-permute-done | bytes 327712 | tf_op jit(solution)/shard_map/ppermute | solution.py:406
  61.6 4.7 %project.1 = (bf16[8,64,480]{2,1,0:T(8,128)(2,1)S(1)}, bf16[8,64,480]{2,1,0:T(8,128)(2,1)S(1)}, bf16[4,64,640]{2,1,0:T(8,128)(2,1)S(1)}, bf16[4,64,640]{2,1,0:T(8,128)(2,1)S(1)}) custom-call(s32[2]{0:T(128)S(1)} %pad_add_fusion.flags, bf16[64,2560]{1,0:T(8,128)(2,1)S(1)} %collective-permute-done.refs_0_, ...), custom_call_target="tpu_custom_call" | custom-call | flops 2516582400 | bytes 8388608 | tf_op jit(solution)/shard_map/project/pallas_call | solution.py:149
  66.3 3.4 %collective-permute-start.13 = (bf16[4,64,640]{2,1,0:T(8,128)(2,1)S(1)}, bf16[4,64,640]{2,1,0:T(8,128)(2,1)S(1)}, u32[]{:S(2)}, u32[]{:S(2)}) collective-permute-start(bf16[4,64,640]{2,1,0:T(8,128)(2,1)S(1)} %get-tuple-element.43), channel_id=1, source_target_pairs={{0,1},{1,0},{2,3},{3,2},{4,5},{5,4},{6,7},{7,6},{8,9},{9,8},{10,11... | collective-permute-start | bytes 983048 | tf_op jit(solution)/shard_map/ppermute | solution.py:417
  72.7 3.4 %inner.1 = (bf16[8,128,160]{2,1,0:T(8,128)(2,1)S(1)}, f32[8,128,256]{2,1,0:T(8,128)S(1)}) custom-call(s32[19]{0:T(128)S(1)} %stack.137.ints, f32[1]{0:T(128)S(6)} %mul.261.factor_ref, f32[64]{0:T(128)S(1)} %reshape.21.band, f32[16,128]{1,0:T(8,128)S(1)} %fusion.4.usable, bf16[8,64,480]{2,1,0:T(8,128)(2,1)S(1)} %get-tuple-element.39.refs_0_, ...), custom_call_target="tpu_custom_call" | custom-call | flops 10000000 | bytes 100000 | tf_op jit(solution)/shard_map/inner/pallas_call | solution.py:247
  76.1 1.6 %collective-permute-done.12.refs_2_ = bf16[4,64,640]{2,1,0:T(8,128)(2,1)S(1)} collective-permute-done((bf16[4,64,640]{2,1,0:T(8,128)(2,1)S(1)}, bf16[4,64,640]{2,1,0:T(8,128)(2,1)S(1)}, u32[]{:S(2)}, u32[]{:S(2)}) %collective-permute-start.12) | collective-permute-done | bytes 327712 | tf_op jit(solution)/shard_map/ppermute | solution.py:416
  77.7 3.5 %collective-permute-done.14.refs_3_ = bf16[4,64,640]{2,1,0:T(8,128)(2,1)S(1)} collective-permute-done((bf16[4,64,640]{2,1,0:T(8,128)(2,1)S(1)}, bf16[4,64,640]{2,1,0:T(8,128)(2,1)S(1)}, u32[]{:S(2)}, u32[]{:S(2)}) %collective-permute-start.14) | collective-permute-done | bytes 327712 | tf_op jit(solution)/shard_map/ppermute | solution.py:417
  83.3 2.2 %outer.1 = (bf16[4,2,8,1280]{3,2,1,0:T(8,128)(2,1)S(1)}, bf16[4,2,8,1280]{3,2,1,0:T(8,128)(2,1)S(1)}) custom-call(s32[19]{0:T(128)S(1)} %stack.137.ints, f32[1]{0:T(128)S(6)} %mul.261.factor_ref, f32[16,128]{1,0:T(8,128)S(1)} %fusion.4.usable, bf16[8,128,160]{2,1,0:T(8,128)(2,1)S(1)} %get-tuple-element.41.zonal_ref, ...), custom_call_target="tpu_custom_call" | custom-call | flops 1000000000 | bytes 4194304 | tf_op jit(solution)/shard_map/outer/pallas_call | solution.py:303
  85.5 3.3 %collective-permute-start.17 = (bf16[4,2,8,1280]{3,2,1,0:T(8,128)(2,1)S(1)}, bf16[4,2,8,1280]{3,2,1,0:T(8,128)(2,1)S(1)}, u32[]{:S(2)}, u32[]{:S(2)}) collective-permute-start(bf16[4,2,8,1280]{3,2,1,0:T(8,128)(2,1)S(1)} %get-tuple-element.48), channel_id=1, source_target_pairs={{0,0},{1,128},{8,8},{9,136},{128,1},{129,129},{136,9},{137,137},{2... | collective-permute-start | bytes 491528 | tf_op jit(solution)/shard_map/ppermute | solution.py:424
  89.9 3.1 %collective-permute-done.17.near.refs_0_ = bf16[4,2,8,1280]{3,2,1,0:T(8,128)(2,1)S(1)} collective-permute-done((bf16[4,2,8,1280]{3,2,1,0:T(8,128)(2,1)S(1)}, bf16[4,2,8,1280]{3,2,1,0:T(8,128)(2,1)S(1)}, u32[]{:S(2)}, u32[]{:S(2)}) %collective-permute-start.17) | collective-permute-done | bytes 163872 | tf_op jit(solution)/shard_map/ppermute | solution.py:424
  93.0 2.3 %collective-permute-done.18.far.refs_1_ = bf16[4,2,8,1280]{3,2,1,0:T(8,128)(2,1)S(1)} collective-permute-done((bf16[4,2,8,1280]{3,2,1,0:T(8,128)(2,1)S(1)}, bf16[4,2,8,1280]{3,2,1,0:T(8,128)(2,1)S(1)}, u32[]{:S(2)}, u32[]{:S(2)}) %collective-permute-start.18) | collective-permute-done | bytes 163872 | tf_op jit(solution)/shard_map/ppermute | solution.py:424
  95.8 5.6 %collective-permute-start.20 = (bf16[2,2,8,1280]{3,2,1,0:T(8,128)(2,1)S(1)}, bf16[2,2,8,1280]{3,2,1,0:T(8,128)(2,1)S(1)}, u32[]{:S(2)}, u32[]{:S(2)}) collective-permute-start(bf16[2,2,8,1280]{3,2,1,0:T(8,128)(2,1)S(1)} %get-tuple-element.51), channel_id=1, source_target_pairs={{0,4},{2,6},{4,0},{6,2},{1,5},{3,7},{5,1},{7,3},{8,12},{10,14},{12... | collective-permute-start | bytes 245768 | tf_op jit(solution)/shard_map/ppermute | solution.py:427
  101.8 2.3 %collective-permute-done.20.refs_3_ = bf16[2,2,8,1280]{3,2,1,0:T(8,128)(2,1)S(1)} collective-permute-done((bf16[2,2,8,1280]{3,2,1,0:T(8,128)(2,1)S(1)}, bf16[2,2,8,1280]{3,2,1,0:T(8,128)(2,1)S(1)}, u32[]{:S(2)}, u32[]{:S(2)}) %collective-permute-start.20) | collective-permute-done | bytes 81952 | tf_op jit(solution)/shard_map/ppermute | solution.py:427
  104.1 1.7 %collective-permute-done.21.refs_4_ = bf16[2,2,8,1280]{3,2,1,0:T(8,128)(2,1)S(1)} collective-permute-done((bf16[2,2,8,1280]{3,2,1,0:T(8,128)(2,1)S(1)}, bf16[2,2,8,1280]{3,2,1,0:T(8,128)(2,1)S(1)}, u32[]{:S(2)}, u32[]{:S(2)}) %collective-permute-start.21) | collective-permute-done | bytes 81952 | tf_op jit(solution)/shard_map/ppermute | solution.py:427
  (60 shorter events, 19.6 us)
Async XLA Ops:
  2.4 19.1 %collective-permute-start = (bf16[64,2560]{1,0:T(8,128)(2,1)S(1)}, bf16[64,2560]{1,0:T(8,128)(2,1)S(1)}, u32[]{:S(2)}, u32[]{:S(2)}) collective-permute-start(bf16[64,2560]{1,0:T(8,128)(2,1)S(1)} %bitcast.46), channel_id=1, source_target_pairs={{0,0},{1,65},{2,16},{3,81},{4,32},{5,97},{6,48},{7,113},{8,64},{9,... | collective-permute-start | bytes 983048 | tf_op jit(solution)/shard_map/ppermute | solution.py:373
  14.6 28.5 %collective-permute-start.4 = (bf16[480,1280]{1,0:T(8,128)(2,1)}, bf16[480,1280]{1,0:T(8,128)(2,1)}, u32[]{:S(2)}, u32[]{:S(2)}) collective-permute-start(bf16[480,1280]{1,0:T(8,128)(2,1)} %dynamic-slice_bitcast_fusion), channel_id=1, source_target_pairs={{0,128},{128,0},{1,129},{129,1},{2,130},{130,2},{3,131},{131,3},{4... | collective-permute-start | bytes 3686408 | tf_op jit(solution)/shard_map/ppermute | solution.py:377
  21.4 9.8 %collective-permute-start.2 = (bf16[64,2560]{1,0:T(8,128)(2,1)S(1)}, bf16[64,2560]{1,0:T(8,128)(2,1)S(1)}, u32[]{:S(2)}, u32[]{:S(2)}) collective-permute-start(bf16[64,2560]{1,0:T(8,128)(2,1)S(1)} %collective-permute-done.refs_0_), channel_id=1, source_target_pairs={{0,1},{1,0},{2,3},{3,2},{4,5},{5,4},{6,7},{7,6},{8,9},{9,8},{10,11... | collective-permute-start | bytes 983048 | tf_op jit(solution)/shard_map/ppermute | solution.py:403
  21.5 13.7 %collective-permute-start.1 = (bf16[64,2560]{1,0:T(8,128)(2,1)S(1)}, bf16[64,2560]{1,0:T(8,128)(2,1)S(1)}, u32[]{:S(2)}, u32[]{:S(2)}) collective-permute-start(bf16[64,2560]{1,0:T(8,128)(2,1)S(1)} %collective-permute-done.refs_0_), channel_id=1, source_target_pairs={{0,16},{1,113},{16,32},{17,1},{32,48},{33,17},{48,64},{49,33},{64,... | collective-permute-start | bytes 983048 | tf_op jit(solution)/shard_map/ppermute | solution.py:406
  31.3 7.5 %collective-permute-start.3 = (bf16[64,2560]{1,0:T(8,128)(2,1)S(1)}, bf16[64,2560]{1,0:T(8,128)(2,1)S(1)}, u32[]{:S(2)}, u32[]{:S(2)}) collective-permute-start(bf16[64,2560]{1,0:T(8,128)(2,1)S(1)} %collective-permute-done.2), channel_id=1, source_target_pairs={{0,16},{1,113},{16,32},{17,1},{32,48},{33,17},{48,64},{49,33},{64,... | collective-permute-start | bytes 983048 | tf_op jit(solution)/shard_map/ppermute | solution.py:409
  35.3 7.1 %collective-permute-start.5 = (bf16[64,2560]{1,0:T(8,128)(2,1)S(1)}, bf16[64,2560]{1,0:T(8,128)(2,1)S(1)}, u32[]{:S(2)}, u32[]{:S(2)}) collective-permute-start(bf16[64,2560]{1,0:T(8,128)(2,1)S(1)} %collective-permute-done.1.refs_1_), channel_id=1, source_target_pairs={{0,16},{1,113},{16,32},{17,1},{32,48},{33,17},{48,64},{49,33},{64,... | collective-permute-start | bytes 983048 | tf_op jit(solution)/shard_map/ppermute | solution.py:406
  38.8 7.1 %collective-permute-start.6 = (bf16[64,2560]{1,0:T(8,128)(2,1)S(1)}, bf16[64,2560]{1,0:T(8,128)(2,1)S(1)}, u32[]{:S(2)}, u32[]{:S(2)}) collective-permute-start(bf16[64,2560]{1,0:T(8,128)(2,1)S(1)} %collective-permute-done.3.refs_2_), channel_id=1, source_target_pairs={{0,16},{1,113},{16,32},{17,1},{32,48},{33,17},{48,64},{49,33},{64,... | collective-permute-start | bytes 983048 | tf_op jit(solution)/shard_map/ppermute | solution.py:409
  45.9 15.7 %collective-permute-start.10 = (bf16[480,1280]{1,0:T(8,128)(2,1)}, bf16[480,1280]{1,0:T(8,128)(2,1)S(1)}, u32[]{:S(2)}, u32[]{:S(2)}) collective-permute-start(bf16[480,1280]{1,0:T(8,128)(2,1)} %collective-permute-done.4.refs_9_), channel_id=1, source_target_pairs={{0,1},{1,0},{2,3},{3,2},{4,5},{5,4},{6,7},{7,6},{8,9},{9,8},{10,11... | collective-permute-start | bytes 3686408 | tf_op jit(solution)/shard_map/ppermute | solution.py:412
  48.4 6.2 %collective-permute-start.7 = (bf16[64,2560]{1,0:T(8,128)(2,1)S(1)}, bf16[64,2560]{1,0:T(8,128)(2,1)S(1)}, u32[]{:S(2)}, u32[]{:S(2)}) collective-permute-start(bf16[64,2560]{1,0:T(8,128)(2,1)S(1)} %collective-permute-done.5.refs_3_), channel_id=1, source_target_pairs={{0,16},{1,113},{16,32},{17,1},{32,48},{33,17},{48,64},{49,33},{64,... | collective-permute-start | bytes 983048 | tf_op jit(solution)/shard_map/ppermute | solution.py:406
  49.0 9.1 %collective-permute-start.8 = (bf16[64,2560]{1,0:T(8,128)(2,1)S(1)}, bf16[64,2560]{1,0:T(8,128)(2,1)S(1)}, u32[]{:S(2)}, u32[]{:S(2)}) collective-permute-start(bf16[64,2560]{1,0:T(8,128)(2,1)S(1)} %collective-permute-done.6.refs_4_), channel_id=1, source_target_pairs={{0,16},{1,113},{16,32},{17,1},{32,48},{33,17},{48,64},{49,33},{64,... | collective-permute-start | bytes 983048 | tf_op jit(solution)/shard_map/ppermute | solution.py:409
  54.6 7.0 %collective-permute-start.9 = (bf16[64,2560]{1,0:T(8,128)(2,1)S(1)}, bf16[64,2560]{1,0:T(8,128)(2,1)S(1)}, u32[]{:S(2)}, u32[]{:S(2)}) collective-permute-start(bf16[64,2560]{1,0:T(8,128)(2,1)S(1)} %collective-permute-done.7.refs_5_), channel_id=1, source_target_pairs={{0,16},{1,113},{16,32},{17,1},{32,48},{33,17},{48,64},{49,33},{64,... | collective-permute-start | bytes 983048 | tf_op jit(solution)/shard_map/ppermute | solution.py:406
  66.3 5.0 %collective-permute-start.13 = (bf16[4,64,640]{2,1,0:T(8,128)(2,1)S(1)}, bf16[4,64,640]{2,1,0:T(8,128)(2,1)S(1)}, u32[]{:S(2)}, u32[]{:S(2)}) collective-permute-start(bf16[4,64,640]{2,1,0:T(8,128)(2,1)S(1)} %get-tuple-element.43), channel_id=1, source_target_pairs={{0,1},{1,0},{2,3},{3,2},{4,5},{5,4},{6,7},{7,6},{8,9},{9,8},{10,11... | collective-permute-start | bytes 983048 | tf_op jit(solution)/shard_map/ppermute | solution.py:417
  69.8 2.9 %collective-permute-start.11 = (bf16[8,64,480]{2,1,0:T(8,128)(2,1)S(1)}, bf16[8,64,480]{2,1,0:T(8,128)(2,1)S(1)}, u32[]{:S(2)}, u32[]{:S(2)}) collective-permute-start(bf16[8,64,480]{2,1,0:T(8,128)(2,1)S(1)} %get-tuple-element.40), channel_id=1, source_target_pairs={{0,1},{1,0},{2,3},{3,2},{4,5},{5,4},{6,7},{7,6},{8,9},{9,8},{10,11... | collective-permute-start | bytes 1474568 | tf_op jit(solution)/shard_map/ppermute | solution.py:418
  69.9 7.8 %collective-permute-start.12 = (bf16[4,64,640]{2,1,0:T(8,128)(2,1)S(1)}, bf16[4,64,640]{2,1,0:T(8,128)(2,1)S(1)}, u32[]{:S(2)}, u32[]{:S(2)}) collective-permute-start(bf16[4,64,640]{2,1,0:T(8,128)(2,1)S(1)} %get-tuple-element.42), channel_id=1, source_target_pairs={{0,2},{2,4},{3,1},{4,6},{5,3},{6,14},{7,5},{14,12},{15,7},{12,10},... | collective-permute-start | bytes 983048 | tf_op jit(solution)/shard_map/ppermute | solution.py:416
  71.4 9.8 %collective-permute-start.14 = (bf16[4,64,640]{2,1,0:T(8,128)(2,1)S(1)}, bf16[4,64,640]{2,1,0:T(8,128)(2,1)S(1)}, u32[]{:S(2)}, u32[]{:S(2)}) collective-permute-start(bf16[4,64,640]{2,1,0:T(8,128)(2,1)S(1)} %collective-permute-done.13), channel_id=1, source_target_pairs={{0,2},{2,4},{3,1},{4,6},{5,3},{6,14},{7,5},{14,12},{15,7},{12,10},... | collective-permute-start | bytes 983048 | tf_op jit(solution)/shard_map/ppermute | solution.py:417
  81.2 2.1 %collective-permute-start.16 = (bf16[4,64,640]{2,1,0:T(8,128)(2,1)S(1)}, bf16[4,64,640]{2,1,0:T(8,128)(2,1)S(1)}, u32[]{:S(2)}, u32[]{:S(2)}) collective-permute-start(bf16[4,64,640]{2,1,0:T(8,128)(2,1)S(1)} %collective-permute-done.14.refs_3_), channel_id=1, source_target_pairs={{0,1},{1,0},{2,3},{3,2},{4,5},{5,4},{6,7},{7,6},{8,9},{9,8},{10,11... | collective-permute-start | bytes 983048 | tf_op jit(solution)/shard_map/ppermute | solution.py:421
  85.5 7.5 %collective-permute-start.17 = (bf16[4,2,8,1280]{3,2,1,0:T(8,128)(2,1)S(1)}, bf16[4,2,8,1280]{3,2,1,0:T(8,128)(2,1)S(1)}, u32[]{:S(2)}, u32[]{:S(2)}) collective-permute-start(bf16[4,2,8,1280]{3,2,1,0:T(8,128)(2,1)S(1)} %get-tuple-element.48), channel_id=1, source_target_pairs={{0,0},{1,128},{8,8},{9,136},{128,1},{129,129},{136,9},{137,137},{2... | collective-permute-start | bytes 491528 | tf_op jit(solution)/shard_map/ppermute | solution.py:424
  88.8 6.5 %collective-permute-start.18 = (bf16[4,2,8,1280]{3,2,1,0:T(8,128)(2,1)S(1)}, bf16[4,2,8,1280]{3,2,1,0:T(8,128)(2,1)S(1)}, u32[]{:S(2)}, u32[]{:S(2)}) collective-permute-start(bf16[4,2,8,1280]{3,2,1,0:T(8,128)(2,1)S(1)} %get-tuple-element.49), channel_id=1, source_target_pairs={{0,8},{1,136},{8,0},{9,128},{128,9},{129,137},{136,1},{137,129},{2... | collective-permute-start | bytes 491528 | tf_op jit(solution)/shard_map/ppermute | solution.py:424
  95.3 6.5 %collective-permute-start.19 = (bf16[2,2,8,1280]{3,2,1,0:T(8,128)(2,1)S(1)}, bf16[2,2,8,1280]{3,2,1,0:T(8,128)(2,1)S(1)}, u32[]{:S(2)}, u32[]{:S(2)}) collective-permute-start(bf16[2,2,8,1280]{3,2,1,0:T(8,128)(2,1)S(1)} %get-tuple-element.50), channel_id=1, source_target_pairs={{0,2},{2,0},{4,6},{6,4},{1,3},{3,1},{5,7},{7,5},{8,10},{10,8},{12,... | collective-permute-start | bytes 245768 | tf_op jit(solution)/shard_map/ppermute | solution.py:427
  95.8 8.3 %collective-permute-start.20 = (bf16[2,2,8,1280]{3,2,1,0:T(8,128)(2,1)S(1)}, bf16[2,2,8,1280]{3,2,1,0:T(8,128)(2,1)S(1)}, u32[]{:S(2)}, u32[]{:S(2)}) collective-permute-start(bf16[2,2,8,1280]{3,2,1,0:T(8,128)(2,1)S(1)} %get-tuple-element.51), channel_id=1, source_target_pairs={{0,4},{2,6},{4,0},{6,2},{1,5},{3,7},{5,1},{7,3},{8,12},{10,14},{12... | collective-permute-start | bytes 245768 | tf_op jit(solution)/shard_map/ppermute | solution.py:427
  101.3 4.5 %collective-permute-start.21 = (bf16[2,2,8,1280]{3,2,1,0:T(8,128)(2,1)S(1)}, bf16[2,2,8,1280]{3,2,1,0:T(8,128)(2,1)S(1)}, u32[]{:S(2)}, u32[]{:S(2)}) collective-permute-start(bf16[2,2,8,1280]{3,2,1,0:T(8,128)(2,1)S(1)} %get-tuple-element.52), channel_id=1, source_target_pairs={{0,6},{2,4},{4,2},{6,0},{1,7},{3,5},{5,3},{7,1},{8,14},{10,12},{12... | collective-permute-start | bytes 245768 | tf_op jit(solution)/shard_map/ppermute | solution.py:427
  101.3 5.8 %collective-permute-start.22 = (bf16[4,2,8,1280]{3,2,1,0:T(8,128)(2,1)S(1)}, bf16[4,2,8,1280]{3,2,1,0:T(8,128)(2,1)S(1)}, u32[]{:S(2)}, u32[]{:S(2)}) collective-permute-start(bf16[4,2,8,1280]{3,2,1,0:T(8,128)(2,1)S(1)} %collective-permute-done.17.near.refs_0_), channel_id=1, source_target_pairs={{0,1},{1,0},{2,3},{3,2},{4,5},{5,4},{6,7},{7,6},{8,9},{9,8},{10,11... | collective-permute-start | bytes 491528 | tf_op jit(solution)/shard_map/ppermute | solution.py:428
  101.3 5.8 %collective-permute-start.23 = (bf16[4,2,8,1280]{3,2,1,0:T(8,128)(2,1)S(1)}, bf16[4,2,8,1280]{3,2,1,0:T(8,128)(2,1)S(1)}, u32[]{:S(2)}, u32[]{:S(2)}) collective-permute-start(bf16[4,2,8,1280]{3,2,1,0:T(8,128)(2,1)S(1)} %collective-permute-done.18.far.refs_1_), channel_id=1, source_target_pairs={{0,1},{1,0},{2,3},{3,2},{4,5},{5,4},{6,7},{7,6},{8,9},{9,8},{10,11... | collective-permute-start | bytes 491528 | tf_op jit(solution)/shard_map/ppermute | solution.py:428
  101.8 4.0 %collective-permute-start.24 = (bf16[2,2,8,1280]{3,2,1,0:T(8,128)(2,1)S(1)}, bf16[2,2,8,1280]{3,2,1,0:T(8,128)(2,1)S(1)}, u32[]{:S(2)}, u32[]{:S(2)}) collective-permute-start(bf16[2,2,8,1280]{3,2,1,0:T(8,128)(2,1)S(1)} %collective-permute-done.19.refs_2_), channel_id=1, source_target_pairs={{0,1},{1,0},{2,3},{3,2},{4,5},{5,4},{6,7},{7,6},{8,9},{9,8},{10,11... | collective-permute-start | bytes 245768 | tf_op jit(solution)/shard_map/ppermute | solution.py:428
  (8 other events, 90.6 us)

commit v7 on v6

--- a/solution.py
+++ b/solution.py
@@ -65,6 +65,16 @@
     return pairs
 
 
+def weight_perm():
+    pairs = []
+    for y in range(4):
+        for core in range(2):
+            there = (y + 1 - 2 * core) % 4
+            source = flat((y % 2, 2), (y // 2, 2), (core, 2))
+            pairs.append((source, flat((there % 2, 2), (there // 2, 2), (core, 2))))
+    return pairs
+
+
 def neighbour_perm():
     pairs = []
     for block in range(16):
@@ -211,7 +221,7 @@
 
 
 def inner_kernel(ints, factor_ref, band, usable, *refs):
-    parts, (zonal_ref, window_ref, ks, vs, masks) = refs[:2], refs[2:]
+    parts, (zonal_ref, window_ref, masks_ref, shifts_ref, ks, vs, masks) = refs[:2], refs[2:]
     factor = factor_ref[0]
     start = 0
     for part in parts:
@@ -219,8 +229,13 @@
             whole = part[r]
             put(ks, vs, r * COLS + start, whole[:, HEAD_DIM : 2 * HEAD_DIM], whole[:, 2 * HEAD_DIM :])
         start += part.shape[1]
-    fill_masks(masks, 0, ints[0], ints[0], ints[1], ints[2])
-    bias = shifts(usable, ints[0], ints[1])
+    base, core, radius = ints[0], ints[1], ints[2]
+    fill_masks(masks, 0, base, base, core, radius)
+    bias = shifts(usable, base, core)
+    fill_masks(masks_ref, 0, base, base + 2, core, radius)
+    fill_masks(masks_ref, WIN + 1, base, base - 2, core, radius)
+    shifts_ref[0] = shifts(usable, base + 2, core)
+    shifts_ref[1] = shifts(usable, base - 2, core)
     eye = lax.broadcasted_iota(jnp.int32, (COLS, COLS), 0) == lax.broadcasted_iota(jnp.int32, (COLS, COLS), 1)
     for r in range(ROWS):
         query = query_of(parts, r)
@@ -249,9 +264,11 @@
         out_shape=[
             jax.ShapeDtypeStruct((ROWS, COLS, HEAD_DIM), jnp.bfloat16),
             jax.ShapeDtypeStruct((ROWS, COLS, 256), jnp.float32),
+            jax.ShapeDtypeStruct((2 * WIN + 2, COLS, COLS), jnp.float32),
+            jax.ShapeDtypeStruct((2, KEY_ROWS, COLS), jnp.float32),
         ],
         in_specs=[SMEM] * 3 + [VMEM] * 3,
-        out_specs=[VMEM] * 2,
+        out_specs=[VMEM] * 4,
         scratch_shapes=[
             pltpu.VMEM((ROWS * COLS, HEAD_DIM), jnp.bfloat16),
             pltpu.VMEM((ROWS * COLS, 256), jnp.bfloat16),
@@ -263,19 +280,17 @@
     )(ints, factor, band, usable, *parts)
 
 
-def outer_kernel(ints, factor_ref, usable, zonal_ref, window_ref, *refs):
-    parts, (own, oth, far_own, far_oth), chunks, (ks, vs, masks, out) = refs[:2], refs[2:6], refs[6:8], refs[8:]
+def outer_kernel(ints, factor_ref, zonal_ref, window_ref, masks, shifts_ref, *refs):
+    parts, (own, oth, far_own, far_oth), chunks, (ks, vs, out) = refs[:2], refs[2:6], refs[6:8], refs[8:]
     factor = factor_ref[0]
-    base, core, radius = ints[0], ints[1], ints[2]
+    core = ints[1]
     for edge, side, half, second in ((own, core, 0, 0), (oth, core, 1, 1), (far_own, 1 - core, 1, 1), (far_oth, 1 - core, 0, 0)):
         at = 2 * HEAD_DIM * second
         for r in range(WIN):
             whole = edge[r][:, at : at + 2 * HEAD_DIM]
             first = pl.multiple_of(side * (WIN * COLS) + r * COLS + half * HALF, HALF)
             put(ks, vs, first, whole[:, :HEAD_DIM], whole[:, HEAD_DIM:])
-    fill_masks(masks, 0, base, base + 2, core, radius)
-    fill_masks(masks, WIN + 1, base, base - 2, core, radius)
-    above, below = shifts(usable, base + 2, core), shifts(usable, base - 2, core)
+    above, below = shifts_ref[0], shifts_ref[1]
     for r in range(ROWS):
         query = query_of(parts, r)
         rows = range(r, WIN) if r < WIN else range(WIN, r + 1)
@@ -298,17 +313,16 @@
         chunks[k // 4][k % 4, 1] = out[ints[11 + k]].astype(jnp.bfloat16)
 
 
-def outer(ints, factor, usable, zonal, window, parts, edges):
+def outer(ints, factor, inner_results, parts, edges):
     chunk = jax.ShapeDtypeStruct((4, 2, 8, ROWS * HEAD_DIM), jnp.bfloat16)
     return pl.pallas_call(
         outer_kernel,
         out_shape=[chunk] * 2,
-        in_specs=[SMEM, SMEM] + [VMEM] * 9,
+        in_specs=[SMEM, SMEM] + [VMEM] * 10,
         out_specs=[VMEM] * 2,
         scratch_shapes=[
             pltpu.VMEM((2 * WIN * COLS, HEAD_DIM), jnp.bfloat16),
             pltpu.VMEM((2 * WIN * COLS, 256), jnp.bfloat16),
-            pltpu.VMEM((2 * WIN + 2, COLS, COLS), jnp.float32),
             pltpu.VMEM((16, 8, ROWS * HEAD_DIM), jnp.float32),
         ],
         compiler_params=pltpu.CompilerParams(vmem_limit_bytes=16 * MIB),
@@ -316,7 +330,7 @@
             flops=10**9, bytes_accessed=4 * MIB, transcendentals=10**6
         ),
         name="outer",
-    )(ints, factor, usable, zonal, window, *parts, *edges)
+    )(ints, factor, *inner_results, *parts, *edges)
 
 
 def regroup_kernel(near, far, *parts):
@@ -374,7 +388,7 @@
 
     own = w_qkv[0]
     half = lax.dynamic_slice_in_dim(own, core * (model // 2), model // 2, 1)
-    mine = lax.ppermute(half, "y_lo", SWAP)
+    mine = lax.ppermute(half, ("y_lo", "y_hi", "core"), weight_perm())
 
     base = (z - 2 * block) & 7
     padded = jnp.pad(key_mask, ((0, 0), (WIN, WIN)))
@@ -408,7 +422,7 @@
         if k < 4:
             b = lax.ppermute(b, ("z", "core"), ring_perm())
             pieces.append(b)
-    mine, *pieces[3:5] = lax.optimization_barrier((mine, *pieces[3:5]))
+    mine, *pieces[5:7] = lax.optimization_barrier((mine, *pieces[5:7]))
     theirs = lax.ppermute(mine, "core", SWAP)
 
     corners = ("y_lo", "y_hi", "x", "core")
@@ -416,10 +430,10 @@
     halo_own = lax.ppermute(edge, corners, neighbour_perm())
     halo_oth = lax.ppermute(lax.ppermute(give, "core", SWAP), corners, neighbour_perm())
     parts = keep, lax.ppermute(send, "core", SWAP)
-    zonal, window = inner(ints, factor, band, usable, parts)
-    halo_own, halo_oth, window = lax.optimization_barrier((halo_own, halo_oth, window))
+    results = inner(ints, factor, band, usable, parts)
+    halo_own, halo_oth, *results = lax.optimization_barrier((halo_own, halo_oth, *results))
     halos = [halo_own, halo_oth] + [lax.ppermute(halo, "core", SWAP) for halo in (halo_own, halo_oth)]
-    chunks = outer(ints, factor, usable, zonal, window, parts, halos)
+    chunks = outer(ints, factor, results, parts, halos)
 
     near, far = (lax.ppermute(chunks[k], ("y_lo", "y_hi", "core"), return_perm(k)) for k in range(2))
     passed = regroup(near, far)

time: 109 us -> 110 us (level)
  starting transfers between devices: 52.5 us -> 60.5 us
  waiting for transfers between devices: 35.4 us -> 32.2 us
  local copies, waits for them, and re-layouts: 4.85 us -> 2.42 us
    ppermute x4, starting transfers between devices: 15.1 us -> 18.2 us  [body(): a = lax.ppermute(a, ('z', 'core'), ring_perm())]
    ppermute x3, starting transfers between devices: 4.54 us -> 7.28 us  [body(): b = lax.ppermute(b, ('z', 'core'), ring_perm())]
    dynamic_slice x1, local copies, waits for them, and re-layouts: 2.56 us -> 0.08 us  [body(): half = lax.dynamic_slice_in_dim(own, core * (model // 2), model // 2, 1)]
    ppermute x2, waiting for transfers between devices: 5.39 us -> 3.41 us  [body(): lax.ppermute(chunks[k], ('y_lo', 'y_hi', 'core'), return_perm(k))]
    ppermute x2, starting transfers between devices: 4.39 us -> 6.17 us  [body(): lax.ppermute(chunks[k], ('y_lo', 'y_hi', 'core'), return_perm(k))]
    ppermute x4, waiting for transfers between devices: 12.2 us -> 10.6 us  [body(): a = lax.ppermute(a, ('z', 'core'), ring_perm())]
    ppermute x3, waiting for transfers between devices: 5.15 us -> 3.71 us  [body(): b = lax.ppermute(b, ('z', 'core'), ring_perm())]
    ppermute x3, waiting for transfers between devices: 3.98 us -> 5.37 us  [body(): lax.ppermute(part, 'x', perm)]
  transfers between devices with their start and end apart: 27 -> 27, of which waited for: 17 -> 17; matrix products, arithmetic and copies ran while one was open for 5% -> 2% of each run, Pallas kernels for 3% -> 3%
where the time goes in v7:
time: 110 us
  starting transfers between devices  60.5 us (55%)
  waiting for transfers between devices  32.2 us (29%)
  Pallas kernels  10.9 us (10%)
  other arithmetic  2.6 us (2%)
  local copies, waits for them, and re-layouts  2.42 us (2%)
  between operations  1.68 us (2%)
    ppermute x4, starting transfers between devices, body(): a = lax.ppermute(a, ('z', 'core'), ring_perm())  18.2 us
    ppermute x4, waiting for transfers between devices, body(): a = lax.ppermute(a, ('z', 'core'), ring_perm())  10.6 us
    ppermute x1, starting transfers between devices, body(): first = lax.ppermute(normed, AXES, spread_perm())  9.65 us
    ppermute x3, starting transfers between devices, body(): b = lax.ppermute(b, ('z', 'core'), ring_perm())  7.28 us
    ppermute x2, starting transfers between devices, body(): lax.ppermute(chunks[k], ('y_lo', 'y_hi', 'core'), return_perm(k))  6.17 us
    ppermute x3, starting transfers between devices, body(): lax.ppermute(part, 'x', perm)  6.08 us
    ppermute x3, waiting for transfers between devices, body(): lax.ppermute(part, 'x', perm)  5.37 us
    pallas_call x1, Pallas kernels, project(): pl.pallas_call(project_kernel, out_shape=[whole, whole, part, part], in_s...  3.93 us
  transfers between devices with their start and end apart: 27, of which 17 were waited for; matrix products, arithmetic and copies ran while one was open for 2% of the time, Pallas kernels for 3%

profile of v7, /device:TPU:1, one launch (start us, length us, event | category | flops | bytes accessed | tf_op | source)
XLA Modules:
  0.0 110.3 jit_solution(5052152064060612616)
XLA Ops:
  2.6 9.6 %collective-permute-start = (bf16[64,2560]{1,0:T(8,128)(2,1)S(1)}, bf16[64,2560]{1,0:T(8,128)(2,1)S(1)}, u32[]{:S(2)}, u32[]{:S(2)}) collective-permute-start(bf16[64,2560]{1,0:T(8,128)(2,1)S(1)} %bitcast.46), channel_id=1, source_target_pairs={{0,0},{1,65},{2,16},{3,81},{4,32},{5,97},{6,48},{7,113},{8,64},{9,... | collective-permute-start | bytes 983048 | tf_op jit(solution)/shard_map/ppermute | solution.py:387
  17.5 3.2 %collective-permute-start.6 = (bf16[480,1280]{1,0:T(8,128)(2,1)S(1)}, bf16[480,1280]{1,0:T(8,128)(2,1)S(1)}, u32[]{:S(2)}, u32[]{:S(2)}) collective-permute-start(bf16[480,1280]{1,0:T(8,128)(2,1)S(1)} %dynamic-slice_bitcast_fusion), channel_id=1, source_target_pairs={{0,128},{1,137},{128,8},{129,1},{8,136},{9,129},{136,0},{137,9},{2... | collective-permute-start | bytes 3686408 | tf_op jit(solution)/shard_map/ppermute | solution.py:391
  20.7 11.2 %collective-permute-start.1 = (bf16[64,2560]{1,0:T(8,128)(2,1)S(1)}, bf16[64,2560]{1,0:T(8,128)(2,1)S(1)}, u32[]{:S(2)}, u32[]{:S(2)}) collective-permute-start(bf16[64,2560]{1,0:T(8,128)(2,1)S(1)} %collective-permute-done.refs_0_), channel_id=1, source_target_pairs={{0,16},{1,113},{16,32},{17,1},{32,48},{33,17},{48,64},{49,33},{64,... | collective-permute-start | bytes 983048 | tf_op jit(solution)/shard_map/ppermute | solution.py:420
  32.6 3.3 %collective-permute-done.1.refs_1_ = bf16[64,2560]{1,0:T(8,128)(2,1)S(1)} collective-permute-done((bf16[64,2560]{1,0:T(8,128)(2,1)S(1)}, bf16[64,2560]{1,0:T(8,128)(2,1)S(1)}, u32[]{:S(2)}, u32[]{:S(2)}) %collective-permute-start.1) | collective-permute-done | bytes 327712 | tf_op jit(solution)/shard_map/ppermute | solution.py:420
  35.9 3.4 %collective-permute-start.4 = (bf16[64,2560]{1,0:T(8,128)(2,1)S(1)}, bf16[64,2560]{1,0:T(8,128)(2,1)S(1)}, u32[]{:S(2)}, u32[]{:S(2)}) collective-permute-start(bf16[64,2560]{1,0:T(8,128)(2,1)S(1)} %collective-permute-done.1.refs_1_), channel_id=1, source_target_pairs={{0,16},{1,113},{16,32},{17,1},{32,48},{33,17},{48,64},{49,33},{64,... | collective-permute-start | bytes 983048 | tf_op jit(solution)/shard_map/ppermute | solution.py:420
  39.4 3.4 %collective-permute-start.5 = (bf16[64,2560]{1,0:T(8,128)(2,1)S(1)}, bf16[64,2560]{1,0:T(8,128)(2,1)S(1)}, u32[]{:S(2)}, u32[]{:S(2)}) collective-permute-start(bf16[64,2560]{1,0:T(8,128)(2,1)S(1)} %collective-permute-done.3.refs_2_), channel_id=1, source_target_pairs={{0,16},{1,113},{16,32},{17,1},{32,48},{33,17},{48,64},{49,33},{64,... | collective-permute-start | bytes 983048 | tf_op jit(solution)/shard_map/ppermute | solution.py:423
  43.3 3.4 %collective-permute-start.7 = (bf16[64,2560]{1,0:T(8,128)(2,1)S(1)}, bf16[64,2560]{1,0:T(8,128)(2,1)S(1)}, u32[]{:S(2)}, u32[]{:S(2)}) collective-permute-start(bf16[64,2560]{1,0:T(8,128)(2,1)S(1)} %collective-permute-done.4.refs_3_), channel_id=1, source_target_pairs={{0,16},{1,113},{16,32},{17,1},{32,48},{33,17},{48,64},{49,33},{64,... | collective-permute-start | bytes 983048 | tf_op jit(solution)/shard_map/ppermute | solution.py:420
  46.8 3.1 %collective-permute-start.8 = (bf16[64,2560]{1,0:T(8,128)(2,1)S(1)}, bf16[64,2560]{1,0:T(8,128)(2,1)S(1)}, u32[]{:S(2)}, u32[]{:S(2)}) collective-permute-start(bf16[64,2560]{1,0:T(8,128)(2,1)S(1)} %collective-permute-done.5.refs_4_), channel_id=1, source_target_pairs={{0,16},{1,113},{16,32},{17,1},{32,48},{33,17},{48,64},{49,33},{64,... | collective-permute-start | bytes 983048 | tf_op jit(solution)/shard_map/ppermute | solution.py:423
  50.7 3.5 %collective-permute-done.8.refs_6_ = bf16[64,2560]{1,0:T(8,128)(2,1)S(1)} collective-permute-done((bf16[64,2560]{1,0:T(8,128)(2,1)S(1)}, bf16[64,2560]{1,0:T(8,128)(2,1)S(1)}, u32[]{:S(2)}, u32[]{:S(2)}) %collective-permute-start.8) | collective-permute-done | bytes 327712 | tf_op jit(solution)/shard_map/ppermute | solution.py:423
  54.3 2.9 %collective-permute-start.10 = (bf16[480,1280]{1,0:T(8,128)(2,1)S(1)}, bf16[480,1280]{1,0:T(8,128)(2,1)S(1)}, u32[]{:S(2)}, u32[]{:S(2)}) collective-permute-start(bf16[480,1280]{1,0:T(8,128)(2,1)S(1)} %collective-permute-done.6.refs_9_), channel_id=1, source_target_pairs={{0,1},{1,0},{2,3},{3,2},{4,5},{5,4},{6,7},{7,6},{8,9},{9,8},{10,11... | collective-permute-start | bytes 3686408 | tf_op jit(solution)/shard_map/ppermute | solution.py:426
  57.4 6.0 %collective-permute-done.9.refs_7_ = bf16[64,2560]{1,0:T(8,128)(2,1)S(1)} collective-permute-done((bf16[64,2560]{1,0:T(8,128)(2,1)S(1)}, bf16[64,2560]{1,0:T(8,128)(2,1)S(1)}, u32[]{:S(2)}, u32[]{:S(2)}) %collective-permute-start.9) | collective-permute-done | bytes 327712 | tf_op jit(solution)/shard_map/ppermute | solution.py:420
  63.4 3.9 %project.1 = (bf16[8,64,480]{2,1,0:T(8,128)(2,1)S(1)}, bf16[8,64,480]{2,1,0:T(8,128)(2,1)S(1)}, bf16[4,64,640]{2,1,0:T(8,128)(2,1)S(1)}, bf16[4,64,640]{2,1,0:T(8,128)(2,1)S(1)}) custom-call(s32[2]{0:T(128)S(1)} %pad_add_fusion.flags, bf16[64,2560]{1,0:T(8,128)(2,1)S(1)} %collective-permute-done.refs_0_, ...), custom_call_target="tpu_custom_call" | custom-call | flops 2516582400 | bytes 8388608 | tf_op jit(solution)/shard_map/project/pallas_call | solution.py:159
  67.3 2.2 %collective-permute-start.12 = (bf16[4,64,640]{2,1,0:T(8,128)(2,1)S(1)}, bf16[4,64,640]{2,1,0:T(8,128)(2,1)S(1)}, u32[]{:S(2)}, u32[]{:S(2)}) collective-permute-start(bf16[4,64,640]{2,1,0:T(8,128)(2,1)S(1)} %get-tuple-element.43), channel_id=1, source_target_pairs={{0,1},{1,0},{2,3},{3,2},{4,5},{5,4},{6,7},{7,6},{8,9},{9,8},{10,11... | collective-permute-start | bytes 983048 | tf_op jit(solution)/shard_map/ppermute | solution.py:431
  72.4 3.4 %inner.1 = (bf16[8,128,160]{2,1,0:T(8,128)(2,1)S(1)}, f32[8,128,256]{2,1,0:T(8,128)S(1)}, f32[10,128,128]{2,1,0:T(8,128)S(1)}, f32[2,16,128]{2,1,0:T(8,128)S(1)}) custom-call(s32[19]{0:T(128)S(1)} %stack.137.ints, f32[1]{0:T(128)S(6)} %mul.261.factor_ref, f32[64]{0:T(128)S(1)} %reshape.21.band, f32[16,128]{1,0:T(8,128)S(1)} %fusion.4.usable, ...), custom_call_target="tpu_custom_call" | custom-call | flops 10000000 | bytes 100000 | tf_op jit(solution)/shard_map/inner/pallas_call | solution.py:262
  75.8 1.8 %collective-permute-done.11.refs_2_ = bf16[4,64,640]{2,1,0:T(8,128)(2,1)S(1)} collective-permute-done((bf16[4,64,640]{2,1,0:T(8,128)(2,1)S(1)}, bf16[4,64,640]{2,1,0:T(8,128)(2,1)S(1)}, u32[]{:S(2)}, u32[]{:S(2)}) %collective-permute-start.11) | collective-permute-done | bytes 327712 | tf_op jit(solution)/shard_map/ppermute | solution.py:430
  77.6 3.5 %collective-permute-done.13.refs_3_ = bf16[4,64,640]{2,1,0:T(8,128)(2,1)S(1)} collective-permute-done((bf16[4,64,640]{2,1,0:T(8,128)(2,1)S(1)}, bf16[4,64,640]{2,1,0:T(8,128)(2,1)S(1)}, u32[]{:S(2)}, u32[]{:S(2)}) %collective-permute-start.13) | collective-permute-done | bytes 327712 | tf_op jit(solution)/shard_map/ppermute | solution.py:431
  83.2 2.3 %outer.1 = (bf16[4,2,8,1280]{3,2,1,0:T(8,128)(2,1)S(1)}, bf16[4,2,8,1280]{3,2,1,0:T(8,128)(2,1)S(1)}) custom-call(s32[19]{0:T(128)S(1)} %stack.137.ints, f32[1]{0:T(128)S(6)} %mul.261.factor_ref, bf16[8,128,160]{2,1,0:T(8,128)(2,1)S(1)} %get-tuple-element.52.zonal_ref, f32[8,128,256]{2,1,0:T(8,128)S(1)} %get-tuple-element.53.window_ref, ...), custom_call_target="tpu_custom_call" | custom-call | flops 1000000000 | bytes 4194304 | tf_op jit(solution)/shard_map/outer/pallas_call | solution.py:318
  85.5 3.5 %collective-permute-start.17 = (bf16[4,2,8,1280]{3,2,1,0:T(8,128)(2,1)S(1)}, bf16[4,2,8,1280]{3,2,1,0:T(8,128)(2,1)S(1)}, u32[]{:S(2)}, u32[]{:S(2)}) collective-permute-start(bf16[4,2,8,1280]{3,2,1,0:T(8,128)(2,1)S(1)} %get-tuple-element.58), channel_id=1, source_target_pairs={{0,0},{1,128},{8,8},{9,136},{128,1},{129,129},{136,9},{137,137},{2... | collective-permute-start | bytes 491528 | tf_op jit(solution)/shard_map/ppermute | solution.py:438
  89.0 2.6 %collective-permute-start.18 = (bf16[4,2,8,1280]{3,2,1,0:T(8,128)(2,1)S(1)}, bf16[4,2,8,1280]{3,2,1,0:T(8,128)(2,1)S(1)}, u32[]{:S(2)}, u32[]{:S(2)}) collective-permute-start(bf16[4,2,8,1280]{3,2,1,0:T(8,128)(2,1)S(1)} %get-tuple-element.59), channel_id=1, source_target_pairs={{0,8},{1,136},{8,0},{9,128},{128,9},{129,137},{136,1},{137,129},{2... | collective-permute-start | bytes 491528 | tf_op jit(solution)/shard_map/ppermute | solution.py:438
  91.6 1.3 %collective-permute-done.17.near.refs_0_ = bf16[4,2,8,1280]{3,2,1,0:T(8,128)(2,1)S(1)} collective-permute-done((bf16[4,2,8,1280]{3,2,1,0:T(8,128)(2,1)S(1)}, bf16[4,2,8,1280]{3,2,1,0:T(8,128)(2,1)S(1)}, u32[]{:S(2)}, u32[]{:S(2)}) %collective-permute-start.17) | collective-permute-done | bytes 163872 | tf_op jit(solution)/shard_map/ppermute | solution.py:438
  93.0 2.1 %collective-permute-done.18.far.refs_1_ = bf16[4,2,8,1280]{3,2,1,0:T(8,128)(2,1)S(1)} collective-permute-done((bf16[4,2,8,1280]{3,2,1,0:T(8,128)(2,1)S(1)}, bf16[4,2,8,1280]{3,2,1,0:T(8,128)(2,1)S(1)}, u32[]{:S(2)}, u32[]{:S(2)}) %collective-permute-start.18) | collective-permute-done | bytes 163872 | tf_op jit(solution)/shard_map/ppermute | solution.py:438
  96.1 5.1 %collective-permute-start.20 = (bf16[2,2,8,1280]{3,2,1,0:T(8,128)(2,1)S(1)}, bf16[2,2,8,1280]{3,2,1,0:T(8,128)(2,1)S(1)}, u32[]{:S(2)}, u32[]{:S(2)}) collective-permute-start(bf16[2,2,8,1280]{3,2,1,0:T(8,128)(2,1)S(1)} %get-tuple-element.61), channel_id=1, source_target_pairs={{0,4},{2,6},{4,0},{6,2},{1,5},{3,7},{5,1},{7,3},{8,12},{10,14},{12... | collective-permute-start | bytes 245768 | tf_op jit(solution)/shard_map/ppermute | solution.py:441
  101.7 4.1 %collective-permute-done.20.refs_3_ = bf16[2,2,8,1280]{3,2,1,0:T(8,128)(2,1)S(1)} collective-permute-done((bf16[2,2,8,1280]{3,2,1,0:T(8,128)(2,1)S(1)}, bf16[2,2,8,1280]{3,2,1,0:T(8,128)(2,1)S(1)}, u32[]{:S(2)}, u32[]{:S(2)}) %collective-permute-start.20) | collective-permute-done | bytes 81952 | tf_op jit(solution)/shard_map/ppermute | solution.py:441
  109.0 1.3 %assemble.1 = bf16[1,8,20480]{2,1,0:T(8,128)(2,1)} custom-call(s32[16]{0:T(128)S(1)} %stack.154.at, bf16[4,2,8,1280]{3,2,1,0:T(8,128)(2,1)S(1)} %collective-permute-done.17.near.refs_0_, bf16[4,2,8,1280]{3,2,1,0:T(8,128)(2,1)S(1)} %collective-permute-done.18.far.refs_1_, bf16[2,2,8,1280]{3,2,1,0:T(8,128)(2,1)S(1)} %collective-permute-done.19.refs_2_, ...), custom_call_target="tpu_custom_call" | custom-call | bytes 1048576 | tf_op jit(solution)/shard_map/assemble/pallas_call | solution.py:366
  (60 shorter events, 18.4 us)
Async XLA Ops:
  2.6 14.9 %collective-permute-start = (bf16[64,2560]{1,0:T(8,128)(2,1)S(1)}, bf16[64,2560]{1,0:T(8,128)(2,1)S(1)}, u32[]{:S(2)}, u32[]{:S(2)}) collective-permute-start(bf16[64,2560]{1,0:T(8,128)(2,1)S(1)} %bitcast.46), channel_id=1, source_target_pairs={{0,0},{1,65},{2,16},{3,81},{4,32},{5,97},{6,48},{7,113},{8,64},{9,... | collective-permute-start | bytes 983048 | tf_op jit(solution)/shard_map/ppermute | solution.py:387
  17.4 14.4 %collective-permute-start.2 = (bf16[64,2560]{1,0:T(8,128)(2,1)S(1)}, bf16[64,2560]{1,0:T(8,128)(2,1)S(1)}, u32[]{:S(2)}, u32[]{:S(2)}) collective-permute-start(bf16[64,2560]{1,0:T(8,128)(2,1)S(1)} %collective-permute-done.refs_0_), channel_id=1, source_target_pairs={{0,1},{1,0},{2,3},{3,2},{4,5},{5,4},{6,7},{7,6},{8,9},{9,8},{10,11... | collective-permute-start | bytes 983048 | tf_op jit(solution)/shard_map/ppermute | solution.py:417
  17.5 32.4 %collective-permute-start.6 = (bf16[480,1280]{1,0:T(8,128)(2,1)S(1)}, bf16[480,1280]{1,0:T(8,128)(2,1)S(1)}, u32[]{:S(2)}, u32[]{:S(2)}) collective-permute-start(bf16[480,1280]{1,0:T(8,128)(2,1)S(1)} %dynamic-slice_bitcast_fusion), channel_id=1, source_target_pairs={{0,128},{1,137},{128,8},{129,1},{8,136},{9,129},{136,0},{137,9},{2... | collective-permute-start | bytes 3686408 | tf_op jit(solution)/shard_map/ppermute | solution.py:391
  20.7 15.2 %collective-permute-start.1 = (bf16[64,2560]{1,0:T(8,128)(2,1)S(1)}, bf16[64,2560]{1,0:T(8,128)(2,1)S(1)}, u32[]{:S(2)}, u32[]{:S(2)}) collective-permute-start(bf16[64,2560]{1,0:T(8,128)(2,1)S(1)} %collective-permute-done.refs_0_), channel_id=1, source_target_pairs={{0,16},{1,113},{16,32},{17,1},{32,48},{33,17},{48,64},{49,33},{64,... | collective-permute-start | bytes 983048 | tf_op jit(solution)/shard_map/ppermute | solution.py:420
  31.9 7.5 %collective-permute-start.3 = (bf16[64,2560]{1,0:T(8,128)(2,1)S(1)}, bf16[64,2560]{1,0:T(8,128)(2,1)S(1)}, u32[]{:S(2)}, u32[]{:S(2)}) collective-permute-start(bf16[64,2560]{1,0:T(8,128)(2,1)S(1)} %collective-permute-done.2), channel_id=1, source_target_pairs={{0,16},{1,113},{16,32},{17,1},{32,48},{33,17},{48,64},{49,33},{64,... | collective-permute-start | bytes 983048 | tf_op jit(solution)/shard_map/ppermute | solution.py:423
  35.9 7.4 %collective-permute-start.4 = (bf16[64,2560]{1,0:T(8,128)(2,1)S(1)}, bf16[64,2560]{1,0:T(8,128)(2,1)S(1)}, u32[]{:S(2)}, u32[]{:S(2)}) collective-permute-start(bf16[64,2560]{1,0:T(8,128)(2,1)S(1)} %collective-permute-done.1.refs_1_), channel_id=1, source_target_pairs={{0,16},{1,113},{16,32},{17,1},{32,48},{33,17},{48,64},{49,33},{64,... | collective-permute-start | bytes 983048 | tf_op jit(solution)/shard_map/ppermute | solution.py:420
  39.4 7.4 %collective-permute-start.5 = (bf16[64,2560]{1,0:T(8,128)(2,1)S(1)}, bf16[64,2560]{1,0:T(8,128)(2,1)S(1)}, u32[]{:S(2)}, u32[]{:S(2)}) collective-permute-start(bf16[64,2560]{1,0:T(8,128)(2,1)S(1)} %collective-permute-done.3.refs_2_), channel_id=1, source_target_pairs={{0,16},{1,113},{16,32},{17,1},{32,48},{33,17},{48,64},{49,33},{64,... | collective-permute-start | bytes 983048 | tf_op jit(solution)/shard_map/ppermute | solution.py:423
  43.3 7.4 %collective-permute-start.7 = (bf16[64,2560]{1,0:T(8,128)(2,1)S(1)}, bf16[64,2560]{1,0:T(8,128)(2,1)S(1)}, u32[]{:S(2)}, u32[]{:S(2)}) collective-permute-start(bf16[64,2560]{1,0:T(8,128)(2,1)S(1)} %collective-permute-done.4.refs_3_), channel_id=1, source_target_pairs={{0,16},{1,113},{16,32},{17,1},{32,48},{33,17},{48,64},{49,33},{64,... | collective-permute-start | bytes 983048 | tf_op jit(solution)/shard_map/ppermute | solution.py:420
  46.8 7.4 %collective-permute-start.8 = (bf16[64,2560]{1,0:T(8,128)(2,1)S(1)}, bf16[64,2560]{1,0:T(8,128)(2,1)S(1)}, u32[]{:S(2)}, u32[]{:S(2)}) collective-permute-start(bf16[64,2560]{1,0:T(8,128)(2,1)S(1)} %collective-permute-done.5.refs_4_), channel_id=1, source_target_pairs={{0,16},{1,113},{16,32},{17,1},{32,48},{33,17},{48,64},{49,33},{64,... | collective-permute-start | bytes 983048 | tf_op jit(solution)/shard_map/ppermute | solution.py:423
  54.3 9.1 %collective-permute-start.10 = (bf16[480,1280]{1,0:T(8,128)(2,1)S(1)}, bf16[480,1280]{1,0:T(8,128)(2,1)S(1)}, u32[]{:S(2)}, u32[]{:S(2)}) collective-permute-start(bf16[480,1280]{1,0:T(8,128)(2,1)S(1)} %collective-permute-done.6.refs_9_), channel_id=1, source_target_pairs={{0,1},{1,0},{2,3},{3,2},{4,5},{5,4},{6,7},{7,6},{8,9},{9,8},{10,11... | collective-permute-start | bytes 3686408 | tf_op jit(solution)/shard_map/ppermute | solution.py:426
  57.2 6.2 %collective-permute-start.9 = (bf16[64,2560]{1,0:T(8,128)(2,1)S(1)}, bf16[64,2560]{1,0:T(8,128)(2,1)S(1)}, u32[]{:S(2)}, u32[]{:S(2)}) collective-permute-start(bf16[64,2560]{1,0:T(8,128)(2,1)S(1)} %collective-permute-done.7.refs_5_), channel_id=1, source_target_pairs={{0,16},{1,113},{16,32},{17,1},{32,48},{33,17},{48,64},{49,33},{64,... | collective-permute-start | bytes 983048 | tf_op jit(solution)/shard_map/ppermute | solution.py:420
  67.3 3.7 %collective-permute-start.12 = (bf16[4,64,640]{2,1,0:T(8,128)(2,1)S(1)}, bf16[4,64,640]{2,1,0:T(8,128)(2,1)S(1)}, u32[]{:S(2)}, u32[]{:S(2)}) collective-permute-start(bf16[4,64,640]{2,1,0:T(8,128)(2,1)S(1)} %get-tuple-element.43), channel_id=1, source_target_pairs={{0,1},{1,0},{2,3},{3,2},{4,5},{5,4},{6,7},{7,6},{8,9},{9,8},{10,11... | collective-permute-start | bytes 983048 | tf_op jit(solution)/shard_map/ppermute | solution.py:431
  69.5 2.9 %collective-permute-start.14 = (bf16[8,64,480]{2,1,0:T(8,128)(2,1)S(1)}, bf16[8,64,480]{2,1,0:T(8,128)(2,1)S(1)}, u32[]{:S(2)}, u32[]{:S(2)}) collective-permute-start(bf16[8,64,480]{2,1,0:T(8,128)(2,1)S(1)} %get-tuple-element.47), channel_id=1, source_target_pairs={{0,1},{1,0},{2,3},{3,2},{4,5},{5,4},{6,7},{7,6},{8,9},{9,8},{10,11... | collective-permute-start | bytes 1474568 | tf_op jit(solution)/shard_map/ppermute | solution.py:432
  69.8 7.8 %collective-permute-start.11 = (bf16[4,64,640]{2,1,0:T(8,128)(2,1)S(1)}, bf16[4,64,640]{2,1,0:T(8,128)(2,1)S(1)}, u32[]{:S(2)}, u32[]{:S(2)}) collective-permute-start(bf16[4,64,640]{2,1,0:T(8,128)(2,1)S(1)} %get-tuple-element.42), channel_id=1, source_target_pairs={{0,2},{2,4},{3,1},{4,6},{5,3},{6,14},{7,5},{14,12},{15,7},{12,10},... | collective-permute-start | bytes 983048 | tf_op jit(solution)/shard_map/ppermute | solution.py:430
  71.1 10.0 %collective-permute-start.13 = (bf16[4,64,640]{2,1,0:T(8,128)(2,1)S(1)}, bf16[4,64,640]{2,1,0:T(8,128)(2,1)S(1)}, u32[]{:S(2)}, u32[]{:S(2)}) collective-permute-start(bf16[4,64,640]{2,1,0:T(8,128)(2,1)S(1)} %collective-permute-done.12), channel_id=1, source_target_pairs={{0,2},{2,4},{3,1},{4,6},{5,3},{6,14},{7,5},{14,12},{15,7},{12,10},... | collective-permute-start | bytes 983048 | tf_op jit(solution)/shard_map/ppermute | solution.py:431
  85.5 7.5 %collective-permute-start.17 = (bf16[4,2,8,1280]{3,2,1,0:T(8,128)(2,1)S(1)}, bf16[4,2,8,1280]{3,2,1,0:T(8,128)(2,1)S(1)}, u32[]{:S(2)}, u32[]{:S(2)}) collective-permute-start(bf16[4,2,8,1280]{3,2,1,0:T(8,128)(2,1)S(1)} %get-tuple-element.58), channel_id=1, source_target_pairs={{0,0},{1,128},{8,8},{9,136},{128,1},{129,129},{136,9},{137,137},{2... | collective-permute-start | bytes 491528 | tf_op jit(solution)/shard_map/ppermute | solution.py:438
  89.0 6.0 %collective-permute-start.18 = (bf16[4,2,8,1280]{3,2,1,0:T(8,128)(2,1)S(1)}, bf16[4,2,8,1280]{3,2,1,0:T(8,128)(2,1)S(1)}, u32[]{:S(2)}, u32[]{:S(2)}) collective-permute-start(bf16[4,2,8,1280]{3,2,1,0:T(8,128)(2,1)S(1)} %get-tuple-element.59), channel_id=1, source_target_pairs={{0,8},{1,136},{8,0},{9,128},{128,9},{129,137},{136,1},{137,129},{2... | collective-permute-start | bytes 491528 | tf_op jit(solution)/shard_map/ppermute | solution.py:438
  95.1 6.6 %collective-permute-start.19 = (bf16[2,2,8,1280]{3,2,1,0:T(8,128)(2,1)S(1)}, bf16[2,2,8,1280]{3,2,1,0:T(8,128)(2,1)S(1)}, u32[]{:S(2)}, u32[]{:S(2)}) collective-permute-start(bf16[2,2,8,1280]{3,2,1,0:T(8,128)(2,1)S(1)} %get-tuple-element.60), channel_id=1, source_target_pairs={{0,2},{2,0},{4,6},{6,4},{1,3},{3,1},{5,7},{7,5},{8,10},{10,8},{12,... | collective-permute-start | bytes 245768 | tf_op jit(solution)/shard_map/ppermute | solution.py:441
  96.1 9.8 %collective-permute-start.20 = (bf16[2,2,8,1280]{3,2,1,0:T(8,128)(2,1)S(1)}, bf16[2,2,8,1280]{3,2,1,0:T(8,128)(2,1)S(1)}, u32[]{:S(2)}, u32[]{:S(2)}) collective-permute-start(bf16[2,2,8,1280]{3,2,1,0:T(8,128)(2,1)S(1)} %get-tuple-element.61), channel_id=1, source_target_pairs={{0,4},{2,6},{4,0},{6,2},{1,5},{3,7},{5,1},{7,3},{8,12},{10,14},{12... | collective-permute-start | bytes 245768 | tf_op jit(solution)/shard_map/ppermute | solution.py:441
  101.2 6.4 %collective-permute-start.21 = (bf16[2,2,8,1280]{3,2,1,0:T(8,128)(2,1)S(1)}, bf16[2,2,8,1280]{3,2,1,0:T(8,128)(2,1)S(1)}, u32[]{:S(2)}, u32[]{:S(2)}) collective-permute-start(bf16[2,2,8,1280]{3,2,1,0:T(8,128)(2,1)S(1)} %get-tuple-element.62), channel_id=1, source_target_pairs={{0,6},{2,4},{4,2},{6,0},{1,7},{3,5},{5,3},{7,1},{8,14},{10,12},{12... | collective-permute-start | bytes 245768 | tf_op jit(solution)/shard_map/ppermute | solution.py:441
  101.2 7.8 %collective-permute-start.22 = (bf16[4,2,8,1280]{3,2,1,0:T(8,128)(2,1)S(1)}, bf16[4,2,8,1280]{3,2,1,0:T(8,128)(2,1)S(1)}, u32[]{:S(2)}, u32[]{:S(2)}) collective-permute-start(bf16[4,2,8,1280]{3,2,1,0:T(8,128)(2,1)S(1)} %collective-permute-done.17.near.refs_0_), channel_id=1, source_target_pairs={{0,1},{1,0},{2,3},{3,2},{4,5},{5,4},{6,7},{7,6},{8,9},{9,8},{10,11... | collective-permute-start | bytes 491528 | tf_op jit(solution)/shard_map/ppermute | solution.py:442
  101.2 7.7 %collective-permute-start.23 = (bf16[4,2,8,1280]{3,2,1,0:T(8,128)(2,1)S(1)}, bf16[4,2,8,1280]{3,2,1,0:T(8,128)(2,1)S(1)}, u32[]{:S(2)}, u32[]{:S(2)}) collective-permute-start(bf16[4,2,8,1280]{3,2,1,0:T(8,128)(2,1)S(1)} %collective-permute-done.18.far.refs_1_), channel_id=1, source_target_pairs={{0,1},{1,0},{2,3},{3,2},{4,5},{5,4},{6,7},{7,6},{8,9},{9,8},{10,11... | collective-permute-start | bytes 491528 | tf_op jit(solution)/shard_map/ppermute | solution.py:442
  101.7 6.4 %collective-permute-start.24 = (bf16[2,2,8,1280]{3,2,1,0:T(8,128)(2,1)S(1)}, bf16[2,2,8,1280]{3,2,1,0:T(8,128)(2,1)S(1)}, u32[]{:S(2)}, u32[]{:S(2)}) collective-permute-start(bf16[2,2,8,1280]{3,2,1,0:T(8,128)(2,1)S(1)} %collective-permute-done.19.refs_2_), channel_id=1, source_target_pairs={{0,1},{1,0},{2,3},{3,2},{4,5},{5,4},{6,7},{7,6},{8,9},{9,8},{10,11... | collective-permute-start | bytes 245768 | tf_op jit(solution)/shard_map/ppermute | solution.py:442
  105.9 2.2 %collective-permute-start.25 = (bf16[2,2,8,1280]{3,2,1,0:T(8,128)(2,1)S(1)}, bf16[2,2,8,1280]{3,2,1,0:T(8,128)(2,1)S(1)}, u32[]{:S(2)}, u32[]{:S(2)}) collective-permute-start(bf16[2,2,8,1280]{3,2,1,0:T(8,128)(2,1)S(1)} %collective-permute-done.20.refs_3_), channel_id=1, source_target_pairs={{0,1},{1,0},{2,3},{3,2},{4,5},{5,4},{6,7},{7,6},{8,9},{9,8},{10,11... | collective-permute-start | bytes 245768 | tf_op jit(solution)/shard_map/ppermute | solution.py:442
  (8 other events, 74.6 us)

commit v8 on v7

--- a/solution.py
+++ b/solution.py
@@ -56,12 +56,12 @@
     return pairs
 
 
-def ring_perm():
+def ring_perm(cross=0):
     pairs = []
     for z in range(8):
         for core in range(2):
             there = (z + 1 - 2 * core) % 8
-            pairs.append((flat((z, 8), (core, 2)), flat((there, 8), (core, 2))))
+            pairs.append((flat((z, 8), (core ^ cross, 2)), flat((there, 8), (core, 2))))
     return pairs
 
 
@@ -114,16 +114,12 @@
 
 
 def project_kernel(flags, *refs):
-    pieces, (own, mine, theirs), (keep, send, edge, give, x_ref) = refs[:8], refs[8:11], refs[11:]
+    pieces, (own, partner), (keep, send, edge, give, x_ref) = refs[:8], refs[8:10], refs[10:]
     for g, piece in enumerate(pieces):
         x_ref[64 * g : 64 * (g + 1), :] = piece[...]
-    width = mine.shape[1]
-    near = pl.ds(pl.multiple_of(flags[1] * width, width), width)
-    far = pl.ds(pl.multiple_of((1 - flags[1]) * width, width), width)
     p = lax.dot_general(x_ref[...], own[...], NT, preferred_element_type=jnp.float32)
     own_rows = normalized(p)
-    p = lax.dot_general(x_ref[:, near], mine[...], NT, preferred_element_type=jnp.float32)
-    p += lax.dot_general(x_ref[:, far], theirs[...], NT, preferred_element_type=jnp.float32)
+    p = lax.dot_general(x_ref[...], partner[...], NT, preferred_element_type=jnp.float32)
     other_rows = normalized(p)
 
     def store(first, second):
@@ -153,13 +149,13 @@
         store_edges(edge, give)
 
 
-def project(flags, pieces, own, mine, theirs):
+def project(flags, pieces, own, partner):
     whole = jax.ShapeDtypeStruct((ROWS, HALF, QKV), jnp.bfloat16)
     part = jax.ShapeDtypeStruct((WIN, HALF, 4 * HEAD_DIM), jnp.bfloat16)
     return pl.pallas_call(
         project_kernel,
         out_shape=[whole, whole, part, part],
-        in_specs=[SMEM] + [VMEM] * 11,
+        in_specs=[SMEM] + [VMEM] * 10,
         out_specs=[VMEM] * 4,
         scratch_shapes=[pltpu.VMEM((512, own.shape[1]), jnp.bfloat16)],
         compiler_params=pltpu.CompilerParams(vmem_limit_bytes=20 * MIB),
@@ -167,7 +163,7 @@
             flops=2 * 512 * 960 * 2560, bytes_accessed=8 * MIB, transcendentals=0
         ),
         name="project",
-    )(flags, *pieces, own, mine, theirs)
+    )(flags, *pieces, own, partner)
 
 
 def put(ks, vs, first, key, value):
@@ -384,11 +380,10 @@
     wide = tokens.astype(jnp.float32)
     normed = wide * lax.rsqrt(jnp.mean(wide * wide, axis=-1, keepdims=True) + EPS)
     normed = jnp.transpose(normed.astype(jnp.bfloat16), (1, 0, 2)).reshape(64, model)
+    normed, own = lax.optimization_barrier((normed, w_qkv[0]))
     first = lax.ppermute(normed, AXES, spread_perm())
 
-    own = w_qkv[0]
-    half = lax.dynamic_slice_in_dim(own, core * (model // 2), model // 2, 1)
-    mine = lax.ppermute(half, ("y_lo", "y_hi", "core"), weight_perm())
+    partner = lax.ppermute(own, ("y_lo", "y_hi", "core"), weight_perm())
 
     base = (z - 2 * block) & 7
     padded = jnp.pad(key_mask, ((0, 0), (WIN, WIN)))
@@ -414,19 +409,17 @@
         (first, usable, band, ints, factor, at, flags)
     )
 
-    a, b = first, lax.ppermute(first, "core", SWAP)
+    a = b = first
     pieces = [first]
     for k in range(1, 5):
         a = lax.ppermute(a, ("z", "core"), ring_perm())
         pieces.append(a)
         if k < 4:
-            b = lax.ppermute(b, ("z", "core"), ring_perm())
+            b = lax.ppermute(b, ("z", "core"), ring_perm(cross=int(k == 1)))
             pieces.append(b)
-    mine, *pieces[5:7] = lax.optimization_barrier((mine, *pieces[5:7]))
-    theirs = lax.ppermute(mine, "core", SWAP)
 
     corners = ("y_lo", "y_hi", "x", "core")
-    keep, send, edge, give = project(flags, pieces, own, mine, theirs)
+    keep, send, edge, give = project(flags, pieces, own, partner)
     halo_own = lax.ppermute(edge, corners, neighbour_perm())
     halo_oth = lax.ppermute(lax.ppermute(give, "core", SWAP), corners, neighbour_perm())
     parts = keep, lax.ppermute(send, "core", SWAP)

time: 110 us -> 116 us (1.055)
  waiting for transfers between devices: 32.2 us -> 34.4 us
  local copies, waits for them, and re-layouts: 2.42 us -> 4.6 us
  Pallas kernels: 10.9 us -> 12.1 us
    ppermute x2, starting transfers between devices: 0.51 us -> 8.15 us  [body(): lax.ppermute(halo, 'core', SWAP)]
    ppermute x6 -> x4, starting transfers between devices: 13.4 us -> 7.31 us  [the longest x3 3.67 us: body(): b = lax.ppermute(b, ('z', 'core'), ring_perm(cross=int(k == 1)))]
    ppermute x2, starting transfers between devices: 6.17 us -> 2.01 us  [body(): lax.ppermute(chunks[k], ('y_lo', 'y_hi', 'core'), return_perm(k))]
    ppermute x1, starting transfers between devices: 2.17 us -> 6.19 us  [body(): lax.ppermute(give, 'core', SWAP)]
    ppermute x4, waiting for transfers between devices: 10.6 us -> 14.6 us  [body(): a = lax.ppermute(a, ('z', 'core'), ring_perm())]
    ppermute x2, waiting for transfers between devices: 3.41 us -> 7 us  [body(): lax.ppermute(chunks[k], ('y_lo', 'y_hi', 'core'), return_perm(k))]
    ppermute x6 -> x4, waiting for transfers between devices: 3.72 us -> 0.79 us  [the longest x3 0.79 us: body(): b = lax.ppermute(b, ('z', 'core'), ring_perm(cross=int(k == 1)))]
    ppermute x3, starting transfers between devices: 6.08 us -> 4.78 us  [body(): lax.ppermute(part, 'x', perm)]
  transfers between devices with their start and end apart: 27 -> 25, of which waited for: 17 -> 15; matrix products, arithmetic and copies ran while one was open for 2% -> 4% of each run, Pallas kernels for 3% -> 3%
where the time goes in v8:
time: 116 us; the launch traced here: 115 us
  starting transfers between devices  60.1 us (52%)
  waiting for transfers between devices  34.4 us (30%)
  Pallas kernels  12.1 us (10%)
  local copies, waits for them, and re-layouts  4.6 us (4%)
  other arithmetic  2.55 us (2%)
  between operations  1.71 us (1%)
    ppermute x4, starting transfers between devices, body(): a = lax.ppermute(a, ('z', 'core'), ring_perm())  18.7 us
    ppermute x4, waiting for transfers between devices, body(): a = lax.ppermute(a, ('z', 'core'), ring_perm())  14.6 us
    ppermute x1, starting transfers between devices, body(): first = lax.ppermute(normed, AXES, spread_perm())  8.81 us
    ppermute x2, starting transfers between devices, body(): lax.ppermute(halo, 'core', SWAP)  8.15 us
    ppermute x2, waiting for transfers between devices, body(): lax.ppermute(chunks[k], ('y_lo', 'y_hi', 'core'), return_perm(k))  7 us
    ppermute x1, starting transfers between devices, body(): lax.ppermute(give, 'core', SWAP)  6.19 us
    pallas_call x1, Pallas kernels, project(): pl.pallas_call(project_kernel, out_shape=[whole, whole, part, part], in_s...  5.09 us
    ppermute x3, starting transfers between devices, body(): lax.ppermute(part, 'x', perm)  4.78 us
  transfers between devices with their start and end apart: 25, of which 15 were waited for; matrix products, arithmetic and copies ran while one was open for 4% of the time, Pallas kernels for 3%

profile of v8, /device:TPU:1, one launch (start us, length us, event | category | flops | bytes accessed | tf_op | source)
XLA Modules:
  0.0 115.4 jit_solution(5847096043707104946)
XLA Ops:
  2.5 3.6 %collective-permute-start.8 = (bf16[480,2560]{1,0:T(8,128)(2,1)}, bf16[480,2560]{1,0:T(8,128)(2,1)}, u32[]{:S(2)}, u32[]{:S(2)}) collective-permute-start(bf16[480,2560]{1,0:T(8,128)(2,1)} %bitcast.43), channel_id=1, source_target_pairs={{0,128},{1,137},{128,8},{129,1},{8,136},{9,129},{136,0},{137,9},{2... | collective-permute-start | bytes 7372808 | tf_op jit(solution)/shard_map/ppermute | solution.py:386
  6.2 8.8 %collective-permute-start = (bf16[64,2560]{1,0:T(8,128)(2,1)S(1)}, bf16[64,2560]{1,0:T(8,128)(2,1)S(1)}, u32[]{:S(2)}, u32[]{:S(2)}) collective-permute-start(bf16[64,2560]{1,0:T(8,128)(2,1)S(1)} %bitcast.45), channel_id=1, source_target_pairs={{0,0},{1,65},{2,16},{3,81},{4,32},{5,97},{6,48},{7,113},{8,64},{9,... | collective-permute-start | bytes 983048 | tf_op jit(solution)/shard_map/ppermute | solution.py:384
  21.2 8.9 %collective-permute-start.1 = (bf16[64,2560]{1,0:T(8,128)(2,1)S(1)}, bf16[64,2560]{1,0:T(8,128)(2,1)S(1)}, u32[]{:S(2)}, u32[]{:S(2)}) collective-permute-start(bf16[64,2560]{1,0:T(8,128)(2,1)S(1)} %collective-permute-done.refs_0_), channel_id=1, source_target_pairs={{0,16},{1,113},{16,32},{17,1},{32,48},{33,17},{48,64},{49,33},{64,... | collective-permute-start | bytes 983048 | tf_op jit(solution)/shard_map/ppermute | solution.py:415
  30.2 7.0 %collective-permute-done.1.refs_1_ = bf16[64,2560]{1,0:T(8,128)(2,1)S(1)} collective-permute-done((bf16[64,2560]{1,0:T(8,128)(2,1)S(1)}, bf16[64,2560]{1,0:T(8,128)(2,1)S(1)}, u32[]{:S(2)}, u32[]{:S(2)}) %collective-permute-start.1) | collective-permute-done | bytes 327712 | tf_op jit(solution)/shard_map/ppermute | solution.py:415
  37.1 3.5 %collective-permute-start.3 = (bf16[64,2560]{1,0:T(8,128)(2,1)S(1)}, bf16[64,2560]{1,0:T(8,128)(2,1)S(1)}, u32[]{:S(2)}, u32[]{:S(2)}) collective-permute-start(bf16[64,2560]{1,0:T(8,128)(2,1)S(1)} %collective-permute-done.1.refs_1_), channel_id=1, source_target_pairs={{0,16},{1,113},{16,32},{17,1},{32,48},{33,17},{48,64},{49,33},{64,... | collective-permute-start | bytes 983048 | tf_op jit(solution)/shard_map/ppermute | solution.py:415
  41.2 3.5 %collective-permute-done.3.refs_3_ = bf16[64,2560]{1,0:T(8,128)(2,1)S(1)} collective-permute-done((bf16[64,2560]{1,0:T(8,128)(2,1)S(1)}, bf16[64,2560]{1,0:T(8,128)(2,1)S(1)}, u32[]{:S(2)}, u32[]{:S(2)}) %collective-permute-start.3) | collective-permute-done | bytes 327712 | tf_op jit(solution)/shard_map/ppermute | solution.py:415
  44.7 3.1 %collective-permute-start.5 = (bf16[64,2560]{1,0:T(8,128)(2,1)S(1)}, bf16[64,2560]{1,0:T(8,128)(2,1)S(1)}, u32[]{:S(2)}, u32[]{:S(2)}) collective-permute-start(bf16[64,2560]{1,0:T(8,128)(2,1)S(1)} %collective-permute-done.3.refs_3_), channel_id=1, source_target_pairs={{0,16},{1,113},{16,32},{17,1},{32,48},{33,17},{48,64},{49,33},{64,... | collective-permute-start | bytes 983048 | tf_op jit(solution)/shard_map/ppermute | solution.py:415
  48.2 3.1 %collective-permute-start.6 = (bf16[64,2560]{1,0:T(8,128)(2,1)S(1)}, bf16[64,2560]{1,0:T(8,128)(2,1)S(1)}, u32[]{:S(2)}, u32[]{:S(2)}) collective-permute-start(bf16[64,2560]{1,0:T(8,128)(2,1)S(1)} %collective-permute-done.4.refs_4_), channel_id=1, source_target_pairs={{0,16},{1,113},{16,32},{17,1},{32,48},{33,17},{48,64},{49,33},{64,... | collective-permute-start | bytes 983048 | tf_op jit(solution)/shard_map/ppermute | solution.py:418
  51.8 3.1 %collective-permute-start.7 = (bf16[64,2560]{1,0:T(8,128)(2,1)S(1)}, bf16[64,2560]{1,0:T(8,128)(2,1)S(1)}, u32[]{:S(2)}, u32[]{:S(2)}) collective-permute-start(bf16[64,2560]{1,0:T(8,128)(2,1)S(1)} %collective-permute-done.5.refs_5_), channel_id=1, source_target_pairs={{0,16},{1,113},{16,32},{17,1},{32,48},{33,17},{48,64},{49,33},{64,... | collective-permute-start | bytes 983048 | tf_op jit(solution)/shard_map/ppermute | solution.py:415
  55.3 3.6 %collective-permute-done.7.refs_7_ = bf16[64,2560]{1,0:T(8,128)(2,1)S(1)} collective-permute-done((bf16[64,2560]{1,0:T(8,128)(2,1)S(1)}, bf16[64,2560]{1,0:T(8,128)(2,1)S(1)}, u32[]{:S(2)}, u32[]{:S(2)}) %collective-permute-start.7) | collective-permute-done | bytes 327712 | tf_op jit(solution)/shard_map/ppermute | solution.py:415
  59.0 5.1 %project.1 = (bf16[8,64,480]{2,1,0:T(8,128)(2,1)S(1)}, bf16[8,64,480]{2,1,0:T(8,128)(2,1)S(1)}, bf16[4,64,640]{2,1,0:T(8,128)(2,1)S(1)}, bf16[4,64,640]{2,1,0:T(8,128)(2,1)S(1)}) custom-call(s32[2]{0:T(128)S(1)} %pad_add_fusion.flags, bf16[64,2560]{1,0:T(8,128)(2,1)S(1)} %collective-permute-done.refs_0_, ...), custom_call_target="tpu_custom_call" | custom-call | flops 2516582400 | bytes 8388608 | tf_op jit(solution)/shard_map/project/pallas_call | solution.py:155
  64.1 6.2 %collective-permute-start.10 = (bf16[4,64,640]{2,1,0:T(8,128)(2,1)S(1)}, bf16[4,64,640]{2,1,0:T(8,128)(2,1)S(1)}, u32[]{:S(2)}, u32[]{:S(2)}) collective-permute-start(bf16[4,64,640]{2,1,0:T(8,128)(2,1)S(1)} %get-tuple-element.41), channel_id=1, source_target_pairs={{0,1},{1,0},{2,3},{3,2},{4,5},{5,4},{6,7},{7,6},{8,9},{9,8},{10,11... | collective-permute-start | bytes 983048 | tf_op jit(solution)/shard_map/ppermute | solution.py:424
  73.1 3.4 %inner.1 = (bf16[8,128,160]{2,1,0:T(8,128)(2,1)S(1)}, f32[8,128,256]{2,1,0:T(8,128)S(1)}, f32[10,128,128]{2,1,0:T(8,128)S(1)}, f32[2,16,128]{2,1,0:T(8,128)S(1)}) custom-call(s32[19]{0:T(128)S(1)} %stack.137.ints, f32[1]{0:T(128)S(6)} %mul.258.factor_ref, f32[64]{0:T(128)S(1)} %reshape.20.band, f32[16,128]{1,0:T(8,128)S(1)} %fusion.4.usable, ...), custom_call_target="tpu_custom_call" | custom-call | flops 10000000 | bytes 100000 | tf_op jit(solution)/shard_map/inner/pallas_call | solution.py:258
  76.5 1.6 %collective-permute-done.9.refs_2_ = bf16[4,64,640]{2,1,0:T(8,128)(2,1)S(1)} collective-permute-done((bf16[4,64,640]{2,1,0:T(8,128)(2,1)S(1)}, bf16[4,64,640]{2,1,0:T(8,128)(2,1)S(1)}, u32[]{:S(2)}, u32[]{:S(2)}) %collective-permute-start.9) | collective-permute-done | bytes 327712 | tf_op jit(solution)/shard_map/ppermute | solution.py:423
  78.2 3.5 %collective-permute-done.11.refs_3_ = bf16[4,64,640]{2,1,0:T(8,128)(2,1)S(1)} collective-permute-done((bf16[4,64,640]{2,1,0:T(8,128)(2,1)S(1)}, bf16[4,64,640]{2,1,0:T(8,128)(2,1)S(1)}, u32[]{:S(2)}, u32[]{:S(2)}) %collective-permute-start.11) | collective-permute-done | bytes 327712 | tf_op jit(solution)/shard_map/ppermute | solution.py:424
  81.7 8.1 %collective-permute-start.13 = (bf16[4,64,640]{2,1,0:T(8,128)(2,1)S(1)}, bf16[4,64,640]{2,1,0:T(8,128)(2,1)S(1)}, u32[]{:S(2)}, u32[]{:S(2)}) collective-permute-start(bf16[4,64,640]{2,1,0:T(8,128)(2,1)S(1)} %collective-permute-done.9.refs_2_), channel_id=1, source_target_pairs={{0,1},{1,0},{2,3},{3,2},{4,5},{5,4},{6,7},{7,6},{8,9},{9,8},{10,11... | collective-permute-start | bytes 983048 | tf_op jit(solution)/shard_map/ppermute | solution.py:428
  91.5 2.3 %outer.1 = (bf16[4,2,8,1280]{3,2,1,0:T(8,128)(2,1)S(1)}, bf16[4,2,8,1280]{3,2,1,0:T(8,128)(2,1)S(1)}) custom-call(s32[19]{0:T(128)S(1)} %stack.137.ints, f32[1]{0:T(128)S(6)} %mul.258.factor_ref, bf16[8,128,160]{2,1,0:T(8,128)(2,1)S(1)} %get-tuple-element.50.zonal_ref, f32[8,128,256]{2,1,0:T(8,128)S(1)} %get-tuple-element.51.window_ref, ...), custom_call_target="tpu_custom_call" | custom-call | flops 1000000000 | bytes 4194304 | tf_op jit(solution)/shard_map/outer/pallas_call | solution.py:314
  93.8 1.9 %collective-permute-start.15 = (bf16[4,2,8,1280]{3,2,1,0:T(8,128)(2,1)S(1)}, bf16[4,2,8,1280]{3,2,1,0:T(8,128)(2,1)S(1)}, u32[]{:S(2)}, u32[]{:S(2)}) collective-permute-start(bf16[4,2,8,1280]{3,2,1,0:T(8,128)(2,1)S(1)} %get-tuple-element.56), channel_id=1, source_target_pairs={{0,0},{1,128},{8,8},{9,136},{128,1},{129,129},{136,9},{137,137},{2... | collective-permute-start | bytes 491528 | tf_op jit(solution)/shard_map/ppermute | solution.py:431
  95.8 4.9 %collective-permute-done.15.near.refs_0_ = bf16[4,2,8,1280]{3,2,1,0:T(8,128)(2,1)S(1)} collective-permute-done((bf16[4,2,8,1280]{3,2,1,0:T(8,128)(2,1)S(1)}, bf16[4,2,8,1280]{3,2,1,0:T(8,128)(2,1)S(1)}, u32[]{:S(2)}, u32[]{:S(2)}) %collective-permute-start.15) | collective-permute-done | bytes 163872 | tf_op jit(solution)/shard_map/ppermute | solution.py:431
  100.7 2.1 %collective-permute-done.16.far.refs_1_ = bf16[4,2,8,1280]{3,2,1,0:T(8,128)(2,1)S(1)} collective-permute-done((bf16[4,2,8,1280]{3,2,1,0:T(8,128)(2,1)S(1)}, bf16[4,2,8,1280]{3,2,1,0:T(8,128)(2,1)S(1)}, u32[]{:S(2)}, u32[]{:S(2)}) %collective-permute-start.16) | collective-permute-done | bytes 163872 | tf_op jit(solution)/shard_map/ppermute | solution.py:431
  102.9 2.3 %collective-permute-start.17 = (bf16[2,2,8,1280]{3,2,1,0:T(8,128)(2,1)S(1)}, bf16[2,2,8,1280]{3,2,1,0:T(8,128)(2,1)S(1)}, u32[]{:S(2)}, u32[]{:S(2)}) collective-permute-start(bf16[2,2,8,1280]{3,2,1,0:T(8,128)(2,1)S(1)} %get-tuple-element.58), channel_id=1, source_target_pairs={{0,2},{2,0},{4,6},{6,4},{1,3},{3,1},{5,7},{7,5},{8,10},{10,8},{12,... | collective-permute-start | bytes 245768 | tf_op jit(solution)/shard_map/ppermute | solution.py:434
  105.1 1.7 %collective-permute-start.18 = (bf16[2,2,8,1280]{3,2,1,0:T(8,128)(2,1)S(1)}, bf16[2,2,8,1280]{3,2,1,0:T(8,128)(2,1)S(1)}, u32[]{:S(2)}, u32[]{:S(2)}) collective-permute-start(bf16[2,2,8,1280]{3,2,1,0:T(8,128)(2,1)S(1)} %get-tuple-element.59), channel_id=1, source_target_pairs={{0,4},{2,6},{4,0},{6,2},{1,5},{3,7},{5,1},{7,3},{8,12},{10,14},{12... | collective-permute-start | bytes 245768 | tf_op jit(solution)/shard_map/ppermute | solution.py:434
  108.2 2.7 %collective-permute-done.18.refs_3_ = bf16[2,2,8,1280]{3,2,1,0:T(8,128)(2,1)S(1)} collective-permute-done((bf16[2,2,8,1280]{3,2,1,0:T(8,128)(2,1)S(1)}, bf16[2,2,8,1280]{3,2,1,0:T(8,128)(2,1)S(1)}, u32[]{:S(2)}, u32[]{:S(2)}) %collective-permute-start.18) | collective-permute-done | bytes 81952 | tf_op jit(solution)/shard_map/ppermute | solution.py:434
  111.3 1.5 %collective-permute-done.19.refs_4_ = bf16[2,2,8,1280]{3,2,1,0:T(8,128)(2,1)S(1)} collective-permute-done((bf16[2,2,8,1280]{3,2,1,0:T(8,128)(2,1)S(1)}, bf16[2,2,8,1280]{3,2,1,0:T(8,128)(2,1)S(1)}, u32[]{:S(2)}, u32[]{:S(2)}) %collective-permute-start.19) | collective-permute-done | bytes 81952 | tf_op jit(solution)/shard_map/ppermute | solution.py:434
  (49 shorter events, 18.0 us)
Async XLA Ops:
  2.5 56.5 %collective-permute-start.8 = (bf16[480,2560]{1,0:T(8,128)(2,1)}, bf16[480,2560]{1,0:T(8,128)(2,1)}, u32[]{:S(2)}, u32[]{:S(2)}) collective-permute-start(bf16[480,2560]{1,0:T(8,128)(2,1)} %bitcast.43), channel_id=1, source_target_pairs={{0,128},{1,137},{128,8},{129,1},{8,136},{9,129},{136,0},{137,9},{2... | collective-permute-start | bytes 7372808 | tf_op jit(solution)/shard_map/ppermute | solution.py:386
  6.2 15.1 %collective-permute-start = (bf16[64,2560]{1,0:T(8,128)(2,1)S(1)}, bf16[64,2560]{1,0:T(8,128)(2,1)S(1)}, u32[]{:S(2)}, u32[]{:S(2)}) collective-permute-start(bf16[64,2560]{1,0:T(8,128)(2,1)S(1)} %bitcast.45), channel_id=1, source_target_pairs={{0,0},{1,65},{2,16},{3,81},{4,32},{5,97},{6,48},{7,113},{8,64},{9,... | collective-permute-start | bytes 983048 | tf_op jit(solution)/shard_map/ppermute | solution.py:384
  21.2 15.9 %collective-permute-start.1 = (bf16[64,2560]{1,0:T(8,128)(2,1)S(1)}, bf16[64,2560]{1,0:T(8,128)(2,1)S(1)}, u32[]{:S(2)}, u32[]{:S(2)}) collective-permute-start(bf16[64,2560]{1,0:T(8,128)(2,1)S(1)} %collective-permute-done.refs_0_), channel_id=1, source_target_pairs={{0,16},{1,113},{16,32},{17,1},{32,48},{33,17},{48,64},{49,33},{64,... | collective-permute-start | bytes 983048 | tf_op jit(solution)/shard_map/ppermute | solution.py:415
  30.2 10.5 %collective-permute-start.2 = (bf16[64,2560]{1,0:T(8,128)(2,1)S(1)}, bf16[64,2560]{1,0:T(8,128)(2,1)S(1)}, u32[]{:S(2)}, u32[]{:S(2)}) collective-permute-start(bf16[64,2560]{1,0:T(8,128)(2,1)S(1)} %collective-permute-done.refs_0_), channel_id=1, source_target_pairs={{1,16},{0,113},{17,32},{16,1},{33,48},{32,17},{49,64},{48,33},{65,... | collective-permute-start | bytes 983048 | tf_op jit(solution)/shard_map/ppermute | solution.py:418
  37.1 7.5 %collective-permute-start.3 = (bf16[64,2560]{1,0:T(8,128)(2,1)S(1)}, bf16[64,2560]{1,0:T(8,128)(2,1)S(1)}, u32[]{:S(2)}, u32[]{:S(2)}) collective-permute-start(bf16[64,2560]{1,0:T(8,128)(2,1)S(1)} %collective-permute-done.1.refs_1_), channel_id=1, source_target_pairs={{0,16},{1,113},{16,32},{17,1},{32,48},{33,17},{48,64},{49,33},{64,... | collective-permute-start | bytes 983048 | tf_op jit(solution)/shard_map/ppermute | solution.py:415
  40.7 7.5 %collective-permute-start.4 = (bf16[64,2560]{1,0:T(8,128)(2,1)S(1)}, bf16[64,2560]{1,0:T(8,128)(2,1)S(1)}, u32[]{:S(2)}, u32[]{:S(2)}) collective-permute-start(bf16[64,2560]{1,0:T(8,128)(2,1)S(1)} %collective-permute-done.2.refs_2_), channel_id=1, source_target_pairs={{0,16},{1,113},{16,32},{17,1},{32,48},{33,17},{48,64},{49,33},{64,... | collective-permute-start | bytes 983048 | tf_op jit(solution)/shard_map/ppermute | solution.py:418
  44.7 7.1 %collective-permute-start.5 = (bf16[64,2560]{1,0:T(8,128)(2,1)S(1)}, bf16[64,2560]{1,0:T(8,128)(2,1)S(1)}, u32[]{:S(2)}, u32[]{:S(2)}) collective-permute-start(bf16[64,2560]{1,0:T(8,128)(2,1)S(1)} %collective-permute-done.3.refs_3_), channel_id=1, source_target_pairs={{0,16},{1,113},{16,32},{17,1},{32,48},{33,17},{48,64},{49,33},{64,... | collective-permute-start | bytes 983048 | tf_op jit(solution)/shard_map/ppermute | solution.py:415
  48.2 7.1 %collective-permute-start.6 = (bf16[64,2560]{1,0:T(8,128)(2,1)S(1)}, bf16[64,2560]{1,0:T(8,128)(2,1)S(1)}, u32[]{:S(2)}, u32[]{:S(2)}) collective-permute-start(bf16[64,2560]{1,0:T(8,128)(2,1)S(1)} %collective-permute-done.4.refs_4_), channel_id=1, source_target_pairs={{0,16},{1,113},{16,32},{17,1},{32,48},{33,17},{48,64},{49,33},{64,... | collective-permute-start | bytes 983048 | tf_op jit(solution)/shard_map/ppermute | solution.py:418
  51.8 7.1 %collective-permute-start.7 = (bf16[64,2560]{1,0:T(8,128)(2,1)S(1)}, bf16[64,2560]{1,0:T(8,128)(2,1)S(1)}, u32[]{:S(2)}, u32[]{:S(2)}) collective-permute-start(bf16[64,2560]{1,0:T(8,128)(2,1)S(1)} %collective-permute-done.5.refs_5_), channel_id=1, source_target_pairs={{0,16},{1,113},{16,32},{17,1},{32,48},{33,17},{48,64},{49,33},{64,... | collective-permute-start | bytes 983048 | tf_op jit(solution)/shard_map/ppermute | solution.py:415
  64.1 7.6 %collective-permute-start.10 = (bf16[4,64,640]{2,1,0:T(8,128)(2,1)S(1)}, bf16[4,64,640]{2,1,0:T(8,128)(2,1)S(1)}, u32[]{:S(2)}, u32[]{:S(2)}) collective-permute-start(bf16[4,64,640]{2,1,0:T(8,128)(2,1)S(1)} %get-tuple-element.41), channel_id=1, source_target_pairs={{0,1},{1,0},{2,3},{3,2},{4,5},{5,4},{6,7},{7,6},{8,9},{9,8},{10,11... | collective-permute-start | bytes 983048 | tf_op jit(solution)/shard_map/ppermute | solution.py:424
  70.3 2.9 %collective-permute-start.12 = (bf16[8,64,480]{2,1,0:T(8,128)(2,1)S(1)}, bf16[8,64,480]{2,1,0:T(8,128)(2,1)S(1)}, u32[]{:S(2)}, u32[]{:S(2)}) collective-permute-start(bf16[8,64,480]{2,1,0:T(8,128)(2,1)S(1)} %get-tuple-element.45), channel_id=1, source_target_pairs={{0,1},{1,0},{2,3},{3,2},{4,5},{5,4},{6,7},{7,6},{8,9},{9,8},{10,11... | collective-permute-start | bytes 1474568 | tf_op jit(solution)/shard_map/ppermute | solution.py:425
  70.4 7.8 %collective-permute-start.9 = (bf16[4,64,640]{2,1,0:T(8,128)(2,1)S(1)}, bf16[4,64,640]{2,1,0:T(8,128)(2,1)S(1)}, u32[]{:S(2)}, u32[]{:S(2)}) collective-permute-start(bf16[4,64,640]{2,1,0:T(8,128)(2,1)S(1)} %get-tuple-element.40), channel_id=1, source_target_pairs={{0,2},{2,4},{3,1},{4,6},{5,3},{6,14},{7,5},{14,12},{15,7},{12,10},... | collective-permute-start | bytes 983048 | tf_op jit(solution)/shard_map/ppermute | solution.py:423
  71.7 10.0 %collective-permute-start.11 = (bf16[4,64,640]{2,1,0:T(8,128)(2,1)S(1)}, bf16[4,64,640]{2,1,0:T(8,128)(2,1)S(1)}, u32[]{:S(2)}, u32[]{:S(2)}) collective-permute-start(bf16[4,64,640]{2,1,0:T(8,128)(2,1)S(1)} %collective-permute-done.10), channel_id=1, source_target_pairs={{0,2},{2,4},{3,1},{4,6},{5,3},{6,14},{7,5},{14,12},{15,7},{12,10},... | collective-permute-start | bytes 983048 | tf_op jit(solution)/shard_map/ppermute | solution.py:424
  81.7 9.4 %collective-permute-start.13 = (bf16[4,64,640]{2,1,0:T(8,128)(2,1)S(1)}, bf16[4,64,640]{2,1,0:T(8,128)(2,1)S(1)}, u32[]{:S(2)}, u32[]{:S(2)}) collective-permute-start(bf16[4,64,640]{2,1,0:T(8,128)(2,1)S(1)} %collective-permute-done.9.refs_2_), channel_id=1, source_target_pairs={{0,1},{1,0},{2,3},{3,2},{4,5},{5,4},{6,7},{7,6},{8,9},{9,8},{10,11... | collective-permute-start | bytes 983048 | tf_op jit(solution)/shard_map/ppermute | solution.py:428
  89.8 1.7 %collective-permute-start.14 = (bf16[4,64,640]{2,1,0:T(8,128)(2,1)S(1)}, bf16[4,64,640]{2,1,0:T(8,128)(2,1)S(1)}, u32[]{:S(2)}, u32[]{:S(2)}) collective-permute-start(bf16[4,64,640]{2,1,0:T(8,128)(2,1)S(1)} %collective-permute-done.11.refs_3_), channel_id=1, source_target_pairs={{0,1},{1,0},{2,3},{3,2},{4,5},{5,4},{6,7},{7,6},{8,9},{9,8},{10,11... | collective-permute-start | bytes 983048 | tf_op jit(solution)/shard_map/ppermute | solution.py:428
  93.8 6.9 %collective-permute-start.15 = (bf16[4,2,8,1280]{3,2,1,0:T(8,128)(2,1)S(1)}, bf16[4,2,8,1280]{3,2,1,0:T(8,128)(2,1)S(1)}, u32[]{:S(2)}, u32[]{:S(2)}) collective-permute-start(bf16[4,2,8,1280]{3,2,1,0:T(8,128)(2,1)S(1)} %get-tuple-element.56), channel_id=1, source_target_pairs={{0,0},{1,128},{8,8},{9,136},{128,1},{129,129},{136,9},{137,137},{2... | collective-permute-start | bytes 491528 | tf_op jit(solution)/shard_map/ppermute | solution.py:431
  95.7 7.1 %collective-permute-start.16 = (bf16[4,2,8,1280]{3,2,1,0:T(8,128)(2,1)S(1)}, bf16[4,2,8,1280]{3,2,1,0:T(8,128)(2,1)S(1)}, u32[]{:S(2)}, u32[]{:S(2)}) collective-permute-start(bf16[4,2,8,1280]{3,2,1,0:T(8,128)(2,1)S(1)} %get-tuple-element.57), channel_id=1, source_target_pairs={{0,8},{1,136},{8,0},{9,128},{128,9},{129,137},{136,1},{137,129},{2... | collective-permute-start | bytes 491528 | tf_op jit(solution)/shard_map/ppermute | solution.py:431
  102.9 5.3 %collective-permute-start.17 = (bf16[2,2,8,1280]{3,2,1,0:T(8,128)(2,1)S(1)}, bf16[2,2,8,1280]{3,2,1,0:T(8,128)(2,1)S(1)}, u32[]{:S(2)}, u32[]{:S(2)}) collective-permute-start(bf16[2,2,8,1280]{3,2,1,0:T(8,128)(2,1)S(1)} %get-tuple-element.58), channel_id=1, source_target_pairs={{0,2},{2,0},{4,6},{6,4},{1,3},{3,1},{5,7},{7,5},{8,10},{10,8},{12,... | collective-permute-start | bytes 245768 | tf_op jit(solution)/shard_map/ppermute | solution.py:434
  105.1 5.8 %collective-permute-start.18 = (bf16[2,2,8,1280]{3,2,1,0:T(8,128)(2,1)S(1)}, bf16[2,2,8,1280]{3,2,1,0:T(8,128)(2,1)S(1)}, u32[]{:S(2)}, u32[]{:S(2)}) collective-permute-start(bf16[2,2,8,1280]{3,2,1,0:T(8,128)(2,1)S(1)} %get-tuple-element.59), channel_id=1, source_target_pairs={{0,4},{2,6},{4,0},{6,2},{1,5},{3,7},{5,1},{7,3},{8,12},{10,14},{12... | collective-permute-start | bytes 245768 | tf_op jit(solution)/shard_map/ppermute | solution.py:434
  106.9 5.9 %collective-permute-start.19 = (bf16[2,2,8,1280]{3,2,1,0:T(8,128)(2,1)S(1)}, bf16[2,2,8,1280]{3,2,1,0:T(8,128)(2,1)S(1)}, u32[]{:S(2)}, u32[]{:S(2)}) collective-permute-start(bf16[2,2,8,1280]{3,2,1,0:T(8,128)(2,1)S(1)} %get-tuple-element.60), channel_id=1, source_target_pairs={{0,6},{2,4},{4,2},{6,0},{1,7},{3,5},{5,3},{7,1},{8,14},{10,12},{12... | collective-permute-start | bytes 245768 | tf_op jit(solution)/shard_map/ppermute | solution.py:434
  107.6 6.5 %collective-permute-start.20 = (bf16[4,2,8,1280]{3,2,1,0:T(8,128)(2,1)S(1)}, bf16[4,2,8,1280]{3,2,1,0:T(8,128)(2,1)S(1)}, u32[]{:S(2)}, u32[]{:S(2)}) collective-permute-start(bf16[4,2,8,1280]{3,2,1,0:T(8,128)(2,1)S(1)} %collective-permute-done.15.near.refs_0_), channel_id=1, source_target_pairs={{0,1},{1,0},{2,3},{3,2},{4,5},{5,4},{6,7},{7,6},{8,9},{9,8},{10,11... | collective-permute-start | bytes 491528 | tf_op jit(solution)/shard_map/ppermute | solution.py:435
  107.6 6.5 %collective-permute-start.21 = (bf16[4,2,8,1280]{3,2,1,0:T(8,128)(2,1)S(1)}, bf16[4,2,8,1280]{3,2,1,0:T(8,128)(2,1)S(1)}, u32[]{:S(2)}, u32[]{:S(2)}) collective-permute-start(bf16[4,2,8,1280]{3,2,1,0:T(8,128)(2,1)S(1)} %collective-permute-done.16.far.refs_1_), channel_id=1, source_target_pairs={{0,1},{1,0},{2,3},{3,2},{4,5},{5,4},{6,7},{7,6},{8,9},{9,8},{10,11... | collective-permute-start | bytes 491528 | tf_op jit(solution)/shard_map/ppermute | solution.py:435
  108.2 5.0 %collective-permute-start.22 = (bf16[2,2,8,1280]{3,2,1,0:T(8,128)(2,1)S(1)}, bf16[2,2,8,1280]{3,2,1,0:T(8,128)(2,1)S(1)}, u32[]{:S(2)}, u32[]{:S(2)}) collective-permute-start(bf16[2,2,8,1280]{3,2,1,0:T(8,128)(2,1)S(1)} %collective-permute-done.17.refs_2_), channel_id=1, source_target_pairs={{0,1},{1,0},{2,3},{3,2},{4,5},{5,4},{6,7},{7,6},{8,9},{9,8},{10,11... | collective-permute-start | bytes 245768 | tf_op jit(solution)/shard_map/ppermute | solution.py:435
  110.9 2.3 %collective-permute-start.23 = (bf16[2,2,8,1280]{3,2,1,0:T(8,128)(2,1)S(1)}, bf16[2,2,8,1280]{3,2,1,0:T(8,128)(2,1)S(1)}, u32[]{:S(2)}, u32[]{:S(2)}) collective-permute-start(bf16[2,2,8,1280]{3,2,1,0:T(8,128)(2,1)S(1)} %collective-permute-done.18.refs_3_), channel_id=1, source_target_pairs={{0,1},{1,0},{2,3},{3,2},{4,5},{5,4},{6,7},{7,6},{8,9},{9,8},{10,11... | collective-permute-start | bytes 245768 | tf_op jit(solution)/shard_map/ppermute | solution.py:435
  (3 other events, 78.0 us)

commit v9 on v8

--- a/solution.py
+++ b/solution.py
@@ -114,12 +114,15 @@
 
 
 def project_kernel(flags, *refs):
-    pieces, (own, partner), (keep, send, edge, give, x_ref) = refs[:8], refs[8:10], refs[10:]
+    pieces, (own, partner), (keep, send, edge, give, x_ref, w_ref, sem) = refs[:8], refs[8:10], refs[10:]
+    load = pltpu.make_async_copy(partner, w_ref, sem)
+    load.start()
     for g, piece in enumerate(pieces):
         x_ref[64 * g : 64 * (g + 1), :] = piece[...]
     p = lax.dot_general(x_ref[...], own[...], NT, preferred_element_type=jnp.float32)
     own_rows = normalized(p)
-    p = lax.dot_general(x_ref[...], partner[...], NT, preferred_element_type=jnp.float32)
+    load.wait()
+    p = lax.dot_general(x_ref[...], w_ref[...], NT, preferred_element_type=jnp.float32)
     other_rows = normalized(p)
 
     def store(first, second):
@@ -155,9 +158,13 @@
     return pl.pallas_call(
         project_kernel,
         out_shape=[whole, whole, part, part],
-        in_specs=[SMEM] + [VMEM] * 10,
+        in_specs=[SMEM] + [VMEM] * 9 + [pl.BlockSpec(memory_space=pl.ANY)],
         out_specs=[VMEM] * 4,
-        scratch_shapes=[pltpu.VMEM((512, own.shape[1]), jnp.bfloat16)],
+        scratch_shapes=[
+            pltpu.VMEM((512, own.shape[1]), jnp.bfloat16),
+            pltpu.VMEM(own.shape, jnp.bfloat16),
+            pltpu.SemaphoreType.DMA,
+        ],
         compiler_params=pltpu.CompilerParams(vmem_limit_bytes=20 * MIB),
         cost_estimate=pl.CostEstimate(
             flops=2 * 512 * 960 * 2560, bytes_accessed=8 * MIB, transcendentals=0
@@ -380,10 +387,7 @@
     wide = tokens.astype(jnp.float32)
     normed = wide * lax.rsqrt(jnp.mean(wide * wide, axis=-1, keepdims=True) + EPS)
     normed = jnp.transpose(normed.astype(jnp.bfloat16), (1, 0, 2)).reshape(64, model)
-    normed, own = lax.optimization_barrier((normed, w_qkv[0]))
     first = lax.ppermute(normed, AXES, spread_perm())
-
-    partner = lax.ppermute(own, ("y_lo", "y_hi", "core"), weight_perm())
 
     base = (z - 2 * block) & 7
     padded = jnp.pad(key_mask, ((0, 0), (WIN, WIN)))
@@ -405,9 +409,11 @@
     at = jnp.stack(at).astype(jnp.int32)
     flags = jnp.stack([core == y_lo, core]).astype(jnp.int32)
 
-    first, usable, band, ints, factor, at, flags = lax.optimization_barrier(
-        (first, usable, band, ints, factor, at, flags)
+    first, own, usable, band, ints, factor, at, flags = lax.optimization_barrier(
+        (first, w_qkv[0], usable, band, ints, factor, at, flags)
     )
+
+    partner = lax.ppermute(own, ("y_lo", "y_hi", "core"), weight_perm())
 
     a = b = first
     pieces = [first]

time: 116 us -> 109 us (0.940)
  waiting for transfers between devices: 34.4 us -> 24.7 us
  starting transfers between devices: 60.1 us -> 64.3 us
    ppermute x2, starting transfers between devices: 8.15 us -> 0.51 us  [body(): lax.ppermute(halo, 'core', SWAP)]
    ppermute x3, starting transfers between devices: 3.67 us -> 11.2 us  [body(): b = lax.ppermute(b, ('z', 'core'), ring_perm(cross=int(k == 1)))]
    ppermute x4, waiting for transfers between devices: 14.6 us -> 7.31 us  [body(): a = lax.ppermute(a, ('z', 'core'), ring_perm())]
    ppermute x2, starting transfers between devices: 2.01 us -> 6.01 us  [body(): lax.ppermute(chunks[k], ('y_lo', 'y_hi', 'core'), return_perm(k))]
    ppermute x1, starting transfers between devices: 3.64 us -> 0.08 us  [body(): partner = lax.ppermute(own, ('y_lo', 'y_hi', 'core'), weight_perm())]
    ppermute x2, waiting for transfers between devices: 7 us -> 4.62 us  [body(): lax.ppermute(chunks[k], ('y_lo', 'y_hi', 'core'), return_perm(k))]
    ppermute x4, starting transfers between devices: 18.7 us -> 20.6 us  [body(): a = lax.ppermute(a, ('z', 'core'), ring_perm())]
  transfers between devices with their start and end apart: 25 -> 25, of which waited for: 15 -> 13; matrix products, arithmetic and copies ran while one was open for 4% -> 4% of each run, Pallas kernels for 3% -> 3%
where the time goes in v9:
time: 109 us; the launch traced here: 108 us
  starting transfers between devices  64.3 us (59%)
  waiting for transfers between devices  24.7 us (23%)
  Pallas kernels  11.5 us (11%)
  local copies, waits for them, and re-layouts  3.78 us (3%)
  other arithmetic  2.54 us (2%)
  between operations  1.59 us (1%)
    ppermute x4, starting transfers between devices, body(): a = lax.ppermute(a, ('z', 'core'), ring_perm())  20.6 us
    ppermute x3, starting transfers between devices, body(): b = lax.ppermute(b, ('z', 'core'), ring_perm(cross=int(k == 1)))  11.2 us
    ppermute x1, starting transfers between devices, body(): first = lax.ppermute(normed, AXES, spread_perm())  9.65 us
    ppermute x4, waiting for transfers between devices, body(): a = lax.ppermute(a, ('z', 'core'), ring_perm())  7.31 us
    ppermute x1, starting transfers between devices, body(): lax.ppermute(give, 'core', SWAP)  7.08 us
    ppermute x2, starting transfers between devices, body(): lax.ppermute(chunks[k], ('y_lo', 'y_hi', 'core'), return_perm(k))  6.01 us
    ppermute x3, starting transfers between devices, body(): lax.ppermute(part, 'x', perm)  5.37 us
    ppermute x3, waiting for transfers between devices, body(): lax.ppermute(part, 'x', perm)  4.96 us
  transfers between devices with their start and end apart: 25, of which 13 were waited for; matrix products, arithmetic and copies ran while one was open for 4% of the time, Pallas kernels for 3%

profile of v9, /device:TPU:1, one launch (start us, length us, event | category | flops | bytes accessed | tf_op | source)
XLA Modules:
  0.0 108.4 jit_solution(6081591722724535020)
XLA Ops:
  2.5 9.6 %collective-permute-start = (bf16[64,2560]{1,0:T(8,128)(2,1)S(1)}, bf16[64,2560]{1,0:T(8,128)(2,1)S(1)}, u32[]{:S(2)}, u32[]{:S(2)}) collective-permute-start(bf16[64,2560]{1,0:T(8,128)(2,1)S(1)} %bitcast.45), channel_id=1, source_target_pairs={{0,0},{1,65},{2,16},{3,81},{4,32},{5,97},{6,48},{7,113},{8,64},{9,... | collective-permute-start | bytes 983048 | tf_op jit(solution)/shard_map/ppermute | solution.py:390
  17.6 9.8 %collective-permute-start.1 = (bf16[64,2560]{1,0:T(8,128)(2,1)S(1)}, bf16[64,2560]{1,0:T(8,128)(2,1)S(1)}, u32[]{:S(2)}, u32[]{:S(2)}) collective-permute-start(bf16[64,2560]{1,0:T(8,128)(2,1)S(1)} %collective-permute-done.refs_0_), channel_id=1, source_target_pairs={{0,16},{1,113},{16,32},{17,1},{32,48},{33,17},{48,64},{49,33},{64,... | collective-permute-start | bytes 983048 | tf_op jit(solution)/shard_map/ppermute | solution.py:421
  27.4 2.9 %collective-permute-start.2 = (bf16[64,2560]{1,0:T(8,128)(2,1)S(1)}, bf16[64,2560]{1,0:T(8,128)(2,1)S(1)}, u32[]{:S(2)}, u32[]{:S(2)}) collective-permute-start(bf16[64,2560]{1,0:T(8,128)(2,1)S(1)} %collective-permute-done.refs_0_), channel_id=1, source_target_pairs={{1,16},{0,113},{17,32},{16,1},{33,48},{32,17},{49,64},{48,33},{65,... | collective-permute-start | bytes 983048 | tf_op jit(solution)/shard_map/ppermute | solution.py:424
  30.2 2.9 %collective-permute-done.1.refs_1_ = bf16[64,2560]{1,0:T(8,128)(2,1)S(1)} collective-permute-done((bf16[64,2560]{1,0:T(8,128)(2,1)S(1)}, bf16[64,2560]{1,0:T(8,128)(2,1)S(1)}, u32[]{:S(2)}, u32[]{:S(2)}) %collective-permute-start.1) | collective-permute-done | bytes 327712 | tf_op jit(solution)/shard_map/ppermute | solution.py:421
  33.1 3.4 %collective-permute-start.3 = (bf16[64,2560]{1,0:T(8,128)(2,1)S(1)}, bf16[64,2560]{1,0:T(8,128)(2,1)S(1)}, u32[]{:S(2)}, u32[]{:S(2)}) collective-permute-start(bf16[64,2560]{1,0:T(8,128)(2,1)S(1)} %collective-permute-done.1.refs_1_), channel_id=1, source_target_pairs={{0,16},{1,113},{16,32},{17,1},{32,48},{33,17},{48,64},{49,33},{64,... | collective-permute-start | bytes 983048 | tf_op jit(solution)/shard_map/ppermute | solution.py:421
  36.5 4.8 %collective-permute-start.4 = (bf16[64,2560]{1,0:T(8,128)(2,1)S(1)}, bf16[64,2560]{1,0:T(8,128)(2,1)S(1)}, u32[]{:S(2)}, u32[]{:S(2)}) collective-permute-start(bf16[64,2560]{1,0:T(8,128)(2,1)S(1)} %collective-permute-done.2.refs_2_), channel_id=1, source_target_pairs={{0,16},{1,113},{16,32},{17,1},{32,48},{33,17},{48,64},{49,33},{64,... | collective-permute-start | bytes 983048 | tf_op jit(solution)/shard_map/ppermute | solution.py:424
  41.4 4.0 %collective-permute-start.5 = (bf16[64,2560]{1,0:T(8,128)(2,1)S(1)}, bf16[64,2560]{1,0:T(8,128)(2,1)S(1)}, u32[]{:S(2)}, u32[]{:S(2)}) collective-permute-start(bf16[64,2560]{1,0:T(8,128)(2,1)S(1)} %collective-permute-done.3.refs_3_), channel_id=1, source_target_pairs={{0,16},{1,113},{16,32},{17,1},{32,48},{33,17},{48,64},{49,33},{64,... | collective-permute-start | bytes 983048 | tf_op jit(solution)/shard_map/ppermute | solution.py:421
  45.4 3.5 %collective-permute-start.6 = (bf16[64,2560]{1,0:T(8,128)(2,1)S(1)}, bf16[64,2560]{1,0:T(8,128)(2,1)S(1)}, u32[]{:S(2)}, u32[]{:S(2)}) collective-permute-start(bf16[64,2560]{1,0:T(8,128)(2,1)S(1)} %collective-permute-done.4.refs_4_), channel_id=1, source_target_pairs={{0,16},{1,113},{16,32},{17,1},{32,48},{33,17},{48,64},{49,33},{64,... | collective-permute-start | bytes 983048 | tf_op jit(solution)/shard_map/ppermute | solution.py:424
  49.4 3.4 %collective-permute-start.7 = (bf16[64,2560]{1,0:T(8,128)(2,1)S(1)}, bf16[64,2560]{1,0:T(8,128)(2,1)S(1)}, u32[]{:S(2)}, u32[]{:S(2)}) collective-permute-start(bf16[64,2560]{1,0:T(8,128)(2,1)S(1)} %collective-permute-done.5.refs_5_), channel_id=1, source_target_pairs={{0,16},{1,113},{16,32},{17,1},{32,48},{33,17},{48,64},{49,33},{64,... | collective-permute-start | bytes 983048 | tf_op jit(solution)/shard_map/ppermute | solution.py:421
  52.9 3.9 %collective-permute-done.7.refs_7_ = bf16[64,2560]{1,0:T(8,128)(2,1)S(1)} collective-permute-done((bf16[64,2560]{1,0:T(8,128)(2,1)S(1)}, bf16[64,2560]{1,0:T(8,128)(2,1)S(1)}, u32[]{:S(2)}, u32[]{:S(2)}) %collective-permute-start.7) | collective-permute-done | bytes 327712 | tf_op jit(solution)/shard_map/ppermute | solution.py:421
  56.8 4.5 %project.1 = (bf16[8,64,480]{2,1,0:T(8,128)(2,1)S(1)}, bf16[8,64,480]{2,1,0:T(8,128)(2,1)S(1)}, bf16[4,64,640]{2,1,0:T(8,128)(2,1)S(1)}, bf16[4,64,640]{2,1,0:T(8,128)(2,1)S(1)}) custom-call(s32[2]{0:T(128)S(1)} %pad_add_fusion.flags, bf16[64,2560]{1,0:T(8,128)(2,1)S(1)} %collective-permute-done.refs_0_, ...), custom_call_target="tpu_custom_call" | custom-call | flops 2516582400 | bytes 8388608 | tf_op jit(solution)/shard_map/project/pallas_call | solution.py:158
  61.3 7.1 %collective-permute-start.10 = (bf16[4,64,640]{2,1,0:T(8,128)(2,1)S(1)}, bf16[4,64,640]{2,1,0:T(8,128)(2,1)S(1)}, u32[]{:S(2)}, u32[]{:S(2)}) collective-permute-start(bf16[4,64,640]{2,1,0:T(8,128)(2,1)S(1)} %get-tuple-element.39), channel_id=1, source_target_pairs={{0,1},{1,0},{2,3},{3,2},{4,5},{5,4},{6,7},{7,6},{8,9},{9,8},{10,11... | collective-permute-start | bytes 983048 | tf_op jit(solution)/shard_map/ppermute | solution.py:430
  69.8 1.5 %collective-permute-start.11 = (bf16[4,64,640]{2,1,0:T(8,128)(2,1)S(1)}, bf16[4,64,640]{2,1,0:T(8,128)(2,1)S(1)}, u32[]{:S(2)}, u32[]{:S(2)}) collective-permute-start(bf16[4,64,640]{2,1,0:T(8,128)(2,1)S(1)} %collective-permute-done.10), channel_id=1, source_target_pairs={{0,2},{2,4},{3,1},{4,6},{5,3},{6,14},{7,5},{14,12},{15,7},{12,10},... | collective-permute-start | bytes 983048 | tf_op jit(solution)/shard_map/ppermute | solution.py:430
  71.3 3.4 %inner.1 = (bf16[8,128,160]{2,1,0:T(8,128)(2,1)S(1)}, f32[8,128,256]{2,1,0:T(8,128)S(1)}, f32[10,128,128]{2,1,0:T(8,128)S(1)}, f32[2,16,128]{2,1,0:T(8,128)S(1)}) custom-call(s32[19]{0:T(128)S(1)} %stack.137.ints, f32[1]{0:T(128)S(6)} %mul.258.factor_ref, f32[64]{0:T(128)S(1)} %reshape.20.band, f32[16,128]{1,0:T(8,128)S(1)} %fusion.4.usable, ...), custom_call_target="tpu_custom_call" | custom-call | flops 10000000 | bytes 100000 | tf_op jit(solution)/shard_map/inner/pallas_call | solution.py:265
  74.7 1.6 %collective-permute-done.9.refs_2_ = bf16[4,64,640]{2,1,0:T(8,128)(2,1)S(1)} collective-permute-done((bf16[4,64,640]{2,1,0:T(8,128)(2,1)S(1)}, bf16[4,64,640]{2,1,0:T(8,128)(2,1)S(1)}, u32[]{:S(2)}, u32[]{:S(2)}) %collective-permute-start.9) | collective-permute-done | bytes 327712 | tf_op jit(solution)/shard_map/ppermute | solution.py:429
  76.3 3.5 %collective-permute-done.11.refs_3_ = bf16[4,64,640]{2,1,0:T(8,128)(2,1)S(1)} collective-permute-done((bf16[4,64,640]{2,1,0:T(8,128)(2,1)S(1)}, bf16[4,64,640]{2,1,0:T(8,128)(2,1)S(1)}, u32[]{:S(2)}, u32[]{:S(2)}) %collective-permute-start.11) | collective-permute-done | bytes 327712 | tf_op jit(solution)/shard_map/ppermute | solution.py:430
  81.9 2.3 %outer.1 = (bf16[4,2,8,1280]{3,2,1,0:T(8,128)(2,1)S(1)}, bf16[4,2,8,1280]{3,2,1,0:T(8,128)(2,1)S(1)}) custom-call(s32[19]{0:T(128)S(1)} %stack.137.ints, f32[1]{0:T(128)S(6)} %mul.258.factor_ref, bf16[8,128,160]{2,1,0:T(8,128)(2,1)S(1)} %get-tuple-element.48.zonal_ref, f32[8,128,256]{2,1,0:T(8,128)S(1)} %get-tuple-element.49.window_ref, ...), custom_call_target="tpu_custom_call" | custom-call | flops 1000000000 | bytes 4194304 | tf_op jit(solution)/shard_map/outer/pallas_call | solution.py:321
  84.2 4.6 %collective-permute-start.15 = (bf16[4,2,8,1280]{3,2,1,0:T(8,128)(2,1)S(1)}, bf16[4,2,8,1280]{3,2,1,0:T(8,128)(2,1)S(1)}, u32[]{:S(2)}, u32[]{:S(2)}) collective-permute-start(bf16[4,2,8,1280]{3,2,1,0:T(8,128)(2,1)S(1)} %get-tuple-element.54), channel_id=1, source_target_pairs={{0,0},{1,128},{8,8},{9,136},{128,1},{129,129},{136,9},{137,137},{2... | collective-permute-start | bytes 491528 | tf_op jit(solution)/shard_map/ppermute | solution.py:437
  88.8 1.4 %collective-permute-start.16 = (bf16[4,2,8,1280]{3,2,1,0:T(8,128)(2,1)S(1)}, bf16[4,2,8,1280]{3,2,1,0:T(8,128)(2,1)S(1)}, u32[]{:S(2)}, u32[]{:S(2)}) collective-permute-start(bf16[4,2,8,1280]{3,2,1,0:T(8,128)(2,1)S(1)} %get-tuple-element.55), channel_id=1, source_target_pairs={{0,8},{1,136},{8,0},{9,128},{128,9},{129,137},{136,1},{137,129},{2... | collective-permute-start | bytes 491528 | tf_op jit(solution)/shard_map/ppermute | solution.py:437
  90.2 3.3 %collective-permute-done.15.near.refs_0_ = bf16[4,2,8,1280]{3,2,1,0:T(8,128)(2,1)S(1)} collective-permute-done((bf16[4,2,8,1280]{3,2,1,0:T(8,128)(2,1)S(1)}, bf16[4,2,8,1280]{3,2,1,0:T(8,128)(2,1)S(1)}, u32[]{:S(2)}, u32[]{:S(2)}) %collective-permute-start.15) | collective-permute-done | bytes 163872 | tf_op jit(solution)/shard_map/ppermute | solution.py:437
  93.5 1.3 %collective-permute-done.16.far.refs_1_ = bf16[4,2,8,1280]{3,2,1,0:T(8,128)(2,1)S(1)} collective-permute-done((bf16[4,2,8,1280]{3,2,1,0:T(8,128)(2,1)S(1)}, bf16[4,2,8,1280]{3,2,1,0:T(8,128)(2,1)S(1)}, u32[]{:S(2)}, u32[]{:S(2)}) %collective-permute-start.16) | collective-permute-done | bytes 163872 | tf_op jit(solution)/shard_map/ppermute | solution.py:437
  95.7 4.5 %collective-permute-start.18 = (bf16[2,2,8,1280]{3,2,1,0:T(8,128)(2,1)S(1)}, bf16[2,2,8,1280]{3,2,1,0:T(8,128)(2,1)S(1)}, u32[]{:S(2)}, u32[]{:S(2)}) collective-permute-start(bf16[2,2,8,1280]{3,2,1,0:T(8,128)(2,1)S(1)} %get-tuple-element.57), channel_id=1, source_target_pairs={{0,4},{2,6},{4,0},{6,2},{1,5},{3,7},{5,1},{7,3},{8,12},{10,14},{12... | collective-permute-start | bytes 245768 | tf_op jit(solution)/shard_map/ppermute | solution.py:440
  100.8 3.0 %collective-permute-done.18.refs_3_ = bf16[2,2,8,1280]{3,2,1,0:T(8,128)(2,1)S(1)} collective-permute-done((bf16[2,2,8,1280]{3,2,1,0:T(8,128)(2,1)S(1)}, bf16[2,2,8,1280]{3,2,1,0:T(8,128)(2,1)S(1)}, u32[]{:S(2)}, u32[]{:S(2)}) %collective-permute-start.18) | collective-permute-done | bytes 81952 | tf_op jit(solution)/shard_map/ppermute | solution.py:440
  103.8 1.9 %collective-permute-done.19.refs_4_ = bf16[2,2,8,1280]{3,2,1,0:T(8,128)(2,1)S(1)} collective-permute-done((bf16[2,2,8,1280]{3,2,1,0:T(8,128)(2,1)S(1)}, bf16[2,2,8,1280]{3,2,1,0:T(8,128)(2,1)S(1)}, u32[]{:S(2)}, u32[]{:S(2)}) %collective-permute-start.19) | collective-permute-done | bytes 81952 | tf_op jit(solution)/shard_map/ppermute | solution.py:440
  (51 shorter events, 14.5 us)
Async XLA Ops:
  2.5 14.9 %collective-permute-start = (bf16[64,2560]{1,0:T(8,128)(2,1)S(1)}, bf16[64,2560]{1,0:T(8,128)(2,1)S(1)}, u32[]{:S(2)}, u32[]{:S(2)}) collective-permute-start(bf16[64,2560]{1,0:T(8,128)(2,1)S(1)} %bitcast.45), channel_id=1, source_target_pairs={{0,0},{1,65},{2,16},{3,81},{4,32},{5,97},{6,48},{7,113},{8,64},{9,... | collective-permute-start | bytes 983048 | tf_op jit(solution)/shard_map/ppermute | solution.py:390
  17.5 39.3 %collective-permute-start.8 = (bf16[480,2560]{1,0:T(8,128)(2,1)S(1)}, bf16[480,2560]{1,0:T(8,128)(2,1)S(1)}, u32[]{:S(2)}, u32[]{:S(2)}) collective-permute-start(bf16[480,2560]{1,0:T(8,128)(2,1)S(1)} %bitcast.43), channel_id=1, source_target_pairs={{0,128},{1,137},{128,8},{129,1},{8,136},{9,129},{136,0},{137,9},{2... | collective-permute-start | bytes 7372808 | tf_op jit(solution)/shard_map/ppermute | solution.py:416
  17.6 15.5 %collective-permute-start.1 = (bf16[64,2560]{1,0:T(8,128)(2,1)S(1)}, bf16[64,2560]{1,0:T(8,128)(2,1)S(1)}, u32[]{:S(2)}, u32[]{:S(2)}) collective-permute-start(bf16[64,2560]{1,0:T(8,128)(2,1)S(1)} %collective-permute-done.refs_0_), channel_id=1, source_target_pairs={{0,16},{1,113},{16,32},{17,1},{32,48},{33,17},{48,64},{49,33},{64,... | collective-permute-start | bytes 983048 | tf_op jit(solution)/shard_map/ppermute | solution.py:421
  27.4 9.2 %collective-permute-start.2 = (bf16[64,2560]{1,0:T(8,128)(2,1)S(1)}, bf16[64,2560]{1,0:T(8,128)(2,1)S(1)}, u32[]{:S(2)}, u32[]{:S(2)}) collective-permute-start(bf16[64,2560]{1,0:T(8,128)(2,1)S(1)} %collective-permute-done.refs_0_), channel_id=1, source_target_pairs={{1,16},{0,113},{17,32},{16,1},{33,48},{32,17},{49,64},{48,33},{65,... | collective-permute-start | bytes 983048 | tf_op jit(solution)/shard_map/ppermute | solution.py:424
  33.1 8.2 %collective-permute-start.3 = (bf16[64,2560]{1,0:T(8,128)(2,1)S(1)}, bf16[64,2560]{1,0:T(8,128)(2,1)S(1)}, u32[]{:S(2)}, u32[]{:S(2)}) collective-permute-start(bf16[64,2560]{1,0:T(8,128)(2,1)S(1)} %collective-permute-done.1.refs_1_), channel_id=1, source_target_pairs={{0,16},{1,113},{16,32},{17,1},{32,48},{33,17},{48,64},{49,33},{64,... | collective-permute-start | bytes 983048 | tf_op jit(solution)/shard_map/ppermute | solution.py:421
  36.5 8.8 %collective-permute-start.4 = (bf16[64,2560]{1,0:T(8,128)(2,1)S(1)}, bf16[64,2560]{1,0:T(8,128)(2,1)S(1)}, u32[]{:S(2)}, u32[]{:S(2)}) collective-permute-start(bf16[64,2560]{1,0:T(8,128)(2,1)S(1)} %collective-permute-done.2.refs_2_), channel_id=1, source_target_pairs={{0,16},{1,113},{16,32},{17,1},{32,48},{33,17},{48,64},{49,33},{64,... | collective-permute-start | bytes 983048 | tf_op jit(solution)/shard_map/ppermute | solution.py:424
  41.4 8.0 %collective-permute-start.5 = (bf16[64,2560]{1,0:T(8,128)(2,1)S(1)}, bf16[64,2560]{1,0:T(8,128)(2,1)S(1)}, u32[]{:S(2)}, u32[]{:S(2)}) collective-permute-start(bf16[64,2560]{1,0:T(8,128)(2,1)S(1)} %collective-permute-done.3.refs_3_), channel_id=1, source_target_pairs={{0,16},{1,113},{16,32},{17,1},{32,48},{33,17},{48,64},{49,33},{64,... | collective-permute-start | bytes 983048 | tf_op jit(solution)/shard_map/ppermute | solution.py:421
  45.4 7.5 %collective-permute-start.6 = (bf16[64,2560]{1,0:T(8,128)(2,1)S(1)}, bf16[64,2560]{1,0:T(8,128)(2,1)S(1)}, u32[]{:S(2)}, u32[]{:S(2)}) collective-permute-start(bf16[64,2560]{1,0:T(8,128)(2,1)S(1)} %collective-permute-done.4.refs_4_), channel_id=1, source_target_pairs={{0,16},{1,113},{16,32},{17,1},{32,48},{33,17},{48,64},{49,33},{64,... | collective-permute-start | bytes 983048 | tf_op jit(solution)/shard_map/ppermute | solution.py:424
  49.4 7.4 %collective-permute-start.7 = (bf16[64,2560]{1,0:T(8,128)(2,1)S(1)}, bf16[64,2560]{1,0:T(8,128)(2,1)S(1)}, u32[]{:S(2)}, u32[]{:S(2)}) collective-permute-start(bf16[64,2560]{1,0:T(8,128)(2,1)S(1)} %collective-permute-done.5.refs_5_), channel_id=1, source_target_pairs={{0,16},{1,113},{16,32},{17,1},{32,48},{33,17},{48,64},{49,33},{64,... | collective-permute-start | bytes 983048 | tf_op jit(solution)/shard_map/ppermute | solution.py:421
  61.3 8.5 %collective-permute-start.10 = (bf16[4,64,640]{2,1,0:T(8,128)(2,1)S(1)}, bf16[4,64,640]{2,1,0:T(8,128)(2,1)S(1)}, u32[]{:S(2)}, u32[]{:S(2)}) collective-permute-start(bf16[4,64,640]{2,1,0:T(8,128)(2,1)S(1)} %get-tuple-element.39), channel_id=1, source_target_pairs={{0,1},{1,0},{2,3},{3,2},{4,5},{5,4},{6,7},{7,6},{8,9},{9,8},{10,11... | collective-permute-start | bytes 983048 | tf_op jit(solution)/shard_map/ppermute | solution.py:430
  68.4 2.9 %collective-permute-start.12 = (bf16[8,64,480]{2,1,0:T(8,128)(2,1)S(1)}, bf16[8,64,480]{2,1,0:T(8,128)(2,1)S(1)}, u32[]{:S(2)}, u32[]{:S(2)}) collective-permute-start(bf16[8,64,480]{2,1,0:T(8,128)(2,1)S(1)} %get-tuple-element.43), channel_id=1, source_target_pairs={{0,1},{1,0},{2,3},{3,2},{4,5},{5,4},{6,7},{7,6},{8,9},{9,8},{10,11... | collective-permute-start | bytes 1474568 | tf_op jit(solution)/shard_map/ppermute | solution.py:431
  68.5 7.8 %collective-permute-start.9 = (bf16[4,64,640]{2,1,0:T(8,128)(2,1)S(1)}, bf16[4,64,640]{2,1,0:T(8,128)(2,1)S(1)}, u32[]{:S(2)}, u32[]{:S(2)}) collective-permute-start(bf16[4,64,640]{2,1,0:T(8,128)(2,1)S(1)} %get-tuple-element.38), channel_id=1, source_target_pairs={{0,2},{2,4},{3,1},{4,6},{5,3},{6,14},{7,5},{14,12},{15,7},{12,10},... | collective-permute-start | bytes 983048 | tf_op jit(solution)/shard_map/ppermute | solution.py:429
  69.8 10.0 %collective-permute-start.11 = (bf16[4,64,640]{2,1,0:T(8,128)(2,1)S(1)}, bf16[4,64,640]{2,1,0:T(8,128)(2,1)S(1)}, u32[]{:S(2)}, u32[]{:S(2)}) collective-permute-start(bf16[4,64,640]{2,1,0:T(8,128)(2,1)S(1)} %collective-permute-done.10), channel_id=1, source_target_pairs={{0,2},{2,4},{3,1},{4,6},{5,3},{6,14},{7,5},{14,12},{15,7},{12,10},... | collective-permute-start | bytes 983048 | tf_op jit(solution)/shard_map/ppermute | solution.py:430
  79.8 1.6 %collective-permute-start.13 = (bf16[4,64,640]{2,1,0:T(8,128)(2,1)S(1)}, bf16[4,64,640]{2,1,0:T(8,128)(2,1)S(1)}, u32[]{:S(2)}, u32[]{:S(2)}) collective-permute-start(bf16[4,64,640]{2,1,0:T(8,128)(2,1)S(1)} %collective-permute-done.9.refs_2_), channel_id=1, source_target_pairs={{0,1},{1,0},{2,3},{3,2},{4,5},{5,4},{6,7},{7,6},{8,9},{9,8},{10,11... | collective-permute-start | bytes 983048 | tf_op jit(solution)/shard_map/ppermute | solution.py:434
  79.8 2.1 %collective-permute-start.14 = (bf16[4,64,640]{2,1,0:T(8,128)(2,1)S(1)}, bf16[4,64,640]{2,1,0:T(8,128)(2,1)S(1)}, u32[]{:S(2)}, u32[]{:S(2)}) collective-permute-start(bf16[4,64,640]{2,1,0:T(8,128)(2,1)S(1)} %collective-permute-done.11.refs_3_), channel_id=1, source_target_pairs={{0,1},{1,0},{2,3},{3,2},{4,5},{5,4},{6,7},{7,6},{8,9},{9,8},{10,11... | collective-permute-start | bytes 983048 | tf_op jit(solution)/shard_map/ppermute | solution.py:434
  84.2 9.3 %collective-permute-start.15 = (bf16[4,2,8,1280]{3,2,1,0:T(8,128)(2,1)S(1)}, bf16[4,2,8,1280]{3,2,1,0:T(8,128)(2,1)S(1)}, u32[]{:S(2)}, u32[]{:S(2)}) collective-permute-start(bf16[4,2,8,1280]{3,2,1,0:T(8,128)(2,1)S(1)} %get-tuple-element.54), channel_id=1, source_target_pairs={{0,0},{1,128},{8,8},{9,136},{128,1},{129,129},{136,9},{137,137},{2... | collective-permute-start | bytes 491528 | tf_op jit(solution)/shard_map/ppermute | solution.py:437
  88.8 6.0 %collective-permute-start.16 = (bf16[4,2,8,1280]{3,2,1,0:T(8,128)(2,1)S(1)}, bf16[4,2,8,1280]{3,2,1,0:T(8,128)(2,1)S(1)}, u32[]{:S(2)}, u32[]{:S(2)}) collective-permute-start(bf16[4,2,8,1280]{3,2,1,0:T(8,128)(2,1)S(1)} %get-tuple-element.55), channel_id=1, source_target_pairs={{0,8},{1,136},{8,0},{9,128},{128,9},{129,137},{136,1},{137,129},{2... | collective-permute-start | bytes 491528 | tf_op jit(solution)/shard_map/ppermute | solution.py:437
  94.9 5.9 %collective-permute-start.17 = (bf16[2,2,8,1280]{3,2,1,0:T(8,128)(2,1)S(1)}, bf16[2,2,8,1280]{3,2,1,0:T(8,128)(2,1)S(1)}, u32[]{:S(2)}, u32[]{:S(2)}) collective-permute-start(bf16[2,2,8,1280]{3,2,1,0:T(8,128)(2,1)S(1)} %get-tuple-element.56), channel_id=1, source_target_pairs={{0,2},{2,0},{4,6},{6,4},{1,3},{3,1},{5,7},{7,5},{8,10},{10,8},{12,... | collective-permute-start | bytes 245768 | tf_op jit(solution)/shard_map/ppermute | solution.py:440
  95.7 8.1 %collective-permute-start.18 = (bf16[2,2,8,1280]{3,2,1,0:T(8,128)(2,1)S(1)}, bf16[2,2,8,1280]{3,2,1,0:T(8,128)(2,1)S(1)}, u32[]{:S(2)}, u32[]{:S(2)}) collective-permute-start(bf16[2,2,8,1280]{3,2,1,0:T(8,128)(2,1)S(1)} %get-tuple-element.57), channel_id=1, source_target_pairs={{0,4},{2,6},{4,0},{6,2},{1,5},{3,7},{5,1},{7,3},{8,12},{10,14},{12... | collective-permute-start | bytes 245768 | tf_op jit(solution)/shard_map/ppermute | solution.py:440
  100.2 5.5 %collective-permute-start.19 = (bf16[2,2,8,1280]{3,2,1,0:T(8,128)(2,1)S(1)}, bf16[2,2,8,1280]{3,2,1,0:T(8,128)(2,1)S(1)}, u32[]{:S(2)}, u32[]{:S(2)}) collective-permute-start(bf16[2,2,8,1280]{3,2,1,0:T(8,128)(2,1)S(1)} %get-tuple-element.58), channel_id=1, source_target_pairs={{0,6},{2,4},{4,2},{6,0},{1,7},{3,5},{5,3},{7,1},{8,14},{10,12},{12... | collective-permute-start | bytes 245768 | tf_op jit(solution)/shard_map/ppermute | solution.py:440
  100.2 6.8 %collective-permute-start.20 = (bf16[4,2,8,1280]{3,2,1,0:T(8,128)(2,1)S(1)}, bf16[4,2,8,1280]{3,2,1,0:T(8,128)(2,1)S(1)}, u32[]{:S(2)}, u32[]{:S(2)}) collective-permute-start(bf16[4,2,8,1280]{3,2,1,0:T(8,128)(2,1)S(1)} %collective-permute-done.15.near.refs_0_), channel_id=1, source_target_pairs={{0,1},{1,0},{2,3},{3,2},{4,5},{5,4},{6,7},{7,6},{8,9},{9,8},{10,11... | collective-permute-start | bytes 491528 | tf_op jit(solution)/shard_map/ppermute | solution.py:441
  100.3 6.8 %collective-permute-start.21 = (bf16[4,2,8,1280]{3,2,1,0:T(8,128)(2,1)S(1)}, bf16[4,2,8,1280]{3,2,1,0:T(8,128)(2,1)S(1)}, u32[]{:S(2)}, u32[]{:S(2)}) collective-permute-start(bf16[4,2,8,1280]{3,2,1,0:T(8,128)(2,1)S(1)} %collective-permute-done.16.far.refs_1_), channel_id=1, source_target_pairs={{0,1},{1,0},{2,3},{3,2},{4,5},{5,4},{6,7},{7,6},{8,9},{9,8},{10,11... | collective-permute-start | bytes 491528 | tf_op jit(solution)/shard_map/ppermute | solution.py:441
  100.8 5.4 %collective-permute-start.22 = (bf16[2,2,8,1280]{3,2,1,0:T(8,128)(2,1)S(1)}, bf16[2,2,8,1280]{3,2,1,0:T(8,128)(2,1)S(1)}, u32[]{:S(2)}, u32[]{:S(2)}) collective-permute-start(bf16[2,2,8,1280]{3,2,1,0:T(8,128)(2,1)S(1)} %collective-permute-done.17.refs_2_), channel_id=1, source_target_pairs={{0,1},{1,0},{2,3},{3,2},{4,5},{5,4},{6,7},{7,6},{8,9},{9,8},{10,11... | collective-permute-start | bytes 245768 | tf_op jit(solution)/shard_map/ppermute | solution.py:441
  103.8 2.3 %collective-permute-start.23 = (bf16[2,2,8,1280]{3,2,1,0:T(8,128)(2,1)S(1)}, bf16[2,2,8,1280]{3,2,1,0:T(8,128)(2,1)S(1)}, u32[]{:S(2)}, u32[]{:S(2)}) collective-permute-start(bf16[2,2,8,1280]{3,2,1,0:T(8,128)(2,1)S(1)} %collective-permute-done.18.refs_3_), channel_id=1, source_target_pairs={{0,1},{1,0},{2,3},{3,2},{4,5},{5,4},{6,7},{7,6},{8,9},{9,8},{10,11... | collective-permute-start | bytes 245768 | tf_op jit(solution)/shard_map/ppermute | solution.py:441
  (4 other events, 49.1 us)

commit v10 on v9

--- a/solution.py
+++ b/solution.py
@@ -56,12 +56,12 @@
     return pairs
 
 
-def ring_perm(cross=0):
+def ring_perm():
     pairs = []
     for z in range(8):
         for core in range(2):
             there = (z + 1 - 2 * core) % 8
-            pairs.append((flat((z, 8), (core ^ cross, 2)), flat((there, 8), (core, 2))))
+            pairs.append((flat((z, 8), (core, 2)), flat((there, 8), (core, 2))))
     return pairs
 
 
@@ -415,13 +415,13 @@
 
     partner = lax.ppermute(own, ("y_lo", "y_hi", "core"), weight_perm())
 
-    a = b = first
+    a, b = first, lax.ppermute(first, "core", SWAP)
     pieces = [first]
     for k in range(1, 5):
         a = lax.ppermute(a, ("z", "core"), ring_perm())
         pieces.append(a)
         if k < 4:
-            b = lax.ppermute(b, ("z", "core"), ring_perm(cross=int(k == 1)))
+            b = lax.ppermute(b, ("z", "core"), ring_perm())
             pieces.append(b)
 
     corners = ("y_lo", "y_hi", "x", "core")

time: 109 us -> 107 us (0.982)
    ppermute x3 -> x4, starting transfers between devices: 11.2 us -> 18.3 us  [the longest x1 10.2 us: body(): a, b = (first, lax.ppermute(first, 'core', SWAP))]
    ppermute x4, starting transfers between devices: 20.6 us -> 13.8 us  [body(): a = lax.ppermute(a, ('z', 'core'), ring_perm())]
    ppermute x1, starting transfers between devices: 7.08 us -> 4.05 us  [body(): lax.ppermute(give, 'core', SWAP)]
    ppermute x2, waiting for transfers between devices: 4.62 us -> 3.41 us  [body(): lax.ppermute(chunks[k], ('y_lo', 'y_hi', 'core'), return_perm(k))]
  transfers between devices with their start and end apart: 25 -> 26, of which waited for: 13 -> 16; matrix products, arithmetic and copies ran while one was open for 4% -> 3% of each run, Pallas kernels for 3% -> 3%
where the time goes in v10:
time: 107 us
  starting transfers between devices  63.4 us (59%)
  waiting for transfers between devices  24.2 us (23%)
  Pallas kernels  11.5 us (11%)
  local copies, waits for them, and re-layouts  3.62 us (3%)
  other arithmetic  2.54 us (2%)
  between operations  1.68 us (2%)
    ppermute x4, starting transfers between devices, body(): a = lax.ppermute(a, ('z', 'core'), ring_perm())  13.8 us
    ppermute x1, starting transfers between devices, body(): a, b = (first, lax.ppermute(first, 'core', SWAP))  10.2 us
    ppermute x1, starting transfers between devices, body(): first = lax.ppermute(normed, AXES, spread_perm())  9.65 us
    ppermute x3, starting transfers between devices, body(): b = lax.ppermute(b, ('z', 'core'), ring_perm())  8.07 us
    ppermute x4, waiting for transfers between devices, body(): a = lax.ppermute(a, ('z', 'core'), ring_perm())  7.7 us
    ppermute x2, starting transfers between devices, body(): lax.ppermute(chunks[k], ('y_lo', 'y_hi', 'core'), return_perm(k))  6.49 us
    ppermute x3, starting transfers between devices, body(): lax.ppermute(part, 'x', perm)  5.92 us
    ppermute x3, waiting for transfers between devices, body(): lax.ppermute(part, 'x', perm)  5.18 us
  transfers between devices with their start and end apart: 26, of which 16 were waited for; matrix products, arithmetic and copies ran while one was open for 3% of the time, Pallas kernels for 3%

profile of v10, /device:TPU:1, one launch (start us, length us, event | category | flops | bytes accessed | tf_op | source)
XLA Modules:
  0.0 107.0 jit_solution(4780052828917631633)
XLA Ops:
  2.5 9.6 %collective-permute-start = (bf16[64,2560]{1,0:T(8,128)(2,1)S(1)}, bf16[64,2560]{1,0:T(8,128)(2,1)S(1)}, u32[]{:S(2)}, u32[]{:S(2)}) collective-permute-start(bf16[64,2560]{1,0:T(8,128)(2,1)S(1)} %bitcast.45), channel_id=1, source_target_pairs={{0,0},{1,65},{2,16},{3,81},{4,32},{5,97},{6,48},{7,113},{8,64},{9,... | collective-permute-start | bytes 983048 | tf_op jit(solution)/shard_map/ppermute | solution.py:390
  17.5 10.2 %collective-permute-start.2 = (bf16[64,2560]{1,0:T(8,128)(2,1)S(1)}, bf16[64,2560]{1,0:T(8,128)(2,1)S(1)}, u32[]{:S(2)}, u32[]{:S(2)}) collective-permute-start(bf16[64,2560]{1,0:T(8,128)(2,1)S(1)} %collective-permute-done.refs_0_), channel_id=1, source_target_pairs={{0,1},{1,0},{2,3},{3,2},{4,5},{5,4},{6,7},{7,6},{8,9},{9,8},{10,11... | collective-permute-start | bytes 983048 | tf_op jit(solution)/shard_map/ppermute | solution.py:418
  27.7 3.6 %collective-permute-start.1 = (bf16[64,2560]{1,0:T(8,128)(2,1)S(1)}, bf16[64,2560]{1,0:T(8,128)(2,1)S(1)}, u32[]{:S(2)}, u32[]{:S(2)}) collective-permute-start(bf16[64,2560]{1,0:T(8,128)(2,1)S(1)} %collective-permute-done.refs_0_), channel_id=1, source_target_pairs={{0,16},{1,113},{16,32},{17,1},{32,48},{33,17},{48,64},{49,33},{64,... | collective-permute-start | bytes 983048 | tf_op jit(solution)/shard_map/ppermute | solution.py:421
  32.6 2.8 %collective-permute-done.1.refs_1_ = bf16[64,2560]{1,0:T(8,128)(2,1)S(1)} collective-permute-done((bf16[64,2560]{1,0:T(8,128)(2,1)S(1)}, bf16[64,2560]{1,0:T(8,128)(2,1)S(1)}, u32[]{:S(2)}, u32[]{:S(2)}) %collective-permute-start.1) | collective-permute-done | bytes 327712 | tf_op jit(solution)/shard_map/ppermute | solution.py:421
  35.3 3.4 %collective-permute-start.4 = (bf16[64,2560]{1,0:T(8,128)(2,1)S(1)}, bf16[64,2560]{1,0:T(8,128)(2,1)S(1)}, u32[]{:S(2)}, u32[]{:S(2)}) collective-permute-start(bf16[64,2560]{1,0:T(8,128)(2,1)S(1)} %collective-permute-done.1.refs_1_), channel_id=1, source_target_pairs={{0,16},{1,113},{16,32},{17,1},{32,48},{33,17},{48,64},{49,33},{64,... | collective-permute-start | bytes 983048 | tf_op jit(solution)/shard_map/ppermute | solution.py:421
  38.8 3.4 %collective-permute-start.5 = (bf16[64,2560]{1,0:T(8,128)(2,1)S(1)}, bf16[64,2560]{1,0:T(8,128)(2,1)S(1)}, u32[]{:S(2)}, u32[]{:S(2)}) collective-permute-start(bf16[64,2560]{1,0:T(8,128)(2,1)S(1)} %collective-permute-done.3.refs_2_), channel_id=1, source_target_pairs={{0,16},{1,113},{16,32},{17,1},{32,48},{33,17},{48,64},{49,33},{64,... | collective-permute-start | bytes 983048 | tf_op jit(solution)/shard_map/ppermute | solution.py:424
  42.8 3.4 %collective-permute-start.6 = (bf16[64,2560]{1,0:T(8,128)(2,1)S(1)}, bf16[64,2560]{1,0:T(8,128)(2,1)S(1)}, u32[]{:S(2)}, u32[]{:S(2)}) collective-permute-start(bf16[64,2560]{1,0:T(8,128)(2,1)S(1)} %collective-permute-done.4.refs_3_), channel_id=1, source_target_pairs={{0,16},{1,113},{16,32},{17,1},{32,48},{33,17},{48,64},{49,33},{64,... | collective-permute-start | bytes 983048 | tf_op jit(solution)/shard_map/ppermute | solution.py:421
  46.3 3.4 %collective-permute-start.7 = (bf16[64,2560]{1,0:T(8,128)(2,1)S(1)}, bf16[64,2560]{1,0:T(8,128)(2,1)S(1)}, u32[]{:S(2)}, u32[]{:S(2)}) collective-permute-start(bf16[64,2560]{1,0:T(8,128)(2,1)S(1)} %collective-permute-done.5.refs_4_), channel_id=1, source_target_pairs={{0,16},{1,113},{16,32},{17,1},{32,48},{33,17},{48,64},{49,33},{64,... | collective-permute-start | bytes 983048 | tf_op jit(solution)/shard_map/ppermute | solution.py:424
  50.2 3.4 %collective-permute-start.8 = (bf16[64,2560]{1,0:T(8,128)(2,1)S(1)}, bf16[64,2560]{1,0:T(8,128)(2,1)S(1)}, u32[]{:S(2)}, u32[]{:S(2)}) collective-permute-start(bf16[64,2560]{1,0:T(8,128)(2,1)S(1)} %collective-permute-done.6.refs_5_), channel_id=1, source_target_pairs={{0,16},{1,113},{16,32},{17,1},{32,48},{33,17},{48,64},{49,33},{64,... | collective-permute-start | bytes 983048 | tf_op jit(solution)/shard_map/ppermute | solution.py:421
  53.7 3.9 %collective-permute-done.8.refs_7_ = bf16[64,2560]{1,0:T(8,128)(2,1)S(1)} collective-permute-done((bf16[64,2560]{1,0:T(8,128)(2,1)S(1)}, bf16[64,2560]{1,0:T(8,128)(2,1)S(1)}, u32[]{:S(2)}, u32[]{:S(2)}) %collective-permute-start.8) | collective-permute-done | bytes 327712 | tf_op jit(solution)/shard_map/ppermute | solution.py:421
  57.6 4.5 %project.1 = (bf16[8,64,480]{2,1,0:T(8,128)(2,1)S(1)}, bf16[8,64,480]{2,1,0:T(8,128)(2,1)S(1)}, bf16[4,64,640]{2,1,0:T(8,128)(2,1)S(1)}, bf16[4,64,640]{2,1,0:T(8,128)(2,1)S(1)}) custom-call(s32[2]{0:T(128)S(1)} %pad_add_fusion.flags, bf16[64,2560]{1,0:T(8,128)(2,1)S(1)} %collective-permute-done.refs_0_, ...), custom_call_target="tpu_custom_call" | custom-call | flops 2516582400 | bytes 8388608 | tf_op jit(solution)/shard_map/project/pallas_call | solution.py:158
  62.1 4.0 %collective-permute-start.11 = (bf16[4,64,640]{2,1,0:T(8,128)(2,1)S(1)}, bf16[4,64,640]{2,1,0:T(8,128)(2,1)S(1)}, u32[]{:S(2)}, u32[]{:S(2)}) collective-permute-start(bf16[4,64,640]{2,1,0:T(8,128)(2,1)S(1)} %get-tuple-element.39), channel_id=1, source_target_pairs={{0,1},{1,0},{2,3},{3,2},{4,5},{5,4},{6,7},{7,6},{8,9},{9,8},{10,11... | collective-permute-start | bytes 983048 | tf_op jit(solution)/shard_map/ppermute | solution.py:430
  66.3 1.3 %collective-permute-start.10 = (bf16[4,64,640]{2,1,0:T(8,128)(2,1)S(1)}, bf16[4,64,640]{2,1,0:T(8,128)(2,1)S(1)}, u32[]{:S(2)}, u32[]{:S(2)}) collective-permute-start(bf16[4,64,640]{2,1,0:T(8,128)(2,1)S(1)} %get-tuple-element.38), channel_id=1, source_target_pairs={{0,2},{2,4},{3,1},{4,6},{5,3},{6,14},{7,5},{14,12},{15,7},{12,10},... | collective-permute-start | bytes 983048 | tf_op jit(solution)/shard_map/ppermute | solution.py:429
  67.6 1.5 %collective-permute-start.12 = (bf16[4,64,640]{2,1,0:T(8,128)(2,1)S(1)}, bf16[4,64,640]{2,1,0:T(8,128)(2,1)S(1)}, u32[]{:S(2)}, u32[]{:S(2)}) collective-permute-start(bf16[4,64,640]{2,1,0:T(8,128)(2,1)S(1)} %collective-permute-done.11), channel_id=1, source_target_pairs={{0,2},{2,4},{3,1},{4,6},{5,3},{6,14},{7,5},{14,12},{15,7},{12,10},... | collective-permute-start | bytes 983048 | tf_op jit(solution)/shard_map/ppermute | solution.py:430
  69.1 3.4 %inner.1 = (bf16[8,128,160]{2,1,0:T(8,128)(2,1)S(1)}, f32[8,128,256]{2,1,0:T(8,128)S(1)}, f32[10,128,128]{2,1,0:T(8,128)S(1)}, f32[2,16,128]{2,1,0:T(8,128)S(1)}) custom-call(s32[19]{0:T(128)S(1)} %stack.137.ints, f32[1]{0:T(128)S(6)} %mul.258.factor_ref, f32[64]{0:T(128)S(1)} %reshape.20.band, f32[16,128]{1,0:T(8,128)S(1)} %fusion.4.usable, ...), custom_call_target="tpu_custom_call" | custom-call | flops 10000000 | bytes 100000 | tf_op jit(solution)/shard_map/inner/pallas_call | solution.py:265
  72.5 1.6 %collective-permute-done.10.refs_2_ = bf16[4,64,640]{2,1,0:T(8,128)(2,1)S(1)} collective-permute-done((bf16[4,64,640]{2,1,0:T(8,128)(2,1)S(1)}, bf16[4,64,640]{2,1,0:T(8,128)(2,1)S(1)}, u32[]{:S(2)}, u32[]{:S(2)}) %collective-permute-start.10) | collective-permute-done | bytes 327712 | tf_op jit(solution)/shard_map/ppermute | solution.py:429
  74.1 3.5 %collective-permute-done.12.refs_3_ = bf16[4,64,640]{2,1,0:T(8,128)(2,1)S(1)} collective-permute-done((bf16[4,64,640]{2,1,0:T(8,128)(2,1)S(1)}, bf16[4,64,640]{2,1,0:T(8,128)(2,1)S(1)}, u32[]{:S(2)}, u32[]{:S(2)}) %collective-permute-start.12) | collective-permute-done | bytes 327712 | tf_op jit(solution)/shard_map/ppermute | solution.py:430
  79.7 2.3 %outer.1 = (bf16[4,2,8,1280]{3,2,1,0:T(8,128)(2,1)S(1)}, bf16[4,2,8,1280]{3,2,1,0:T(8,128)(2,1)S(1)}) custom-call(s32[19]{0:T(128)S(1)} %stack.137.ints, f32[1]{0:T(128)S(6)} %mul.258.factor_ref, bf16[8,128,160]{2,1,0:T(8,128)(2,1)S(1)} %get-tuple-element.48.zonal_ref, f32[8,128,256]{2,1,0:T(8,128)S(1)} %get-tuple-element.49.window_ref, ...), custom_call_target="tpu_custom_call" | custom-call | flops 1000000000 | bytes 4194304 | tf_op jit(solution)/shard_map/outer/pallas_call | solution.py:321
  82.0 3.9 %collective-permute-start.16 = (bf16[4,2,8,1280]{3,2,1,0:T(8,128)(2,1)S(1)}, bf16[4,2,8,1280]{3,2,1,0:T(8,128)(2,1)S(1)}, u32[]{:S(2)}, u32[]{:S(2)}) collective-permute-start(bf16[4,2,8,1280]{3,2,1,0:T(8,128)(2,1)S(1)} %get-tuple-element.54), channel_id=1, source_target_pairs={{0,0},{1,128},{8,8},{9,136},{128,1},{129,129},{136,9},{137,137},{2... | collective-permute-start | bytes 491528 | tf_op jit(solution)/shard_map/ppermute | solution.py:437
  85.8 2.6 %collective-permute-start.17 = (bf16[4,2,8,1280]{3,2,1,0:T(8,128)(2,1)S(1)}, bf16[4,2,8,1280]{3,2,1,0:T(8,128)(2,1)S(1)}, u32[]{:S(2)}, u32[]{:S(2)}) collective-permute-start(bf16[4,2,8,1280]{3,2,1,0:T(8,128)(2,1)S(1)} %get-tuple-element.55), channel_id=1, source_target_pairs={{0,8},{1,136},{8,0},{9,128},{128,9},{129,137},{136,1},{137,129},{2... | collective-permute-start | bytes 491528 | tf_op jit(solution)/shard_map/ppermute | solution.py:437
  89.6 2.3 %collective-permute-done.17.far.refs_1_ = bf16[4,2,8,1280]{3,2,1,0:T(8,128)(2,1)S(1)} collective-permute-done((bf16[4,2,8,1280]{3,2,1,0:T(8,128)(2,1)S(1)}, bf16[4,2,8,1280]{3,2,1,0:T(8,128)(2,1)S(1)}, u32[]{:S(2)}, u32[]{:S(2)}) %collective-permute-start.17) | collective-permute-done | bytes 163872 | tf_op jit(solution)/shard_map/ppermute | solution.py:437
  92.9 4.9 %collective-permute-start.19 = (bf16[2,2,8,1280]{3,2,1,0:T(8,128)(2,1)S(1)}, bf16[2,2,8,1280]{3,2,1,0:T(8,128)(2,1)S(1)}, u32[]{:S(2)}, u32[]{:S(2)}) collective-permute-start(bf16[2,2,8,1280]{3,2,1,0:T(8,128)(2,1)S(1)} %get-tuple-element.57), channel_id=1, source_target_pairs={{0,4},{2,6},{4,0},{6,2},{1,5},{3,7},{5,1},{7,3},{8,12},{10,14},{12... | collective-permute-start | bytes 245768 | tf_op jit(solution)/shard_map/ppermute | solution.py:440
  98.5 4.0 %collective-permute-done.19.refs_3_ = bf16[2,2,8,1280]{3,2,1,0:T(8,128)(2,1)S(1)} collective-permute-done((bf16[2,2,8,1280]{3,2,1,0:T(8,128)(2,1)S(1)}, bf16[2,2,8,1280]{3,2,1,0:T(8,128)(2,1)S(1)}, u32[]{:S(2)}, u32[]{:S(2)}) %collective-permute-start.19) | collective-permute-done | bytes 81952 | tf_op jit(solution)/shard_map/ppermute | solution.py:440
  105.7 1.3 %assemble.1 = bf16[1,8,20480]{2,1,0:T(8,128)(2,1)} custom-call(s32[16]{0:T(128)S(1)} %stack.154.at, bf16[4,2,8,1280]{3,2,1,0:T(8,128)(2,1)S(1)} %collective-permute-done.16.near.refs_0_, bf16[4,2,8,1280]{3,2,1,0:T(8,128)(2,1)S(1)} %collective-permute-done.17.far.refs_1_, bf16[2,2,8,1280]{3,2,1,0:T(8,128)(2,1)S(1)} %collective-permute-done.18.refs_2_, ...), custom_call_target="tpu_custom_call" | custom-call | bytes 1048576 | tf_op jit(solution)/shard_map/assemble/pallas_call | solution.py:369
  (53 shorter events, 17.0 us)
Async XLA Ops:
  2.5 14.9 %collective-permute-start = (bf16[64,2560]{1,0:T(8,128)(2,1)S(1)}, bf16[64,2560]{1,0:T(8,128)(2,1)S(1)}, u32[]{:S(2)}, u32[]{:S(2)}) collective-permute-start(bf16[64,2560]{1,0:T(8,128)(2,1)S(1)} %bitcast.45), channel_id=1, source_target_pairs={{0,0},{1,65},{2,16},{3,81},{4,32},{5,97},{6,48},{7,113},{8,64},{9,... | collective-permute-start | bytes 983048 | tf_op jit(solution)/shard_map/ppermute | solution.py:390
  17.4 40.2 %collective-permute-start.9 = (bf16[480,2560]{1,0:T(8,128)(2,1)S(1)}, bf16[480,2560]{1,0:T(8,128)(2,1)S(1)}, u32[]{:S(2)}, u32[]{:S(2)}) collective-permute-start(bf16[480,2560]{1,0:T(8,128)(2,1)S(1)} %bitcast.43), channel_id=1, source_target_pairs={{0,128},{1,137},{128,8},{129,1},{8,136},{9,129},{136,0},{137,9},{2... | collective-permute-start | bytes 7372808 | tf_op jit(solution)/shard_map/ppermute | solution.py:416
  17.5 13.8 %collective-permute-start.2 = (bf16[64,2560]{1,0:T(8,128)(2,1)S(1)}, bf16[64,2560]{1,0:T(8,128)(2,1)S(1)}, u32[]{:S(2)}, u32[]{:S(2)}) collective-permute-start(bf16[64,2560]{1,0:T(8,128)(2,1)S(1)} %collective-permute-done.refs_0_), channel_id=1, source_target_pairs={{0,1},{1,0},{2,3},{3,2},{4,5},{5,4},{6,7},{7,6},{8,9},{9,8},{10,11... | collective-permute-start | bytes 983048 | tf_op jit(solution)/shard_map/ppermute | solution.py:418
  27.7 7.6 %collective-permute-start.1 = (bf16[64,2560]{1,0:T(8,128)(2,1)S(1)}, bf16[64,2560]{1,0:T(8,128)(2,1)S(1)}, u32[]{:S(2)}, u32[]{:S(2)}) collective-permute-start(bf16[64,2560]{1,0:T(8,128)(2,1)S(1)} %collective-permute-done.refs_0_), channel_id=1, source_target_pairs={{0,16},{1,113},{16,32},{17,1},{32,48},{33,17},{48,64},{49,33},{64,... | collective-permute-start | bytes 983048 | tf_op jit(solution)/shard_map/ppermute | solution.py:421
  31.3 7.5 %collective-permute-start.3 = (bf16[64,2560]{1,0:T(8,128)(2,1)S(1)}, bf16[64,2560]{1,0:T(8,128)(2,1)S(1)}, u32[]{:S(2)}, u32[]{:S(2)}) collective-permute-start(bf16[64,2560]{1,0:T(8,128)(2,1)S(1)} %collective-permute-done.2), channel_id=1, source_target_pairs={{0,16},{1,113},{16,32},{17,1},{32,48},{33,17},{48,64},{49,33},{64,... | collective-permute-start | bytes 983048 | tf_op jit(solution)/shard_map/ppermute | solution.py:424
  35.3 7.4 %collective-permute-start.4 = (bf16[64,2560]{1,0:T(8,128)(2,1)S(1)}, bf16[64,2560]{1,0:T(8,128)(2,1)S(1)}, u32[]{:S(2)}, u32[]{:S(2)}) collective-permute-start(bf16[64,2560]{1,0:T(8,128)(2,1)S(1)} %collective-permute-done.1.refs_1_), channel_id=1, source_target_pairs={{0,16},{1,113},{16,32},{17,1},{32,48},{33,17},{48,64},{49,33},{64,... | collective-permute-start | bytes 983048 | tf_op jit(solution)/shard_map/ppermute | solution.py:421
  38.8 7.4 %collective-permute-start.5 = (bf16[64,2560]{1,0:T(8,128)(2,1)S(1)}, bf16[64,2560]{1,0:T(8,128)(2,1)S(1)}, u32[]{:S(2)}, u32[]{:S(2)}) collective-permute-start(bf16[64,2560]{1,0:T(8,128)(2,1)S(1)} %collective-permute-done.3.refs_2_), channel_id=1, source_target_pairs={{0,16},{1,113},{16,32},{17,1},{32,48},{33,17},{48,64},{49,33},{64,... | collective-permute-start | bytes 983048 | tf_op jit(solution)/shard_map/ppermute | solution.py:424
  42.8 7.4 %collective-permute-start.6 = (bf16[64,2560]{1,0:T(8,128)(2,1)S(1)}, bf16[64,2560]{1,0:T(8,128)(2,1)S(1)}, u32[]{:S(2)}, u32[]{:S(2)}) collective-permute-start(bf16[64,2560]{1,0:T(8,128)(2,1)S(1)} %collective-permute-done.4.refs_3_), channel_id=1, source_target_pairs={{0,16},{1,113},{16,32},{17,1},{32,48},{33,17},{48,64},{49,33},{64,... | collective-permute-start | bytes 983048 | tf_op jit(solution)/shard_map/ppermute | solution.py:421
  46.3 7.4 %collective-permute-start.7 = (bf16[64,2560]{1,0:T(8,128)(2,1)S(1)}, bf16[64,2560]{1,0:T(8,128)(2,1)S(1)}, u32[]{:S(2)}, u32[]{:S(2)}) collective-permute-start(bf16[64,2560]{1,0:T(8,128)(2,1)S(1)} %collective-permute-done.5.refs_4_), channel_id=1, source_target_pairs={{0,16},{1,113},{16,32},{17,1},{32,48},{33,17},{48,64},{49,33},{64,... | collective-permute-start | bytes 983048 | tf_op jit(solution)/shard_map/ppermute | solution.py:424
  50.2 7.4 %collective-permute-start.8 = (bf16[64,2560]{1,0:T(8,128)(2,1)S(1)}, bf16[64,2560]{1,0:T(8,128)(2,1)S(1)}, u32[]{:S(2)}, u32[]{:S(2)}) collective-permute-start(bf16[64,2560]{1,0:T(8,128)(2,1)S(1)} %collective-permute-done.6.refs_5_), channel_id=1, source_target_pairs={{0,16},{1,113},{16,32},{17,1},{32,48},{33,17},{48,64},{49,33},{64,... | collective-permute-start | bytes 983048 | tf_op jit(solution)/shard_map/ppermute | solution.py:421
  62.1 5.4 %collective-permute-start.11 = (bf16[4,64,640]{2,1,0:T(8,128)(2,1)S(1)}, bf16[4,64,640]{2,1,0:T(8,128)(2,1)S(1)}, u32[]{:S(2)}, u32[]{:S(2)}) collective-permute-start(bf16[4,64,640]{2,1,0:T(8,128)(2,1)S(1)} %get-tuple-element.39), channel_id=1, source_target_pairs={{0,1},{1,0},{2,3},{3,2},{4,5},{5,4},{6,7},{7,6},{8,9},{9,8},{10,11... | collective-permute-start | bytes 983048 | tf_op jit(solution)/shard_map/ppermute | solution.py:430
  66.2 2.9 %collective-permute-start.13 = (bf16[8,64,480]{2,1,0:T(8,128)(2,1)S(1)}, bf16[8,64,480]{2,1,0:T(8,128)(2,1)S(1)}, u32[]{:S(2)}, u32[]{:S(2)}) collective-permute-start(bf16[8,64,480]{2,1,0:T(8,128)(2,1)S(1)} %get-tuple-element.43), channel_id=1, source_target_pairs={{0,1},{1,0},{2,3},{3,2},{4,5},{5,4},{6,7},{7,6},{8,9},{9,8},{10,11... | collective-permute-start | bytes 1474568 | tf_op jit(solution)/shard_map/ppermute | solution.py:431
  66.3 7.8 %collective-permute-start.10 = (bf16[4,64,640]{2,1,0:T(8,128)(2,1)S(1)}, bf16[4,64,640]{2,1,0:T(8,128)(2,1)S(1)}, u32[]{:S(2)}, u32[]{:S(2)}) collective-permute-start(bf16[4,64,640]{2,1,0:T(8,128)(2,1)S(1)} %get-tuple-element.38), channel_id=1, source_target_pairs={{0,2},{2,4},{3,1},{4,6},{5,3},{6,14},{7,5},{14,12},{15,7},{12,10},... | collective-permute-start | bytes 983048 | tf_op jit(solution)/shard_map/ppermute | solution.py:429
  67.6 10.0 %collective-permute-start.12 = (bf16[4,64,640]{2,1,0:T(8,128)(2,1)S(1)}, bf16[4,64,640]{2,1,0:T(8,128)(2,1)S(1)}, u32[]{:S(2)}, u32[]{:S(2)}) collective-permute-start(bf16[4,64,640]{2,1,0:T(8,128)(2,1)S(1)} %collective-permute-done.11), channel_id=1, source_target_pairs={{0,2},{2,4},{3,1},{4,6},{5,3},{6,14},{7,5},{14,12},{15,7},{12,10},... | collective-permute-start | bytes 983048 | tf_op jit(solution)/shard_map/ppermute | solution.py:430
  77.6 2.1 %collective-permute-start.15 = (bf16[4,64,640]{2,1,0:T(8,128)(2,1)S(1)}, bf16[4,64,640]{2,1,0:T(8,128)(2,1)S(1)}, u32[]{:S(2)}, u32[]{:S(2)}) collective-permute-start(bf16[4,64,640]{2,1,0:T(8,128)(2,1)S(1)} %collective-permute-done.12.refs_3_), channel_id=1, source_target_pairs={{0,1},{1,0},{2,3},{3,2},{4,5},{5,4},{6,7},{7,6},{8,9},{9,8},{10,11... | collective-permute-start | bytes 983048 | tf_op jit(solution)/shard_map/ppermute | solution.py:434
  82.0 7.6 %collective-permute-start.16 = (bf16[4,2,8,1280]{3,2,1,0:T(8,128)(2,1)S(1)}, bf16[4,2,8,1280]{3,2,1,0:T(8,128)(2,1)S(1)}, u32[]{:S(2)}, u32[]{:S(2)}) collective-permute-start(bf16[4,2,8,1280]{3,2,1,0:T(8,128)(2,1)S(1)} %get-tuple-element.54), channel_id=1, source_target_pairs={{0,0},{1,128},{8,8},{9,136},{128,1},{129,129},{136,9},{137,137},{2... | collective-permute-start | bytes 491528 | tf_op jit(solution)/shard_map/ppermute | solution.py:437
  85.8 6.0 %collective-permute-start.17 = (bf16[4,2,8,1280]{3,2,1,0:T(8,128)(2,1)S(1)}, bf16[4,2,8,1280]{3,2,1,0:T(8,128)(2,1)S(1)}, u32[]{:S(2)}, u32[]{:S(2)}) collective-permute-start(bf16[4,2,8,1280]{3,2,1,0:T(8,128)(2,1)S(1)} %get-tuple-element.55), channel_id=1, source_target_pairs={{0,8},{1,136},{8,0},{9,128},{128,9},{129,137},{136,1},{137,129},{2... | collective-permute-start | bytes 491528 | tf_op jit(solution)/shard_map/ppermute | solution.py:437
  91.9 6.4 %collective-permute-start.18 = (bf16[2,2,8,1280]{3,2,1,0:T(8,128)(2,1)S(1)}, bf16[2,2,8,1280]{3,2,1,0:T(8,128)(2,1)S(1)}, u32[]{:S(2)}, u32[]{:S(2)}) collective-permute-start(bf16[2,2,8,1280]{3,2,1,0:T(8,128)(2,1)S(1)} %get-tuple-element.56), channel_id=1, source_target_pairs={{0,2},{2,0},{4,6},{6,4},{1,3},{3,1},{5,7},{7,5},{8,10},{10,8},{12,... | collective-permute-start | bytes 245768 | tf_op jit(solution)/shard_map/ppermute | solution.py:440
  92.9 9.6 %collective-permute-start.19 = (bf16[2,2,8,1280]{3,2,1,0:T(8,128)(2,1)S(1)}, bf16[2,2,8,1280]{3,2,1,0:T(8,128)(2,1)S(1)}, u32[]{:S(2)}, u32[]{:S(2)}) collective-permute-start(bf16[2,2,8,1280]{3,2,1,0:T(8,128)(2,1)S(1)} %get-tuple-element.57), channel_id=1, source_target_pairs={{0,4},{2,6},{4,0},{6,2},{1,5},{3,7},{5,1},{7,3},{8,12},{10,14},{12... | collective-permute-start | bytes 245768 | tf_op jit(solution)/shard_map/ppermute | solution.py:440
  97.8 6.4 %collective-permute-start.20 = (bf16[2,2,8,1280]{3,2,1,0:T(8,128)(2,1)S(1)}, bf16[2,2,8,1280]{3,2,1,0:T(8,128)(2,1)S(1)}, u32[]{:S(2)}, u32[]{:S(2)}) collective-permute-start(bf16[2,2,8,1280]{3,2,1,0:T(8,128)(2,1)S(1)} %get-tuple-element.58), channel_id=1, source_target_pairs={{0,6},{2,4},{4,2},{6,0},{1,7},{3,5},{5,3},{7,1},{8,14},{10,12},{12... | collective-permute-start | bytes 245768 | tf_op jit(solution)/shard_map/ppermute | solution.py:440
  97.8 7.8 %collective-permute-start.21 = (bf16[4,2,8,1280]{3,2,1,0:T(8,128)(2,1)S(1)}, bf16[4,2,8,1280]{3,2,1,0:T(8,128)(2,1)S(1)}, u32[]{:S(2)}, u32[]{:S(2)}) collective-permute-start(bf16[4,2,8,1280]{3,2,1,0:T(8,128)(2,1)S(1)} %collective-permute-done.16.near.refs_0_), channel_id=1, source_target_pairs={{0,1},{1,0},{2,3},{3,2},{4,5},{5,4},{6,7},{7,6},{8,9},{9,8},{10,11... | collective-permute-start | bytes 491528 | tf_op jit(solution)/shard_map/ppermute | solution.py:441
  98.0 7.6 %collective-permute-start.22 = (bf16[4,2,8,1280]{3,2,1,0:T(8,128)(2,1)S(1)}, bf16[4,2,8,1280]{3,2,1,0:T(8,128)(2,1)S(1)}, u32[]{:S(2)}, u32[]{:S(2)}) collective-permute-start(bf16[4,2,8,1280]{3,2,1,0:T(8,128)(2,1)S(1)} %collective-permute-done.17.far.refs_1_), channel_id=1, source_target_pairs={{0,1},{1,0},{2,3},{3,2},{4,5},{5,4},{6,7},{7,6},{8,9},{9,8},{10,11... | collective-permute-start | bytes 491528 | tf_op jit(solution)/shard_map/ppermute | solution.py:441
  98.3 6.4 %collective-permute-start.23 = (bf16[2,2,8,1280]{3,2,1,0:T(8,128)(2,1)S(1)}, bf16[2,2,8,1280]{3,2,1,0:T(8,128)(2,1)S(1)}, u32[]{:S(2)}, u32[]{:S(2)}) collective-permute-start(bf16[2,2,8,1280]{3,2,1,0:T(8,128)(2,1)S(1)} %collective-permute-done.18.refs_2_), channel_id=1, source_target_pairs={{0,1},{1,0},{2,3},{3,2},{4,5},{5,4},{6,7},{7,6},{8,9},{9,8},{10,11... | collective-permute-start | bytes 245768 | tf_op jit(solution)/shard_map/ppermute | solution.py:441
  102.5 2.2 %collective-permute-start.24 = (bf16[2,2,8,1280]{3,2,1,0:T(8,128)(2,1)S(1)}, bf16[2,2,8,1280]{3,2,1,0:T(8,128)(2,1)S(1)}, u32[]{:S(2)}, u32[]{:S(2)}) collective-permute-start(bf16[2,2,8,1280]{3,2,1,0:T(8,128)(2,1)S(1)} %collective-permute-done.19.refs_3_), channel_id=1, source_target_pairs={{0,1},{1,0},{2,3},{3,2},{4,5},{5,4},{6,7},{7,6},{8,9},{9,8},{10,11... | collective-permute-start | bytes 245768 | tf_op jit(solution)/shard_map/ppermute | solution.py:441
  (5 other events, 50.8 us)

commit v11 on v10

--- a/solution.py
+++ b/solution.py
@@ -75,13 +75,13 @@
     return pairs
 
 
-def neighbour_perm():
+def neighbour_perm(cross):
     pairs = []
     for block in range(16):
         for core in range(2):
             if 0 <= block + 1 - 2 * core < 16:
                 here, there = place_of(block), place_of(block + 1 - 2 * core)
-                source = flat((here[0], 2), (here[1], 2), (here[2], 4), (core, 2))
+                source = flat((here[0], 2), (here[1], 2), (here[2], 4), (core ^ cross, 2))
                 target = flat((there[0], 2), (there[1], 2), (there[2], 4), (core, 2))
                 pairs.append((source, target))
     return pairs
@@ -114,15 +114,12 @@
 
 
 def project_kernel(flags, *refs):
-    pieces, (own, partner), (keep, send, edge, give, x_ref, w_ref, sem) = refs[:8], refs[8:10], refs[10:]
-    load = pltpu.make_async_copy(partner, w_ref, sem)
-    load.start()
+    pieces, (own, partner), (keep, send, edge, give, x_ref) = refs[:8], refs[8:10], refs[10:]
     for g, piece in enumerate(pieces):
         x_ref[64 * g : 64 * (g + 1), :] = piece[...]
     p = lax.dot_general(x_ref[...], own[...], NT, preferred_element_type=jnp.float32)
     own_rows = normalized(p)
-    load.wait()
-    p = lax.dot_general(x_ref[...], w_ref[...], NT, preferred_element_type=jnp.float32)
+    p = lax.dot_general(x_ref[...], partner[...], NT, preferred_element_type=jnp.float32)
     other_rows = normalized(p)
 
     def store(first, second):
@@ -158,13 +155,9 @@
     return pl.pallas_call(
         project_kernel,
         out_shape=[whole, whole, part, part],
-        in_specs=[SMEM] + [VMEM] * 9 + [pl.BlockSpec(memory_space=pl.ANY)],
+        in_specs=[SMEM] + [VMEM] * 10,
         out_specs=[VMEM] * 4,
-        scratch_shapes=[
-            pltpu.VMEM((512, own.shape[1]), jnp.bfloat16),
-            pltpu.VMEM(own.shape, jnp.bfloat16),
-            pltpu.SemaphoreType.DMA,
-        ],
+        scratch_shapes=[pltpu.VMEM((512, own.shape[1]), jnp.bfloat16)],
         compiler_params=pltpu.CompilerParams(vmem_limit_bytes=20 * MIB),
         cost_estimate=pl.CostEstimate(
             flops=2 * 512 * 960 * 2560, bytes_accessed=8 * MIB, transcendentals=0
@@ -336,13 +329,13 @@
     )(ints, factor, *inner_results, *parts, *edges)
 
 
-def regroup_kernel(near, far, *parts):
+def regroup_kernel(far, near, *parts):
     for k, part in enumerate(parts):
         part[0] = near[k + 1]
         part[1] = far[k + 1]
 
 
-def regroup(near, far):
+def regroup(far, near):
     part = jax.ShapeDtypeStruct((2, *near.shape[1:]), near.dtype)
     return pl.pallas_call(
         regroup_kernel,
@@ -352,7 +345,7 @@
         compiler_params=pltpu.CompilerParams(vmem_limit_bytes=4 * MIB),
         cost_estimate=pl.CostEstimate(flops=0, bytes_accessed=MIB, transcendentals=0),
         name="regroup",
-    )(near, far)
+    )(far, near)
 
 
 def assemble_kernel(at, *refs):
@@ -361,7 +354,7 @@
         landed = refs[5 * part : 5 * part + 5]
         for k in range(8):
             kind, x = k // 4, k % 4
-            value = landed[kind][0, part] if x == 0 else landed[x + 1][kind, part]
+            value = landed[1 - kind][0, part] if x == 0 else landed[(0, 3, 2, 4)[x]][kind, part]
             out[0, :, pl.ds(pl.multiple_of(at[8 * part + k] * width, 128), width)] = value
 
 
@@ -426,18 +419,19 @@
 
     corners = ("y_lo", "y_hi", "x", "core")
     keep, send, edge, give = project(flags, pieces, own, partner)
-    halo_own = lax.ppermute(edge, corners, neighbour_perm())
-    halo_oth = lax.ppermute(lax.ppermute(give, "core", SWAP), corners, neighbour_perm())
+    halo_own = lax.ppermute(edge, corners, neighbour_perm(0))
+    halo_oth = lax.ppermute(give, corners, neighbour_perm(1))
     parts = keep, lax.ppermute(send, "core", SWAP)
     results = inner(ints, factor, band, usable, parts)
     halo_own, halo_oth, *results = lax.optimization_barrier((halo_own, halo_oth, *results))
     halos = [halo_own, halo_oth] + [lax.ppermute(halo, "core", SWAP) for halo in (halo_own, halo_oth)]
     chunks = outer(ints, factor, results, parts, halos)
 
-    near, far = (lax.ppermute(chunks[k], ("y_lo", "y_hi", "core"), return_perm(k)) for k in range(2))
-    passed = regroup(near, far)
-    along = [[(i, i ^ k) for i in range(4)] for k in range(1, 4)]
-    landed = [near, far] + [lax.ppermute(part, "x", perm) for part, perm in zip(passed, along)]
+    far, near = (lax.ppermute(chunks[k], ("y_lo", "y_hi", "core"), return_perm(k)) for k in (1, 0))
+    passed = regroup(far, near)
+    landed = [far, near]
+    for k in (2, 1, 3):
+        landed.append(lax.ppermute(passed[k - 1], "x", [(i, i ^ k) for i in range(4)]))
     return assemble(at, landed + [lax.ppermute(part, "core", SWAP) for part in landed])
 
 

time: 107 us -> 103 us (0.963)
  starting transfers between devices: 63.4 us -> 60.5 us
  waiting for transfers between devices: 24.2 us -> 23 us
    ppermute x6 -> x5, starting transfers between devices: 12.7 us -> 6.72 us  [the longest x3 3.34 us: body(): lax.ppermute(passed[k - 1], 'x', [(i, i ^ k) for i in range(4)])]
    ppermute x1, starting transfers between devices: 0.1 us -> 4.05 us  [body(): parts = (keep, lax.ppermute(send, 'core', SWAP))]
    ppermute x6 -> x5, waiting for transfers between devices: 10.3 us -> 7.75 us  [the longest x3 3.23 us: body(): lax.ppermute(passed[k - 1], 'x', [(i, i ^ k) for i in range(4)])]
    ppermute x2, waiting for transfers between devices: 3.41 us -> 4.71 us  [body(): lax.ppermute(chunks[k], ('y_lo', 'y_hi', 'core'), return_perm(k))]
  transfers between devices with their start and end apart: 26 -> 25, of which waited for: 16 -> 17; matrix products, arithmetic and copies ran while one was open for 3% -> 4% of each run, Pallas kernels for 3% -> 3%
where the time goes in v11:
time: 103 us; the launch traced here: 102 us
  starting transfers between devices  60.5 us (59%)
  waiting for transfers between devices  23 us (22%)
  Pallas kernels  10.9 us (11%)
  local copies, waits for them, and re-layouts  3.78 us (4%)
  other arithmetic  2.54 us (2%)
  between operations  1.58 us (2%)
    ppermute x4, starting transfers between devices, body(): a = lax.ppermute(a, ('z', 'core'), ring_perm())  13.8 us
    ppermute x1, starting transfers between devices, body(): a, b = (first, lax.ppermute(first, 'core', SWAP))  10.1 us
    ppermute x1, starting transfers between devices, body(): first = lax.ppermute(normed, AXES, spread_perm())  9.65 us
    ppermute x3, starting transfers between devices, body(): b = lax.ppermute(b, ('z', 'core'), ring_perm())  8.07 us
    ppermute x4, waiting for transfers between devices, body(): a = lax.ppermute(a, ('z', 'core'), ring_perm())  7.7 us
    ppermute x2, starting transfers between devices, body(): lax.ppermute(chunks[k], ('y_lo', 'y_hi', 'core'), return_perm(k))  5.93 us
    ppermute x2, waiting for transfers between devices, body(): lax.ppermute(chunks[k], ('y_lo', 'y_hi', 'core'), return_perm(k))  4.71 us
    ppermute x1, starting transfers between devices, body(): parts = (keep, lax.ppermute(send, 'core', SWAP))  4.05 us
  transfers between devices with their start and end apart: 25, of which 17 were waited for; matrix products, arithmetic and copies ran while one was open for 4% of the time, Pallas kernels for 3%

profile of v11, /device:TPU:1, one launch (start us, length us, event | category | flops | bytes accessed | tf_op | source)
XLA Modules:
  0.0 102.2 jit_solution(11486478628040530770)
XLA Ops:
  2.5 9.6 %collective-permute-start = (bf16[64,2560]{1,0:T(8,128)(2,1)S(1)}, bf16[64,2560]{1,0:T(8,128)(2,1)S(1)}, u32[]{:S(2)}, u32[]{:S(2)}) collective-permute-start(bf16[64,2560]{1,0:T(8,128)(2,1)S(1)} %bitcast.45), channel_id=1, source_target_pairs={{0,0},{1,65},{2,16},{3,81},{4,32},{5,97},{6,48},{7,113},{8,64},{9,... | collective-permute-start | bytes 983048 | tf_op jit(solution)/shard_map/ppermute | solution.py:383
  17.6 10.1 %collective-permute-start.2 = (bf16[64,2560]{1,0:T(8,128)(2,1)S(1)}, bf16[64,2560]{1,0:T(8,128)(2,1)S(1)}, u32[]{:S(2)}, u32[]{:S(2)}) collective-permute-start(bf16[64,2560]{1,0:T(8,128)(2,1)S(1)} %collective-permute-done.refs_0_), channel_id=1, source_target_pairs={{0,1},{1,0},{2,3},{3,2},{4,5},{5,4},{6,7},{7,6},{8,9},{9,8},{10,11... | collective-permute-start | bytes 983048 | tf_op jit(solution)/shard_map/ppermute | solution.py:411
  27.7 3.6 %collective-permute-start.1 = (bf16[64,2560]{1,0:T(8,128)(2,1)S(1)}, bf16[64,2560]{1,0:T(8,128)(2,1)S(1)}, u32[]{:S(2)}, u32[]{:S(2)}) collective-permute-start(bf16[64,2560]{1,0:T(8,128)(2,1)S(1)} %collective-permute-done.refs_0_), channel_id=1, source_target_pairs={{0,16},{1,113},{16,32},{17,1},{32,48},{33,17},{48,64},{49,33},{64,... | collective-permute-start | bytes 983048 | tf_op jit(solution)/shard_map/ppermute | solution.py:414
  32.6 2.8 %collective-permute-done.1.refs_1_ = bf16[64,2560]{1,0:T(8,128)(2,1)S(1)} collective-permute-done((bf16[64,2560]{1,0:T(8,128)(2,1)S(1)}, bf16[64,2560]{1,0:T(8,128)(2,1)S(1)}, u32[]{:S(2)}, u32[]{:S(2)}) %collective-permute-start.1) | collective-permute-done | bytes 327712 | tf_op jit(solution)/shard_map/ppermute | solution.py:414
  35.3 3.4 %collective-permute-start.4 = (bf16[64,2560]{1,0:T(8,128)(2,1)S(1)}, bf16[64,2560]{1,0:T(8,128)(2,1)S(1)}, u32[]{:S(2)}, u32[]{:S(2)}) collective-permute-start(bf16[64,2560]{1,0:T(8,128)(2,1)S(1)} %collective-permute-done.1.refs_1_), channel_id=1, source_target_pairs={{0,16},{1,113},{16,32},{17,1},{32,48},{33,17},{48,64},{49,33},{64,... | collective-permute-start | bytes 983048 | tf_op jit(solution)/shard_map/ppermute | solution.py:414
  38.8 3.4 %collective-permute-start.5 = (bf16[64,2560]{1,0:T(8,128)(2,1)S(1)}, bf16[64,2560]{1,0:T(8,128)(2,1)S(1)}, u32[]{:S(2)}, u32[]{:S(2)}) collective-permute-start(bf16[64,2560]{1,0:T(8,128)(2,1)S(1)} %collective-permute-done.3.refs_2_), channel_id=1, source_target_pairs={{0,16},{1,113},{16,32},{17,1},{32,48},{33,17},{48,64},{49,33},{64,... | collective-permute-start | bytes 983048 | tf_op jit(solution)/shard_map/ppermute | solution.py:417
  42.8 3.4 %collective-permute-start.6 = (bf16[64,2560]{1,0:T(8,128)(2,1)S(1)}, bf16[64,2560]{1,0:T(8,128)(2,1)S(1)}, u32[]{:S(2)}, u32[]{:S(2)}) collective-permute-start(bf16[64,2560]{1,0:T(8,128)(2,1)S(1)} %collective-permute-done.4.refs_3_), channel_id=1, source_target_pairs={{0,16},{1,113},{16,32},{17,1},{32,48},{33,17},{48,64},{49,33},{64,... | collective-permute-start | bytes 983048 | tf_op jit(solution)/shard_map/ppermute | solution.py:414
  46.3 3.4 %collective-permute-start.7 = (bf16[64,2560]{1,0:T(8,128)(2,1)S(1)}, bf16[64,2560]{1,0:T(8,128)(2,1)S(1)}, u32[]{:S(2)}, u32[]{:S(2)}) collective-permute-start(bf16[64,2560]{1,0:T(8,128)(2,1)S(1)} %collective-permute-done.5.refs_4_), channel_id=1, source_target_pairs={{0,16},{1,113},{16,32},{17,1},{32,48},{33,17},{48,64},{49,33},{64,... | collective-permute-start | bytes 983048 | tf_op jit(solution)/shard_map/ppermute | solution.py:417
  50.2 3.4 %collective-permute-start.8 = (bf16[64,2560]{1,0:T(8,128)(2,1)S(1)}, bf16[64,2560]{1,0:T(8,128)(2,1)S(1)}, u32[]{:S(2)}, u32[]{:S(2)}) collective-permute-start(bf16[64,2560]{1,0:T(8,128)(2,1)S(1)} %collective-permute-done.6.refs_5_), channel_id=1, source_target_pairs={{0,16},{1,113},{16,32},{17,1},{32,48},{33,17},{48,64},{49,33},{64,... | collective-permute-start | bytes 983048 | tf_op jit(solution)/shard_map/ppermute | solution.py:414
  53.7 3.9 %collective-permute-done.8.refs_7_ = bf16[64,2560]{1,0:T(8,128)(2,1)S(1)} collective-permute-done((bf16[64,2560]{1,0:T(8,128)(2,1)S(1)}, bf16[64,2560]{1,0:T(8,128)(2,1)S(1)}, u32[]{:S(2)}, u32[]{:S(2)}) %collective-permute-start.8) | collective-permute-done | bytes 327712 | tf_op jit(solution)/shard_map/ppermute | solution.py:414
  57.6 3.9 %project.1 = (bf16[8,64,480]{2,1,0:T(8,128)(2,1)S(1)}, bf16[8,64,480]{2,1,0:T(8,128)(2,1)S(1)}, bf16[4,64,640]{2,1,0:T(8,128)(2,1)S(1)}, bf16[4,64,640]{2,1,0:T(8,128)(2,1)S(1)}) custom-call(s32[2]{0:T(128)S(1)} %pad_add_fusion.flags, bf16[64,2560]{1,0:T(8,128)(2,1)S(1)} %collective-permute-done.refs_0_, ...), custom_call_target="tpu_custom_call" | custom-call | flops 2516582400 | bytes 8388608 | tf_op jit(solution)/shard_map/project/pallas_call | solution.py:155
  61.6 4.1 %collective-permute-start.12 = (bf16[8,64,480]{2,1,0:T(8,128)(2,1)S(1)}, bf16[8,64,480]{2,1,0:T(8,128)(2,1)S(1)}, u32[]{:S(2)}, u32[]{:S(2)}) collective-permute-start(bf16[8,64,480]{2,1,0:T(8,128)(2,1)S(1)} %get-tuple-element.43), channel_id=1, source_target_pairs={{0,1},{1,0},{2,3},{3,2},{4,5},{5,4},{6,7},{7,6},{8,9},{9,8},{10,11... | collective-permute-start | bytes 1474568 | tf_op jit(solution)/shard_map/ppermute | solution.py:424
  66.9 2.1 %collective-permute-start.11 = (bf16[4,64,640]{2,1,0:T(8,128)(2,1)S(1)}, bf16[4,64,640]{2,1,0:T(8,128)(2,1)S(1)}, u32[]{:S(2)}, u32[]{:S(2)}) collective-permute-start(bf16[4,64,640]{2,1,0:T(8,128)(2,1)S(1)} %get-tuple-element.39), channel_id=1, source_target_pairs={{1,2},{3,4},{2,1},{5,6},{4,3},{7,14},{6,5},{15,12},{14,7},{13,10},... | collective-permute-start | bytes 983048 | tf_op jit(solution)/shard_map/ppermute | solution.py:423
  69.0 3.4 %inner.1 = (bf16[8,128,160]{2,1,0:T(8,128)(2,1)S(1)}, f32[8,128,256]{2,1,0:T(8,128)S(1)}, f32[10,128,128]{2,1,0:T(8,128)S(1)}, f32[2,16,128]{2,1,0:T(8,128)S(1)}) custom-call(s32[19]{0:T(128)S(1)} %stack.137.ints, f32[1]{0:T(128)S(6)} %mul.258.factor_ref, f32[64]{0:T(128)S(1)} %reshape.20.band, f32[16,128]{1,0:T(8,128)S(1)} %fusion.4.usable, ...), custom_call_target="tpu_custom_call" | custom-call | flops 10000000 | bytes 100000 | tf_op jit(solution)/shard_map/inner/pallas_call | solution.py:258
  72.4 2.6 %collective-permute-done.10.refs_2_ = bf16[4,64,640]{2,1,0:T(8,128)(2,1)S(1)} collective-permute-done((bf16[4,64,640]{2,1,0:T(8,128)(2,1)S(1)}, bf16[4,64,640]{2,1,0:T(8,128)(2,1)S(1)}, u32[]{:S(2)}, u32[]{:S(2)}) %collective-permute-start.10) | collective-permute-done | bytes 327712 | tf_op jit(solution)/shard_map/ppermute | solution.py:422
  75.0 1.9 %collective-permute-done.11.refs_3_ = bf16[4,64,640]{2,1,0:T(8,128)(2,1)S(1)} collective-permute-done((bf16[4,64,640]{2,1,0:T(8,128)(2,1)S(1)}, bf16[4,64,640]{2,1,0:T(8,128)(2,1)S(1)}, u32[]{:S(2)}, u32[]{:S(2)}) %collective-permute-start.11) | collective-permute-done | bytes 327712 | tf_op jit(solution)/shard_map/ppermute | solution.py:423
  79.0 2.3 %outer.1 = (bf16[4,2,8,1280]{3,2,1,0:T(8,128)(2,1)S(1)}, bf16[4,2,8,1280]{3,2,1,0:T(8,128)(2,1)S(1)}) custom-call(s32[19]{0:T(128)S(1)} %stack.137.ints, f32[1]{0:T(128)S(6)} %mul.258.factor_ref, bf16[8,128,160]{2,1,0:T(8,128)(2,1)S(1)} %get-tuple-element.48.zonal_ref, f32[8,128,256]{2,1,0:T(8,128)S(1)} %get-tuple-element.49.window_ref, ...), custom_call_target="tpu_custom_call" | custom-call | flops 1000000000 | bytes 4194304 | tf_op jit(solution)/shard_map/outer/pallas_call | solution.py:314
  81.3 4.0 %collective-permute-start.15 = (bf16[4,2,8,1280]{3,2,1,0:T(8,128)(2,1)S(1)}, bf16[4,2,8,1280]{3,2,1,0:T(8,128)(2,1)S(1)}, u32[]{:S(2)}, u32[]{:S(2)}) collective-permute-start(bf16[4,2,8,1280]{3,2,1,0:T(8,128)(2,1)S(1)} %get-tuple-element.54), channel_id=1, source_target_pairs={{0,8},{1,136},{8,0},{9,128},{128,9},{129,137},{136,1},{137,129},{2... | collective-permute-start | bytes 491528 | tf_op jit(solution)/shard_map/ppermute | solution.py:430
  85.3 1.9 %collective-permute-start.16 = (bf16[4,2,8,1280]{3,2,1,0:T(8,128)(2,1)S(1)}, bf16[4,2,8,1280]{3,2,1,0:T(8,128)(2,1)S(1)}, u32[]{:S(2)}, u32[]{:S(2)}) collective-permute-start(bf16[4,2,8,1280]{3,2,1,0:T(8,128)(2,1)S(1)} %get-tuple-element.55), channel_id=1, source_target_pairs={{0,0},{1,128},{8,8},{9,136},{128,1},{129,129},{136,9},{137,137},{2... | collective-permute-start | bytes 491528 | tf_op jit(solution)/shard_map/ppermute | solution.py:430
  87.2 2.2 %collective-permute-done.15.far.refs_0_ = bf16[4,2,8,1280]{3,2,1,0:T(8,128)(2,1)S(1)} collective-permute-done((bf16[4,2,8,1280]{3,2,1,0:T(8,128)(2,1)S(1)}, bf16[4,2,8,1280]{3,2,1,0:T(8,128)(2,1)S(1)}, u32[]{:S(2)}, u32[]{:S(2)}) %collective-permute-start.15) | collective-permute-done | bytes 163872 | tf_op jit(solution)/shard_map/ppermute | solution.py:430
  89.4 2.5 %collective-permute-done.16.near.refs_1_ = bf16[4,2,8,1280]{3,2,1,0:T(8,128)(2,1)S(1)} collective-permute-done((bf16[4,2,8,1280]{3,2,1,0:T(8,128)(2,1)S(1)}, bf16[4,2,8,1280]{3,2,1,0:T(8,128)(2,1)S(1)}, u32[]{:S(2)}, u32[]{:S(2)}) %collective-permute-start.16) | collective-permute-done | bytes 163872 | tf_op jit(solution)/shard_map/ppermute | solution.py:430
  92.5 1.4 %collective-permute-start.18 = (bf16[2,2,8,1280]{3,2,1,0:T(8,128)(2,1)S(1)}, bf16[2,2,8,1280]{3,2,1,0:T(8,128)(2,1)S(1)}, u32[]{:S(2)}, u32[]{:S(2)}) collective-permute-start(bf16[2,2,8,1280]{3,2,1,0:T(8,128)(2,1)S(1)} %get-tuple-element.57), channel_id=1, source_target_pairs={{0,2},{2,0},{4,6},{6,4},{1,3},{3,1},{5,7},{7,5},{8,10},{10,8},{12,... | collective-permute-start | bytes 245768 | tf_op jit(solution)/shard_map/ppermute | solution.py:434
  93.9 1.4 %collective-permute-start.19 = (bf16[2,2,8,1280]{3,2,1,0:T(8,128)(2,1)S(1)}, bf16[2,2,8,1280]{3,2,1,0:T(8,128)(2,1)S(1)}, u32[]{:S(2)}, u32[]{:S(2)}) collective-permute-start(bf16[2,2,8,1280]{3,2,1,0:T(8,128)(2,1)S(1)} %get-tuple-element.58), channel_id=1, source_target_pairs={{0,6},{2,4},{4,2},{6,0},{1,7},{3,5},{5,3},{7,1},{8,14},{10,12},{12... | collective-permute-start | bytes 245768 | tf_op jit(solution)/shard_map/ppermute | solution.py:434
  95.8 1.4 %collective-permute-done.17.refs_2_ = bf16[2,2,8,1280]{3,2,1,0:T(8,128)(2,1)S(1)} collective-permute-done((bf16[2,2,8,1280]{3,2,1,0:T(8,128)(2,1)S(1)}, bf16[2,2,8,1280]{3,2,1,0:T(8,128)(2,1)S(1)}, u32[]{:S(2)}, u32[]{:S(2)}) %collective-permute-start.17) | collective-permute-done | bytes 81952 | tf_op jit(solution)/shard_map/ppermute | solution.py:434
  (51 shorter events, 18.5 us)
Async XLA Ops:
  2.5 14.9 %collective-permute-start = (bf16[64,2560]{1,0:T(8,128)(2,1)S(1)}, bf16[64,2560]{1,0:T(8,128)(2,1)S(1)}, u32[]{:S(2)}, u32[]{:S(2)}) collective-permute-start(bf16[64,2560]{1,0:T(8,128)(2,1)S(1)} %bitcast.45), channel_id=1, source_target_pairs={{0,0},{1,65},{2,16},{3,81},{4,32},{5,97},{6,48},{7,113},{8,64},{9,... | collective-permute-start | bytes 983048 | tf_op jit(solution)/shard_map/ppermute | solution.py:383
  17.5 40.2 %collective-permute-start.9 = (bf16[480,2560]{1,0:T(8,128)(2,1)S(1)}, bf16[480,2560]{1,0:T(8,128)(2,1)S(1)}, u32[]{:S(2)}, u32[]{:S(2)}) collective-permute-start(bf16[480,2560]{1,0:T(8,128)(2,1)S(1)} %bitcast.43), channel_id=1, source_target_pairs={{0,128},{1,137},{128,8},{129,1},{8,136},{9,129},{136,0},{137,9},{2... | collective-permute-start | bytes 7372808 | tf_op jit(solution)/shard_map/ppermute | solution.py:409
  17.6 13.7 %collective-permute-start.2 = (bf16[64,2560]{1,0:T(8,128)(2,1)S(1)}, bf16[64,2560]{1,0:T(8,128)(2,1)S(1)}, u32[]{:S(2)}, u32[]{:S(2)}) collective-permute-start(bf16[64,2560]{1,0:T(8,128)(2,1)S(1)} %collective-permute-done.refs_0_), channel_id=1, source_target_pairs={{0,1},{1,0},{2,3},{3,2},{4,5},{5,4},{6,7},{7,6},{8,9},{9,8},{10,11... | collective-permute-start | bytes 983048 | tf_op jit(solution)/shard_map/ppermute | solution.py:411
  27.7 7.6 %collective-permute-start.1 = (bf16[64,2560]{1,0:T(8,128)(2,1)S(1)}, bf16[64,2560]{1,0:T(8,128)(2,1)S(1)}, u32[]{:S(2)}, u32[]{:S(2)}) collective-permute-start(bf16[64,2560]{1,0:T(8,128)(2,1)S(1)} %collective-permute-done.refs_0_), channel_id=1, source_target_pairs={{0,16},{1,113},{16,32},{17,1},{32,48},{33,17},{48,64},{49,33},{64,... | collective-permute-start | bytes 983048 | tf_op jit(solution)/shard_map/ppermute | solution.py:414
  31.3 7.5 %collective-permute-start.3 = (bf16[64,2560]{1,0:T(8,128)(2,1)S(1)}, bf16[64,2560]{1,0:T(8,128)(2,1)S(1)}, u32[]{:S(2)}, u32[]{:S(2)}) collective-permute-start(bf16[64,2560]{1,0:T(8,128)(2,1)S(1)} %collective-permute-done.2), channel_id=1, source_target_pairs={{0,16},{1,113},{16,32},{17,1},{32,48},{33,17},{48,64},{49,33},{64,... | collective-permute-start | bytes 983048 | tf_op jit(solution)/shard_map/ppermute | solution.py:417
  35.3 7.4 %collective-permute-start.4 = (bf16[64,2560]{1,0:T(8,128)(2,1)S(1)}, bf16[64,2560]{1,0:T(8,128)(2,1)S(1)}, u32[]{:S(2)}, u32[]{:S(2)}) collective-permute-start(bf16[64,2560]{1,0:T(8,128)(2,1)S(1)} %collective-permute-done.1.refs_1_), channel_id=1, source_target_pairs={{0,16},{1,113},{16,32},{17,1},{32,48},{33,17},{48,64},{49,33},{64,... | collective-permute-start | bytes 983048 | tf_op jit(solution)/shard_map/ppermute | solution.py:414
  38.8 7.4 %collective-permute-start.5 = (bf16[64,2560]{1,0:T(8,128)(2,1)S(1)}, bf16[64,2560]{1,0:T(8,128)(2,1)S(1)}, u32[]{:S(2)}, u32[]{:S(2)}) collective-permute-start(bf16[64,2560]{1,0:T(8,128)(2,1)S(1)} %collective-permute-done.3.refs_2_), channel_id=1, source_target_pairs={{0,16},{1,113},{16,32},{17,1},{32,48},{33,17},{48,64},{49,33},{64,... | collective-permute-start | bytes 983048 | tf_op jit(solution)/shard_map/ppermute | solution.py:417
  42.8 7.4 %collective-permute-start.6 = (bf16[64,2560]{1,0:T(8,128)(2,1)S(1)}, bf16[64,2560]{1,0:T(8,128)(2,1)S(1)}, u32[]{:S(2)}, u32[]{:S(2)}) collective-permute-start(bf16[64,2560]{1,0:T(8,128)(2,1)S(1)} %collective-permute-done.4.refs_3_), channel_id=1, source_target_pairs={{0,16},{1,113},{16,32},{17,1},{32,48},{33,17},{48,64},{49,33},{64,... | collective-permute-start | bytes 983048 | tf_op jit(solution)/shard_map/ppermute | solution.py:414
  46.3 7.4 %collective-permute-start.7 = (bf16[64,2560]{1,0:T(8,128)(2,1)S(1)}, bf16[64,2560]{1,0:T(8,128)(2,1)S(1)}, u32[]{:S(2)}, u32[]{:S(2)}) collective-permute-start(bf16[64,2560]{1,0:T(8,128)(2,1)S(1)} %collective-permute-done.5.refs_4_), channel_id=1, source_target_pairs={{0,16},{1,113},{16,32},{17,1},{32,48},{33,17},{48,64},{49,33},{64,... | collective-permute-start | bytes 983048 | tf_op jit(solution)/shard_map/ppermute | solution.py:417
  50.2 7.4 %collective-permute-start.8 = (bf16[64,2560]{1,0:T(8,128)(2,1)S(1)}, bf16[64,2560]{1,0:T(8,128)(2,1)S(1)}, u32[]{:S(2)}, u32[]{:S(2)}) collective-permute-start(bf16[64,2560]{1,0:T(8,128)(2,1)S(1)} %collective-permute-done.6.refs_5_), channel_id=1, source_target_pairs={{0,16},{1,113},{16,32},{17,1},{32,48},{33,17},{48,64},{49,33},{64,... | collective-permute-start | bytes 983048 | tf_op jit(solution)/shard_map/ppermute | solution.py:414
  61.6 7.5 %collective-permute-start.12 = (bf16[8,64,480]{2,1,0:T(8,128)(2,1)S(1)}, bf16[8,64,480]{2,1,0:T(8,128)(2,1)S(1)}, u32[]{:S(2)}, u32[]{:S(2)}) collective-permute-start(bf16[8,64,480]{2,1,0:T(8,128)(2,1)S(1)} %get-tuple-element.43), channel_id=1, source_target_pairs={{0,1},{1,0},{2,3},{3,2},{4,5},{5,4},{6,7},{7,6},{8,9},{9,8},{10,11... | collective-permute-start | bytes 1474568 | tf_op jit(solution)/shard_map/ppermute | solution.py:424
  65.6 9.4 %collective-permute-start.10 = (bf16[4,64,640]{2,1,0:T(8,128)(2,1)S(1)}, bf16[4,64,640]{2,1,0:T(8,128)(2,1)S(1)}, u32[]{:S(2)}, u32[]{:S(2)}) collective-permute-start(bf16[4,64,640]{2,1,0:T(8,128)(2,1)S(1)} %get-tuple-element.38), channel_id=1, source_target_pairs={{0,2},{2,4},{3,1},{4,6},{5,3},{6,14},{7,5},{14,12},{15,7},{12,10},... | collective-permute-start | bytes 983048 | tf_op jit(solution)/shard_map/ppermute | solution.py:422
  66.9 10.0 %collective-permute-start.11 = (bf16[4,64,640]{2,1,0:T(8,128)(2,1)S(1)}, bf16[4,64,640]{2,1,0:T(8,128)(2,1)S(1)}, u32[]{:S(2)}, u32[]{:S(2)}) collective-permute-start(bf16[4,64,640]{2,1,0:T(8,128)(2,1)S(1)} %get-tuple-element.39), channel_id=1, source_target_pairs={{1,2},{3,4},{2,1},{5,6},{4,3},{7,14},{6,5},{15,12},{14,7},{13,10},... | collective-permute-start | bytes 983048 | tf_op jit(solution)/shard_map/ppermute | solution.py:423
  76.9 1.6 %collective-permute-start.13 = (bf16[4,64,640]{2,1,0:T(8,128)(2,1)S(1)}, bf16[4,64,640]{2,1,0:T(8,128)(2,1)S(1)}, u32[]{:S(2)}, u32[]{:S(2)}) collective-permute-start(bf16[4,64,640]{2,1,0:T(8,128)(2,1)S(1)} %collective-permute-done.10.refs_2_), channel_id=1, source_target_pairs={{0,1},{1,0},{2,3},{3,2},{4,5},{5,4},{6,7},{7,6},{8,9},{9,8},{10,11... | collective-permute-start | bytes 983048 | tf_op jit(solution)/shard_map/ppermute | solution.py:427
  76.9 2.1 %collective-permute-start.14 = (bf16[4,64,640]{2,1,0:T(8,128)(2,1)S(1)}, bf16[4,64,640]{2,1,0:T(8,128)(2,1)S(1)}, u32[]{:S(2)}, u32[]{:S(2)}) collective-permute-start(bf16[4,64,640]{2,1,0:T(8,128)(2,1)S(1)} %collective-permute-done.11.refs_3_), channel_id=1, source_target_pairs={{0,1},{1,0},{2,3},{3,2},{4,5},{5,4},{6,7},{7,6},{8,9},{9,8},{10,11... | collective-permute-start | bytes 983048 | tf_op jit(solution)/shard_map/ppermute | solution.py:427
  81.3 8.1 %collective-permute-start.15 = (bf16[4,2,8,1280]{3,2,1,0:T(8,128)(2,1)S(1)}, bf16[4,2,8,1280]{3,2,1,0:T(8,128)(2,1)S(1)}, u32[]{:S(2)}, u32[]{:S(2)}) collective-permute-start(bf16[4,2,8,1280]{3,2,1,0:T(8,128)(2,1)S(1)} %get-tuple-element.54), channel_id=1, source_target_pairs={{0,8},{1,136},{8,0},{9,128},{128,9},{129,137},{136,1},{137,129},{2... | collective-permute-start | bytes 491528 | tf_op jit(solution)/shard_map/ppermute | solution.py:430
  85.3 6.6 %collective-permute-start.16 = (bf16[4,2,8,1280]{3,2,1,0:T(8,128)(2,1)S(1)}, bf16[4,2,8,1280]{3,2,1,0:T(8,128)(2,1)S(1)}, u32[]{:S(2)}, u32[]{:S(2)}) collective-permute-start(bf16[4,2,8,1280]{3,2,1,0:T(8,128)(2,1)S(1)} %get-tuple-element.55), channel_id=1, source_target_pairs={{0,0},{1,128},{8,8},{9,136},{128,1},{129,129},{136,9},{137,137},{2... | collective-permute-start | bytes 491528 | tf_op jit(solution)/shard_map/ppermute | solution.py:430
  92.0 5.3 %collective-permute-start.17 = (bf16[2,2,8,1280]{3,2,1,0:T(8,128)(2,1)S(1)}, bf16[2,2,8,1280]{3,2,1,0:T(8,128)(2,1)S(1)}, u32[]{:S(2)}, u32[]{:S(2)}) collective-permute-start(bf16[2,2,8,1280]{3,2,1,0:T(8,128)(2,1)S(1)} %get-tuple-element.56), channel_id=1, source_target_pairs={{0,4},{2,6},{4,0},{6,2},{1,5},{3,7},{5,1},{7,3},{8,12},{10,14},{12... | collective-permute-start | bytes 245768 | tf_op jit(solution)/shard_map/ppermute | solution.py:434
  92.5 6.0 %collective-permute-start.18 = (bf16[2,2,8,1280]{3,2,1,0:T(8,128)(2,1)S(1)}, bf16[2,2,8,1280]{3,2,1,0:T(8,128)(2,1)S(1)}, u32[]{:S(2)}, u32[]{:S(2)}) collective-permute-start(bf16[2,2,8,1280]{3,2,1,0:T(8,128)(2,1)S(1)} %get-tuple-element.57), channel_id=1, source_target_pairs={{0,2},{2,0},{4,6},{6,4},{1,3},{3,1},{5,7},{7,5},{8,10},{10,8},{12,... | collective-permute-start | bytes 245768 | tf_op jit(solution)/shard_map/ppermute | solution.py:434
  93.9 5.3 %collective-permute-start.19 = (bf16[2,2,8,1280]{3,2,1,0:T(8,128)(2,1)S(1)}, bf16[2,2,8,1280]{3,2,1,0:T(8,128)(2,1)S(1)}, u32[]{:S(2)}, u32[]{:S(2)}) collective-permute-start(bf16[2,2,8,1280]{3,2,1,0:T(8,128)(2,1)S(1)} %get-tuple-element.58), channel_id=1, source_target_pairs={{0,6},{2,4},{4,2},{6,0},{1,7},{3,5},{5,3},{7,1},{8,14},{10,12},{12... | collective-permute-start | bytes 245768 | tf_op jit(solution)/shard_map/ppermute | solution.py:434
  95.3 5.6 %collective-permute-start.20 = (bf16[4,2,8,1280]{3,2,1,0:T(8,128)(2,1)S(1)}, bf16[4,2,8,1280]{3,2,1,0:T(8,128)(2,1)S(1)}, u32[]{:S(2)}, u32[]{:S(2)}) collective-permute-start(bf16[4,2,8,1280]{3,2,1,0:T(8,128)(2,1)S(1)} %collective-permute-done.15.far.refs_0_), channel_id=1, source_target_pairs={{0,1},{1,0},{2,3},{3,2},{4,5},{5,4},{6,7},{7,6},{8,9},{9,8},{10,11... | collective-permute-start | bytes 491528 | tf_op jit(solution)/shard_map/ppermute | solution.py:435
  95.3 5.6 %collective-permute-start.21 = (bf16[4,2,8,1280]{3,2,1,0:T(8,128)(2,1)S(1)}, bf16[4,2,8,1280]{3,2,1,0:T(8,128)(2,1)S(1)}, u32[]{:S(2)}, u32[]{:S(2)}) collective-permute-start(bf16[4,2,8,1280]{3,2,1,0:T(8,128)(2,1)S(1)} %collective-permute-done.16.near.refs_1_), channel_id=1, source_target_pairs={{0,1},{1,0},{2,3},{3,2},{4,5},{5,4},{6,7},{7,6},{8,9},{9,8},{10,11... | collective-permute-start | bytes 491528 | tf_op jit(solution)/shard_map/ppermute | solution.py:435
  97.2 2.8 %collective-permute-start.22 = (bf16[2,2,8,1280]{3,2,1,0:T(8,128)(2,1)S(1)}, bf16[2,2,8,1280]{3,2,1,0:T(8,128)(2,1)S(1)}, u32[]{:S(2)}, u32[]{:S(2)}) collective-permute-start(bf16[2,2,8,1280]{3,2,1,0:T(8,128)(2,1)S(1)} %collective-permute-done.17.refs_2_), channel_id=1, source_target_pairs={{0,1},{1,0},{2,3},{3,2},{4,5},{5,4},{6,7},{7,6},{8,9},{9,8},{10,11... | collective-permute-start | bytes 245768 | tf_op jit(solution)/shard_map/ppermute | solution.py:435
  99.3 1.7 %collective-permute-start.24 = (bf16[2,2,8,1280]{3,2,1,0:T(8,128)(2,1)S(1)}, bf16[2,2,8,1280]{3,2,1,0:T(8,128)(2,1)S(1)}, u32[]{:S(2)}, u32[]{:S(2)}) collective-permute-start(bf16[2,2,8,1280]{3,2,1,0:T(8,128)(2,1)S(1)} %collective-permute-done.19.refs_4_), channel_id=1, source_target_pairs={{0,1},{1,0},{2,3},{3,2},{4,5},{5,4},{6,7},{7,6},{8,9},{9,8},{10,11... | collective-permute-start | bytes 245768 | tf_op jit(solution)/shard_map/ppermute | solution.py:435
  (4 other events, 49.3 us)

commit v12 on v11

--- a/solution.py
+++ b/solution.py
@@ -12,6 +12,7 @@
 COLS = 128
 HALF = COLS // 2
 KEY_ROWS = ROWS + 2 * WIN
+EARLY = 6
 EPS = 1e-06
 BIG = 1e30
 LOG2E = 1.4426950408889634
@@ -113,27 +114,49 @@
     return [p[:, r].reshape(8 * groups, QKV).astype(jnp.bfloat16) for r in range(ROWS)]
 
 
-def project_kernel(flags, *refs):
-    pieces, (own, partner), (keep, send, edge, give, x_ref) = refs[:8], refs[8:10], refs[10:]
+def products(flags, pieces, own, partner, x_ref):
     for g, piece in enumerate(pieces):
         x_ref[64 * g : 64 * (g + 1), :] = piece[...]
-    p = lax.dot_general(x_ref[...], own[...], NT, preferred_element_type=jnp.float32)
-    own_rows = normalized(p)
-    p = lax.dot_general(x_ref[...], partner[...], NT, preferred_element_type=jnp.float32)
-    other_rows = normalized(p)
+    return [
+        normalized(lax.dot_general(x_ref[...], w[...], NT, preferred_element_type=jnp.float32))
+        for w in (own, partner)
+    ]
+
+
+def by_head(flags, rows, store):
+    @pl.when(flags[0] == 1)
+    def _():
+        store(rows[0], rows[1])
+
+    @pl.when(flags[0] != 1)
+    def _():
+        store(rows[1], rows[0])
+
+
+def project_first_kernel(flags, *refs):
+    pieces, (own, partner, keep, send, x_ref) = refs[:EARLY], refs[EARLY:]
 
     def store(first, second):
         for r in range(ROWS):
             keep[r] = first[r]
             send[r] = second[r]
 
-    @pl.when(flags[0] == 1)
-    def _():
-        store(own_rows, other_rows)
-
-    @pl.when(flags[0] != 1)
-    def _():
-        store(other_rows, own_rows)
+    by_head(flags, products(flags, pieces, own, partner, x_ref), store)
+
+
+def project_last_kernel(flags, *refs):
+    pieces, (own, partner, keep_0, send_0, keep, send, edge, give, x_ref) = refs[: 8 - EARLY], refs[8 - EARLY :]
+    early = 8 * EARLY
+    for r in range(ROWS):
+        keep[r, :early] = keep_0[r]
+        send[r, :early] = send_0[r]
+
+    def store(first, second):
+        for r in range(ROWS):
+            keep[r, early:] = first[r]
+            send[r, early:] = second[r]
+
+    by_head(flags, products(flags, pieces, own, partner, x_ref), store)
 
     def store_edges(top, bottom):
         for r in range(ROWS):
@@ -150,20 +173,22 @@
 
 
 def project(flags, pieces, own, partner):
-    whole = jax.ShapeDtypeStruct((ROWS, HALF, QKV), jnp.bfloat16)
-    part = jax.ShapeDtypeStruct((WIN, HALF, 4 * HEAD_DIM), jnp.bfloat16)
-    return pl.pallas_call(
-        project_kernel,
-        out_shape=[whole, whole, part, part],
-        in_specs=[SMEM] + [VMEM] * 10,
-        out_specs=[VMEM] * 4,
-        scratch_shapes=[pltpu.VMEM((512, own.shape[1]), jnp.bfloat16)],
-        compiler_params=pltpu.CompilerParams(vmem_limit_bytes=20 * MIB),
-        cost_estimate=pl.CostEstimate(
-            flops=2 * 512 * 960 * 2560, bytes_accessed=8 * MIB, transcendentals=0
-        ),
-        name="project",
-    )(flags, *pieces, own, partner)
+    def call(kernel, shapes, pieces, extra, cost, name):
+        return pl.pallas_call(
+            kernel,
+            out_shape=[jax.ShapeDtypeStruct(shape, jnp.bfloat16) for shape in shapes],
+            in_specs=[SMEM] + [VMEM] * (len(pieces) + 2 + len(extra)),
+            out_specs=[VMEM] * len(shapes),
+            scratch_shapes=[pltpu.VMEM((64 * len(pieces), own.shape[1]), jnp.bfloat16)],
+            compiler_params=pltpu.CompilerParams(vmem_limit_bytes=20 * MIB),
+            cost_estimate=pl.CostEstimate(flops=cost, bytes_accessed=MIB, transcendentals=0),
+            name=name,
+        )(flags, *pieces, own, partner, *extra)
+
+    some, whole = (ROWS, 8 * EARLY, QKV), (ROWS, HALF, QKV)
+    part = (WIN, HALF, 4 * HEAD_DIM)
+    first = call(project_first_kernel, [some] * 2, pieces[:EARLY], [], 2 * 10**10, "project_first")
+    return call(project_last_kernel, [whole] * 2 + [part] * 2, pieces[EARLY:], first, 10**8, "project_last")
 
 
 def put(ks, vs, first, key, value):

time: 103 us -> 102 us (level)
  Pallas kernels: 10.9 us -> 12.4 us
  waiting for transfers between devices: 23 us -> 21.5 us
    ppermute x4, waiting for transfers between devices: 7.7 us -> 3.78 us  [body(): a = lax.ppermute(a, ('z', 'core'), ring_perm())]
    ppermute x1, waiting for transfers between devices: 0.01 us -> 1.77 us  [body(): partner = lax.ppermute(own, ('y_lo', 'y_hi', 'core'), weight_perm())]
    pallas_call x1 -> x2, Pallas kernels: 3.92 us -> 5.47 us  [call(): pl.pallas_call(kernel, out_shape=[jax.ShapeDtypeStruct(shape, jnp.bfloat1...]
  transfers between devices with their start and end apart: 25 -> 25, of which waited for: 17 -> 17; matrix products, arithmetic and copies ran while one was open for 4% -> 3% of each run, Pallas kernels for 3% -> 6%
where the time goes in v12:
time: 102 us; the launch traced here: 101 us
  starting transfers between devices  59.8 us (59%)
  waiting for transfers between devices  21.5 us (21%)
  Pallas kernels  12.4 us (12%)
  local copies, waits for them, and re-layouts  3.15 us (3%)
  other arithmetic  2.54 us (2%)
  between operations  1.41 us (1%)
    ppermute x4, starting transfers between devices, body(): a = lax.ppermute(a, ('z', 'core'), ring_perm())  13.8 us
    ppermute x1, starting transfers between devices, body(): a, b = (first, lax.ppermute(first, 'core', SWAP))  10.3 us
    ppermute x1, starting transfers between devices, body(): first = lax.ppermute(normed, AXES, spread_perm())  9.65 us
    ppermute x3, starting transfers between devices, body(): b = lax.ppermute(b, ('z', 'core'), ring_perm())  8.07 us
    ppermute x2, starting transfers between devices, body(): lax.ppermute(chunks[k], ('y_lo', 'y_hi', 'core'), return_perm(k))  5.92 us
    pallas_call x2, Pallas kernels, call(): pl.pallas_call(kernel, out_shape=[jax.ShapeDtypeStruct(shape, jnp.bfloat1...  5.47 us
    ppermute x2, waiting for transfers between devices, body(): lax.ppermute(chunks[k], ('y_lo', 'y_hi', 'core'), return_perm(k))  4.71 us
    ppermute x4, waiting for transfers between devices, body(): a = lax.ppermute(a, ('z', 'core'), ring_perm())  3.78 us
  transfers between devices with their start and end apart: 25, of which 17 were waited for; matrix products, arithmetic and copies ran while one was open for 3% of the time, Pallas kernels for 6%

profile of v12, /device:TPU:1, one launch (start us, length us, event | category | flops | bytes accessed | tf_op | source)
XLA Modules:
  0.0 100.9 jit_solution(17199908743021653237)
XLA Ops:
  2.5 9.6 %collective-permute-start = (bf16[64,2560]{1,0:T(8,128)(2,1)S(1)}, bf16[64,2560]{1,0:T(8,128)(2,1)S(1)}, u32[]{:S(2)}, u32[]{:S(2)}) collective-permute-start(bf16[64,2560]{1,0:T(8,128)(2,1)S(1)} %bitcast.46), channel_id=1, source_target_pairs={{0,0},{1,65},{2,16},{3,81},{4,32},{5,97},{6,48},{7,113},{8,64},{9,... | collective-permute-start | bytes 983048 | tf_op jit(solution)/shard_map/ppermute | solution.py:408
  17.4 10.3 %collective-permute-start.1 = (bf16[64,2560]{1,0:T(8,128)(2,1)S(1)}, bf16[64,2560]{1,0:T(8,128)(2,1)S(1)}, u32[]{:S(2)}, u32[]{:S(2)}) collective-permute-start(bf16[64,2560]{1,0:T(8,128)(2,1)S(1)} %collective-permute-done.refs_0_), channel_id=1, source_target_pairs={{0,1},{1,0},{2,3},{3,2},{4,5},{5,4},{6,7},{7,6},{8,9},{9,8},{10,11... | collective-permute-start | bytes 983048 | tf_op jit(solution)/shard_map/ppermute | solution.py:436
  27.7 3.6 %collective-permute-start.5 = (bf16[64,2560]{1,0:T(8,128)(2,1)S(1)}, bf16[64,2560]{1,0:T(8,128)(2,1)S(1)}, u32[]{:S(2)}, u32[]{:S(2)}) collective-permute-start(bf16[64,2560]{1,0:T(8,128)(2,1)S(1)} %collective-permute-done.refs_0_), channel_id=1, source_target_pairs={{0,16},{1,113},{16,32},{17,1},{32,48},{33,17},{48,64},{49,33},{64,... | collective-permute-start | bytes 983048 | tf_op jit(solution)/shard_map/ppermute | solution.py:439
  32.6 2.8 %collective-permute-done.5.refs_1_ = bf16[64,2560]{1,0:T(8,128)(2,1)S(1)} collective-permute-done((bf16[64,2560]{1,0:T(8,128)(2,1)S(1)}, bf16[64,2560]{1,0:T(8,128)(2,1)S(1)}, u32[]{:S(2)}, u32[]{:S(2)}) %collective-permute-start.5) | collective-permute-done | bytes 327712 | tf_op jit(solution)/shard_map/ppermute | solution.py:439
  35.3 3.4 %collective-permute-start.6 = (bf16[64,2560]{1,0:T(8,128)(2,1)S(1)}, bf16[64,2560]{1,0:T(8,128)(2,1)S(1)}, u32[]{:S(2)}, u32[]{:S(2)}) collective-permute-start(bf16[64,2560]{1,0:T(8,128)(2,1)S(1)} %collective-permute-done.5.refs_1_), channel_id=1, source_target_pairs={{0,16},{1,113},{16,32},{17,1},{32,48},{33,17},{48,64},{49,33},{64,... | collective-permute-start | bytes 983048 | tf_op jit(solution)/shard_map/ppermute | solution.py:439
  38.8 3.4 %collective-permute-start.3 = (bf16[64,2560]{1,0:T(8,128)(2,1)S(1)}, bf16[64,2560]{1,0:T(8,128)(2,1)S(1)}, u32[]{:S(2)}, u32[]{:S(2)}) collective-permute-start(bf16[64,2560]{1,0:T(8,128)(2,1)S(1)} %collective-permute-done.2.refs_2_), channel_id=1, source_target_pairs={{0,16},{1,113},{16,32},{17,1},{32,48},{33,17},{48,64},{49,33},{64,... | collective-permute-start | bytes 983048 | tf_op jit(solution)/shard_map/ppermute | solution.py:442
  42.8 3.4 %collective-permute-start.7 = (bf16[64,2560]{1,0:T(8,128)(2,1)S(1)}, bf16[64,2560]{1,0:T(8,128)(2,1)S(1)}, u32[]{:S(2)}, u32[]{:S(2)}) collective-permute-start(bf16[64,2560]{1,0:T(8,128)(2,1)S(1)} %collective-permute-done.6.refs_3_), channel_id=1, source_target_pairs={{0,16},{1,113},{16,32},{17,1},{32,48},{33,17},{48,64},{49,33},{64,... | collective-permute-start | bytes 983048 | tf_op jit(solution)/shard_map/ppermute | solution.py:439
  46.3 3.4 %collective-permute-start.4 = (bf16[64,2560]{1,0:T(8,128)(2,1)S(1)}, bf16[64,2560]{1,0:T(8,128)(2,1)S(1)}, u32[]{:S(2)}, u32[]{:S(2)}) collective-permute-start(bf16[64,2560]{1,0:T(8,128)(2,1)S(1)} %collective-permute-done.3.refs_4_), channel_id=1, source_target_pairs={{0,16},{1,113},{16,32},{17,1},{32,48},{33,17},{48,64},{49,33},{64,... | collective-permute-start | bytes 983048 | tf_op jit(solution)/shard_map/ppermute | solution.py:442
  50.2 3.4 %collective-permute-start.8 = (bf16[64,2560]{1,0:T(8,128)(2,1)S(1)}, bf16[64,2560]{1,0:T(8,128)(2,1)S(1)}, u32[]{:S(2)}, u32[]{:S(2)}) collective-permute-start(bf16[64,2560]{1,0:T(8,128)(2,1)S(1)} %collective-permute-done.7.refs_5_), channel_id=1, source_target_pairs={{0,16},{1,113},{16,32},{17,1},{32,48},{33,17},{48,64},{49,33},{64,... | collective-permute-start | bytes 983048 | tf_op jit(solution)/shard_map/ppermute | solution.py:439
  53.6 1.8 %collective-permute-done.9.refs_7_.refs_3_ = bf16[480,2560]{1,0:T(8,128)(2,1)S(1)} collective-permute-done((bf16[480,2560]{1,0:T(8,128)(2,1)S(1)}, bf16[480,2560]{1,0:T(8,128)(2,1)S(1)}, u32[]{:S(2)}, u32[]{:S(2)}) %collective-permute-start.9) | collective-permute-done | bytes 2457632 | tf_op jit(solution)/shard_map/ppermute | solution.py:434
  55.4 2.9 %project_first.1 = (bf16[8,48,480]{2,1,0:T(8,128)(2,1)S(1)}, bf16[8,48,480]{2,1,0:T(8,128)(2,1)S(1)}) custom-call(s32[2]{0:T(128)S(1)} %pad_add_fusion.flags, bf16[64,2560]{1,0:T(8,128)(2,1)S(1)} %collective-permute-done.refs_0_, bf16[64,2560]{1,0:T(8,128)(2,1)S(1)} %collective-permute-done.5.refs_1_, bf16[64,2560]{1,0:T(8,128)(2,1)S(1)} %collective-permute-done.2.refs_2_, ...), custom_call_target="tpu_custom_call" | custom-call | flops 20000000000 | bytes 1048576 | tf_op jit(solution)/shard_map/project_first/pallas_call | solution.py:177
  58.3 2.5 %project_last.1 = (bf16[8,64,480]{2,1,0:T(8,128)(2,1)S(1)}, bf16[8,64,480]{2,1,0:T(8,128)(2,1)S(1)}, bf16[4,64,640]{2,1,0:T(8,128)(2,1)S(1)}, bf16[4,64,640]{2,1,0:T(8,128)(2,1)S(1)}) custom-call(s32[2]{0:T(128)S(1)} %pad_add_fusion.flags, bf16[64,2560]{1,0:T(8,128)(2,1)S(1)} %collective-permute-done.4.refs_0_, ...), custom_call_target="tpu_custom_call" | custom-call | flops 100000000 | bytes 1048576 | tf_op jit(solution)/shard_map/project_last/pallas_call | solution.py:177
  60.9 3.3 %collective-permute-start.12 = (bf16[8,64,480]{2,1,0:T(8,128)(2,1)S(1)}, bf16[8,64,480]{2,1,0:T(8,128)(2,1)S(1)}, u32[]{:S(2)}, u32[]{:S(2)}) collective-permute-start(bf16[8,64,480]{2,1,0:T(8,128)(2,1)S(1)} %get-tuple-element.47), channel_id=1, source_target_pairs={{0,1},{1,0},{2,3},{3,2},{4,5},{5,4},{6,7},{7,6},{8,9},{9,8},{10,11... | collective-permute-start | bytes 1474568 | tf_op jit(solution)/shard_map/ppermute | solution.py:449
  65.5 2.1 %collective-permute-start.11 = (bf16[4,64,640]{2,1,0:T(8,128)(2,1)S(1)}, bf16[4,64,640]{2,1,0:T(8,128)(2,1)S(1)}, u32[]{:S(2)}, u32[]{:S(2)}) collective-permute-start(bf16[4,64,640]{2,1,0:T(8,128)(2,1)S(1)} %get-tuple-element.43), channel_id=1, source_target_pairs={{1,2},{3,4},{2,1},{5,6},{4,3},{7,14},{6,5},{15,12},{14,7},{13,10},... | collective-permute-start | bytes 983048 | tf_op jit(solution)/shard_map/ppermute | solution.py:448
  67.6 3.4 %inner.1 = (bf16[8,128,160]{2,1,0:T(8,128)(2,1)S(1)}, f32[8,128,256]{2,1,0:T(8,128)S(1)}, f32[10,128,128]{2,1,0:T(8,128)S(1)}, f32[2,16,128]{2,1,0:T(8,128)S(1)}) custom-call(s32[19]{0:T(128)S(1)} %stack.137.ints, f32[1]{0:T(128)S(6)} %mul.258.factor_ref, f32[64]{0:T(128)S(1)} %reshape.20.band, f32[16,128]{1,0:T(8,128)S(1)} %fusion.4.usable, ...), custom_call_target="tpu_custom_call" | custom-call | flops 10000000 | bytes 100000 | tf_op jit(solution)/shard_map/inner/pallas_call | solution.py:283
  71.0 2.6 %collective-permute-done.10.refs_2_ = bf16[4,64,640]{2,1,0:T(8,128)(2,1)S(1)} collective-permute-done((bf16[4,64,640]{2,1,0:T(8,128)(2,1)S(1)}, bf16[4,64,640]{2,1,0:T(8,128)(2,1)S(1)}, u32[]{:S(2)}, u32[]{:S(2)}) %collective-permute-start.10) | collective-permute-done | bytes 327712 | tf_op jit(solution)/shard_map/ppermute | solution.py:447
  73.6 1.9 %collective-permute-done.11.refs_3_ = bf16[4,64,640]{2,1,0:T(8,128)(2,1)S(1)} collective-permute-done((bf16[4,64,640]{2,1,0:T(8,128)(2,1)S(1)}, bf16[4,64,640]{2,1,0:T(8,128)(2,1)S(1)}, u32[]{:S(2)}, u32[]{:S(2)}) %collective-permute-start.11) | collective-permute-done | bytes 327712 | tf_op jit(solution)/shard_map/ppermute | solution.py:448
  77.6 2.3 %outer.1 = (bf16[4,2,8,1280]{3,2,1,0:T(8,128)(2,1)S(1)}, bf16[4,2,8,1280]{3,2,1,0:T(8,128)(2,1)S(1)}) custom-call(s32[19]{0:T(128)S(1)} %stack.137.ints, f32[1]{0:T(128)S(6)} %mul.258.factor_ref, bf16[8,128,160]{2,1,0:T(8,128)(2,1)S(1)} %get-tuple-element.52.zonal_ref, f32[8,128,256]{2,1,0:T(8,128)S(1)} %get-tuple-element.53.window_ref, ...), custom_call_target="tpu_custom_call" | custom-call | flops 1000000000 | bytes 4194304 | tf_op jit(solution)/shard_map/outer/pallas_call | solution.py:339
  79.9 4.0 %collective-permute-start.15 = (bf16[4,2,8,1280]{3,2,1,0:T(8,128)(2,1)S(1)}, bf16[4,2,8,1280]{3,2,1,0:T(8,128)(2,1)S(1)}, u32[]{:S(2)}, u32[]{:S(2)}) collective-permute-start(bf16[4,2,8,1280]{3,2,1,0:T(8,128)(2,1)S(1)} %get-tuple-element.58), channel_id=1, source_target_pairs={{0,8},{1,136},{8,0},{9,128},{128,9},{129,137},{136,1},{137,129},{2... | collective-permute-start | bytes 491528 | tf_op jit(solution)/shard_map/ppermute | solution.py:455
  83.9 1.9 %collective-permute-start.16 = (bf16[4,2,8,1280]{3,2,1,0:T(8,128)(2,1)S(1)}, bf16[4,2,8,1280]{3,2,1,0:T(8,128)(2,1)S(1)}, u32[]{:S(2)}, u32[]{:S(2)}) collective-permute-start(bf16[4,2,8,1280]{3,2,1,0:T(8,128)(2,1)S(1)} %get-tuple-element.59), channel_id=1, source_target_pairs={{0,0},{1,128},{8,8},{9,136},{128,1},{129,129},{136,9},{137,137},{2... | collective-permute-start | bytes 491528 | tf_op jit(solution)/shard_map/ppermute | solution.py:455
  85.8 2.2 %collective-permute-done.15.far.refs_0_ = bf16[4,2,8,1280]{3,2,1,0:T(8,128)(2,1)S(1)} collective-permute-done((bf16[4,2,8,1280]{3,2,1,0:T(8,128)(2,1)S(1)}, bf16[4,2,8,1280]{3,2,1,0:T(8,128)(2,1)S(1)}, u32[]{:S(2)}, u32[]{:S(2)}) %collective-permute-start.15) | collective-permute-done | bytes 163872 | tf_op jit(solution)/shard_map/ppermute | solution.py:455
  88.0 2.5 %collective-permute-done.16.near.refs_1_ = bf16[4,2,8,1280]{3,2,1,0:T(8,128)(2,1)S(1)} collective-permute-done((bf16[4,2,8,1280]{3,2,1,0:T(8,128)(2,1)S(1)}, bf16[4,2,8,1280]{3,2,1,0:T(8,128)(2,1)S(1)}, u32[]{:S(2)}, u32[]{:S(2)}) %collective-permute-start.16) | collective-permute-done | bytes 163872 | tf_op jit(solution)/shard_map/ppermute | solution.py:455
  91.2 1.4 %collective-permute-start.18 = (bf16[2,2,8,1280]{3,2,1,0:T(8,128)(2,1)S(1)}, bf16[2,2,8,1280]{3,2,1,0:T(8,128)(2,1)S(1)}, u32[]{:S(2)}, u32[]{:S(2)}) collective-permute-start(bf16[2,2,8,1280]{3,2,1,0:T(8,128)(2,1)S(1)} %get-tuple-element.61), channel_id=1, source_target_pairs={{0,2},{2,0},{4,6},{6,4},{1,3},{3,1},{5,7},{7,5},{8,10},{10,8},{12,... | collective-permute-start | bytes 245768 | tf_op jit(solution)/shard_map/ppermute | solution.py:459
  94.4 1.4 %collective-permute-done.17.refs_2_ = bf16[2,2,8,1280]{3,2,1,0:T(8,128)(2,1)S(1)} collective-permute-done((bf16[2,2,8,1280]{3,2,1,0:T(8,128)(2,1)S(1)}, bf16[2,2,8,1280]{3,2,1,0:T(8,128)(2,1)S(1)}, u32[]{:S(2)}, u32[]{:S(2)}) %collective-permute-start.17) | collective-permute-done | bytes 81952 | tf_op jit(solution)/shard_map/ppermute | solution.py:459
  (54 shorter events, 19.8 us)
Async XLA Ops:
  2.5 14.9 %collective-permute-start = (bf16[64,2560]{1,0:T(8,128)(2,1)S(1)}, bf16[64,2560]{1,0:T(8,128)(2,1)S(1)}, u32[]{:S(2)}, u32[]{:S(2)}) collective-permute-start(bf16[64,2560]{1,0:T(8,128)(2,1)S(1)} %bitcast.46), channel_id=1, source_target_pairs={{0,0},{1,65},{2,16},{3,81},{4,32},{5,97},{6,48},{7,113},{8,64},{9,... | collective-permute-start | bytes 983048 | tf_op jit(solution)/shard_map/ppermute | solution.py:408
  17.4 38.0 %collective-permute-start.9 = (bf16[480,2560]{1,0:T(8,128)(2,1)S(1)}, bf16[480,2560]{1,0:T(8,128)(2,1)S(1)}, u32[]{:S(2)}, u32[]{:S(2)}) collective-permute-start(bf16[480,2560]{1,0:T(8,128)(2,1)S(1)} %bitcast.43), channel_id=1, source_target_pairs={{0,128},{1,137},{128,8},{129,1},{8,136},{9,129},{136,0},{137,9},{2... | collective-permute-start | bytes 7372808 | tf_op jit(solution)/shard_map/ppermute | solution.py:434
  17.4 13.9 %collective-permute-start.1 = (bf16[64,2560]{1,0:T(8,128)(2,1)S(1)}, bf16[64,2560]{1,0:T(8,128)(2,1)S(1)}, u32[]{:S(2)}, u32[]{:S(2)}) collective-permute-start(bf16[64,2560]{1,0:T(8,128)(2,1)S(1)} %collective-permute-done.refs_0_), channel_id=1, source_target_pairs={{0,1},{1,0},{2,3},{3,2},{4,5},{5,4},{6,7},{7,6},{8,9},{9,8},{10,11... | collective-permute-start | bytes 983048 | tf_op jit(solution)/shard_map/ppermute | solution.py:436
  27.7 7.6 %collective-permute-start.5 = (bf16[64,2560]{1,0:T(8,128)(2,1)S(1)}, bf16[64,2560]{1,0:T(8,128)(2,1)S(1)}, u32[]{:S(2)}, u32[]{:S(2)}) collective-permute-start(bf16[64,2560]{1,0:T(8,128)(2,1)S(1)} %collective-permute-done.refs_0_), channel_id=1, source_target_pairs={{0,16},{1,113},{16,32},{17,1},{32,48},{33,17},{48,64},{49,33},{64,... | collective-permute-start | bytes 983048 | tf_op jit(solution)/shard_map/ppermute | solution.py:439
  31.3 7.5 %collective-permute-start.2 = (bf16[64,2560]{1,0:T(8,128)(2,1)S(1)}, bf16[64,2560]{1,0:T(8,128)(2,1)S(1)}, u32[]{:S(2)}, u32[]{:S(2)}) collective-permute-start(bf16[64,2560]{1,0:T(8,128)(2,1)S(1)} %collective-permute-done.1), channel_id=1, source_target_pairs={{0,16},{1,113},{16,32},{17,1},{32,48},{33,17},{48,64},{49,33},{64,... | collective-permute-start | bytes 983048 | tf_op jit(solution)/shard_map/ppermute | solution.py:442
  35.3 7.4 %collective-permute-start.6 = (bf16[64,2560]{1,0:T(8,128)(2,1)S(1)}, bf16[64,2560]{1,0:T(8,128)(2,1)S(1)}, u32[]{:S(2)}, u32[]{:S(2)}) collective-permute-start(bf16[64,2560]{1,0:T(8,128)(2,1)S(1)} %collective-permute-done.5.refs_1_), channel_id=1, source_target_pairs={{0,16},{1,113},{16,32},{17,1},{32,48},{33,17},{48,64},{49,33},{64,... | collective-permute-start | bytes 983048 | tf_op jit(solution)/shard_map/ppermute | solution.py:439
  38.8 7.4 %collective-permute-start.3 = (bf16[64,2560]{1,0:T(8,128)(2,1)S(1)}, bf16[64,2560]{1,0:T(8,128)(2,1)S(1)}, u32[]{:S(2)}, u32[]{:S(2)}) collective-permute-start(bf16[64,2560]{1,0:T(8,128)(2,1)S(1)} %collective-permute-done.2.refs_2_), channel_id=1, source_target_pairs={{0,16},{1,113},{16,32},{17,1},{32,48},{33,17},{48,64},{49,33},{64,... | collective-permute-start | bytes 983048 | tf_op jit(solution)/shard_map/ppermute | solution.py:442
  42.8 7.4 %collective-permute-start.7 = (bf16[64,2560]{1,0:T(8,128)(2,1)S(1)}, bf16[64,2560]{1,0:T(8,128)(2,1)S(1)}, u32[]{:S(2)}, u32[]{:S(2)}) collective-permute-start(bf16[64,2560]{1,0:T(8,128)(2,1)S(1)} %collective-permute-done.6.refs_3_), channel_id=1, source_target_pairs={{0,16},{1,113},{16,32},{17,1},{32,48},{33,17},{48,64},{49,33},{64,... | collective-permute-start | bytes 983048 | tf_op jit(solution)/shard_map/ppermute | solution.py:439
  46.3 12.0 %collective-permute-start.4 = (bf16[64,2560]{1,0:T(8,128)(2,1)S(1)}, bf16[64,2560]{1,0:T(8,128)(2,1)S(1)}, u32[]{:S(2)}, u32[]{:S(2)}) collective-permute-start(bf16[64,2560]{1,0:T(8,128)(2,1)S(1)} %collective-permute-done.3.refs_4_), channel_id=1, source_target_pairs={{0,16},{1,113},{16,32},{17,1},{32,48},{33,17},{48,64},{49,33},{64,... | collective-permute-start | bytes 983048 | tf_op jit(solution)/shard_map/ppermute | solution.py:442
  50.2 8.1 %collective-permute-start.8 = (bf16[64,2560]{1,0:T(8,128)(2,1)S(1)}, bf16[64,2560]{1,0:T(8,128)(2,1)S(1)}, u32[]{:S(2)}, u32[]{:S(2)}) collective-permute-start(bf16[64,2560]{1,0:T(8,128)(2,1)S(1)} %collective-permute-done.7.refs_5_), channel_id=1, source_target_pairs={{0,16},{1,113},{16,32},{17,1},{32,48},{33,17},{48,64},{49,33},{64,... | collective-permute-start | bytes 983048 | tf_op jit(solution)/shard_map/ppermute | solution.py:439
  60.9 6.7 %collective-permute-start.12 = (bf16[8,64,480]{2,1,0:T(8,128)(2,1)S(1)}, bf16[8,64,480]{2,1,0:T(8,128)(2,1)S(1)}, u32[]{:S(2)}, u32[]{:S(2)}) collective-permute-start(bf16[8,64,480]{2,1,0:T(8,128)(2,1)S(1)} %get-tuple-element.47), channel_id=1, source_target_pairs={{0,1},{1,0},{2,3},{3,2},{4,5},{5,4},{6,7},{7,6},{8,9},{9,8},{10,11... | collective-permute-start | bytes 1474568 | tf_op jit(solution)/shard_map/ppermute | solution.py:449
  64.2 9.4 %collective-permute-start.10 = (bf16[4,64,640]{2,1,0:T(8,128)(2,1)S(1)}, bf16[4,64,640]{2,1,0:T(8,128)(2,1)S(1)}, u32[]{:S(2)}, u32[]{:S(2)}) collective-permute-start(bf16[4,64,640]{2,1,0:T(8,128)(2,1)S(1)} %get-tuple-element.42), channel_id=1, source_target_pairs={{0,2},{2,4},{3,1},{4,6},{5,3},{6,14},{7,5},{14,12},{15,7},{12,10},... | collective-permute-start | bytes 983048 | tf_op jit(solution)/shard_map/ppermute | solution.py:447
  65.5 10.0 %collective-permute-start.11 = (bf16[4,64,640]{2,1,0:T(8,128)(2,1)S(1)}, bf16[4,64,640]{2,1,0:T(8,128)(2,1)S(1)}, u32[]{:S(2)}, u32[]{:S(2)}) collective-permute-start(bf16[4,64,640]{2,1,0:T(8,128)(2,1)S(1)} %get-tuple-element.43), channel_id=1, source_target_pairs={{1,2},{3,4},{2,1},{5,6},{4,3},{7,14},{6,5},{15,12},{14,7},{13,10},... | collective-permute-start | bytes 983048 | tf_op jit(solution)/shard_map/ppermute | solution.py:448
  75.5 1.6 %collective-permute-start.13 = (bf16[4,64,640]{2,1,0:T(8,128)(2,1)S(1)}, bf16[4,64,640]{2,1,0:T(8,128)(2,1)S(1)}, u32[]{:S(2)}, u32[]{:S(2)}) collective-permute-start(bf16[4,64,640]{2,1,0:T(8,128)(2,1)S(1)} %collective-permute-done.10.refs_2_), channel_id=1, source_target_pairs={{0,1},{1,0},{2,3},{3,2},{4,5},{5,4},{6,7},{7,6},{8,9},{9,8},{10,11... | collective-permute-start | bytes 983048 | tf_op jit(solution)/shard_map/ppermute | solution.py:452
  75.6 2.1 %collective-permute-start.14 = (bf16[4,64,640]{2,1,0:T(8,128)(2,1)S(1)}, bf16[4,64,640]{2,1,0:T(8,128)(2,1)S(1)}, u32[]{:S(2)}, u32[]{:S(2)}) collective-permute-start(bf16[4,64,640]{2,1,0:T(8,128)(2,1)S(1)} %collective-permute-done.11.refs_3_), channel_id=1, source_target_pairs={{0,1},{1,0},{2,3},{3,2},{4,5},{5,4},{6,7},{7,6},{8,9},{9,8},{10,11... | collective-permute-start | bytes 983048 | tf_op jit(solution)/shard_map/ppermute | solution.py:452
  79.9 8.1 %collective-permute-start.15 = (bf16[4,2,8,1280]{3,2,1,0:T(8,128)(2,1)S(1)}, bf16[4,2,8,1280]{3,2,1,0:T(8,128)(2,1)S(1)}, u32[]{:S(2)}, u32[]{:S(2)}) collective-permute-start(bf16[4,2,8,1280]{3,2,1,0:T(8,128)(2,1)S(1)} %get-tuple-element.58), channel_id=1, source_target_pairs={{0,8},{1,136},{8,0},{9,128},{128,9},{129,137},{136,1},{137,129},{2... | collective-permute-start | bytes 491528 | tf_op jit(solution)/shard_map/ppermute | solution.py:455
  83.9 6.6 %collective-permute-start.16 = (bf16[4,2,8,1280]{3,2,1,0:T(8,128)(2,1)S(1)}, bf16[4,2,8,1280]{3,2,1,0:T(8,128)(2,1)S(1)}, u32[]{:S(2)}, u32[]{:S(2)}) collective-permute-start(bf16[4,2,8,1280]{3,2,1,0:T(8,128)(2,1)S(1)} %get-tuple-element.59), channel_id=1, source_target_pairs={{0,0},{1,128},{8,8},{9,136},{128,1},{129,129},{136,9},{137,137},{2... | collective-permute-start | bytes 491528 | tf_op jit(solution)/shard_map/ppermute | solution.py:455
  90.6 5.2 %collective-permute-start.17 = (bf16[2,2,8,1280]{3,2,1,0:T(8,128)(2,1)S(1)}, bf16[2,2,8,1280]{3,2,1,0:T(8,128)(2,1)S(1)}, u32[]{:S(2)}, u32[]{:S(2)}) collective-permute-start(bf16[2,2,8,1280]{3,2,1,0:T(8,128)(2,1)S(1)} %get-tuple-element.60), channel_id=1, source_target_pairs={{0,4},{2,6},{4,0},{6,2},{1,5},{3,7},{5,1},{7,3},{8,12},{10,14},{12... | collective-permute-start | bytes 245768 | tf_op jit(solution)/shard_map/ppermute | solution.py:459
  91.2 6.0 %collective-permute-start.18 = (bf16[2,2,8,1280]{3,2,1,0:T(8,128)(2,1)S(1)}, bf16[2,2,8,1280]{3,2,1,0:T(8,128)(2,1)S(1)}, u32[]{:S(2)}, u32[]{:S(2)}) collective-permute-start(bf16[2,2,8,1280]{3,2,1,0:T(8,128)(2,1)S(1)} %get-tuple-element.61), channel_id=1, source_target_pairs={{0,2},{2,0},{4,6},{6,4},{1,3},{3,1},{5,7},{7,5},{8,10},{10,8},{12,... | collective-permute-start | bytes 245768 | tf_op jit(solution)/shard_map/ppermute | solution.py:459
  92.6 5.4 %collective-permute-start.19 = (bf16[2,2,8,1280]{3,2,1,0:T(8,128)(2,1)S(1)}, bf16[2,2,8,1280]{3,2,1,0:T(8,128)(2,1)S(1)}, u32[]{:S(2)}, u32[]{:S(2)}) collective-permute-start(bf16[2,2,8,1280]{3,2,1,0:T(8,128)(2,1)S(1)} %get-tuple-element.62), channel_id=1, source_target_pairs={{0,6},{2,4},{4,2},{6,0},{1,7},{3,5},{5,3},{7,1},{8,14},{10,12},{12... | collective-permute-start | bytes 245768 | tf_op jit(solution)/shard_map/ppermute | solution.py:459
  93.9 5.6 %collective-permute-start.20 = (bf16[4,2,8,1280]{3,2,1,0:T(8,128)(2,1)S(1)}, bf16[4,2,8,1280]{3,2,1,0:T(8,128)(2,1)S(1)}, u32[]{:S(2)}, u32[]{:S(2)}) collective-permute-start(bf16[4,2,8,1280]{3,2,1,0:T(8,128)(2,1)S(1)} %collective-permute-done.15.far.refs_0_), channel_id=1, source_target_pairs={{0,1},{1,0},{2,3},{3,2},{4,5},{5,4},{6,7},{7,6},{8,9},{9,8},{10,11... | collective-permute-start | bytes 491528 | tf_op jit(solution)/shard_map/ppermute | solution.py:460
  93.9 5.6 %collective-permute-start.21 = (bf16[4,2,8,1280]{3,2,1,0:T(8,128)(2,1)S(1)}, bf16[4,2,8,1280]{3,2,1,0:T(8,128)(2,1)S(1)}, u32[]{:S(2)}, u32[]{:S(2)}) collective-permute-start(bf16[4,2,8,1280]{3,2,1,0:T(8,128)(2,1)S(1)} %collective-permute-done.16.near.refs_1_), channel_id=1, source_target_pairs={{0,1},{1,0},{2,3},{3,2},{4,5},{5,4},{6,7},{7,6},{8,9},{9,8},{10,11... | collective-permute-start | bytes 491528 | tf_op jit(solution)/shard_map/ppermute | solution.py:460
  95.8 2.8 %collective-permute-start.22 = (bf16[2,2,8,1280]{3,2,1,0:T(8,128)(2,1)S(1)}, bf16[2,2,8,1280]{3,2,1,0:T(8,128)(2,1)S(1)}, u32[]{:S(2)}, u32[]{:S(2)}) collective-permute-start(bf16[2,2,8,1280]{3,2,1,0:T(8,128)(2,1)S(1)} %collective-permute-done.17.refs_2_), channel_id=1, source_target_pairs={{0,1},{1,0},{2,3},{3,2},{4,5},{5,4},{6,7},{7,6},{8,9},{9,8},{10,11... | collective-permute-start | bytes 245768 | tf_op jit(solution)/shard_map/ppermute | solution.py:460
  97.9 1.6 %collective-permute-start.24 = (bf16[2,2,8,1280]{3,2,1,0:T(8,128)(2,1)S(1)}, bf16[2,2,8,1280]{3,2,1,0:T(8,128)(2,1)S(1)}, u32[]{:S(2)}, u32[]{:S(2)}) collective-permute-start(bf16[2,2,8,1280]{3,2,1,0:T(8,128)(2,1)S(1)} %collective-permute-done.19.refs_4_), channel_id=1, source_target_pairs={{0,1},{1,0},{2,3},{3,2},{4,5},{5,4},{6,7},{7,6},{8,9},{9,8},{10,11... | collective-permute-start | bytes 245768 | tf_op jit(solution)/shard_map/ppermute | solution.py:460
  (5 other events, 60.7 us)

commit v13 on v12

--- a/solution.py
+++ b/solution.py
@@ -99,6 +99,26 @@
 
 
 SWAP = [(0, 1), (1, 0)]
+
+
+def normalize_kernel(tokens, normed):
+    wide = tokens[...].astype(jnp.float32)
+    wide = wide * lax.rsqrt(jnp.mean(wide * wide, axis=-1, keepdims=True) + EPS)
+    for r in range(0, ROWS, 2):
+        pair = jnp.concatenate([wide[:, r], wide[:, r + 1]], axis=0)
+        normed[8 * r : 8 * r + 16, :] = pair.astype(jnp.bfloat16)
+
+
+def normalize(tokens):
+    columns, rows, model = tokens.shape
+    return pl.pallas_call(
+        normalize_kernel,
+        out_shape=jax.ShapeDtypeStruct((columns * rows, model), jnp.bfloat16),
+        in_specs=[VMEM],
+        out_specs=VMEM,
+        compiler_params=pltpu.CompilerParams(vmem_limit_bytes=8 * MIB),
+        name="normalize",
+    )(tokens)
 
 
 def normalized(p):
@@ -400,11 +420,8 @@
     sector = y_hi * 4 + x
     block = block_of(y_lo, y_hi, x)
     head = core * 8 + z
-    model = tokens.shape[-1]
-
-    wide = tokens.astype(jnp.float32)
-    normed = wide * lax.rsqrt(jnp.mean(wide * wide, axis=-1, keepdims=True) + EPS)
-    normed = jnp.transpose(normed.astype(jnp.bfloat16), (1, 0, 2)).reshape(64, model)
+
+    normed = normalize(tokens)
     first = lax.ppermute(normed, AXES, spread_perm())
 
     base = (z - 2 * block) & 7
@@ -448,8 +465,12 @@
     halo_oth = lax.ppermute(give, corners, neighbour_perm(1))
     parts = keep, lax.ppermute(send, "core", SWAP)
     results = inner(ints, factor, band, usable, parts)
-    halo_own, halo_oth, *results = lax.optimization_barrier((halo_own, halo_oth, *results))
-    halos = [halo_own, halo_oth] + [lax.ppermute(halo, "core", SWAP) for halo in (halo_own, halo_oth)]
+    halos, far = [], []
+    for halo in (halo_own, halo_oth):
+        halo, *results = lax.optimization_barrier((halo, *results))
+        halos.append(halo)
+        far.append(lax.ppermute(halo, "core", SWAP))
+    halos += far
     chunks = outer(ints, factor, results, parts, halos)
 
     far, near = (lax.ppermute(chunks[k], ("y_lo", "y_hi", "core"), return_perm(k)) for k in (1, 0))

time: 102 us -> 102 us (level)
  the two profiles are of different devices: /device:TPU:1 before, /device:TPU:41 now
where the time goes in v13:
time: 102 us
  starting transfers between devices  65.3 us (64%)
  waiting for transfers between devices  14.5 us (14%)
  Pallas kernels  12.9 us (13%)
  local copies, waits for them, and re-layouts  7.75 us (8%)
  between operations  1.43 us (1%)
    ppermute x4, starting transfers between devices, body(): a = lax.ppermute(a, ('z', 'core'), ring_perm())  12.8 us
    ppermute x5, starting transfers between devices, body(): lax.ppermute(part, 'core', SWAP)  10.3 us
    ppermute x1, starting transfers between devices, body(): first = lax.ppermute(normed, AXES, spread_perm())  10.1 us
    ppermute x3, starting transfers between devices, body(): lax.ppermute(passed[k - 1], 'x', [(i, i ^ k) for i in range(4)])  8.77 us
    ppermute x3, starting transfers between devices, body(): b = lax.ppermute(b, ('z', 'core'), ring_perm())  5.64 us
    pallas_call x2, Pallas kernels, call(): pl.pallas_call(kernel, out_shape=[jax.ShapeDtypeStruct(shape, jnp.bfloat1...  5.48 us
    ppermute x2, starting transfers between devices, body(): far.append(lax.ppermute(halo, 'core', SWAP))  5.41 us
    ppermute x4, waiting for transfers between devices, body(): a = lax.ppermute(a, ('z', 'core'), ring_perm())  5.4 us
  transfers between devices with their start and end apart: 25, of which 10 were waited for; matrix products, arithmetic and copies ran while one was open for 5% of the time, Pallas kernels for 6%

profile of v13, /device:TPU:41, one launch (start us, length us, event | category | flops | bytes accessed | tf_op | source)
XLA Modules:
  0.0 102.1 jit_solution(12896356217114466433)
XLA Ops:
  1.4 10.1 %collective-permute-start = (bf16[64,2560]{1,0:T(8,128)(2,1)S(1)}, bf16[64,2560]{1,0:T(8,128)(2,1)S(1)}, u32[]{:S(2)}, u32[]{:S(2)}) collective-permute-start(bf16[64,2560]{1,0:T(8,128)(2,1)S(1)} %normalize.1), channel_id=1, source_target_pairs={{0,0},{1,65},{2,16},{3,81},{4,32},{5,97},{6,48},{7,113},{8,64},{9,... | collective-permute-start | bytes 983048 | tf_op jit(solution)/shard_map/ppermute | solution.py:425
  19.4 6.2 %collective-permute-start.5 = (bf16[64,2560]{1,0:T(8,128)(2,1)S(1)}, bf16[64,2560]{1,0:T(8,128)(2,1)S(1)}, u32[]{:S(2)}, u32[]{:S(2)}) collective-permute-start(bf16[64,2560]{1,0:T(8,128)(2,1)S(1)} %collective-permute-done.refs_0_), channel_id=1, source_target_pairs={{0,16},{1,113},{16,32},{17,1},{32,48},{33,17},{48,64},{49,33},{64,... | collective-permute-start | bytes 983048 | tf_op jit(solution)/shard_map/ppermute | solution.py:456
  26.8 2.8 %collective-permute-done.5.refs_1_ = bf16[64,2560]{1,0:T(8,128)(2,1)S(1)} collective-permute-done((bf16[64,2560]{1,0:T(8,128)(2,1)S(1)}, bf16[64,2560]{1,0:T(8,128)(2,1)S(1)}, u32[]{:S(2)}, u32[]{:S(2)}) %collective-permute-start.5) | collective-permute-done | bytes 327712 | tf_op jit(solution)/shard_map/ppermute | solution.py:456
  29.6 2.2 %collective-permute-start.6 = (bf16[64,2560]{1,0:T(8,128)(2,1)S(1)}, bf16[64,2560]{1,0:T(8,128)(2,1)S(1)}, u32[]{:S(2)}, u32[]{:S(2)}) collective-permute-start(bf16[64,2560]{1,0:T(8,128)(2,1)S(1)} %collective-permute-done.5.refs_1_), channel_id=1, source_target_pairs={{0,16},{1,113},{16,32},{17,1},{32,48},{33,17},{48,64},{49,33},{64,... | collective-permute-start | bytes 983048 | tf_op jit(solution)/shard_map/ppermute | solution.py:456
  33.1 2.2 %collective-permute-start.3 = (bf16[64,2560]{1,0:T(8,128)(2,1)S(1)}, bf16[64,2560]{1,0:T(8,128)(2,1)S(1)}, u32[]{:S(2)}, u32[]{:S(2)}) collective-permute-start(bf16[64,2560]{1,0:T(8,128)(2,1)S(1)} %collective-permute-done.2.refs_2_), channel_id=1, source_target_pairs={{0,16},{1,113},{16,32},{17,1},{32,48},{33,17},{48,64},{49,33},{64,... | collective-permute-start | bytes 983048 | tf_op jit(solution)/shard_map/ppermute | solution.py:459
  36.6 2.2 %collective-permute-start.7 = (bf16[64,2560]{1,0:T(8,128)(2,1)S(1)}, bf16[64,2560]{1,0:T(8,128)(2,1)S(1)}, u32[]{:S(2)}, u32[]{:S(2)}) collective-permute-start(bf16[64,2560]{1,0:T(8,128)(2,1)S(1)} %collective-permute-done.6.refs_3_), channel_id=1, source_target_pairs={{0,16},{1,113},{16,32},{17,1},{32,48},{33,17},{48,64},{49,33},{64,... | collective-permute-start | bytes 983048 | tf_op jit(solution)/shard_map/ppermute | solution.py:456
  40.1 2.2 %collective-permute-start.4 = (bf16[64,2560]{1,0:T(8,128)(2,1)S(1)}, bf16[64,2560]{1,0:T(8,128)(2,1)S(1)}, u32[]{:S(2)}, u32[]{:S(2)}) collective-permute-start(bf16[64,2560]{1,0:T(8,128)(2,1)S(1)} %collective-permute-done.3.refs_4_), channel_id=1, source_target_pairs={{0,16},{1,113},{16,32},{17,1},{32,48},{33,17},{48,64},{49,33},{64,... | collective-permute-start | bytes 983048 | tf_op jit(solution)/shard_map/ppermute | solution.py:459
  43.7 2.2 %collective-permute-start.8 = (bf16[64,2560]{1,0:T(8,128)(2,1)S(1)}, bf16[64,2560]{1,0:T(8,128)(2,1)S(1)}, u32[]{:S(2)}, u32[]{:S(2)}) collective-permute-start(bf16[64,2560]{1,0:T(8,128)(2,1)S(1)} %collective-permute-done.7.refs_5_), channel_id=1, source_target_pairs={{0,16},{1,113},{16,32},{17,1},{32,48},{33,17},{48,64},{49,33},{64,... | collective-permute-start | bytes 983048 | tf_op jit(solution)/shard_map/ppermute | solution.py:456
  45.8 1.6 %collective-permute-done.9.refs_7_.refs_3_ = bf16[480,2560]{1,0:T(8,128)(2,1)S(1)} collective-permute-done((bf16[480,2560]{1,0:T(8,128)(2,1)}, bf16[480,2560]{1,0:T(8,128)(2,1)S(1)}, u32[]{:S(2)}, u32[]{:S(2)}) %collective-permute-start.9) | collective-permute-done | bytes 2457632 | tf_op jit(solution)/shard_map/ppermute | solution.py:451
  47.4 1.7 %copy-done = bf16[1,480,2560]{2,1,0:T(8,128)(2,1)S(1)} copy-done((bf16[1,480,2560]{2,1,0:T(8,128)(2,1)S(1)}, bf16[1,480,2560]{2,1,0:T(8,128)(2,1)}, u32[]{:S(2)}) %copy-start) | copy-done | bytes 2457624
  49.1 2.9 %project_first.1 = (bf16[8,48,480]{2,1,0:T(8,128)(2,1)S(1)}, bf16[8,48,480]{2,1,0:T(8,128)(2,1)S(1)}) custom-call(s32[2]{0:T(128)S(1)} %pad_add_fusion.flags, bf16[64,2560]{1,0:T(8,128)(2,1)S(1)} %collective-permute-done.refs_0_, bf16[64,2560]{1,0:T(8,128)(2,1)S(1)} %collective-permute-done.5.refs_1_, bf16[64,2560]{1,0:T(8,128)(2,1)S(1)} %collective-permute-done.2.refs_2_, ...), custom_call_target="tpu_custom_call" | custom-call | flops 20000000000 | bytes 1048576 | tf_op jit(solution)/shard_map/project_first/pallas_call | solution.py:197
  52.1 2.5 %project_last.1 = (bf16[8,64,480]{2,1,0:T(8,128)(2,1)S(1)}, bf16[8,64,480]{2,1,0:T(8,128)(2,1)S(1)}, bf16[4,64,640]{2,1,0:T(8,128)(2,1)S(1)}, bf16[4,64,640]{2,1,0:T(8,128)(2,1)S(1)}) custom-call(s32[2]{0:T(128)S(1)} %pad_add_fusion.flags, bf16[64,2560]{1,0:T(8,128)(2,1)S(1)} %collective-permute-done.4.refs_0_, ...), custom_call_target="tpu_custom_call" | custom-call | flops 100000000 | bytes 1048576 | tf_op jit(solution)/shard_map/project_last/pallas_call | solution.py:197
  54.7 3.7 %collective-permute-start.12 = (bf16[8,64,480]{2,1,0:T(8,128)(2,1)S(1)}, bf16[8,64,480]{2,1,0:T(8,128)(2,1)S(1)}, u32[]{:S(2)}, u32[]{:S(2)}) collective-permute-start(bf16[8,64,480]{2,1,0:T(8,128)(2,1)S(1)} %get-tuple-element.51), channel_id=1, source_target_pairs={{0,1},{1,0},{2,3},{3,2},{4,5},{5,4},{6,7},{7,6},{8,9},{9,8},{10,11... | collective-permute-start | bytes 1474568 | tf_op jit(solution)/shard_map/ppermute | solution.py:466
  58.4 2.8 %collective-permute-start.11 = (bf16[4,64,640]{2,1,0:T(8,128)(2,1)S(1)}, bf16[4,64,640]{2,1,0:T(8,128)(2,1)S(1)}, u32[]{:S(2)}, u32[]{:S(2)}) collective-permute-start(bf16[4,64,640]{2,1,0:T(8,128)(2,1)S(1)} %get-tuple-element.47), channel_id=1, source_target_pairs={{0,2},{2,4},{3,1},{4,6},{5,3},{6,14},{7,5},{14,12},{15,7},{12,10},... | collective-permute-start | bytes 983048 | tf_op jit(solution)/shard_map/ppermute | solution.py:464
  62.1 3.4 %inner.1 = (bf16[8,128,160]{2,1,0:T(8,128)(2,1)S(1)}, f32[8,128,256]{2,1,0:T(8,128)S(1)}, f32[10,128,128]{2,1,0:T(8,128)S(1)}, f32[2,16,128]{2,1,0:T(8,128)S(1)}) custom-call(s32[19]{0:T(128)S(1)} %stack.137.ints, f32[1]{0:T(128)S(6)} %mul.244.factor_ref, f32[64]{0:T(128)S(1)} %reshape.8.band, f32[16,128]{1,0:T(8,128)S(1)} %fusion.1.usable, ...), custom_call_target="tpu_custom_call" | custom-call | flops 10000000 | bytes 100000 | tf_op jit(solution)/shard_map/inner/pallas_call | solution.py:303
  65.5 5.4 %collective-permute-start.14 = (bf16[4,64,640]{2,1,0:T(8,128)(2,1)S(1)}, bf16[4,64,640]{2,1,0:T(8,128)(2,1)S(1)}, u32[]{:S(2)}, u32[]{:S(2)}) collective-permute-start(bf16[4,64,640]{2,1,0:T(8,128)(2,1)S(1)} %collective-permute-done.10.refs_3_), channel_id=1, source_target_pairs={{0,1},{1,0},{2,3},{3,2},{4,5},{5,4},{6,7},{7,6},{8,9},{9,8},{10,11... | collective-permute-start | bytes 983048 | tf_op jit(solution)/shard_map/ppermute | solution.py:472
  72.6 2.3 %outer.1 = (bf16[4,2,8,1280]{3,2,1,0:T(8,128)(2,1)S(1)}, bf16[4,2,8,1280]{3,2,1,0:T(8,128)(2,1)S(1)}) custom-call(s32[19]{0:T(128)S(1)} %stack.137.ints, f32[1]{0:T(128)S(6)} %mul.244.factor_ref, bf16[8,128,160]{2,1,0:T(8,128)(2,1)S(1)} %get-tuple-element.60.zonal_ref, f32[8,128,256]{2,1,0:T(8,128)S(1)} %get-tuple-element.61.window_ref, ...), custom_call_target="tpu_custom_call" | custom-call | flops 1000000000 | bytes 4194304 | tf_op jit(solution)/shard_map/outer/pallas_call | solution.py:359
  74.9 3.0 %collective-permute-start.15 = (bf16[4,2,8,1280]{3,2,1,0:T(8,128)(2,1)S(1)}, bf16[4,2,8,1280]{3,2,1,0:T(8,128)(2,1)S(1)}, u32[]{:S(2)}, u32[]{:S(2)}) collective-permute-start(bf16[4,2,8,1280]{3,2,1,0:T(8,128)(2,1)S(1)} %get-tuple-element.66), channel_id=1, source_target_pairs={{0,8},{1,136},{8,0},{9,128},{128,9},{129,137},{136,1},{137,129},{2... | collective-permute-start | bytes 491528 | tf_op jit(solution)/shard_map/ppermute | solution.py:476
  78.6 2.2 %collective-permute-done.15.far.refs_0_ = bf16[4,2,8,1280]{3,2,1,0:T(8,128)(2,1)S(1)} collective-permute-done((bf16[4,2,8,1280]{3,2,1,0:T(8,128)(2,1)S(1)}, bf16[4,2,8,1280]{3,2,1,0:T(8,128)(2,1)S(1)}, u32[]{:S(2)}, u32[]{:S(2)}) %collective-permute-start.15) | collective-permute-done | bytes 163872 | tf_op jit(solution)/shard_map/ppermute | solution.py:476
  80.8 6.1 %collective-permute-start.17 = (bf16[2,2,8,1280]{3,2,1,0:T(8,128)(2,1)S(1)}, bf16[2,2,8,1280]{3,2,1,0:T(8,128)(2,1)S(1)}, u32[]{:S(2)}, u32[]{:S(2)}) collective-permute-start(bf16[2,2,8,1280]{3,2,1,0:T(8,128)(2,1)S(1)} %get-tuple-element.68), channel_id=1, source_target_pairs={{0,4},{2,6},{4,0},{6,2},{1,5},{3,7},{5,1},{7,3},{8,12},{10,14},{12... | collective-permute-start | bytes 245768 | tf_op jit(solution)/shard_map/ppermute | solution.py:480
  86.9 2.6 %collective-permute-start.18 = (bf16[2,2,8,1280]{3,2,1,0:T(8,128)(2,1)S(1)}, bf16[2,2,8,1280]{3,2,1,0:T(8,128)(2,1)S(1)}, u32[]{:S(2)}, u32[]{:S(2)}) collective-permute-start(bf16[2,2,8,1280]{3,2,1,0:T(8,128)(2,1)S(1)} %get-tuple-element.69), channel_id=1, source_target_pairs={{0,2},{2,0},{4,6},{6,4},{1,3},{3,1},{5,7},{7,5},{8,10},{10,8},{12,... | collective-permute-start | bytes 245768 | tf_op jit(solution)/shard_map/ppermute | solution.py:480
  89.6 4.6 %collective-permute-start.20 = (bf16[4,2,8,1280]{3,2,1,0:T(8,128)(2,1)S(1)}, bf16[4,2,8,1280]{3,2,1,0:T(8,128)(2,1)S(1)}, u32[]{:S(2)}, u32[]{:S(2)}) collective-permute-start(bf16[4,2,8,1280]{3,2,1,0:T(8,128)(2,1)S(1)} %collective-permute-done.15.far.refs_0_), channel_id=1, source_target_pairs={{0,1},{1,0},{2,3},{3,2},{4,5},{5,4},{6,7},{7,6},{8,9},{9,8},{10,11... | collective-permute-start | bytes 491528 | tf_op jit(solution)/shard_map/ppermute | solution.py:481
  94.7 2.8 %collective-permute-start.23 = (bf16[2,2,8,1280]{3,2,1,0:T(8,128)(2,1)S(1)}, bf16[2,2,8,1280]{3,2,1,0:T(8,128)(2,1)S(1)}, u32[]{:S(2)}, u32[]{:S(2)}) collective-permute-start(bf16[2,2,8,1280]{3,2,1,0:T(8,128)(2,1)S(1)} %collective-permute-done.18.refs_3_), channel_id=1, source_target_pairs={{0,1},{1,0},{2,3},{3,2},{4,5},{5,4},{6,7},{7,6},{8,9},{9,8},{10,11... | collective-permute-start | bytes 245768 | tf_op jit(solution)/shard_map/ppermute | solution.py:481
  97.5 2.4 %collective-permute-start.24 = (bf16[2,2,8,1280]{3,2,1,0:T(8,128)(2,1)S(1)}, bf16[2,2,8,1280]{3,2,1,0:T(8,128)(2,1)S(1)}, u32[]{:S(2)}, u32[]{:S(2)}) collective-permute-start(bf16[2,2,8,1280]{3,2,1,0:T(8,128)(2,1)S(1)} %collective-permute-done.19.refs_4_), channel_id=1, source_target_pairs={{0,1},{1,0},{2,3},{3,2},{4,5},{5,4},{6,7},{7,6},{8,9},{9,8},{10,11... | collective-permute-start | bytes 245768 | tf_op jit(solution)/shard_map/ppermute | solution.py:481
  (49 shorter events, 20.5 us)
Async XLA Ops:
  1.4 16.7 %collective-permute-start = (bf16[64,2560]{1,0:T(8,128)(2,1)S(1)}, bf16[64,2560]{1,0:T(8,128)(2,1)S(1)}, u32[]{:S(2)}, u32[]{:S(2)}) collective-permute-start(bf16[64,2560]{1,0:T(8,128)(2,1)S(1)} %normalize.1), channel_id=1, source_target_pairs={{0,0},{1,65},{2,16},{3,81},{4,32},{5,97},{6,48},{7,113},{8,64},{9,... | collective-permute-start | bytes 983048 | tf_op jit(solution)/shard_map/ppermute | solution.py:425
  18.1 29.3 %collective-permute-start.9 = (bf16[480,2560]{1,0:T(8,128)(2,1)}, bf16[480,2560]{1,0:T(8,128)(2,1)S(1)}, u32[]{:S(2)}, u32[]{:S(2)}) collective-permute-start(bf16[480,2560]{1,0:T(8,128)(2,1)} %bitcast.38), channel_id=1, source_target_pairs={{0,128},{1,137},{128,8},{129,1},{8,136},{9,129},{136,0},{137,9},{2... | collective-permute-start | bytes 7372808 | tf_op jit(solution)/shard_map/ppermute | solution.py:451
  18.2 7.4 %collective-permute-start.1 = (bf16[64,2560]{1,0:T(8,128)(2,1)S(1)}, bf16[64,2560]{1,0:T(8,128)(2,1)S(1)}, u32[]{:S(2)}, u32[]{:S(2)}) collective-permute-start(bf16[64,2560]{1,0:T(8,128)(2,1)S(1)} %collective-permute-done.refs_0_), channel_id=1, source_target_pairs={{0,1},{1,0},{2,3},{3,2},{4,5},{5,4},{6,7},{7,6},{8,9},{9,8},{10,11... | collective-permute-start | bytes 983048 | tf_op jit(solution)/shard_map/ppermute | solution.py:453
  19.4 10.2 %collective-permute-start.5 = (bf16[64,2560]{1,0:T(8,128)(2,1)S(1)}, bf16[64,2560]{1,0:T(8,128)(2,1)S(1)}, u32[]{:S(2)}, u32[]{:S(2)}) collective-permute-start(bf16[64,2560]{1,0:T(8,128)(2,1)S(1)} %collective-permute-done.refs_0_), channel_id=1, source_target_pairs={{0,16},{1,113},{16,32},{17,1},{32,48},{33,17},{48,64},{49,33},{64,... | collective-permute-start | bytes 983048 | tf_op jit(solution)/shard_map/ppermute | solution.py:456
  25.6 7.5 %collective-permute-start.2 = (bf16[64,2560]{1,0:T(8,128)(2,1)S(1)}, bf16[64,2560]{1,0:T(8,128)(2,1)S(1)}, u32[]{:S(2)}, u32[]{:S(2)}) collective-permute-start(bf16[64,2560]{1,0:T(8,128)(2,1)S(1)} %collective-permute-done.1), channel_id=1, source_target_pairs={{0,16},{1,113},{16,32},{17,1},{32,48},{33,17},{48,64},{49,33},{64,... | collective-permute-start | bytes 983048 | tf_op jit(solution)/shard_map/ppermute | solution.py:459
  29.6 7.0 %collective-permute-start.6 = (bf16[64,2560]{1,0:T(8,128)(2,1)S(1)}, bf16[64,2560]{1,0:T(8,128)(2,1)S(1)}, u32[]{:S(2)}, u32[]{:S(2)}) collective-permute-start(bf16[64,2560]{1,0:T(8,128)(2,1)S(1)} %collective-permute-done.5.refs_1_), channel_id=1, source_target_pairs={{0,16},{1,113},{16,32},{17,1},{32,48},{33,17},{48,64},{49,33},{64,... | collective-permute-start | bytes 983048 | tf_op jit(solution)/shard_map/ppermute | solution.py:456
  33.1 7.0 %collective-permute-start.3 = (bf16[64,2560]{1,0:T(8,128)(2,1)S(1)}, bf16[64,2560]{1,0:T(8,128)(2,1)S(1)}, u32[]{:S(2)}, u32[]{:S(2)}) collective-permute-start(bf16[64,2560]{1,0:T(8,128)(2,1)S(1)} %collective-permute-done.2.refs_2_), channel_id=1, source_target_pairs={{0,16},{1,113},{16,32},{17,1},{32,48},{33,17},{48,64},{49,33},{64,... | collective-permute-start | bytes 983048 | tf_op jit(solution)/shard_map/ppermute | solution.py:459
  36.6 7.0 %collective-permute-start.7 = (bf16[64,2560]{1,0:T(8,128)(2,1)S(1)}, bf16[64,2560]{1,0:T(8,128)(2,1)S(1)}, u32[]{:S(2)}, u32[]{:S(2)}) collective-permute-start(bf16[64,2560]{1,0:T(8,128)(2,1)S(1)} %collective-permute-done.6.refs_3_), channel_id=1, source_target_pairs={{0,16},{1,113},{16,32},{17,1},{32,48},{33,17},{48,64},{49,33},{64,... | collective-permute-start | bytes 983048 | tf_op jit(solution)/shard_map/ppermute | solution.py:456
  40.1 11.9 %collective-permute-start.4 = (bf16[64,2560]{1,0:T(8,128)(2,1)S(1)}, bf16[64,2560]{1,0:T(8,128)(2,1)S(1)}, u32[]{:S(2)}, u32[]{:S(2)}) collective-permute-start(bf16[64,2560]{1,0:T(8,128)(2,1)S(1)} %collective-permute-done.3.refs_4_), channel_id=1, source_target_pairs={{0,16},{1,113},{16,32},{17,1},{32,48},{33,17},{48,64},{49,33},{64,... | collective-permute-start | bytes 983048 | tf_op jit(solution)/shard_map/ppermute | solution.py:459
  43.7 8.4 %collective-permute-start.8 = (bf16[64,2560]{1,0:T(8,128)(2,1)S(1)}, bf16[64,2560]{1,0:T(8,128)(2,1)S(1)}, u32[]{:S(2)}, u32[]{:S(2)}) collective-permute-start(bf16[64,2560]{1,0:T(8,128)(2,1)S(1)} %collective-permute-done.7.refs_5_), channel_id=1, source_target_pairs={{0,16},{1,113},{16,32},{17,1},{32,48},{33,17},{48,64},{49,33},{64,... | collective-permute-start | bytes 983048 | tf_op jit(solution)/shard_map/ppermute | solution.py:456
  54.7 7.4 %collective-permute-start.12 = (bf16[8,64,480]{2,1,0:T(8,128)(2,1)S(1)}, bf16[8,64,480]{2,1,0:T(8,128)(2,1)S(1)}, u32[]{:S(2)}, u32[]{:S(2)}) collective-permute-start(bf16[8,64,480]{2,1,0:T(8,128)(2,1)S(1)} %get-tuple-element.51), channel_id=1, source_target_pairs={{0,1},{1,0},{2,3},{3,2},{4,5},{5,4},{6,7},{7,6},{8,9},{9,8},{10,11... | collective-permute-start | bytes 1474568 | tf_op jit(solution)/shard_map/ppermute | solution.py:466
  58.4 7.1 %collective-permute-start.11 = (bf16[4,64,640]{2,1,0:T(8,128)(2,1)S(1)}, bf16[4,64,640]{2,1,0:T(8,128)(2,1)S(1)}, u32[]{:S(2)}, u32[]{:S(2)}) collective-permute-start(bf16[4,64,640]{2,1,0:T(8,128)(2,1)S(1)} %get-tuple-element.47), channel_id=1, source_target_pairs={{0,2},{2,4},{3,1},{4,6},{5,3},{6,14},{7,5},{14,12},{15,7},{12,10},... | collective-permute-start | bytes 983048 | tf_op jit(solution)/shard_map/ppermute | solution.py:464
  61.2 4.3 %collective-permute-start.10 = (bf16[4,64,640]{2,1,0:T(8,128)(2,1)S(1)}, bf16[4,64,640]{2,1,0:T(8,128)(2,1)S(1)}, u32[]{:S(2)}, u32[]{:S(2)}) collective-permute-start(bf16[4,64,640]{2,1,0:T(8,128)(2,1)S(1)} %get-tuple-element.46), channel_id=1, source_target_pairs={{1,2},{3,4},{2,1},{5,6},{4,3},{7,14},{6,5},{15,12},{14,7},{13,10},... | collective-permute-start | bytes 983048 | tf_op jit(solution)/shard_map/ppermute | solution.py:465
  65.5 6.7 %collective-permute-start.14 = (bf16[4,64,640]{2,1,0:T(8,128)(2,1)S(1)}, bf16[4,64,640]{2,1,0:T(8,128)(2,1)S(1)}, u32[]{:S(2)}, u32[]{:S(2)}) collective-permute-start(bf16[4,64,640]{2,1,0:T(8,128)(2,1)S(1)} %collective-permute-done.10.refs_3_), channel_id=1, source_target_pairs={{0,1},{1,0},{2,3},{3,2},{4,5},{5,4},{6,7},{7,6},{8,9},{9,8},{10,11... | collective-permute-start | bytes 983048 | tf_op jit(solution)/shard_map/ppermute | solution.py:472
  74.9 5.9 %collective-permute-start.15 = (bf16[4,2,8,1280]{3,2,1,0:T(8,128)(2,1)S(1)}, bf16[4,2,8,1280]{3,2,1,0:T(8,128)(2,1)S(1)}, u32[]{:S(2)}, u32[]{:S(2)}) collective-permute-start(bf16[4,2,8,1280]{3,2,1,0:T(8,128)(2,1)S(1)} %get-tuple-element.66), channel_id=1, source_target_pairs={{0,8},{1,136},{8,0},{9,128},{128,9},{129,137},{136,1},{137,129},{2... | collective-permute-start | bytes 491528 | tf_op jit(solution)/shard_map/ppermute | solution.py:476
  77.9 2.9 %collective-permute-start.16 = (bf16[4,2,8,1280]{3,2,1,0:T(8,128)(2,1)S(1)}, bf16[4,2,8,1280]{3,2,1,0:T(8,128)(2,1)S(1)}, u32[]{:S(2)}, u32[]{:S(2)}) collective-permute-start(bf16[4,2,8,1280]{3,2,1,0:T(8,128)(2,1)S(1)} %get-tuple-element.67), channel_id=1, source_target_pairs={{0,0},{1,128},{8,8},{9,136},{128,1},{129,129},{136,9},{137,137},{2... | collective-permute-start | bytes 491528 | tf_op jit(solution)/shard_map/ppermute | solution.py:476
  80.8 13.4 %collective-permute-start.17 = (bf16[2,2,8,1280]{3,2,1,0:T(8,128)(2,1)S(1)}, bf16[2,2,8,1280]{3,2,1,0:T(8,128)(2,1)S(1)}, u32[]{:S(2)}, u32[]{:S(2)}) collective-permute-start(bf16[2,2,8,1280]{3,2,1,0:T(8,128)(2,1)S(1)} %get-tuple-element.68), channel_id=1, source_target_pairs={{0,4},{2,6},{4,0},{6,2},{1,5},{3,7},{5,1},{7,3},{8,12},{10,14},{12... | collective-permute-start | bytes 245768 | tf_op jit(solution)/shard_map/ppermute | solution.py:480
  86.9 7.8 %collective-permute-start.18 = (bf16[2,2,8,1280]{3,2,1,0:T(8,128)(2,1)S(1)}, bf16[2,2,8,1280]{3,2,1,0:T(8,128)(2,1)S(1)}, u32[]{:S(2)}, u32[]{:S(2)}) collective-permute-start(bf16[2,2,8,1280]{3,2,1,0:T(8,128)(2,1)S(1)} %get-tuple-element.69), channel_id=1, source_target_pairs={{0,2},{2,0},{4,6},{6,4},{1,3},{3,1},{5,7},{7,5},{8,10},{10,8},{12,... | collective-permute-start | bytes 245768 | tf_op jit(solution)/shard_map/ppermute | solution.py:480
  89.5 7.9 %collective-permute-start.19 = (bf16[2,2,8,1280]{3,2,1,0:T(8,128)(2,1)S(1)}, bf16[2,2,8,1280]{3,2,1,0:T(8,128)(2,1)S(1)}, u32[]{:S(2)}, u32[]{:S(2)}) collective-permute-start(bf16[2,2,8,1280]{3,2,1,0:T(8,128)(2,1)S(1)} %get-tuple-element.70), channel_id=1, source_target_pairs={{0,6},{2,4},{4,2},{6,0},{1,7},{3,5},{5,3},{7,1},{8,14},{10,12},{12... | collective-permute-start | bytes 245768 | tf_op jit(solution)/shard_map/ppermute | solution.py:480
  89.6 11.2 %collective-permute-start.20 = (bf16[4,2,8,1280]{3,2,1,0:T(8,128)(2,1)S(1)}, bf16[4,2,8,1280]{3,2,1,0:T(8,128)(2,1)S(1)}, u32[]{:S(2)}, u32[]{:S(2)}) collective-permute-start(bf16[4,2,8,1280]{3,2,1,0:T(8,128)(2,1)S(1)} %collective-permute-done.15.far.refs_0_), channel_id=1, source_target_pairs={{0,1},{1,0},{2,3},{3,2},{4,5},{5,4},{6,7},{7,6},{8,9},{9,8},{10,11... | collective-permute-start | bytes 491528 | tf_op jit(solution)/shard_map/ppermute | solution.py:481
  94.2 6.6 %collective-permute-start.21 = (bf16[4,2,8,1280]{3,2,1,0:T(8,128)(2,1)S(1)}, bf16[4,2,8,1280]{3,2,1,0:T(8,128)(2,1)S(1)}, u32[]{:S(2)}, u32[]{:S(2)}) collective-permute-start(bf16[4,2,8,1280]{3,2,1,0:T(8,128)(2,1)S(1)} %collective-permute-done.16.near.refs_1_), channel_id=1, source_target_pairs={{0,1},{1,0},{2,3},{3,2},{4,5},{5,4},{6,7},{7,6},{8,9},{9,8},{10,11... | collective-permute-start | bytes 491528 | tf_op jit(solution)/shard_map/ppermute | solution.py:481
  94.2 5.6 %collective-permute-start.22 = (bf16[2,2,8,1280]{3,2,1,0:T(8,128)(2,1)S(1)}, bf16[2,2,8,1280]{3,2,1,0:T(8,128)(2,1)S(1)}, u32[]{:S(2)}, u32[]{:S(2)}) collective-permute-start(bf16[2,2,8,1280]{3,2,1,0:T(8,128)(2,1)S(1)} %collective-permute-done.17.refs_2_), channel_id=1, source_target_pairs={{0,1},{1,0},{2,3},{3,2},{4,5},{5,4},{6,7},{7,6},{8,9},{9,8},{10,11... | collective-permute-start | bytes 245768 | tf_op jit(solution)/shard_map/ppermute | solution.py:481
  94.7 5.1 %collective-permute-start.23 = (bf16[2,2,8,1280]{3,2,1,0:T(8,128)(2,1)S(1)}, bf16[2,2,8,1280]{3,2,1,0:T(8,128)(2,1)S(1)}, u32[]{:S(2)}, u32[]{:S(2)}) collective-permute-start(bf16[2,2,8,1280]{3,2,1,0:T(8,128)(2,1)S(1)} %collective-permute-done.18.refs_3_), channel_id=1, source_target_pairs={{0,1},{1,0},{2,3},{3,2},{4,5},{5,4},{6,7},{7,6},{8,9},{9,8},{10,11... | collective-permute-start | bytes 245768 | tf_op jit(solution)/shard_map/ppermute | solution.py:481
  97.5 3.3 %collective-permute-start.24 = (bf16[2,2,8,1280]{3,2,1,0:T(8,128)(2,1)S(1)}, bf16[2,2,8,1280]{3,2,1,0:T(8,128)(2,1)S(1)}, u32[]{:S(2)}, u32[]{:S(2)}) collective-permute-start(bf16[2,2,8,1280]{3,2,1,0:T(8,128)(2,1)S(1)} %collective-permute-done.19.refs_4_), channel_id=1, source_target_pairs={{0,1},{1,0},{2,3},{3,2},{4,5},{5,4},{6,7},{7,6},{8,9},{9,8},{10,11... | collective-permute-start | bytes 245768 | tf_op jit(solution)/shard_map/ppermute | solution.py:481
  (4 other events, 7.4 us)

commit v14 on v13

--- a/solution.py
+++ b/solution.py
@@ -134,49 +134,42 @@
     return [p[:, r].reshape(8 * groups, QKV).astype(jnp.bfloat16) for r in range(ROWS)]
 
 
-def products(flags, pieces, own, partner, x_ref):
+def gather(pieces, x_ref):
     for g, piece in enumerate(pieces):
         x_ref[64 * g : 64 * (g + 1), :] = piece[...]
-    return [
-        normalized(lax.dot_general(x_ref[...], w[...], NT, preferred_element_type=jnp.float32))
-        for w in (own, partner)
-    ]
-
-
-def by_head(flags, rows, store):
+
+
+def product(x, w):
+    return normalized(lax.dot_general(x, w[...], NT, preferred_element_type=jnp.float32))
+
+
+def project_first_kernel(*refs):
+    pieces, (own, rows, x_ref) = refs[:EARLY], refs[EARLY:]
+    gather(pieces, x_ref)
+    for r, row in enumerate(product(x_ref[...], own)):
+        rows[r] = row
+
+
+def project_last_kernel(flags, *refs):
+    pieces, (own, partner, own_0, keep, send, edge, give, x_ref) = refs[:8], refs[8:]
+    early = 8 * EARLY
+    gather(pieces, x_ref)
+    partner_rows = product(x_ref[...], partner)
+    own_rows = product(x_ref[64 * EARLY :, :], own)
+
+    def store(of_own, of_partner):
+        for r in range(ROWS):
+            of_own[r, :early] = own_0[r]
+            of_own[r, early:] = own_rows[r]
+            of_partner[r] = partner_rows[r]
+
     @pl.when(flags[0] == 1)
     def _():
-        store(rows[0], rows[1])
+        store(keep, send)
 
     @pl.when(flags[0] != 1)
     def _():
-        store(rows[1], rows[0])
-
-
-def project_first_kernel(flags, *refs):
-    pieces, (own, partner, keep, send, x_ref) = refs[:EARLY], refs[EARLY:]
-
-    def store(first, second):
-        for r in range(ROWS):
-            keep[r] = first[r]
-            send[r] = second[r]
-
-    by_head(flags, products(flags, pieces, own, partner, x_ref), store)
-
-
-def project_last_kernel(flags, *refs):
-    pieces, (own, partner, keep_0, send_0, keep, send, edge, give, x_ref) = refs[: 8 - EARLY], refs[8 - EARLY :]
-    early = 8 * EARLY
-    for r in range(ROWS):
-        keep[r, :early] = keep_0[r]
-        send[r, :early] = send_0[r]
-
-    def store(first, second):
-        for r in range(ROWS):
-            keep[r, early:] = first[r]
-            send[r, early:] = second[r]
-
-    by_head(flags, products(flags, pieces, own, partner, x_ref), store)
+        store(send, keep)
 
     def store_edges(top, bottom):
         for r in range(ROWS):
@@ -193,22 +186,24 @@
 
 
 def project(flags, pieces, own, partner):
-    def call(kernel, shapes, pieces, extra, cost, name):
+    def call(kernel, shapes, tokens, operands, specs, cost, name):
         return pl.pallas_call(
             kernel,
             out_shape=[jax.ShapeDtypeStruct(shape, jnp.bfloat16) for shape in shapes],
-            in_specs=[SMEM] + [VMEM] * (len(pieces) + 2 + len(extra)),
+            in_specs=specs + [VMEM] * (len(operands) - len(specs)),
             out_specs=[VMEM] * len(shapes),
-            scratch_shapes=[pltpu.VMEM((64 * len(pieces), own.shape[1]), jnp.bfloat16)],
+            scratch_shapes=[pltpu.VMEM((tokens, own.shape[1]), jnp.bfloat16)],
             compiler_params=pltpu.CompilerParams(vmem_limit_bytes=20 * MIB),
             cost_estimate=pl.CostEstimate(flops=cost, bytes_accessed=MIB, transcendentals=0),
             name=name,
-        )(flags, *pieces, own, partner, *extra)
+        )(*operands)
 
     some, whole = (ROWS, 8 * EARLY, QKV), (ROWS, HALF, QKV)
     part = (WIN, HALF, 4 * HEAD_DIM)
-    first = call(project_first_kernel, [some] * 2, pieces[:EARLY], [], 2 * 10**10, "project_first")
-    return call(project_last_kernel, [whole] * 2 + [part] * 2, pieces[EARLY:], first, 10**8, "project_last")
+    operands = [*pieces[:EARLY], own]
+    (own_0,) = call(project_first_kernel, [some], 64 * EARLY, operands, [], 3 * 10**9, "project_first")
+    operands = [flags, *pieces, own, partner, own_0]
+    return call(project_last_kernel, [whole] * 2 + [part] * 2, 512, operands, [SMEM], 10**8, "project_last")
 
 
 def put(ks, vs, first, key, value):

time: 102 us -> 101 us (level)
  the two profiles are of different devices: /device:TPU:41 before, /device:TPU:1 now
where the time goes in v14:
time: 101 us; the launch traced here: 100 us
  starting transfers between devices  59 us (58%)
  waiting for transfers between devices  20 us (20%)
  Pallas kernels  12 us (12%)
  local copies, waits for them, and re-layouts  7.66 us (8%)
  between operations  1.68 us (2%)
    ppermute x4, starting transfers between devices, body(): a = lax.ppermute(a, ('z', 'core'), ring_perm())  13.8 us
    ppermute x1, starting transfers between devices, body(): first = lax.ppermute(normed, AXES, spread_perm())  9.65 us
    ppermute x1, starting transfers between devices, body(): a, b = (first, lax.ppermute(first, 'core', SWAP))  8.71 us
    ppermute x3, starting transfers between devices, body(): b = lax.ppermute(b, ('z', 'core'), ring_perm())  8.07 us
    ppermute x2, starting transfers between devices, body(): lax.ppermute(chunks[k], ('y_lo', 'y_hi', 'core'), return_perm(k))  6.01 us
    ppermute x4, waiting for transfers between devices, body(): a = lax.ppermute(a, ('z', 'core'), ring_perm())  4.78 us
    ppermute x2, waiting for transfers between devices, body(): lax.ppermute(chunks[k], ('y_lo', 'y_hi', 'core'), return_perm(k))  4.71 us
    pallas_call x2, Pallas kernels, call(): pl.pallas_call(kernel, out_shape=[jax.ShapeDtypeStruct(shape, jnp.bfloat1...  4.56 us
  transfers between devices with their start and end apart: 25, of which 16 were waited for; matrix products, arithmetic and copies ran while one was open for 5% of the time, Pallas kernels for 5%

profile of v14, /device:TPU:1, one launch (start us, length us, event | category | flops | bytes accessed | tf_op | source)
XLA Modules:
  0.0 100.5 jit_solution(15850825680355623741)
XLA Ops:
  1.4 9.6 %collective-permute-start = (bf16[64,2560]{1,0:T(8,128)(2,1)S(1)}, bf16[64,2560]{1,0:T(8,128)(2,1)S(1)}, u32[]{:S(2)}, u32[]{:S(2)}) collective-permute-start(bf16[64,2560]{1,0:T(8,128)(2,1)S(1)} %normalize.1), channel_id=1, source_target_pairs={{0,0},{1,65},{2,16},{3,81},{4,32},{5,97},{6,48},{7,113},{8,64},{9,... | collective-permute-start | bytes 983048 | tf_op jit(solution)/shard_map/ppermute | solution.py:420
  17.9 8.7 %collective-permute-start.2 = (bf16[64,2560]{1,0:T(8,128)(2,1)S(1)}, bf16[64,2560]{1,0:T(8,128)(2,1)S(1)}, u32[]{:S(2)}, u32[]{:S(2)}) collective-permute-start(bf16[64,2560]{1,0:T(8,128)(2,1)S(1)} %collective-permute-done.refs_0_), channel_id=1, source_target_pairs={{0,1},{1,0},{2,3},{3,2},{4,5},{5,4},{6,7},{7,6},{8,9},{9,8},{10,11... | collective-permute-start | bytes 983048 | tf_op jit(solution)/shard_map/ppermute | solution.py:448
  26.6 3.6 %collective-permute-start.1 = (bf16[64,2560]{1,0:T(8,128)(2,1)S(1)}, bf16[64,2560]{1,0:T(8,128)(2,1)S(1)}, u32[]{:S(2)}, u32[]{:S(2)}) collective-permute-start(bf16[64,2560]{1,0:T(8,128)(2,1)S(1)} %collective-permute-done.refs_0_), channel_id=1, source_target_pairs={{0,16},{1,113},{16,32},{17,1},{32,48},{33,17},{48,64},{49,33},{64,... | collective-permute-start | bytes 983048 | tf_op jit(solution)/shard_map/ppermute | solution.py:451
  31.5 2.8 %collective-permute-done.1.refs_1_ = bf16[64,2560]{1,0:T(8,128)(2,1)S(1)} collective-permute-done((bf16[64,2560]{1,0:T(8,128)(2,1)S(1)}, bf16[64,2560]{1,0:T(8,128)(2,1)S(1)}, u32[]{:S(2)}, u32[]{:S(2)}) %collective-permute-start.1) | collective-permute-done | bytes 327712 | tf_op jit(solution)/shard_map/ppermute | solution.py:451
  34.3 3.4 %collective-permute-start.4 = (bf16[64,2560]{1,0:T(8,128)(2,1)S(1)}, bf16[64,2560]{1,0:T(8,128)(2,1)S(1)}, u32[]{:S(2)}, u32[]{:S(2)}) collective-permute-start(bf16[64,2560]{1,0:T(8,128)(2,1)S(1)} %collective-permute-done.1.refs_1_), channel_id=1, source_target_pairs={{0,16},{1,113},{16,32},{17,1},{32,48},{33,17},{48,64},{49,33},{64,... | collective-permute-start | bytes 983048 | tf_op jit(solution)/shard_map/ppermute | solution.py:451
  37.8 3.4 %collective-permute-start.5 = (bf16[64,2560]{1,0:T(8,128)(2,1)S(1)}, bf16[64,2560]{1,0:T(8,128)(2,1)S(1)}, u32[]{:S(2)}, u32[]{:S(2)}) collective-permute-start(bf16[64,2560]{1,0:T(8,128)(2,1)S(1)} %collective-permute-done.3.refs_2_), channel_id=1, source_target_pairs={{0,16},{1,113},{16,32},{17,1},{32,48},{33,17},{48,64},{49,33},{64,... | collective-permute-start | bytes 983048 | tf_op jit(solution)/shard_map/ppermute | solution.py:454
  41.7 3.4 %collective-permute-start.6 = (bf16[64,2560]{1,0:T(8,128)(2,1)S(1)}, bf16[64,2560]{1,0:T(8,128)(2,1)S(1)}, u32[]{:S(2)}, u32[]{:S(2)}) collective-permute-start(bf16[64,2560]{1,0:T(8,128)(2,1)S(1)} %collective-permute-done.4.refs_3_), channel_id=1, source_target_pairs={{0,16},{1,113},{16,32},{17,1},{32,48},{33,17},{48,64},{49,33},{64,... | collective-permute-start | bytes 983048 | tf_op jit(solution)/shard_map/ppermute | solution.py:451
  45.2 3.4 %collective-permute-start.7 = (bf16[64,2560]{1,0:T(8,128)(2,1)S(1)}, bf16[64,2560]{1,0:T(8,128)(2,1)S(1)}, u32[]{:S(2)}, u32[]{:S(2)}) collective-permute-start(bf16[64,2560]{1,0:T(8,128)(2,1)S(1)} %collective-permute-done.5.refs_4_), channel_id=1, source_target_pairs={{0,16},{1,113},{16,32},{17,1},{32,48},{33,17},{48,64},{49,33},{64,... | collective-permute-start | bytes 983048 | tf_op jit(solution)/shard_map/ppermute | solution.py:454
  49.1 3.4 %collective-permute-start.8 = (bf16[64,2560]{1,0:T(8,128)(2,1)S(1)}, bf16[64,2560]{1,0:T(8,128)(2,1)S(1)}, u32[]{:S(2)}, u32[]{:S(2)}) collective-permute-start(bf16[64,2560]{1,0:T(8,128)(2,1)S(1)} %collective-permute-done.6.refs_5_), channel_id=1, source_target_pairs={{0,16},{1,113},{16,32},{17,1},{32,48},{33,17},{48,64},{49,33},{64,... | collective-permute-start | bytes 983048 | tf_op jit(solution)/shard_map/ppermute | solution.py:451
  52.5 1.7 %copy-done = bf16[1,480,2560]{2,1,0:T(8,128)(2,1)S(1)} copy-done((bf16[1,480,2560]{2,1,0:T(8,128)(2,1)S(1)}, bf16[1,480,2560]{2,1,0:T(8,128)(2,1)}, u32[]{:S(2)}) %copy-start) | copy-done | bytes 2457624
  56.5 3.3 %project_last.1 = (bf16[8,64,480]{2,1,0:T(8,128)(2,1)S(1)}, bf16[8,64,480]{2,1,0:T(8,128)(2,1)S(1)}, bf16[4,64,640]{2,1,0:T(8,128)(2,1)S(1)}, bf16[4,64,640]{2,1,0:T(8,128)(2,1)S(1)}) custom-call(s32[2]{0:T(128)S(1)} %pad_add_fusion.flags, bf16[64,2560]{1,0:T(8,128)(2,1)S(1)} %collective-permute-done.refs_0_, ...), custom_call_target="tpu_custom_call" | custom-call | flops 100000000 | bytes 1048576 | tf_op jit(solution)/shard_map/project_last/pallas_call | solution.py:190
  59.8 4.0 %collective-permute-start.12 = (bf16[8,64,480]{2,1,0:T(8,128)(2,1)S(1)}, bf16[8,64,480]{2,1,0:T(8,128)(2,1)S(1)}, u32[]{:S(2)}, u32[]{:S(2)}) collective-permute-start(bf16[8,64,480]{2,1,0:T(8,128)(2,1)S(1)} %get-tuple-element.47), channel_id=1, source_target_pairs={{0,1},{1,0},{2,3},{3,2},{4,5},{5,4},{6,7},{7,6},{8,9},{9,8},{10,11... | collective-permute-start | bytes 1474568 | tf_op jit(solution)/shard_map/ppermute | solution.py:461
  65.1 2.1 %collective-permute-start.10 = (bf16[4,64,640]{2,1,0:T(8,128)(2,1)S(1)}, bf16[4,64,640]{2,1,0:T(8,128)(2,1)S(1)}, u32[]{:S(2)}, u32[]{:S(2)}) collective-permute-start(bf16[4,64,640]{2,1,0:T(8,128)(2,1)S(1)} %get-tuple-element.42), channel_id=1, source_target_pairs={{1,2},{3,4},{2,1},{5,6},{4,3},{7,14},{6,5},{15,12},{14,7},{13,10},... | collective-permute-start | bytes 983048 | tf_op jit(solution)/shard_map/ppermute | solution.py:460
  67.2 3.4 %inner.1 = (bf16[8,128,160]{2,1,0:T(8,128)(2,1)S(1)}, f32[8,128,256]{2,1,0:T(8,128)S(1)}, f32[10,128,128]{2,1,0:T(8,128)S(1)}, f32[2,16,128]{2,1,0:T(8,128)S(1)}) custom-call(s32[19]{0:T(128)S(1)} %stack.137.ints, f32[1]{0:T(128)S(6)} %mul.244.factor_ref, f32[64]{0:T(128)S(1)} %reshape.8.band, f32[16,128]{1,0:T(8,128)S(1)} %fusion.1.usable, ...), custom_call_target="tpu_custom_call" | custom-call | flops 10000000 | bytes 100000 | tf_op jit(solution)/shard_map/inner/pallas_call | solution.py:298
  70.6 2.6 %collective-permute-done.11.refs_2_ = bf16[4,64,640]{2,1,0:T(8,128)(2,1)S(1)} collective-permute-done((bf16[4,64,640]{2,1,0:T(8,128)(2,1)S(1)}, bf16[4,64,640]{2,1,0:T(8,128)(2,1)S(1)}, u32[]{:S(2)}, u32[]{:S(2)}) %collective-permute-start.11) | collective-permute-done | bytes 327712 | tf_op jit(solution)/shard_map/ppermute | solution.py:459
  73.1 1.9 %collective-permute-done.10.refs_3_ = bf16[4,64,640]{2,1,0:T(8,128)(2,1)S(1)} collective-permute-done((bf16[4,64,640]{2,1,0:T(8,128)(2,1)S(1)}, bf16[4,64,640]{2,1,0:T(8,128)(2,1)S(1)}, u32[]{:S(2)}, u32[]{:S(2)}) %collective-permute-start.10) | collective-permute-done | bytes 327712 | tf_op jit(solution)/shard_map/ppermute | solution.py:460
  77.2 2.3 %outer.1 = (bf16[4,2,8,1280]{3,2,1,0:T(8,128)(2,1)S(1)}, bf16[4,2,8,1280]{3,2,1,0:T(8,128)(2,1)S(1)}) custom-call(s32[19]{0:T(128)S(1)} %stack.137.ints, f32[1]{0:T(128)S(6)} %mul.244.factor_ref, bf16[8,128,160]{2,1,0:T(8,128)(2,1)S(1)} %get-tuple-element.56.zonal_ref, f32[8,128,256]{2,1,0:T(8,128)S(1)} %get-tuple-element.57.window_ref, ...), custom_call_target="tpu_custom_call" | custom-call | flops 1000000000 | bytes 4194304 | tf_op jit(solution)/shard_map/outer/pallas_call | solution.py:354
  79.4 4.1 %collective-permute-start.15 = (bf16[4,2,8,1280]{3,2,1,0:T(8,128)(2,1)S(1)}, bf16[4,2,8,1280]{3,2,1,0:T(8,128)(2,1)S(1)}, u32[]{:S(2)}, u32[]{:S(2)}) collective-permute-start(bf16[4,2,8,1280]{3,2,1,0:T(8,128)(2,1)S(1)} %get-tuple-element.62), channel_id=1, source_target_pairs={{0,8},{1,136},{8,0},{9,128},{128,9},{129,137},{136,1},{137,129},{2... | collective-permute-start | bytes 491528 | tf_op jit(solution)/shard_map/ppermute | solution.py:471
  83.5 1.9 %collective-permute-start.16 = (bf16[4,2,8,1280]{3,2,1,0:T(8,128)(2,1)S(1)}, bf16[4,2,8,1280]{3,2,1,0:T(8,128)(2,1)S(1)}, u32[]{:S(2)}, u32[]{:S(2)}) collective-permute-start(bf16[4,2,8,1280]{3,2,1,0:T(8,128)(2,1)S(1)} %get-tuple-element.63), channel_id=1, source_target_pairs={{0,0},{1,128},{8,8},{9,136},{128,1},{129,129},{136,9},{137,137},{2... | collective-permute-start | bytes 491528 | tf_op jit(solution)/shard_map/ppermute | solution.py:471
  85.5 2.1 %collective-permute-done.15.far.refs_0_ = bf16[4,2,8,1280]{3,2,1,0:T(8,128)(2,1)S(1)} collective-permute-done((bf16[4,2,8,1280]{3,2,1,0:T(8,128)(2,1)S(1)}, bf16[4,2,8,1280]{3,2,1,0:T(8,128)(2,1)S(1)}, u32[]{:S(2)}, u32[]{:S(2)}) %collective-permute-start.15) | collective-permute-done | bytes 163872 | tf_op jit(solution)/shard_map/ppermute | solution.py:471
  87.6 2.6 %collective-permute-done.16.near.refs_1_ = bf16[4,2,8,1280]{3,2,1,0:T(8,128)(2,1)S(1)} collective-permute-done((bf16[4,2,8,1280]{3,2,1,0:T(8,128)(2,1)S(1)}, bf16[4,2,8,1280]{3,2,1,0:T(8,128)(2,1)S(1)}, u32[]{:S(2)}, u32[]{:S(2)}) %collective-permute-start.16) | collective-permute-done | bytes 163872 | tf_op jit(solution)/shard_map/ppermute | solution.py:471
  90.8 1.4 %collective-permute-start.18 = (bf16[2,2,8,1280]{3,2,1,0:T(8,128)(2,1)S(1)}, bf16[2,2,8,1280]{3,2,1,0:T(8,128)(2,1)S(1)}, u32[]{:S(2)}, u32[]{:S(2)}) collective-permute-start(bf16[2,2,8,1280]{3,2,1,0:T(8,128)(2,1)S(1)} %get-tuple-element.65), channel_id=1, source_target_pairs={{0,2},{2,0},{4,6},{6,4},{1,3},{3,1},{5,7},{7,5},{8,10},{10,8},{12,... | collective-permute-start | bytes 245768 | tf_op jit(solution)/shard_map/ppermute | solution.py:475
  92.2 1.4 %collective-permute-start.19 = (bf16[2,2,8,1280]{3,2,1,0:T(8,128)(2,1)S(1)}, bf16[2,2,8,1280]{3,2,1,0:T(8,128)(2,1)S(1)}, u32[]{:S(2)}, u32[]{:S(2)}) collective-permute-start(bf16[2,2,8,1280]{3,2,1,0:T(8,128)(2,1)S(1)} %get-tuple-element.66), channel_id=1, source_target_pairs={{0,6},{2,4},{4,2},{6,0},{1,7},{3,5},{5,3},{7,1},{8,14},{10,12},{12... | collective-permute-start | bytes 245768 | tf_op jit(solution)/shard_map/ppermute | solution.py:475
  94.0 1.4 %collective-permute-done.17.refs_2_ = bf16[2,2,8,1280]{3,2,1,0:T(8,128)(2,1)S(1)} collective-permute-done((bf16[2,2,8,1280]{3,2,1,0:T(8,128)(2,1)S(1)}, bf16[2,2,8,1280]{3,2,1,0:T(8,128)(2,1)S(1)}, u32[]{:S(2)}, u32[]{:S(2)}) %collective-permute-start.17) | collective-permute-done | bytes 81952 | tf_op jit(solution)/shard_map/ppermute | solution.py:475
  (47 shorter events, 21.0 us)
Async XLA Ops:
  1.4 16.4 %collective-permute-start = (bf16[64,2560]{1,0:T(8,128)(2,1)S(1)}, bf16[64,2560]{1,0:T(8,128)(2,1)S(1)}, u32[]{:S(2)}, u32[]{:S(2)}) collective-permute-start(bf16[64,2560]{1,0:T(8,128)(2,1)S(1)} %normalize.1), channel_id=1, source_target_pairs={{0,0},{1,65},{2,16},{3,81},{4,32},{5,97},{6,48},{7,113},{8,64},{9,... | collective-permute-start | bytes 983048 | tf_op jit(solution)/shard_map/ppermute | solution.py:420
  17.8 38.7 %collective-permute-start.9 = (bf16[480,2560]{1,0:T(8,128)(2,1)}, bf16[480,2560]{1,0:T(8,128)(2,1)S(1)}, u32[]{:S(2)}, u32[]{:S(2)}) collective-permute-start(bf16[480,2560]{1,0:T(8,128)(2,1)} %bitcast.38), channel_id=1, source_target_pairs={{0,128},{1,137},{128,8},{129,1},{8,136},{9,129},{136,0},{137,9},{2... | collective-permute-start | bytes 7372808 | tf_op jit(solution)/shard_map/ppermute | solution.py:446
  17.9 12.3 %collective-permute-start.2 = (bf16[64,2560]{1,0:T(8,128)(2,1)S(1)}, bf16[64,2560]{1,0:T(8,128)(2,1)S(1)}, u32[]{:S(2)}, u32[]{:S(2)}) collective-permute-start(bf16[64,2560]{1,0:T(8,128)(2,1)S(1)} %collective-permute-done.refs_0_), channel_id=1, source_target_pairs={{0,1},{1,0},{2,3},{3,2},{4,5},{5,4},{6,7},{7,6},{8,9},{9,8},{10,11... | collective-permute-start | bytes 983048 | tf_op jit(solution)/shard_map/ppermute | solution.py:448
  26.6 7.6 %collective-permute-start.1 = (bf16[64,2560]{1,0:T(8,128)(2,1)S(1)}, bf16[64,2560]{1,0:T(8,128)(2,1)S(1)}, u32[]{:S(2)}, u32[]{:S(2)}) collective-permute-start(bf16[64,2560]{1,0:T(8,128)(2,1)S(1)} %collective-permute-done.refs_0_), channel_id=1, source_target_pairs={{0,16},{1,113},{16,32},{17,1},{32,48},{33,17},{48,64},{49,33},{64,... | collective-permute-start | bytes 983048 | tf_op jit(solution)/shard_map/ppermute | solution.py:451
  30.2 7.5 %collective-permute-start.3 = (bf16[64,2560]{1,0:T(8,128)(2,1)S(1)}, bf16[64,2560]{1,0:T(8,128)(2,1)S(1)}, u32[]{:S(2)}, u32[]{:S(2)}) collective-permute-start(bf16[64,2560]{1,0:T(8,128)(2,1)S(1)} %collective-permute-done.2), channel_id=1, source_target_pairs={{0,16},{1,113},{16,32},{17,1},{32,48},{33,17},{48,64},{49,33},{64,... | collective-permute-start | bytes 983048 | tf_op jit(solution)/shard_map/ppermute | solution.py:454
  34.3 7.4 %collective-permute-start.4 = (bf16[64,2560]{1,0:T(8,128)(2,1)S(1)}, bf16[64,2560]{1,0:T(8,128)(2,1)S(1)}, u32[]{:S(2)}, u32[]{:S(2)}) collective-permute-start(bf16[64,2560]{1,0:T(8,128)(2,1)S(1)} %collective-permute-done.1.refs_1_), channel_id=1, source_target_pairs={{0,16},{1,113},{16,32},{17,1},{32,48},{33,17},{48,64},{49,33},{64,... | collective-permute-start | bytes 983048 | tf_op jit(solution)/shard_map/ppermute | solution.py:451
  37.8 7.4 %collective-permute-start.5 = (bf16[64,2560]{1,0:T(8,128)(2,1)S(1)}, bf16[64,2560]{1,0:T(8,128)(2,1)S(1)}, u32[]{:S(2)}, u32[]{:S(2)}) collective-permute-start(bf16[64,2560]{1,0:T(8,128)(2,1)S(1)} %collective-permute-done.3.refs_2_), channel_id=1, source_target_pairs={{0,16},{1,113},{16,32},{17,1},{32,48},{33,17},{48,64},{49,33},{64,... | collective-permute-start | bytes 983048 | tf_op jit(solution)/shard_map/ppermute | solution.py:454
  41.7 7.4 %collective-permute-start.6 = (bf16[64,2560]{1,0:T(8,128)(2,1)S(1)}, bf16[64,2560]{1,0:T(8,128)(2,1)S(1)}, u32[]{:S(2)}, u32[]{:S(2)}) collective-permute-start(bf16[64,2560]{1,0:T(8,128)(2,1)S(1)} %collective-permute-done.4.refs_3_), channel_id=1, source_target_pairs={{0,16},{1,113},{16,32},{17,1},{32,48},{33,17},{48,64},{49,33},{64,... | collective-permute-start | bytes 983048 | tf_op jit(solution)/shard_map/ppermute | solution.py:451
  45.2 10.3 %collective-permute-start.7 = (bf16[64,2560]{1,0:T(8,128)(2,1)S(1)}, bf16[64,2560]{1,0:T(8,128)(2,1)S(1)}, u32[]{:S(2)}, u32[]{:S(2)}) collective-permute-start(bf16[64,2560]{1,0:T(8,128)(2,1)S(1)} %collective-permute-done.5.refs_4_), channel_id=1, source_target_pairs={{0,16},{1,113},{16,32},{17,1},{32,48},{33,17},{48,64},{49,33},{64,... | collective-permute-start | bytes 983048 | tf_op jit(solution)/shard_map/ppermute | solution.py:454
  49.1 7.4 %collective-permute-start.8 = (bf16[64,2560]{1,0:T(8,128)(2,1)S(1)}, bf16[64,2560]{1,0:T(8,128)(2,1)S(1)}, u32[]{:S(2)}, u32[]{:S(2)}) collective-permute-start(bf16[64,2560]{1,0:T(8,128)(2,1)S(1)} %collective-permute-done.6.refs_5_), channel_id=1, source_target_pairs={{0,16},{1,113},{16,32},{17,1},{32,48},{33,17},{48,64},{49,33},{64,... | collective-permute-start | bytes 983048 | tf_op jit(solution)/shard_map/ppermute | solution.py:451
  59.8 7.4 %collective-permute-start.12 = (bf16[8,64,480]{2,1,0:T(8,128)(2,1)S(1)}, bf16[8,64,480]{2,1,0:T(8,128)(2,1)S(1)}, u32[]{:S(2)}, u32[]{:S(2)}) collective-permute-start(bf16[8,64,480]{2,1,0:T(8,128)(2,1)S(1)} %get-tuple-element.47), channel_id=1, source_target_pairs={{0,1},{1,0},{2,3},{3,2},{4,5},{5,4},{6,7},{7,6},{8,9},{9,8},{10,11... | collective-permute-start | bytes 1474568 | tf_op jit(solution)/shard_map/ppermute | solution.py:461
  63.8 9.4 %collective-permute-start.11 = (bf16[4,64,640]{2,1,0:T(8,128)(2,1)S(1)}, bf16[4,64,640]{2,1,0:T(8,128)(2,1)S(1)}, u32[]{:S(2)}, u32[]{:S(2)}) collective-permute-start(bf16[4,64,640]{2,1,0:T(8,128)(2,1)S(1)} %get-tuple-element.43), channel_id=1, source_target_pairs={{0,2},{2,4},{3,1},{4,6},{5,3},{6,14},{7,5},{14,12},{15,7},{12,10},... | collective-permute-start | bytes 983048 | tf_op jit(solution)/shard_map/ppermute | solution.py:459
  65.1 10.0 %collective-permute-start.10 = (bf16[4,64,640]{2,1,0:T(8,128)(2,1)S(1)}, bf16[4,64,640]{2,1,0:T(8,128)(2,1)S(1)}, u32[]{:S(2)}, u32[]{:S(2)}) collective-permute-start(bf16[4,64,640]{2,1,0:T(8,128)(2,1)S(1)} %get-tuple-element.42), channel_id=1, source_target_pairs={{1,2},{3,4},{2,1},{5,6},{4,3},{7,14},{6,5},{15,12},{14,7},{13,10},... | collective-permute-start | bytes 983048 | tf_op jit(solution)/shard_map/ppermute | solution.py:460
  75.1 1.6 %collective-permute-start.14 = (bf16[4,64,640]{2,1,0:T(8,128)(2,1)S(1)}, bf16[4,64,640]{2,1,0:T(8,128)(2,1)S(1)}, u32[]{:S(2)}, u32[]{:S(2)}) collective-permute-start(bf16[4,64,640]{2,1,0:T(8,128)(2,1)S(1)} %collective-permute-done.10.refs_3_), channel_id=1, source_target_pairs={{0,1},{1,0},{2,3},{3,2},{4,5},{5,4},{6,7},{7,6},{8,9},{9,8},{10,11... | collective-permute-start | bytes 983048 | tf_op jit(solution)/shard_map/ppermute | solution.py:467
  75.1 2.1 %collective-permute-start.13 = (bf16[4,64,640]{2,1,0:T(8,128)(2,1)S(1)}, bf16[4,64,640]{2,1,0:T(8,128)(2,1)S(1)}, u32[]{:S(2)}, u32[]{:S(2)}) collective-permute-start(bf16[4,64,640]{2,1,0:T(8,128)(2,1)S(1)} %collective-permute-done.11.refs_2_), channel_id=1, source_target_pairs={{0,1},{1,0},{2,3},{3,2},{4,5},{5,4},{6,7},{7,6},{8,9},{9,8},{10,11... | collective-permute-start | bytes 983048 | tf_op jit(solution)/shard_map/ppermute | solution.py:467
  79.4 8.2 %collective-permute-start.15 = (bf16[4,2,8,1280]{3,2,1,0:T(8,128)(2,1)S(1)}, bf16[4,2,8,1280]{3,2,1,0:T(8,128)(2,1)S(1)}, u32[]{:S(2)}, u32[]{:S(2)}) collective-permute-start(bf16[4,2,8,1280]{3,2,1,0:T(8,128)(2,1)S(1)} %get-tuple-element.62), channel_id=1, source_target_pairs={{0,8},{1,136},{8,0},{9,128},{128,9},{129,137},{136,1},{137,129},{2... | collective-permute-start | bytes 491528 | tf_op jit(solution)/shard_map/ppermute | solution.py:471
  83.5 6.6 %collective-permute-start.16 = (bf16[4,2,8,1280]{3,2,1,0:T(8,128)(2,1)S(1)}, bf16[4,2,8,1280]{3,2,1,0:T(8,128)(2,1)S(1)}, u32[]{:S(2)}, u32[]{:S(2)}) collective-permute-start(bf16[4,2,8,1280]{3,2,1,0:T(8,128)(2,1)S(1)} %get-tuple-element.63), channel_id=1, source_target_pairs={{0,0},{1,128},{8,8},{9,136},{128,1},{129,129},{136,9},{137,137},{2... | collective-permute-start | bytes 491528 | tf_op jit(solution)/shard_map/ppermute | solution.py:471
  90.2 5.2 %collective-permute-start.17 = (bf16[2,2,8,1280]{3,2,1,0:T(8,128)(2,1)S(1)}, bf16[2,2,8,1280]{3,2,1,0:T(8,128)(2,1)S(1)}, u32[]{:S(2)}, u32[]{:S(2)}) collective-permute-start(bf16[2,2,8,1280]{3,2,1,0:T(8,128)(2,1)S(1)} %get-tuple-element.64), channel_id=1, source_target_pairs={{0,4},{2,6},{4,0},{6,2},{1,5},{3,7},{5,1},{7,3},{8,12},{10,14},{12... | collective-permute-start | bytes 245768 | tf_op jit(solution)/shard_map/ppermute | solution.py:475
  90.8 6.0 %collective-permute-start.18 = (bf16[2,2,8,1280]{3,2,1,0:T(8,128)(2,1)S(1)}, bf16[2,2,8,1280]{3,2,1,0:T(8,128)(2,1)S(1)}, u32[]{:S(2)}, u32[]{:S(2)}) collective-permute-start(bf16[2,2,8,1280]{3,2,1,0:T(8,128)(2,1)S(1)} %get-tuple-element.65), channel_id=1, source_target_pairs={{0,2},{2,0},{4,6},{6,4},{1,3},{3,1},{5,7},{7,5},{8,10},{10,8},{12,... | collective-permute-start | bytes 245768 | tf_op jit(solution)/shard_map/ppermute | solution.py:475
  92.2 5.4 %collective-permute-start.19 = (bf16[2,2,8,1280]{3,2,1,0:T(8,128)(2,1)S(1)}, bf16[2,2,8,1280]{3,2,1,0:T(8,128)(2,1)S(1)}, u32[]{:S(2)}, u32[]{:S(2)}) collective-permute-start(bf16[2,2,8,1280]{3,2,1,0:T(8,128)(2,1)S(1)} %get-tuple-element.66), channel_id=1, source_target_pairs={{0,6},{2,4},{4,2},{6,0},{1,7},{3,5},{5,3},{7,1},{8,14},{10,12},{12... | collective-permute-start | bytes 245768 | tf_op jit(solution)/shard_map/ppermute | solution.py:475
  93.5 5.6 %collective-permute-start.20 = (bf16[4,2,8,1280]{3,2,1,0:T(8,128)(2,1)S(1)}, bf16[4,2,8,1280]{3,2,1,0:T(8,128)(2,1)S(1)}, u32[]{:S(2)}, u32[]{:S(2)}) collective-permute-start(bf16[4,2,8,1280]{3,2,1,0:T(8,128)(2,1)S(1)} %collective-permute-done.15.far.refs_0_), channel_id=1, source_target_pairs={{0,1},{1,0},{2,3},{3,2},{4,5},{5,4},{6,7},{7,6},{8,9},{9,8},{10,11... | collective-permute-start | bytes 491528 | tf_op jit(solution)/shard_map/ppermute | solution.py:476
  93.5 5.6 %collective-permute-start.21 = (bf16[4,2,8,1280]{3,2,1,0:T(8,128)(2,1)S(1)}, bf16[4,2,8,1280]{3,2,1,0:T(8,128)(2,1)S(1)}, u32[]{:S(2)}, u32[]{:S(2)}) collective-permute-start(bf16[4,2,8,1280]{3,2,1,0:T(8,128)(2,1)S(1)} %collective-permute-done.16.near.refs_1_), channel_id=1, source_target_pairs={{0,1},{1,0},{2,3},{3,2},{4,5},{5,4},{6,7},{7,6},{8,9},{9,8},{10,11... | collective-permute-start | bytes 491528 | tf_op jit(solution)/shard_map/ppermute | solution.py:476
  95.4 2.8 %collective-permute-start.22 = (bf16[2,2,8,1280]{3,2,1,0:T(8,128)(2,1)S(1)}, bf16[2,2,8,1280]{3,2,1,0:T(8,128)(2,1)S(1)}, u32[]{:S(2)}, u32[]{:S(2)}) collective-permute-start(bf16[2,2,8,1280]{3,2,1,0:T(8,128)(2,1)S(1)} %collective-permute-done.17.refs_2_), channel_id=1, source_target_pairs={{0,1},{1,0},{2,3},{3,2},{4,5},{5,4},{6,7},{7,6},{8,9},{9,8},{10,11... | collective-permute-start | bytes 245768 | tf_op jit(solution)/shard_map/ppermute | solution.py:476
  97.5 1.6 %collective-permute-start.24 = (bf16[2,2,8,1280]{3,2,1,0:T(8,128)(2,1)S(1)}, bf16[2,2,8,1280]{3,2,1,0:T(8,128)(2,1)S(1)}, u32[]{:S(2)}, u32[]{:S(2)}) collective-permute-start(bf16[2,2,8,1280]{3,2,1,0:T(8,128)(2,1)S(1)} %collective-permute-done.19.refs_4_), channel_id=1, source_target_pairs={{0,1},{1,0},{2,3},{3,2},{4,5},{5,4},{6,7},{7,6},{8,9},{9,8},{10,11... | collective-permute-start | bytes 245768 | tf_op jit(solution)/shard_map/ppermute | solution.py:476
  (3 other events, 4.1 us)
